TPU v7x, 32 devices: a whole 2x2x4 slice. The times are simulated.
32 devices in a mesh: clip: 4 (over y, x), feat: 8 (over z, core).
Axes of the slice: x: 2, y: 2, z: 4, core: 2. Of those that a mesh axis runs over, the one named last changes fastest.
Arguments:
- embeds: float32 [4096, 1152], P('clip', 'feat'), may hold values from -6 to 6
- frequencies: float32 [1152, 5120], P('clip', 'feat'), may hold values from -0.5 to 0.5
- phases: float32 [5120], P('feat'), may hold values from -3.140625 to 3.140625
- weights: float32 [5120, 128], P('feat', 'clip'), may hold values from -6 to 6
- labels: int32 [4096, 128], P('clip'), may hold values 0 or 1
Outputs:
- trained: float32 [5120, 128], P('feat', 'clip')
- scores: float32 [4096, 128], P('clip', 'feat')
All inputs are finite; a program needn't handle non-finite values. No bound on the sum of `labels` on one device may be relied on, other than what follows from the above.
Results may differ from a plain program's by a relative error of at most 0.0055.
Values may be sent and summed in bfloat16 or wider, within the bound.
No kernel may reach another device: no remote copies, remote signals or barrier semaphores. Data moves between devices by JAX's collectives and lax.ppermute only.
A program may use at most 64 MiB of HBM per device.

v0:
```python
import math

import jax
import jax.numpy as jnp
from jax import lax
from jax.sharding import PartitionSpec as P

STEPS = 2


def summed_logits(partial_value):
    return lax.psum_scatter(partial_value, "feat", scatter_dimension=1, tiled=True)


def per_device(embeds, frequencies, phases, weights, labels):
    freq_full = lax.all_gather(frequencies, "clip", axis=0, tiled=True)
    feat_count = frequencies.shape[1]
    total_features = feat_count * lax.axis_size("feat")
    out_width = weights.shape[1] * lax.axis_size("clip")
    share_width = out_width // lax.axis_size("feat")
    angles = jnp.dot(
        lax.all_gather(embeds, "feat", axis=1, tiled=True),
        freq_full,
        precision=lax.Precision.HIGHEST,
        preferred_element_type=jnp.float32,
    )
    feature_scale = math.sqrt(2.0 / total_features)
    phi = (feature_scale * jnp.cos(angles + phases[None, :])).astype(jnp.bfloat16)
    full_weights = lax.all_gather(weights, "clip", axis=1, tiled=True)
    own_weights = weights
    weight_half = full_weights.astype(jnp.bfloat16)
    targets = labels.astype(jnp.float32)
    feat_start = lax.axis_index("feat") * share_width
    for step in range(STEPS):
        partial_value = jnp.dot(phi, weight_half, preferred_element_type=jnp.float32)
        summed = summed_logits(partial_value)
        target_share = lax.dynamic_slice_in_dim(targets, feat_start, share_width, 1)
        residual_share = (jax.nn.sigmoid(summed) - target_share).astype(jnp.bfloat16)
        residual = lax.all_gather(residual_share, "feat", axis=1, tiled=True)
        grad_part = lax.dot_general(
            phi, residual, (((0,), (0,)), ((), ())), preferred_element_type=jnp.float32
        )
        grad_own = lax.psum_scatter(grad_part, "clip", scatter_dimension=1, tiled=True)
        own_weights = own_weights - 0.25 * grad_own
        weight_half = lax.all_gather(own_weights.astype(jnp.bfloat16), "clip", axis=1, tiled=True)
    partial_value = jnp.dot(phi, weight_half, preferred_element_type=jnp.float32)
    summed = summed_logits(partial_value)
    return (own_weights, summed)


def solution(mesh):
    placed = (P("clip", "feat"), P("clip", "feat"), P("feat"), P("feat", "clip"), P("clip", None))
    return jax.shard_map(
        per_device,
        mesh=mesh,
        in_specs=placed,
        out_specs=(P("feat", "clip"), P("clip", "feat")),
        check_vma=False,
    )
```

profile of v0, /device:TPU:0, one launch (start us, length us, event | category | flops | bytes accessed | tf_op | source)
XLA Modules:
  0.0 332.4 jit_solution(8276116585995556720)
XLA Ops:
  7.2 0.0 copy-start
  7.2 0.0 copy-start.1
  7.2 0.0 copy-start.3
  7.2 0.0 all-gather.5.cloned.1.call-start
  7.2 0.7 all-gather.5.cloned.1.call-update
  7.9 0.0 all-gather.3.cloned.1.call-start
  8.0 0.7 all-gather.3.cloned.1.call-update
  8.7 0.0 reduce-scatter.16.cloned.1.call-start
  8.7 0.0 copy-done.1
  8.8 10.1 %all_gather.23 = bf16[640,128]{0,1:T(8,128)(2,1)S(1)} all-gather(bf16[640,32]{0,1:T(8,128)(2,1)S(1)} %convert), channel_id=1, replica_groups=mesh['clip'=4,'feat'=8] {'clip'}, dimensions={1}, use_global_device_ids=true | all-gather | bytes 204800 | tf_op jit(solution)/shard_map/all_gather | solution.py:29
  18.8 36.2 %all-gather.5.cloned.1.call-done = f32[1152,640]{1,0:T(8,128)} async-done(((f32[288,640]{1,0:T(8,128)}), f32[1152,640]{1,0:T(8,128)}) %all-gather.5.cloned.1.call-update) | async-done | bytes 2949136 | tf_op jit(solution)/shard_map/all_gather | solution.py:16
  55.0 53.4 %all-gather.3.cloned.1.call-done = f32[1024,1152]{0,1:T(8,128)} async-done(((f32[1024,144]{0,1:T(8,128)}), f32[1024,1152]{0,1:T(8,128)}) %all-gather.3.cloned.1.call-update) | async-done | bytes 4718608 | tf_op jit(solution)/shard_map/all_gather | solution.py:22
  108.3 0.0 copy-done.3
  108.3 23.3 %multiply_convert_fusion = bf16[1024,640]{1,0:T(8,128)(2,1)S(1)} fusion(f32[1024,1152]{0,1:T(8,128)} %all-gather.3.cloned.1.call-done, f32[1152,640]{1,0:T(8,128)} %all-gather.5.cloned.1.call-done, f32[640]{0:T(1024)S(1)} %copy-done.3), kind=kOutput, calls=%fused_computation | convolution fusion | flops 9061662720 | bytes 8980992 | tf_op jit(solution)/shard_map/dot_general | solution.py:21
  131.7 1.3 convolution_bitcast_fusion.1
  133.0 0.0 reduce-scatter.16.cloned.1.call-update
  133.0 0.2 reduce-scatter.10.cloned.1.call-start
  133.3 0.0 copy-done
  133.3 0.2 constant_dynamic-slice_fusion
  133.5 0.2 copy.20
  133.7 29.3 %reduce-scatter.16.cloned.1.call-done = f32[16,1024]{1,0:T(8,128)} async-done(((f32[128,1024]{1,0:T(8,128)}), f32[16,1024]{1,0:T(8,128)}) %reduce-scatter.16.cloned.1.call-update) | async-done | bytes 65552
  163.0 0.9 fusion.9
  163.8 14.2 %all_gather.24 = bf16[1024,128]{0,1:T(8,128)(2,1)S(1)} all-gather(bf16[1024,16]{0,1:T(8,128)(2,1)S(1)} %fusion.9), channel_id=1, replica_groups=mesh['clip'=4,'feat'=8] {'feat'}, dimensions={1}, use_global_device_ids=true | all-gather | bytes 294912 | tf_op jit(solution)/shard_map/all_gather | solution.py:39
  178.0 1.1 fusion.14
  179.1 0.0 reduce-scatter.10.cloned.1.call-update
  179.2 0.0 reduce-scatter.18.cloned.1.call-start
  179.2 22.6 %reduce-scatter.10.cloned.1.call-done = f32[640,32]{0,1:T(8,128)} async-done(((f32[640,128]{0,1:T(8,128)}), f32[640,32]{0,1:T(8,128)}) %reduce-scatter.10.cloned.1.call-update) | async-done | bytes 81936 | tf_op jit(solution)/shard_map/reduce_scatter | solution.py:43
  201.8 0.9 fusion.11
  202.7 8.8 %all_gather.25 = bf16[640,128]{0,1:T(8,128)(2,1)S(1)} all-gather(bf16[640,32]{0,1:T(8,128)(2,1)S(1)} %fusion.11), channel_id=1, replica_groups=mesh['clip'=4,'feat'=8] {'clip'}, dimensions={1}, use_global_device_ids=true | all-gather | bytes 204800 | tf_op jit(solution)/shard_map/all_gather | solution.py:45
  211.5 1.3 convolution_bitcast_fusion
  212.8 0.0 reduce-scatter.18.cloned.1.call-update
  212.8 0.0 copy-start.2
  212.8 0.0 reduce-scatter.12.cloned.1.call-start
  212.9 31.0 %reduce-scatter.18.cloned.1.call-done = f32[16,1024]{1,0:T(8,128)} async-done(((f32[128,1024]{1,0:T(8,128)}), f32[16,1024]{1,0:T(8,128)}) %reduce-scatter.18.cloned.1.call-update) | async-done | bytes 65552
  243.9 0.9 fusion.10
  244.8 14.2 %all_gather.26 = bf16[1024,128]{0,1:T(8,128)(2,1)S(1)} all-gather(bf16[1024,16]{0,1:T(8,128)(2,1)S(1)} %fusion.10), channel_id=1, replica_groups=mesh['clip'=4,'feat'=8] {'feat'}, dimensions={1}, use_global_device_ids=true | all-gather | bytes 294912 | tf_op jit(solution)/shard_map/all_gather | solution.py:39
  259.0 1.1 fusion.15
  260.1 0.0 reduce-scatter.12.cloned.1.call-update
  260.1 0.0 reduce-scatter.14.cloned.1.call-start
  260.1 22.6 %reduce-scatter.12.cloned.1.call-done = f32[640,32]{0,1:T(8,128)} async-done(((f32[640,128]{0,1:T(8,128)}), f32[640,32]{0,1:T(8,128)}) %reduce-scatter.12.cloned.1.call-update) | async-done | bytes 81936 | tf_op jit(solution)/shard_map/reduce_scatter | solution.py:43
  282.8 0.0 copy-done.2
  282.8 1.5 fusion.12
  284.3 8.7 %all_gather.27 = bf16[640,128]{0,1:T(8,128)(2,1)S(1)} all-gather(bf16[640,32]{0,1:T(8,128)(2,1)S(1)} %get-tuple-element.2), channel_id=1, replica_groups=mesh['clip'=4,'feat'=8] {'clip'}, dimensions={1}, use_global_device_ids=true | all-gather | bytes 204800 | tf_op jit(solution)/shard_map/all_gather | solution.py:45
  293.1 1.3 fusion.13
  294.4 0.0 reduce-scatter.14.cloned.1.call-update
  294.4 31.1 %reduce-scatter.14.cloned.1.call-done = f32[1024,16]{0,1:T(8,128)} async-done(((f32[1024,128]{0,1:T(8,128)}), f32[1024,16]{0,1:T(8,128)}) %reduce-scatter.14.cloned.1.call-update) | async-done | bytes 65552 | tf_op jit(solution)/shard_map/reduce_scatter | solution.py:12
  (1 shorter events, 0.0 us)
Async XLA Ops:
  7.2 126.1 %copy-start = (s32[1024,128]{1,0:T(8,128)S(1)}, s32[1024,128]{1,0:T(8,128)}, u32[]{:S(2)}) copy-start(s32[1024,128]{1,0:T(8,128)} %param.9) | copy-start | bytes 1572868
  7.2 1.6 copy-start.1
  7.2 101.2 %copy-start.3 = (f32[640]{0:T(1024)S(1)}, f32[640]{0:T(1024)}, u32[]{:S(2)}) copy-start(f32[640]{0:T(1024)} %param.7) | copy-start | bytes 7684
  7.2 47.8 %all-gather.5.cloned.1.call-start = ((), (), s32[]{:S(2)}) async-start(), calls=%async_computation.6 | async-start | bytes 3686400 | tf_op jit(solution)/shard_map/all_gather | solution.py:16
  7.9 100.4 %all-gather.3.cloned.1.call-start = ((), (), s32[]{:S(2)}) async-start(), calls=%async_computation.5 | async-start | bytes 5308416 | tf_op jit(solution)/shard_map/all_gather | solution.py:22
  8.7 154.3 %reduce-scatter.16.cloned.1.call-start = ((), (), s32[]{:S(2)}) async-start(), calls=%async_computation.10 | async-start | bytes 589824
  133.0 68.7 %reduce-scatter.10.cloned.1.call-start = ((), (), s32[]{:S(2)}) async-start(), calls=%async_computation.7 | async-start | bytes 409600 | tf_op jit(solution)/shard_map/reduce_scatter | solution.py:43
  179.2 64.7 %reduce-scatter.18.cloned.1.call-start = ((), (), s32[]{:S(2)}) async-start(), calls=%async_computation.11 | async-start | bytes 589824
  212.8 69.9 %copy-start.2 = (f32[640,32]{0,1:T(8,128)S(1)}, f32[640,32]{0,1:T(8,128)}, u32[]{:S(2)}) copy-start(f32[640,32]{0,1:T(8,128)} %reduce-scatter.10.cloned.1.call-done) | copy-start | bytes 245764
  212.8 69.9 %reduce-scatter.12.cloned.1.call-start = ((), (), s32[]{:S(2)}) async-start(), calls=%async_computation.8 | async-start | bytes 409600 | tf_op jit(solution)/shard_map/reduce_scatter | solution.py:43
  260.1 65.4 %reduce-scatter.14.cloned.1.call-start = ((), (), s32[]{:S(2)}) async-start(), calls=%async_computation.9 | async-start | bytes 589824 | tf_op jit(solution)/shard_map/reduce_scatter | solution.py:12
Sparse Core Ops, SparseCore 0:
  9.9 45.0 all-gather.4
  56.6 51.6 all-gather.2
  133.2 29.7 reduce-scatter.15
  179.3 22.4 reduce-scatter.9
  213.0 30.9 reduce-scatter.17
  260.2 22.5 reduce-scatter.11
  294.5 30.9 reduce-scatter.13
where the time goes:
time: 333 us; the launch traced here: 332 us
  waiting for transfers between devices  228 us (68%)
  blocking collectives  55.9 us (17%)
  matrix products  29.6 us (9%)
  between operations  14.2 us (4%)
  other arithmetic  4.17 us (1%)
    unnamed x9, waiting for transfers between devices  61.8 us
    all_gather x1, waiting for transfers between devices, per_device(): lax.all_gather(embeds, 'feat', axis=1, tiled=True)  53.4 us
    reduce_scatter x2, waiting for transfers between devices, per_device(): lax.psum_scatter(grad_part, 'clip', scatter_dimension=1, tiled=True)  45.2 us
    all_gather x1, waiting for transfers between devices, per_device(): freq_full = lax.all_gather(frequencies, 'clip', axis=0, tiled=True)  36.2 us
    reduce_scatter x1, waiting for transfers between devices, summed_logits(): lax.psum_scatter(partial_value, 'feat', scatter_dimension=1, tiled=True)  31.1 us
    all_gather x2, blocking collectives, per_device(): residual = lax.all_gather(residual_share, 'feat', axis=1, tiled=True)  28.4 us
    dot_general x1, matrix products, per_device(): jnp.dot(lax.all_gather(embeds, 'feat', axis=1, tiled=True), freq_full, pr...  23.3 us
    all_gather x2, blocking collectives, per_device(): lax.all_gather(own_weights.astype(jnp.bfloat16), 'clip', axis=1, tiled=True)  17.5 us
  transfers between devices with their start and end apart: 7, of which 7 were waited for; matrix products, arithmetic and copies ran while one was open for 0% of the time, Pallas kernels for 0%

commit v1 on v0

v1 whole, which is shorter than its diff:
```python
import math

import jax
import jax.numpy as jnp
from jax import lax
from jax.sharding import PartitionSpec as P

STEPS = 2
EMBED_BOUND = 6.0
FREQ_BOUND = 0.5
CODE_MAX = 32766.0
COS_TURNS = (
    0.9999999890590243,
    -19.739204499454,
    64.93911745989858,
    -85.45013953092679,
    60.16763095123224,
    -25.967599249288032,
    6.528658162158786,
)


def encode(x, bound):
    return jnp.round(x * (CODE_MAX / bound)).astype(jnp.int16)


def split(code):
    wide = code.astype(jnp.int32)
    high = (wide + 128) & ~255
    return high.astype(jnp.bfloat16), (wide - high).astype(jnp.bfloat16)


def folded_ring(n):
    return list(range(0, n, 2)) + list(range(1, n, 2))[::-1]


def core_swap(x):
    n = lax.axis_size("feat")
    return lax.ppermute(x, "feat", [(i, i ^ 1) for i in range(n)])


def line_swap(x, k):
    n = lax.axis_size("feat")
    return lax.ppermute(x, "feat", [(i, i ^ (2 * k)) for i in range(n)])


def clip_swap(x, k):
    n = lax.axis_size("clip")
    return lax.ppermute(x, "clip", [(i, i ^ k) for i in range(n)])


def gather_line(x):
    n = lax.axis_size("feat") // 2
    order = folded_ring(n)
    ring = [(order[i], order[(i + 1) % n]) for i in range(n)]
    perm = [(2 * a + c, 2 * b + c) for a, b in ring for c in range(2)]
    where = [0] * n
    for i, place in enumerate(order):
        where[place] = i
    mine = jnp.asarray(where)[lax.axis_index("feat") // 2]
    found = [(lax.axis_index("feat") // 2, x)]
    for step in range(1, n):
        x = lax.ppermute(x, "feat", perm)
        found.append((jnp.asarray(order)[(mine - step) % n], x))
    return found


def logits_share(partial_value, block):
    lines = lax.axis_size("feat") // 2
    parts = partial_value.reshape(lines, 2, block, -1)
    there = core_swap(parts[:, 1].astype(jnp.bfloat16))
    both = parts[:, 0] + there.astype(jnp.float32)
    half = both.astype(jnp.bfloat16)
    total = both[0]
    for k in range(1, lines):
        total = total + line_swap(half[k], k).astype(jnp.float32)
    return total


def gather_share(share):
    lines = lax.axis_size("feat") // 2
    own = jnp.stack([share] + [line_swap(share, k) for k in range(1, lines)])
    return jnp.stack([own, core_swap(own)], axis=1).reshape(-1, share.shape[-1])


def per_device(embeds, frequencies, phases, weights, labels):
    n_feat, n_clip = lax.axis_size("feat"), lax.axis_size("clip")
    feat, clip = lax.axis_index("feat"), lax.axis_index("clip")
    core = feat % 2
    columns = embeds.shape[1]
    slab, features = frequencies.shape
    total_features = features * n_feat
    outputs = labels.shape[1]
    block = outputs // n_feat

    freq_code = encode(frequencies, FREQ_BOUND)
    embed_code = encode(embeds.T, EMBED_BOUND)
    freq_all = jnp.zeros((n_clip * slab, features), jnp.int16)
    for k in range(n_clip):
        piece = freq_code if k == 0 else clip_swap(freq_code, k)
        freq_all = lax.dynamic_update_slice_in_dim(freq_all, piece, (clip ^ k) * slab, 0)
    embed_all = jnp.zeros((n_feat * columns, embeds.shape[0]), jnp.int16)
    for place, piece in gather_line(embed_code):
        embed_all = lax.dynamic_update_slice_in_dim(embed_all, piece, (2 * place + core) * columns, 0)
        embed_all = lax.dynamic_update_slice_in_dim(
            embed_all, core_swap(piece), (2 * place + 1 - core) * columns, 0
        )

    weights_t = weights.T
    by_clip = jnp.zeros((n_clip, weights_t.shape[0], features), jnp.float32)
    for k in range(n_clip):
        piece = weights_t if k == 0 else clip_swap(weights_t, k)
        by_clip = lax.dynamic_update_slice_in_dim(by_clip, piece[None], clip ^ k, 0)
    by_block = by_clip.reshape(n_feat, block, features)
    beta = jnp.concatenate(
        [lax.dynamic_index_in_dim(by_block, feat ^ b, 0, keepdims=False) for b in range(n_feat)]
    )
    targets = lax.dynamic_slice_in_dim(labels.T, feat * block, block, 0).astype(jnp.float32)

    def dot0(a, b):
        return lax.dot_general(a, b, (((0,), (0,)), ((), ())), preferred_element_type=jnp.float32)

    embed_high, embed_low = split(embed_all)
    freq_high, freq_low = split(freq_all)
    product = dot0(embed_high, freq_high) + (dot0(embed_high, freq_low) + dot0(embed_low, freq_high))
    per_turn = EMBED_BOUND * FREQ_BOUND / (CODE_MAX * CODE_MAX * 2.0 * math.pi)
    turns = product * per_turn + (phases * (0.5 / math.pi))[None, :]
    turns = turns - jnp.round(turns)
    square = turns * turns
    feature_scale = math.sqrt(2.0 / total_features)
    cosine = jnp.full_like(square, COS_TURNS[-1] * feature_scale)
    for coefficient in COS_TURNS[-2::-1]:
        cosine = cosine * square + coefficient * feature_scale
    phi = cosine.astype(jnp.bfloat16)

    def logits_of(beta):
        partial_value = lax.dot_general(
            beta.astype(jnp.bfloat16), phi, (((1,), (1,)), ((), ())), preferred_element_type=jnp.float32
        )
        return logits_share(partial_value, block)

    for step in range(STEPS):
        share = (jax.nn.sigmoid(logits_of(beta)) - targets).astype(jnp.bfloat16)
        residual = gather_share(share)
        grad = jnp.dot(residual, phi, preferred_element_type=jnp.float32)
        sent = grad.astype(jnp.bfloat16)
        total = grad
        for k in range(1, n_clip):
            total = total + clip_swap(sent, k).astype(jnp.float32)
        beta = beta - 0.25 * total
    scores = logits_of(beta).T
    per_clip = n_feat // n_clip
    by_block = beta.reshape(n_feat, block, features)
    trained = jnp.concatenate(
        [
            lax.dynamic_index_in_dim(by_block, feat ^ (clip * per_clip + b), 0, keepdims=False)
            for b in range(per_clip)
        ]
    ).T
    return (trained, scores)


def solution(mesh):
    placed = (P("clip", "feat"), P("clip", "feat"), P("feat"), P("feat", "clip"), P("clip", None))
    return jax.shard_map(
        per_device,
        mesh=mesh,
        in_specs=placed,
        out_specs=(P("feat", "clip"), P("clip", "feat")),
        check_vma=False,
    )
```

time: 333 us -> 145 us (0.44)
  waiting for transfers between devices: 228 us -> 57.2 us
  blocking collectives: 55.9 us -> 0 us
  starting transfers between devices: 0.46 us -> 48.5 us
  matrix products: 29.6 us -> 17.7 us
  local copies, waits for them, and re-layouts: 0.39 us -> 10.6 us
  between operations: 14.2 us -> 5.22 us
    all_gather x2 -> x0, waiting for transfers between devices: 89.5 us -> none  [the longest x1 53.4 us: per_device(): lax.all_gather(embeds, 'feat', axis=1, tiled=True)]
    reduce_scatter x3 -> x0, waiting for transfers between devices: 76.3 us -> none  [the longest x2 45.2 us: per_device(): lax.psum_scatter(grad_part, 'clip', scatter_dimension=1, tiled=True)]
    unnamed x9 -> x0, waiting for transfers between devices: 61.8 us -> none
    ppermute x0 -> x39, waiting for transfers between devices: none -> 57.2 us  [the longest x12 23 us: clip_swap(): return lax.ppermute(x, 'clip', [(i, i ^ k) for i in range(n)])]
    all_gather x5 -> x0, blocking collectives: 55.9 us -> none  [the longest x2 28.4 us: per_device(): residual = lax.all_gather(residual_share, 'feat', axis=1, tiled=True)]
    ppermute x0 -> x39, starting transfers between devices: none -> 48.5 us  [the longest x15 22.7 us: line_swap(): return lax.ppermute(x, 'feat', [(i, i ^ 2 * k) for i in range(n)])]
    dot_general x4 -> x8, matrix products: 26.9 us -> 17.7 us  [the longest x3 15.3 us: dot0(): lax.dot_general(a, b, (((0,), (0,)), ((), ())), preferred_element_type=jn...]
    dynamic_update_slice x0 -> x14, local copies, waits for them, and re-layouts: none -> 6.44 us  [the longest x3 4.3 us: per_device(): lax.dynamic_update_slice_in_dim(freq_all, piece, (clip ^ k) * slab, 0)]
  transfers between devices with their start and end apart: 7 -> 39, of which waited for: 7 -> 24; matrix products, arithmetic and copies ran while one was open for 0% -> 9% of each run, Pallas kernels for 0% -> 0%
where the time goes in v1:
time: 145 us
  waiting for transfers between devices  57.2 us (39%)
  starting transfers between devices  48.5 us (33%)
  matrix products  17.7 us (12%)
  local copies, waits for them, and re-layouts  10.6 us (7%)
  other arithmetic  5.34 us (4%)
  between operations  5.22 us (4%)
    ppermute x12, waiting for transfers between devices, clip_swap(): return lax.ppermute(x, 'clip', [(i, i ^ k) for i in range(n)])  23 us
    ppermute x15, starting transfers between devices, line_swap(): return lax.ppermute(x, 'feat', [(i, i ^ 2 * k) for i in range(n)])  22.7 us
    ppermute x15, waiting for transfers between devices, line_swap(): return lax.ppermute(x, 'feat', [(i, i ^ 2 * k) for i in range(n)])  18.5 us
    ppermute x12, starting transfers between devices, clip_swap(): return lax.ppermute(x, 'clip', [(i, i ^ k) for i in range(n)])  17 us
    dot_general x3, matrix products, dot0(): lax.dot_general(a, b, (((0,), (0,)), ((), ())), preferred_element_type=jn...  15.3 us
    ppermute x9, waiting for transfers between devices, core_swap(): return lax.ppermute(x, 'feat', [(i, i ^ 1) for i in range(n)])  7.98 us
    ppermute x3, starting transfers between devices, gather_line(): x = lax.ppermute(x, 'feat', perm)  7.75 us
    ppermute x3, waiting for transfers between devices, gather_line(): x = lax.ppermute(x, 'feat', perm)  7.74 us
  transfers between devices with their start and end apart: 39, of which 24 were waited for; matrix products, arithmetic and copies ran while one was open for 9% of the time, Pallas kernels for 0%

profile of v1, /device:TPU:0, one launch (start us, length us, event | category | flops | bytes accessed | tf_op | source)
XLA Modules:
  0.0 144.6 jit_solution(111481689594882054)
XLA Ops:
  1.0 0.8 copy-done.2
  1.8 0.8 constant_dynamic-update-slice_fusion.11
  3.1 3.6 %collective-permute-start.4 = (s16[144,1024]{1,0:T(8,128)(2,1)}, s16[144,1024]{1,0:T(8,128)(2,1)}, u32[]{:S(2)}, u32[]{:S(2)}) collective-permute-start(s16[144,1024]{1,0:T(8,128)(2,1)} %get-tuple-element.11), channel_id=1, source_target_pairs={{0,4},{1,5},{4,6},{5,7},{6,2},{7,3},{2,0},{3,1},{8,12},{9,13},{12,... | collective-permute-start | bytes 884744 | tf_op jit(solution)/shard_map/ppermute | solution.py:63
  6.7 1.2 broadcast_in_dim.31
  8.0 2.1 %constant_dynamic-update-slice_fusion.3 = (s16[1152,640]{1,0:T(8,128)(2,1)}, s16[288,640]{1,0:T(8,128)(2,1)}) fusion(s16[1152,640]{1,0:T(8,128)(2,1)} %broadcast_in_dim.31, s32[]{:T(128)S(6)} %select_n.147, f32[288,640]{1,0:T(8,128)} %param.10), kind=kLoop, calls=%fused_computation.100 | loop fusion | flops 552960 | bytes 1474564 | tf_op jit(solution)/shard_map/dynamic_update_slice | solution.py:101
  10.1 1.5 %collective-permute-start.10 = (s16[288,640]{1,0:T(8,128)(2,1)}, s16[288,640]{1,0:T(8,128)(2,1)}, u32[]{:S(2)}, u32[]{:S(2)}) collective-permute-start(s16[288,640]{1,0:T(8,128)(2,1)} %get-tuple-element.9), channel_id=1, source_target_pairs={{0,8},{8,0},{16,24},{24,16},{1,9},{9,1},{17,25},{25,17},{2,10},{10... | collective-permute-start | bytes 1105928 | tf_op jit(solution)/shard_map/ppermute | solution.py:49
  11.6 1.5 %collective-permute-start.11 = (s16[288,640]{1,0:T(8,128)(2,1)}, s16[288,640]{1,0:T(8,128)(2,1)}, u32[]{:S(2)}, u32[]{:S(2)}) collective-permute-start(s16[288,640]{1,0:T(8,128)(2,1)} %get-tuple-element.9), channel_id=1, source_target_pairs={{0,16},{8,24},{16,0},{24,8},{1,17},{9,25},{17,1},{25,9},{2,18},{10... | collective-permute-start | bytes 1105928 | tf_op jit(solution)/shard_map/ppermute | solution.py:49
  13.7 0.6 broadcast_multiply_fusion
  14.3 0.6 dynamic_slice.54
  16.9 0.6 fusion.72
  19.6 3.1 %collective-permute-done = f32[32,640]{1,0:T(8,128)S(1)} collective-permute-done((f32[32,640]{1,0:T(8,128)S(1)}, f32[32,640]{1,0:T(8,128)S(1)}, u32[]{:S(2)}, u32[]{:S(2)}) %collective-permute-start) | collective-permute-done | bytes 81952 | tf_op jit(solution)/shard_map/ppermute | solution.py:49
  22.7 1.5 %collective-permute-start.1 = (f32[32,640]{1,0:T(8,128)S(1)}, f32[32,640]{1,0:T(8,128)S(1)}, u32[]{:S(2)}, u32[]{:S(2)}) collective-permute-start(f32[32,640]{1,0:T(8,128)S(1)} %bitcast.191), channel_id=1, source_target_pairs={{0,16},{8,24},{16,0},{24,8},{1,17},{9,25},{17,1},{25,9},{2,18},{10... | collective-permute-start | bytes 245768 | tf_op jit(solution)/shard_map/ppermute | solution.py:49
  24.2 2.9 %collective-permute-done.1 = f32[32,640]{1,0:T(8,128)S(1)} collective-permute-done((f32[32,640]{1,0:T(8,128)S(1)}, f32[32,640]{1,0:T(8,128)S(1)}, u32[]{:S(2)}, u32[]{:S(2)}) %collective-permute-start.1) | collective-permute-done | bytes 81952 | tf_op jit(solution)/shard_map/ppermute | solution.py:49
  27.1 2.4 %collective-permute-start.2 = (f32[32,640]{1,0:T(8,128)S(1)}, f32[32,640]{1,0:T(8,128)S(1)}, u32[]{:S(2)}, u32[]{:S(2)}) collective-permute-start(f32[32,640]{1,0:T(8,128)S(1)} %bitcast.192), channel_id=1, source_target_pairs={{0,24},{8,16},{16,8},{24,0},{1,25},{9,17},{17,9},{25,1},{2,26},{10... | collective-permute-start | bytes 245768 | tf_op jit(solution)/shard_map/ppermute | solution.py:49
  29.6 2.9 %collective-permute-done.2 = f32[32,640]{1,0:T(8,128)S(1)} collective-permute-done((f32[32,640]{1,0:T(8,128)S(1)}, f32[32,640]{1,0:T(8,128)S(1)}, u32[]{:S(2)}, u32[]{:S(2)}) %collective-permute-start.2) | collective-permute-done | bytes 81952 | tf_op jit(solution)/shard_map/ppermute | solution.py:49
  32.5 2.4 %collective-permute-start.12 = (s16[288,640]{1,0:T(8,128)(2,1)}, s16[288,640]{1,0:T(8,128)(2,1)S(1)}, u32[]{:S(2)}, u32[]{:S(2)}) collective-permute-start(s16[288,640]{1,0:T(8,128)(2,1)} %get-tuple-element.9), channel_id=1, source_target_pairs={{0,24},{8,16},{16,8},{24,0},{1,25},{9,17},{17,9},{25,1},{2,26},{10... | collective-permute-start | bytes 1105928 | tf_op jit(solution)/shard_map/ppermute | solution.py:49
  35.2 1.6 %collective-permute-start.6 = (s16[144,1024]{1,0:T(8,128)(2,1)}, s16[144,1024]{1,0:T(8,128)(2,1)S(1)}, u32[]{:S(2)}, u32[]{:S(2)}) collective-permute-start(s16[144,1024]{1,0:T(8,128)(2,1)} %collective-permute-done.4), channel_id=1, source_target_pairs={{0,4},{1,5},{4,6},{5,7},{6,2},{7,3},{2,0},{3,1},{8,12},{9,13},{12,... | collective-permute-start | bytes 884744 | tf_op jit(solution)/shard_map/ppermute | solution.py:63
  36.8 1.0 constant_dynamic-update-slice_fusion.10
  37.8 1.0 constant_dynamic-update-slice_fusion.9
  38.8 1.8 %constant_dynamic-update-slice_fusion.2 = s16[1152,640]{1,0:T(8,128)(2,1)} fusion(s16[1152,640]{1,0:T(8,128)(2,1)} %get-tuple-element.8, s16[288,640]{1,0:T(8,128)(2,1)} %collective-permute-done.10, s32[]{:T(128)S(6)} %select_n.148), kind=kLoop, calls=%fused_computation.99 | loop fusion | bytes 737284 | tf_op jit(solution)/shard_map/dynamic_update_slice | solution.py:101
  40.6 4.2 %collective-permute-done.6 = s16[144,1024]{1,0:T(8,128)(2,1)S(1)} collective-permute-done((s16[144,1024]{1,0:T(8,128)(2,1)}, s16[144,1024]{1,0:T(8,128)(2,1)S(1)}, u32[]{:S(2)}, u32[]{:S(2)}) %collective-permute-start.6) | collective-permute-done | bytes 294944 | tf_op jit(solution)/shard_map/ppermute | solution.py:63
  44.8 2.5 %collective-permute-start.8 = (s16[144,1024]{1,0:T(8,128)(2,1)S(1)}, s16[144,1024]{1,0:T(8,128)(2,1)S(1)}, u32[]{:S(2)}, u32[]{:S(2)}) collective-permute-start(s16[144,1024]{1,0:T(8,128)(2,1)S(1)} %collective-permute-done.6), channel_id=1, source_target_pairs={{0,4},{1,5},{4,6},{5,7},{6,2},{7,3},{2,0},{3,1},{8,12},{9,13},{12,... | collective-permute-start | bytes 884744 | tf_op jit(solution)/shard_map/ppermute | solution.py:63
  47.3 1.8 %constant_dynamic-update-slice_fusion.1 = s16[1152,640]{1,0:T(8,128)(2,1)} fusion(s16[1152,640]{1,0:T(8,128)(2,1)} %constant_dynamic-update-slice_fusion.2, s16[288,640]{1,0:T(8,128)(2,1)} %collective-permute-done.11, s32[]{:T(128)S(6)} %select_n.149), kind=kLoop, calls=%fused_computation.98 | loop fusion | bytes 737284 | tf_op jit(solution)/shard_map/dynamic_update_slice | solution.py:101
  49.1 0.8 constant_dynamic-update-slice_fusion
  49.9 3.5 %collective-permute-done.8 = s16[144,1024]{1,0:T(8,128)(2,1)S(1)} collective-permute-done((s16[144,1024]{1,0:T(8,128)(2,1)S(1)}, s16[144,1024]{1,0:T(8,128)(2,1)S(1)}, u32[]{:S(2)}, u32[]{:S(2)}) %collective-permute-start.8) | collective-permute-done | bytes 294944 | tf_op jit(solution)/shard_map/ppermute | solution.py:63
  53.5 1.5 %collective-permute-done.9 = s16[144,1024]{1,0:T(8,128)(2,1)S(1)} collective-permute-done((s16[144,1024]{1,0:T(8,128)(2,1)S(1)}, s16[144,1024]{1,0:T(8,128)(2,1)S(1)}, u32[]{:S(2)}, u32[]{:S(2)}) %collective-permute-start.9) | collective-permute-done | bytes 294944 | tf_op jit(solution)/shard_map/ppermute | solution.py:39
  55.0 5.0 %fusion.7 = f32[1024,640]{1,0:T(8,128)S(1)} fusion(s16[1152,1024]{1,0:T(8,128)(2,1)S(1)} %constant_dynamic-update-slice_fusion.4, s16[1152,640]{1,0:T(8,128)(2,1)} %constant_dynamic-update-slice_fusion), kind=kOutput, calls=%fused_computation.13 | convolution fusion | flops 1518796800 | bytes 6455296 | tf_op jit(solution)/shard_map/dot_general | solution.py:121
  60.0 4.1 %fusion.11 = f32[1024,640]{1,0:T(8,128)S(1)} fusion(s16[1152,1024]{1,0:T(8,128)(2,1)S(1)} %constant_dynamic-update-slice_fusion.4, s16[1152,640]{1,0:T(8,128)(2,1)} %constant_dynamic-update-slice_fusion), kind=kOutput, calls=%fused_computation.16 | convolution fusion | flops 1518354432 | bytes 6455296 | tf_op jit(solution)/shard_map/dot_general | solution.py:121
  64.1 6.2 %add_convert_fusion = bf16[1024,640]{1,0:T(8,128)(2,1)S(1)} fusion(f32[1024,640]{1,0:T(8,128)S(1)} %fusion.11, f32[1024,640]{1,0:T(8,128)S(1)} %fusion.7, f32[640]{0:T(1024)S(1)} %copy-done.6, s16[1152,1024]{1,0:T(8,128)(2,1)} %copy-done.1, s16[1152,640]{1,0:T(8,128)(2,1)} %constant_dynamic-update-slice_fusion), kind=kOutput, calls=%fused_computation.12 | convolution fusion | flops 1530724352 | bytes 10390016 | tf_op jit(solution)/shard_map/dot_general | solution.py:121
  71.1 1.2 collective-permute-done.13
  72.4 1.3 collective-permute-start.14
  73.7 2.2 %collective-permute-start.15 = (bf16[16,1024]{1,0:T(8,128)(2,1)S(1)}, bf16[16,1024]{1,0:T(8,128)(2,1)S(1)}, u32[]{:S(2)}, u32[]{:S(2)}) collective-permute-start(bf16[16,1024]{1,0:T(8,128)(2,1)S(1)} %get-tuple-element.26), channel_id=1, source_target_pairs={{0,4},{1,5},{2,6},{3,7},{4,0},{5,1},{6,2},{7,3},{8,12},{9,13},{10,... | collective-permute-start | bytes 98312 | tf_op jit(solution)/shard_map/ppermute | solution.py:44
  75.9 1.4 collective-permute-start.16
  77.6 1.2 collective-permute-done.15
  78.8 2.8 %collective-permute-done.16 = bf16[16,1024]{1,0:T(8,128)(2,1)S(1)} collective-permute-done((bf16[16,1024]{1,0:T(8,128)(2,1)S(1)}, bf16[16,1024]{1,0:T(8,128)(2,1)S(1)}, u32[]{:S(2)}, u32[]{:S(2)}) %collective-permute-start.16) | collective-permute-done | bytes 32800 | tf_op jit(solution)/shard_map/ppermute | solution.py:44
  81.9 1.9 %collective-permute-start.18 = (bf16[16,1024]{1,0:T(8,128)(2,1)S(1)}, bf16[16,1024]{1,0:T(8,128)(2,1)S(1)}, u32[]{:S(2)}, u32[]{:S(2)}) collective-permute-start(bf16[16,1024]{1,0:T(8,128)(2,1)S(1)} %fusion.55), channel_id=1, source_target_pairs={{0,4},{1,5},{2,6},{3,7},{4,0},{5,1},{6,2},{7,3},{8,12},{9,13},{10,... | collective-permute-start | bytes 98312 | tf_op jit(solution)/shard_map/ppermute | solution.py:44
  83.8 2.3 %collective-permute-start.19 = (bf16[16,1024]{1,0:T(8,128)(2,1)S(1)}, bf16[16,1024]{1,0:T(8,128)(2,1)S(1)}, u32[]{:S(2)}, u32[]{:S(2)}) collective-permute-start(bf16[16,1024]{1,0:T(8,128)(2,1)S(1)} %fusion.55), channel_id=1, source_target_pairs={{0,6},{1,7},{2,4},{3,5},{4,2},{5,3},{6,0},{7,1},{8,14},{9,15},{10,... | collective-permute-start | bytes 98312 | tf_op jit(solution)/shard_map/ppermute | solution.py:44
  86.1 0.9 collective-permute-done.18
  87.0 2.5 %collective-permute-done.19 = bf16[16,1024]{1,0:T(8,128)(2,1)S(1)} collective-permute-done((bf16[16,1024]{1,0:T(8,128)(2,1)S(1)}, bf16[16,1024]{1,0:T(8,128)(2,1)S(1)}, u32[]{:S(2)}, u32[]{:S(2)}) %collective-permute-start.19) | collective-permute-done | bytes 32800 | tf_op jit(solution)/shard_map/ppermute | solution.py:44
  89.6 1.3 collective-permute-done.20
  91.3 0.6 collective-permute-start.21
  92.5 2.4 %collective-permute-start.23 = (bf16[128,640]{1,0:T(8,128)(2,1)S(1)}, bf16[128,640]{1,0:T(8,128)(2,1)S(1)}, u32[]{:S(2)}, u32[]{:S(2)}) collective-permute-start(bf16[128,640]{1,0:T(8,128)(2,1)S(1)} %get-tuple-element.30), channel_id=1, source_target_pairs={{0,24},{8,16},{16,8},{24,0},{1,25},{9,17},{17,9},{25,1},{2,26},{10... | collective-permute-start | bytes 491528 | tf_op jit(solution)/shard_map/ppermute | solution.py:49
  94.9 3.6 %collective-permute-done.21 = bf16[128,640]{1,0:T(8,128)(2,1)S(1)} collective-permute-done((bf16[128,640]{1,0:T(8,128)(2,1)S(1)}, bf16[128,640]{1,0:T(8,128)(2,1)S(1)}, u32[]{:S(2)}, u32[]{:S(2)}) %collective-permute-start.21) | collective-permute-done | bytes 163872 | tf_op jit(solution)/shard_map/ppermute | solution.py:49
  98.4 3.0 %collective-permute-done.22 = bf16[128,640]{1,0:T(8,128)(2,1)S(1)} collective-permute-done((bf16[128,640]{1,0:T(8,128)(2,1)S(1)}, bf16[128,640]{1,0:T(8,128)(2,1)S(1)}, u32[]{:S(2)}, u32[]{:S(2)}) %collective-permute-start.22) | collective-permute-done | bytes 163872 | tf_op jit(solution)/shard_map/ppermute | solution.py:49
  101.5 0.5 fusion.28
  102.2 1.3 collective-permute-done.24
  103.7 2.9 %collective-permute-start.26 = (bf16[16,1024]{1,0:T(8,128)(2,1)S(1)}, bf16[16,1024]{1,0:T(8,128)(2,1)S(1)}, u32[]{:S(2)}, u32[]{:S(2)}) collective-permute-start(bf16[16,1024]{1,0:T(8,128)(2,1)S(1)} %get-tuple-element.21), channel_id=1, source_target_pairs={{0,4},{1,5},{2,6},{3,7},{4,0},{5,1},{6,2},{7,3},{8,12},{9,13},{10,... | collective-permute-start | bytes 98312 | tf_op jit(solution)/shard_map/ppermute | solution.py:44
  106.6 1.5 %collective-permute-start.27 = (bf16[16,1024]{1,0:T(8,128)(2,1)S(1)}, bf16[16,1024]{1,0:T(8,128)(2,1)S(1)}, u32[]{:S(2)}, u32[]{:S(2)}) collective-permute-start(bf16[16,1024]{1,0:T(8,128)(2,1)S(1)} %get-tuple-element.20), channel_id=1, source_target_pairs={{0,6},{1,7},{2,4},{3,5},{4,2},{5,3},{6,0},{7,1},{8,14},{9,15},{10,... | collective-permute-start | bytes 98312 | tf_op jit(solution)/shard_map/ppermute | solution.py:44
  108.6 3.7 %collective-permute-done.27 = bf16[16,1024]{1,0:T(8,128)(2,1)S(1)} collective-permute-done((bf16[16,1024]{1,0:T(8,128)(2,1)S(1)}, bf16[16,1024]{1,0:T(8,128)(2,1)S(1)}, u32[]{:S(2)}, u32[]{:S(2)}) %collective-permute-start.27) | collective-permute-done | bytes 32800 | tf_op jit(solution)/shard_map/ppermute | solution.py:44
  112.4 2.0 %collective-permute-start.29 = (bf16[16,1024]{1,0:T(8,128)(2,1)S(1)}, bf16[16,1024]{1,0:T(8,128)(2,1)S(1)}, u32[]{:S(2)}, u32[]{:S(2)}) collective-permute-start(bf16[16,1024]{1,0:T(8,128)(2,1)S(1)} %fusion.56), channel_id=1, source_target_pairs={{0,4},{1,5},{2,6},{3,7},{4,0},{5,1},{6,2},{7,3},{8,12},{9,13},{10,... | collective-permute-start | bytes 98312 | tf_op jit(solution)/shard_map/ppermute | solution.py:44
  114.4 2.3 %collective-permute-start.30 = (bf16[16,1024]{1,0:T(8,128)(2,1)S(1)}, bf16[16,1024]{1,0:T(8,128)(2,1)S(1)}, u32[]{:S(2)}, u32[]{:S(2)}) collective-permute-start(bf16[16,1024]{1,0:T(8,128)(2,1)S(1)} %fusion.56), channel_id=1, source_target_pairs={{0,6},{1,7},{2,4},{3,5},{4,2},{5,3},{6,0},{7,1},{8,14},{9,15},{10,... | collective-permute-start | bytes 98312 | tf_op jit(solution)/shard_map/ppermute | solution.py:44
  116.8 0.9 collective-permute-done.29
  117.6 2.5 %collective-permute-done.30 = bf16[16,1024]{1,0:T(8,128)(2,1)S(1)} collective-permute-done((bf16[16,1024]{1,0:T(8,128)(2,1)S(1)}, bf16[16,1024]{1,0:T(8,128)(2,1)S(1)}, u32[]{:S(2)}, u32[]{:S(2)}) %collective-permute-start.30) | collective-permute-done | bytes 32800 | tf_op jit(solution)/shard_map/ppermute | solution.py:44
  120.3 1.3 collective-permute-done.31
  122.0 1.5 %collective-permute-start.32 = (bf16[128,640]{1,0:T(8,128)(2,1)S(1)}, bf16[128,640]{1,0:T(8,128)(2,1)S(1)}, u32[]{:S(2)}, u32[]{:S(2)}) collective-permute-start(bf16[128,640]{1,0:T(8,128)(2,1)S(1)} %get-tuple-element.32), channel_id=1, source_target_pairs={{0,8},{8,0},{16,24},{24,16},{1,9},{9,1},{17,25},{25,17},{2,10},{10... | collective-permute-start | bytes 491528 | tf_op jit(solution)/shard_map/ppermute | solution.py:49
  124.1 1.5 %collective-permute-start.34 = (bf16[128,640]{1,0:T(8,128)(2,1)S(1)}, bf16[128,640]{1,0:T(8,128)(2,1)S(1)}, u32[]{:S(2)}, u32[]{:S(2)}) collective-permute-start(bf16[128,640]{1,0:T(8,128)(2,1)S(1)} %get-tuple-element.32), channel_id=1, source_target_pairs={{0,24},{8,16},{16,8},{24,0},{1,25},{9,17},{17,9},{25,1},{2,26},{10... | collective-permute-start | bytes 491528 | tf_op jit(solution)/shard_map/ppermute | solution.py:49
  125.6 3.6 %collective-permute-done.32 = bf16[128,640]{1,0:T(8,128)(2,1)S(1)} collective-permute-done((bf16[128,640]{1,0:T(8,128)(2,1)S(1)}, bf16[128,640]{1,0:T(8,128)(2,1)S(1)}, u32[]{:S(2)}, u32[]{:S(2)}) %collective-permute-start.32) | collective-permute-done | bytes 163872 | tf_op jit(solution)/shard_map/ppermute | solution.py:49
  129.1 3.9 %collective-permute-done.33 = bf16[128,640]{1,0:T(8,128)(2,1)S(1)} collective-permute-done((bf16[128,640]{1,0:T(8,128)(2,1)S(1)}, bf16[128,640]{1,0:T(8,128)(2,1)S(1)}, u32[]{:S(2)}, u32[]{:S(2)}) %collective-permute-start.33) | collective-permute-done | bytes 163872 | tf_op jit(solution)/shard_map/ppermute | solution.py:49
  133.9 1.3 collective-permute-done.35
  135.3 2.9 %collective-permute-start.37 = (bf16[16,1024]{1,0:T(8,128)(2,1)S(1)}, bf16[16,1024]{1,0:T(8,128)(2,1)S(1)}, u32[]{:S(2)}, u32[]{:S(2)}) collective-permute-start(bf16[16,1024]{1,0:T(8,128)(2,1)S(1)} %get-tuple-element.16), channel_id=1, source_target_pairs={{0,4},{1,5},{2,6},{3,7},{4,0},{5,1},{6,2},{7,3},{8,12},{9,13},{10,... | collective-permute-start | bytes 98312 | tf_op jit(solution)/shard_map/ppermute | solution.py:44
  138.2 1.5 %collective-permute-start.38 = (bf16[16,1024]{1,0:T(8,128)(2,1)S(1)}, bf16[16,1024]{1,0:T(8,128)(2,1)S(1)}, u32[]{:S(2)}, u32[]{:S(2)}) collective-permute-start(bf16[16,1024]{1,0:T(8,128)(2,1)S(1)} %get-tuple-element.15), channel_id=1, source_target_pairs={{0,6},{1,7},{2,4},{3,5},{4,2},{5,3},{6,0},{7,1},{8,14},{9,15},{10,... | collective-permute-start | bytes 98312 | tf_op jit(solution)/shard_map/ppermute | solution.py:44
  139.7 0.6 maximum_bitcast_fusion
  140.3 3.6 %collective-permute-done.38 = bf16[16,1024]{1,0:T(8,128)(2,1)S(1)} collective-permute-done((bf16[16,1024]{1,0:T(8,128)(2,1)S(1)}, bf16[16,1024]{1,0:T(8,128)(2,1)S(1)}, u32[]{:S(2)}, u32[]{:S(2)}) %collective-permute-start.38) | collective-permute-done | bytes 32800 | tf_op jit(solution)/shard_map/ppermute | solution.py:44
  143.9 0.6 fusion.38
  (91 shorter events, 7.0 us)
Async XLA Ops:
  0.6 76.6 %copy-start = (s32[1024,128]{1,0:T(8,128)S(1)}, s32[1024,128]{1,0:T(8,128)}, u32[]{:S(2)}) copy-start(s32[1024,128]{1,0:T(8,128)} %param.13) | copy-start | bytes 1572868
  0.6 1.1 copy-start.2
  1.8 11.3 %copy-start.3 = (f32[640,32]{0,1:T(8,128)S(1)}, f32[640,32]{0,1:T(8,128)}, u32[]{:S(2)}) copy-start(f32[640,32]{0,1:T(8,128)} %param.12) | copy-start | bytes 245764
  2.6 11.1 %copy-start.5 = (f32[640]{0:T(1024)S(1)}, f32[640]{0:T(1024)}, u32[]{:S(2)}) copy-start(f32[640]{0:T(1024)} %param.11) | copy-start | bytes 7684
  2.6 11.7 %copy-start.7 = (s32[4]{0:T(128)S(1)}, s32[4]{0:T(128)}, u32[]{:S(2)}) copy-start(s32[4]{0:T(128)} %constant.147.clone) | copy-start | bytes 52
  2.6 14.3 %copy-start.4 = (s32[4]{0:T(128)S(1)}, s32[4]{0:T(128)}, u32[]{:S(2)}) copy-start(s32[4]{0:T(128)} %constant.148.clone) | copy-start | bytes 52
  2.6 32.6 %collective-permute-start.3 = (s16[144,1024]{1,0:T(8,128)(2,1)}, s16[144,1024]{1,0:T(8,128)(2,1)}, u32[]{:S(2)}, u32[]{:S(2)}) collective-permute-start(s16[144,1024]{1,0:T(8,128)(2,1)} %get-tuple-element.11), channel_id=1, source_target_pairs={{0,1},{1,0},{2,3},{3,2},{4,5},{5,4},{6,7},{7,6},{8,9},{9,8},{10,11... | collective-permute-start | bytes 884744 | tf_op jit(solution)/shard_map/ppermute | solution.py:39
  3.1 32.0 %collective-permute-start.4 = (s16[144,1024]{1,0:T(8,128)(2,1)}, s16[144,1024]{1,0:T(8,128)(2,1)}, u32[]{:S(2)}, u32[]{:S(2)}) collective-permute-start(s16[144,1024]{1,0:T(8,128)(2,1)} %get-tuple-element.11), channel_id=1, source_target_pairs={{0,4},{1,5},{4,6},{5,7},{6,2},{7,3},{2,0},{3,1},{8,12},{9,13},{12,... | collective-permute-start | bytes 884744 | tf_op jit(solution)/shard_map/ppermute | solution.py:63
  10.1 28.7 %collective-permute-start.10 = (s16[288,640]{1,0:T(8,128)(2,1)}, s16[288,640]{1,0:T(8,128)(2,1)}, u32[]{:S(2)}, u32[]{:S(2)}) collective-permute-start(s16[288,640]{1,0:T(8,128)(2,1)} %get-tuple-element.9), channel_id=1, source_target_pairs={{0,8},{8,0},{16,24},{24,16},{1,9},{9,1},{17,25},{25,17},{2,10},{10... | collective-permute-start | bytes 1105928 | tf_op jit(solution)/shard_map/ppermute | solution.py:49
  11.6 35.7 %collective-permute-start.11 = (s16[288,640]{1,0:T(8,128)(2,1)}, s16[288,640]{1,0:T(8,128)(2,1)}, u32[]{:S(2)}, u32[]{:S(2)}) collective-permute-start(s16[288,640]{1,0:T(8,128)(2,1)} %get-tuple-element.9), channel_id=1, source_target_pairs={{0,16},{8,24},{16,0},{24,8},{1,17},{9,25},{17,1},{25,9},{2,18},{10... | collective-permute-start | bytes 1105928 | tf_op jit(solution)/shard_map/ppermute | solution.py:49
  13.1 9.6 %collective-permute-start = (f32[32,640]{1,0:T(8,128)S(1)}, f32[32,640]{1,0:T(8,128)S(1)}, u32[]{:S(2)}, u32[]{:S(2)}) collective-permute-start(f32[32,640]{1,0:T(8,128)S(1)} %bitcast.190), channel_id=1, source_target_pairs={{0,8},{8,0},{16,24},{24,16},{1,9},{9,1},{17,25},{25,17},{2,10},{10... | collective-permute-start | bytes 245768 | tf_op jit(solution)/shard_map/ppermute | solution.py:49
  22.7 4.4 %collective-permute-start.1 = (f32[32,640]{1,0:T(8,128)S(1)}, f32[32,640]{1,0:T(8,128)S(1)}, u32[]{:S(2)}, u32[]{:S(2)}) collective-permute-start(f32[32,640]{1,0:T(8,128)S(1)} %bitcast.191), channel_id=1, source_target_pairs={{0,16},{8,24},{16,0},{24,8},{1,17},{9,25},{17,1},{25,9},{2,18},{10... | collective-permute-start | bytes 245768 | tf_op jit(solution)/shard_map/ppermute | solution.py:49
  27.1 5.3 %collective-permute-start.2 = (f32[32,640]{1,0:T(8,128)S(1)}, f32[32,640]{1,0:T(8,128)S(1)}, u32[]{:S(2)}, u32[]{:S(2)}) collective-permute-start(f32[32,640]{1,0:T(8,128)S(1)} %bitcast.192), channel_id=1, source_target_pairs={{0,24},{8,16},{16,8},{24,0},{1,25},{9,17},{17,9},{25,1},{2,26},{10... | collective-permute-start | bytes 245768 | tf_op jit(solution)/shard_map/ppermute | solution.py:49
  32.5 16.6 %collective-permute-start.12 = (s16[288,640]{1,0:T(8,128)(2,1)}, s16[288,640]{1,0:T(8,128)(2,1)S(1)}, u32[]{:S(2)}, u32[]{:S(2)}) collective-permute-start(s16[288,640]{1,0:T(8,128)(2,1)} %get-tuple-element.9), channel_id=1, source_target_pairs={{0,24},{8,16},{16,8},{24,0},{1,25},{9,17},{17,9},{25,1},{2,26},{10... | collective-permute-start | bytes 1105928 | tf_op jit(solution)/shard_map/ppermute | solution.py:49
  35.1 14.7 %collective-permute-start.5 = (s16[144,1024]{1,0:T(8,128)(2,1)}, s16[144,1024]{1,0:T(8,128)(2,1)S(1)}, u32[]{:S(2)}, u32[]{:S(2)}) collective-permute-start(s16[144,1024]{1,0:T(8,128)(2,1)} %collective-permute-done.4), channel_id=1, source_target_pairs={{0,1},{1,0},{2,3},{3,2},{4,5},{5,4},{6,7},{7,6},{8,9},{9,8},{10,11... | collective-permute-start | bytes 884744 | tf_op jit(solution)/shard_map/ppermute | solution.py:39
  35.2 9.6 %collective-permute-start.6 = (s16[144,1024]{1,0:T(8,128)(2,1)}, s16[144,1024]{1,0:T(8,128)(2,1)S(1)}, u32[]{:S(2)}, u32[]{:S(2)}) collective-permute-start(s16[144,1024]{1,0:T(8,128)(2,1)} %collective-permute-done.4), channel_id=1, source_target_pairs={{0,4},{1,5},{4,6},{5,7},{6,2},{7,3},{2,0},{3,1},{8,12},{9,13},{12,... | collective-permute-start | bytes 884744 | tf_op jit(solution)/shard_map/ppermute | solution.py:63
  44.8 8.6 %collective-permute-start.8 = (s16[144,1024]{1,0:T(8,128)(2,1)S(1)}, s16[144,1024]{1,0:T(8,128)(2,1)S(1)}, u32[]{:S(2)}, u32[]{:S(2)}) collective-permute-start(s16[144,1024]{1,0:T(8,128)(2,1)S(1)} %collective-permute-done.6), channel_id=1, source_target_pairs={{0,4},{1,5},{4,6},{5,7},{6,2},{7,3},{2,0},{3,1},{8,12},{9,13},{12,... | collective-permute-start | bytes 884744 | tf_op jit(solution)/shard_map/ppermute | solution.py:63
  49.0 4.4 %collective-permute-start.7 = (s16[144,1024]{1,0:T(8,128)(2,1)S(1)}, s16[144,1024]{1,0:T(8,128)(2,1)S(1)}, u32[]{:S(2)}, u32[]{:S(2)}) collective-permute-start(s16[144,1024]{1,0:T(8,128)(2,1)S(1)} %collective-permute-done.6), channel_id=1, source_target_pairs={{0,1},{1,0},{2,3},{3,2},{4,5},{5,4},{6,7},{7,6},{8,9},{9,8},{10,11... | collective-permute-start | bytes 884744 | tf_op jit(solution)/shard_map/ppermute | solution.py:39
  53.4 1.6 %collective-permute-start.9 = (s16[144,1024]{1,0:T(8,128)(2,1)S(1)}, s16[144,1024]{1,0:T(8,128)(2,1)S(1)}, u32[]{:S(2)}, u32[]{:S(2)}) collective-permute-start(s16[144,1024]{1,0:T(8,128)(2,1)S(1)} %collective-permute-done.8), channel_id=1, source_target_pairs={{0,1},{1,0},{2,3},{3,2},{4,5},{5,4},{6,7},{7,6},{8,9},{9,8},{10,11... | collective-permute-start | bytes 884744 | tf_op jit(solution)/shard_map/ppermute | solution.py:39
  55.0 5.0 %copy-start.1 = (s16[1152,1024]{1,0:T(8,128)(2,1)}, s16[1152,1024]{1,0:T(8,128)(2,1)S(1)}, u32[]{:S(2)}) copy-start(s16[1152,1024]{1,0:T(8,128)(2,1)S(1)} %constant_dynamic-update-slice_fusion.4) | copy-start | bytes 7077892
  60.0 4.1 %copy-start.6 = (f32[640]{0:T(1024)S(1)}, f32[640]{0:T(1024)}, u32[]{:S(2)}) copy-start(f32[640]{0:T(1024)} %broadcast_multiply_fusion) | copy-start | bytes 7684
  70.9 1.4 collective-permute-start.13
  72.4 5.3 %collective-permute-start.14 = (bf16[16,1024]{1,0:T(8,128)(2,1)S(1)}, bf16[16,1024]{1,0:T(8,128)(2,1)S(1)}, u32[]{:S(2)}, u32[]{:S(2)}) collective-permute-start(bf16[16,1024]{1,0:T(8,128)(2,1)S(1)} %get-tuple-element.24), channel_id=1, source_target_pairs={{0,2},{1,3},{2,0},{3,1},{4,6},{5,7},{6,4},{7,5},{8,10},{9,11},{10,... | collective-permute-start | bytes 98312 | tf_op jit(solution)/shard_map/ppermute | solution.py:44
  73.7 5.2 %collective-permute-start.15 = (bf16[16,1024]{1,0:T(8,128)(2,1)S(1)}, bf16[16,1024]{1,0:T(8,128)(2,1)S(1)}, u32[]{:S(2)}, u32[]{:S(2)}) collective-permute-start(bf16[16,1024]{1,0:T(8,128)(2,1)S(1)} %get-tuple-element.26), channel_id=1, source_target_pairs={{0,4},{1,5},{2,6},{3,7},{4,0},{5,1},{6,2},{7,3},{8,12},{9,13},{10,... | collective-permute-start | bytes 98312 | tf_op jit(solution)/shard_map/ppermute | solution.py:44
  75.9 5.7 %collective-permute-start.16 = (bf16[16,1024]{1,0:T(8,128)(2,1)S(1)}, bf16[16,1024]{1,0:T(8,128)(2,1)S(1)}, u32[]{:S(2)}, u32[]{:S(2)}) collective-permute-start(bf16[16,1024]{1,0:T(8,128)(2,1)S(1)} %get-tuple-element.25), channel_id=1, source_target_pairs={{0,6},{1,7},{2,4},{3,5},{4,2},{5,3},{6,0},{7,1},{8,14},{9,15},{10,... | collective-permute-start | bytes 98312 | tf_op jit(solution)/shard_map/ppermute | solution.py:44
  81.6 4.5 %collective-permute-start.17 = (bf16[16,1024]{1,0:T(8,128)(2,1)S(1)}, bf16[16,1024]{1,0:T(8,128)(2,1)S(1)}, u32[]{:S(2)}, u32[]{:S(2)}) collective-permute-start(bf16[16,1024]{1,0:T(8,128)(2,1)S(1)} %fusion.55), channel_id=1, source_target_pairs={{0,2},{1,3},{2,0},{3,1},{4,6},{5,7},{6,4},{7,5},{8,10},{9,11},{10,... | collective-permute-start | bytes 98312 | tf_op jit(solution)/shard_map/ppermute | solution.py:44
  81.9 5.2 %collective-permute-start.18 = (bf16[16,1024]{1,0:T(8,128)(2,1)S(1)}, bf16[16,1024]{1,0:T(8,128)(2,1)S(1)}, u32[]{:S(2)}, u32[]{:S(2)}) collective-permute-start(bf16[16,1024]{1,0:T(8,128)(2,1)S(1)} %fusion.55), channel_id=1, source_target_pairs={{0,4},{1,5},{2,6},{3,7},{4,0},{5,1},{6,2},{7,3},{8,12},{9,13},{10,... | collective-permute-start | bytes 98312 | tf_op jit(solution)/shard_map/ppermute | solution.py:44
  83.8 5.7 %collective-permute-start.19 = (bf16[16,1024]{1,0:T(8,128)(2,1)S(1)}, bf16[16,1024]{1,0:T(8,128)(2,1)S(1)}, u32[]{:S(2)}, u32[]{:S(2)}) collective-permute-start(bf16[16,1024]{1,0:T(8,128)(2,1)S(1)} %fusion.55), channel_id=1, source_target_pairs={{0,6},{1,7},{2,4},{3,5},{4,2},{5,3},{6,0},{7,1},{8,14},{9,15},{10,... | collective-permute-start | bytes 98312 | tf_op jit(solution)/shard_map/ppermute | solution.py:44
  89.5 1.4 collective-permute-start.20
  91.3 7.1 %collective-permute-start.21 = (bf16[128,640]{1,0:T(8,128)(2,1)S(1)}, bf16[128,640]{1,0:T(8,128)(2,1)S(1)}, u32[]{:S(2)}, u32[]{:S(2)}) collective-permute-start(bf16[128,640]{1,0:T(8,128)(2,1)S(1)} %get-tuple-element.30), channel_id=1, source_target_pairs={{0,8},{8,0},{16,24},{24,16},{1,9},{9,1},{17,25},{25,17},{2,10},{10... | collective-permute-start | bytes 491528 | tf_op jit(solution)/shard_map/ppermute | solution.py:49
  91.9 9.5 %collective-permute-start.22 = (bf16[128,640]{1,0:T(8,128)(2,1)S(1)}, bf16[128,640]{1,0:T(8,128)(2,1)S(1)}, u32[]{:S(2)}, u32[]{:S(2)}) collective-permute-start(bf16[128,640]{1,0:T(8,128)(2,1)S(1)} %get-tuple-element.30), channel_id=1, source_target_pairs={{0,16},{8,24},{16,0},{24,8},{1,17},{9,25},{17,1},{25,9},{2,18},{10... | collective-permute-start | bytes 491528 | tf_op jit(solution)/shard_map/ppermute | solution.py:49
  92.5 9.0 %collective-permute-start.23 = (bf16[128,640]{1,0:T(8,128)(2,1)S(1)}, bf16[128,640]{1,0:T(8,128)(2,1)S(1)}, u32[]{:S(2)}, u32[]{:S(2)}) collective-permute-start(bf16[128,640]{1,0:T(8,128)(2,1)S(1)} %get-tuple-element.30), channel_id=1, source_target_pairs={{0,24},{8,16},{16,8},{24,0},{1,25},{9,17},{17,9},{25,1},{2,26},{10... | collective-permute-start | bytes 491528 | tf_op jit(solution)/shard_map/ppermute | solution.py:49
  102.1 1.4 collective-permute-start.24
  103.6 4.5 %collective-permute-start.25 = (bf16[16,1024]{1,0:T(8,128)(2,1)S(1)}, bf16[16,1024]{1,0:T(8,128)(2,1)S(1)}, u32[]{:S(2)}, u32[]{:S(2)}) collective-permute-start(bf16[16,1024]{1,0:T(8,128)(2,1)S(1)} %get-tuple-element.19), channel_id=1, source_target_pairs={{0,2},{1,3},{2,0},{3,1},{4,6},{5,7},{6,4},{7,5},{8,10},{9,11},{10,... | collective-permute-start | bytes 98312 | tf_op jit(solution)/shard_map/ppermute | solution.py:44
  103.7 4.9 %collective-permute-start.26 = (bf16[16,1024]{1,0:T(8,128)(2,1)S(1)}, bf16[16,1024]{1,0:T(8,128)(2,1)S(1)}, u32[]{:S(2)}, u32[]{:S(2)}) collective-permute-start(bf16[16,1024]{1,0:T(8,128)(2,1)S(1)} %get-tuple-element.21), channel_id=1, source_target_pairs={{0,4},{1,5},{2,6},{3,7},{4,0},{5,1},{6,2},{7,3},{8,12},{9,13},{10,... | collective-permute-start | bytes 98312 | tf_op jit(solution)/shard_map/ppermute | solution.py:44
  106.6 5.7 %collective-permute-start.27 = (bf16[16,1024]{1,0:T(8,128)(2,1)S(1)}, bf16[16,1024]{1,0:T(8,128)(2,1)S(1)}, u32[]{:S(2)}, u32[]{:S(2)}) collective-permute-start(bf16[16,1024]{1,0:T(8,128)(2,1)S(1)} %get-tuple-element.20), channel_id=1, source_target_pairs={{0,6},{1,7},{2,4},{3,5},{4,2},{5,3},{6,0},{7,1},{8,14},{9,15},{10,... | collective-permute-start | bytes 98312 | tf_op jit(solution)/shard_map/ppermute | solution.py:44
  112.3 4.5 %collective-permute-start.28 = (bf16[16,1024]{1,0:T(8,128)(2,1)S(1)}, bf16[16,1024]{1,0:T(8,128)(2,1)S(1)}, u32[]{:S(2)}, u32[]{:S(2)}) collective-permute-start(bf16[16,1024]{1,0:T(8,128)(2,1)S(1)} %fusion.56), channel_id=1, source_target_pairs={{0,2},{1,3},{2,0},{3,1},{4,6},{5,7},{6,4},{7,5},{8,10},{9,11},{10,... | collective-permute-start | bytes 98312 | tf_op jit(solution)/shard_map/ppermute | solution.py:44
  112.4 5.2 %collective-permute-start.29 = (bf16[16,1024]{1,0:T(8,128)(2,1)S(1)}, bf16[16,1024]{1,0:T(8,128)(2,1)S(1)}, u32[]{:S(2)}, u32[]{:S(2)}) collective-permute-start(bf16[16,1024]{1,0:T(8,128)(2,1)S(1)} %fusion.56), channel_id=1, source_target_pairs={{0,4},{1,5},{2,6},{3,7},{4,0},{5,1},{6,2},{7,3},{8,12},{9,13},{10,... | collective-permute-start | bytes 98312 | tf_op jit(solution)/shard_map/ppermute | solution.py:44
  114.4 5.7 %collective-permute-start.30 = (bf16[16,1024]{1,0:T(8,128)(2,1)S(1)}, bf16[16,1024]{1,0:T(8,128)(2,1)S(1)}, u32[]{:S(2)}, u32[]{:S(2)}) collective-permute-start(bf16[16,1024]{1,0:T(8,128)(2,1)S(1)} %fusion.56), channel_id=1, source_target_pairs={{0,6},{1,7},{2,4},{3,5},{4,2},{5,3},{6,0},{7,1},{8,14},{9,15},{10,... | collective-permute-start | bytes 98312 | tf_op jit(solution)/shard_map/ppermute | solution.py:44
  120.2 1.4 collective-permute-start.31
  122.0 7.1 %collective-permute-start.32 = (bf16[128,640]{1,0:T(8,128)(2,1)S(1)}, bf16[128,640]{1,0:T(8,128)(2,1)S(1)}, u32[]{:S(2)}, u32[]{:S(2)}) collective-permute-start(bf16[128,640]{1,0:T(8,128)(2,1)S(1)} %get-tuple-element.32), channel_id=1, source_target_pairs={{0,8},{8,0},{16,24},{24,16},{1,9},{9,1},{17,25},{25,17},{2,10},{10... | collective-permute-start | bytes 491528 | tf_op jit(solution)/shard_map/ppermute | solution.py:49
  123.6 9.5 %collective-permute-start.33 = (bf16[128,640]{1,0:T(8,128)(2,1)S(1)}, bf16[128,640]{1,0:T(8,128)(2,1)S(1)}, u32[]{:S(2)}, u32[]{:S(2)}) collective-permute-start(bf16[128,640]{1,0:T(8,128)(2,1)S(1)} %get-tuple-element.32), channel_id=1, source_target_pairs={{0,16},{8,24},{16,0},{24,8},{1,17},{9,25},{17,1},{25,9},{2,18},{10... | collective-permute-start | bytes 491528 | tf_op jit(solution)/shard_map/ppermute | solution.py:49
  124.1 9.0 %collective-permute-start.34 = (bf16[128,640]{1,0:T(8,128)(2,1)S(1)}, bf16[128,640]{1,0:T(8,128)(2,1)S(1)}, u32[]{:S(2)}, u32[]{:S(2)}) collective-permute-start(bf16[128,640]{1,0:T(8,128)(2,1)S(1)} %get-tuple-element.32), channel_id=1, source_target_pairs={{0,24},{8,16},{16,8},{24,0},{1,25},{9,17},{17,9},{25,1},{2,26},{10... | collective-permute-start | bytes 491528 | tf_op jit(solution)/shard_map/ppermute | solution.py:49
  133.8 1.4 collective-permute-start.35
  135.2 5.1 %collective-permute-start.36 = (bf16[16,1024]{1,0:T(8,128)(2,1)S(1)}, bf16[16,1024]{1,0:T(8,128)(2,1)S(1)}, u32[]{:S(2)}, u32[]{:S(2)}) collective-permute-start(bf16[16,1024]{1,0:T(8,128)(2,1)S(1)} %get-tuple-element.14), channel_id=1, source_target_pairs={{0,2},{1,3},{2,0},{3,1},{4,6},{5,7},{6,4},{7,5},{8,10},{9,11},{10,... | collective-permute-start | bytes 98312 | tf_op jit(solution)/shard_map/ppermute | solution.py:44
  135.3 5.0 %collective-permute-start.37 = (bf16[16,1024]{1,0:T(8,128)(2,1)S(1)}, bf16[16,1024]{1,0:T(8,128)(2,1)S(1)}, u32[]{:S(2)}, u32[]{:S(2)}) collective-permute-start(bf16[16,1024]{1,0:T(8,128)(2,1)S(1)} %get-tuple-element.16), channel_id=1, source_target_pairs={{0,4},{1,5},{2,6},{3,7},{4,0},{5,1},{6,2},{7,3},{8,12},{9,13},{10,... | collective-permute-start | bytes 98312 | tf_op jit(solution)/shard_map/ppermute | solution.py:44
  138.2 5.7 %collective-permute-start.38 = (bf16[16,1024]{1,0:T(8,128)(2,1)S(1)}, bf16[16,1024]{1,0:T(8,128)(2,1)S(1)}, u32[]{:S(2)}, u32[]{:S(2)}) collective-permute-start(bf16[16,1024]{1,0:T(8,128)(2,1)S(1)} %get-tuple-element.15), channel_id=1, source_target_pairs={{0,6},{1,7},{2,4},{3,5},{4,2},{5,3},{6,0},{7,1},{8,14},{9,15},{10,... | collective-permute-start | bytes 98312 | tf_op jit(solution)/shard_map/ppermute | solution.py:44

commit v2 on v0

v2 whole, which is shorter than its diff:
```python
import functools
import math

import jax
import jax.numpy as jnp
from jax import lax
from jax.experimental import pallas as pl
from jax.experimental.pallas import tpu as pltpu
from jax.sharding import PartitionSpec as P

STEPS = 2
EMBED_BOUND = 6.0
FREQ_BOUND = 0.5
CODE_MAX = 32766.0
LANES = 128
VMEM_BYTES = 48 * 1024 * 1024
COS_TURNS = (
    0.9999999890590243,
    -19.739204499454,
    64.93911745989858,
    -85.45013953092679,
    60.16763095123224,
    -25.967599249288032,
    6.528658162158786,
)
PER_TURN = EMBED_BOUND * FREQ_BOUND / (CODE_MAX * CODE_MAX * 2.0 * math.pi)


def encode(x, bound):
    return jnp.round(x * (CODE_MAX / bound)).astype(jnp.int16)


def split(code):
    wide = code.astype(jnp.float32)
    high = jnp.round(wide * (1.0 / 256.0)) * 256.0
    return high.astype(jnp.bfloat16), (wide - high).astype(jnp.bfloat16)


def scaled_cos(turns, scale):
    turns = turns - jnp.round(turns)
    square = turns * turns
    value = COS_TURNS[-1] * scale
    for coefficient in COS_TURNS[-2::-1]:
        value = value * square + coefficient * scale
    return value.astype(jnp.bfloat16)


def mix(a, b):
    return jnp.dot(a, b, preferred_element_type=jnp.float32)


def core_swap(x):
    n = lax.axis_size("feat")
    return lax.ppermute(x, "feat", [(i, i ^ 1) for i in range(n)])


def line_swap(x, k):
    n = lax.axis_size("feat")
    return lax.ppermute(x, "feat", [(i, i ^ (2 * k)) for i in range(n)])


def line_move(x, pairs):
    return lax.ppermute(x, "feat", [(2 * a + c, 2 * b + c) for a, b in pairs for c in range(2)])


def clip_swap(x, k):
    n = lax.axis_size("clip")
    return lax.ppermute(x, "clip", [(i, i ^ k) for i in range(n)])


def farthest_first(n):
    return range(n - 1, 0, -1)


def gather_four(x, line):
    second = line_swap(x, 2)
    first = line_swap(x, 1)
    middle = line_move(x, [(1, 2), (2, 1)])
    passed = line_move(second, [(1, 0), (2, 3)])
    third = jnp.where((line == 1) | (line == 2), middle, passed)
    return [x, first, second, third]


def early_kernel(at_ref, *refs, slabs, columns):
    embeds, freqs = refs[: 2 * slabs - 2], refs[2 * slabs - 2 : 3 * slabs - 2]
    sum_ref, high_ref, low_ref, freq_ref, f_high, f_low, e_high, e_low = refs[3 * slabs - 2 :]
    depth = e_high.shape[0]
    used = len(embeds) * columns
    for m, ref in enumerate(freqs):
        for h in range(2):
            row = pl.multiple_of(at_ref[2 * m + h], 16)
            freq_ref[pl.ds(row, columns), :] = ref[h * columns : (h + 1) * columns, :].astype(jnp.float32)
    if depth > used:
        freq_ref[used:depth, :] = jnp.zeros((depth - used, freq_ref.shape[1]), jnp.float32)
        e_high[used:depth, :] = jnp.zeros((depth - used, e_high.shape[1]), jnp.bfloat16)
        e_low[used:depth, :] = jnp.zeros((depth - used, e_low.shape[1]), jnp.bfloat16)

    def halves(x):
        high = jnp.round(x * (1.0 / 256.0)) * 256.0
        return high.astype(jnp.bfloat16), (x - high).astype(jnp.bfloat16)

    for start in range(0, depth, LANES):
        f_high[:, start : start + LANES], f_low[:, start : start + LANES] = halves(
            freq_ref[start : start + LANES, :].T
        )
    high_ref[...], low_ref[...] = halves(freq_ref[depth:, :].T)
    for i, ref in enumerate(embeds):
        rows = slice(i * columns, (i + 1) * columns)
        e_high[rows, :], e_low[rows, :] = halves(ref[...].astype(jnp.float32))
    tile = 256 if sum_ref.shape[1] % 256 == 0 else sum_ref.shape[1]
    for start in range(0, sum_ref.shape[1], tile):
        at = slice(start, start + tile)
        sum_ref[:, at] = mix(f_high[...], e_high[:, at]) + (
            mix(f_high[...], e_low[:, at]) + mix(f_low[...], e_high[:, at])
        )


def late_kernel(sum_ref, own_ref, other_ref, high_ref, low_ref, phase_ref, phi_ref, e_high, e_low, *, columns, scale):
    for i, ref in enumerate((own_ref, other_ref)):
        rows = slice(i * columns, (i + 1) * columns)
        e_high[rows, :], e_low[rows, :] = split(ref[...])
    tile = 256 if sum_ref.shape[1] % 256 == 0 else sum_ref.shape[1]
    for start in range(0, sum_ref.shape[1], tile):
        at = slice(start, start + tile)
        total = sum_ref[:, at] + (
            mix(high_ref[...], e_high[:, at])
            + (mix(high_ref[...], e_low[:, at]) + mix(low_ref[...], e_high[:, at]))
        )
        phi_ref[:, at] = scaled_cos(total * PER_TURN + phase_ref[...], scale)


def phi_by_kernels(embed_code, freq_code, phase_turns, scale, line, core, clip):
    slabs = lax.axis_size("clip")
    columns, clips = embed_code.shape
    features = freq_code.shape[1]
    own = gather_four(embed_code, line)
    freqs = [freq_code] + [clip_swap(freq_code, k) for k in range(1, slabs)]
    other = [core_swap(x) for x in own]
    used = 2 * (slabs - 1) * columns
    depth = -(-used // LANES) * LANES
    places = []
    for m in range(slabs):
        k = m ^ line ^ clip
        base = k * 2 * columns + jnp.where(k == slabs - 1, depth - used, 0)
        places += [base + core * columns, base + (1 - core) * columns]
    early = [x for k in range(slabs - 1) for x in (own[k], other[k])]
    vmem = pl.BlockSpec(memory_space=pltpu.VMEM)
    summed, high, low = pl.pallas_call(
        functools.partial(early_kernel, slabs=slabs, columns=columns),
        out_shape=(
            jax.ShapeDtypeStruct((features, clips), jnp.float32),
            jax.ShapeDtypeStruct((features, 2 * columns), jnp.bfloat16),
            jax.ShapeDtypeStruct((features, 2 * columns), jnp.bfloat16),
        ),
        in_specs=[pl.BlockSpec(memory_space=pltpu.SMEM)] + [vmem] * (len(early) + slabs),
        out_specs=(vmem, vmem, vmem),
        scratch_shapes=[
            pltpu.VMEM((depth + 2 * columns, features), jnp.float32),
            pltpu.VMEM((features, depth), jnp.bfloat16),
            pltpu.VMEM((features, depth), jnp.bfloat16),
            pltpu.VMEM((depth, clips), jnp.bfloat16),
            pltpu.VMEM((depth, clips), jnp.bfloat16),
        ],
        compiler_params=pltpu.CompilerParams(vmem_limit_bytes=VMEM_BYTES),
        cost_estimate=pl.CostEstimate(
            flops=6 * features * depth * clips, bytes_accessed=8 * features * clips, transcendentals=0
        ),
        name="early_angles",
    )(jnp.stack(places).astype(jnp.int32), *early, *freqs)
    return pl.pallas_call(
        functools.partial(late_kernel, columns=columns, scale=scale),
        out_shape=jax.ShapeDtypeStruct((features, clips), jnp.bfloat16),
        in_specs=[vmem] * 6,
        out_specs=vmem,
        scratch_shapes=[pltpu.VMEM((2 * columns, clips), jnp.bfloat16)] * 2,
        compiler_params=pltpu.CompilerParams(vmem_limit_bytes=VMEM_BYTES),
        cost_estimate=pl.CostEstimate(
            flops=6 * features * 2 * columns * clips, bytes_accessed=6 * features * clips, transcendentals=0
        ),
        name="late_angles",
    )(summed, own[-1], other[-1], high, low, phase_turns[:, None])


def phi_by_ring(embed_code, freq_code, phase_turns, scale, line, core, clip):
    places, n_clip = lax.axis_size("feat") // 2, lax.axis_size("clip")
    columns, clips = embed_code.shape
    slab, features = freq_code.shape
    freq_all = jnp.zeros((n_clip * slab, features), jnp.int16)
    for k in range(n_clip):
        piece = freq_code if k == 0 else clip_swap(freq_code, k)
        freq_all = lax.dynamic_update_slice_in_dim(freq_all, piece, (clip ^ k) * slab, 0)
    embed_all = jnp.zeros((2 * places * columns, clips), jnp.int16)
    piece = embed_code
    ring = [(i, (i + 1) % places) for i in range(places)]
    for step in range(places):
        if step:
            piece = line_move(piece, ring)
        base = 2 * ((line - step) % places)
        embed_all = lax.dynamic_update_slice_in_dim(embed_all, piece, (base + core) * columns, 0)
        embed_all = lax.dynamic_update_slice_in_dim(
            embed_all, core_swap(piece), (base + 1 - core) * columns, 0
        )

    def dot0(a, b):
        return lax.dot_general(a, b, (((0,), (0,)), ((), ())), preferred_element_type=jnp.float32)

    embed_high, embed_low = split(embed_all)
    freq_high, freq_low = split(freq_all)
    total = dot0(freq_high, embed_high) + (dot0(freq_high, embed_low) + dot0(freq_low, embed_high))
    return scaled_cos(total * PER_TURN + phase_turns[:, None], scale)


def per_device(embeds, frequencies, phases, weights, labels):
    n_feat, n_clip = lax.axis_size("feat"), lax.axis_size("clip")
    feat, clip = lax.axis_index("feat"), lax.axis_index("clip")
    places, line, core = n_feat // 2, feat // 2, feat % 2
    columns = embeds.shape[1]
    features = frequencies.shape[1]
    outputs = labels.shape[1]
    block = outputs // n_feat
    scale = math.sqrt(2.0 / (features * n_feat))

    freq_code = encode(frequencies, FREQ_BOUND)
    embed_code = encode(embeds.T, EMBED_BOUND)
    phase_turns = phases * (0.5 / math.pi)
    by_kernels = places == 4 and n_clip == 4 and columns % 16 == 0 and frequencies.shape[0] == 2 * columns
    phi_of = phi_by_kernels if by_kernels else phi_by_ring
    phi = phi_of(embed_code, freq_code, phase_turns, scale, line, core, clip)
    phi_other = core_swap(phi)

    weights_t = weights.T
    by_clip = jnp.zeros((n_clip, weights_t.shape[0], features), jnp.float32)
    for k in range(n_clip):
        piece = weights_t if k == 0 else clip_swap(weights_t, k)
        by_clip = lax.dynamic_update_slice_in_dim(by_clip, piece[None], clip ^ k, 0)
    by_block = by_clip.reshape(n_feat, block, features)

    def blocks_of(side):
        return jnp.concatenate(
            [
                lax.dynamic_index_in_dim(by_block, 2 * (line ^ k) + side, 0, keepdims=False)
                for k in range(places)
            ]
        )

    beta = blocks_of(core)
    beta_other = core_swap(blocks_of(1 - core))
    targets = lax.dynamic_slice_in_dim(labels.T, feat * block, block, 0).astype(jnp.float32)

    def logits_of(beta, beta_other):
        value = mix(beta.astype(jnp.bfloat16), phi) + mix(beta_other.astype(jnp.bfloat16), phi_other)
        parts = value.reshape(places, block, -1)
        half = parts.astype(jnp.bfloat16)
        total = parts[0]
        for k in farthest_first(places):
            total = total + line_swap(half[k], k).astype(jnp.float32)
        return total

    def gradient_of(residual, phi):
        return lax.dot_general(residual, phi, (((1,), (1,)), ((), ())), preferred_element_type=jnp.float32)

    for step in range(STEPS):
        share = (jax.nn.sigmoid(logits_of(beta, beta_other)) - targets).astype(jnp.bfloat16)
        found = {k: line_swap(share, k) for k in farthest_first(places)}
        residual = jnp.concatenate([share] + [found[k] for k in range(1, places)])
        grad = jnp.concatenate([gradient_of(residual, phi), gradient_of(residual, phi_other)], axis=1)
        sent = grad.astype(jnp.bfloat16)
        for k in farthest_first(n_clip):
            grad = grad + clip_swap(sent, k).astype(jnp.float32)
        beta = beta - 0.25 * grad[:, :features]
        beta_other = beta_other - 0.25 * grad[:, features:]
    scores = logits_of(beta, beta_other).T
    ours = beta.reshape(places, block, features)
    theirs = core_swap(beta_other).reshape(places, block, features)
    rows = []
    for b in range(places // n_clip):
        k = line ^ (clip * (places // n_clip) + b)
        mine = lax.dynamic_index_in_dim(ours, k, 0, keepdims=False)
        their = lax.dynamic_index_in_dim(theirs, k, 0, keepdims=False)
        rows += [jnp.where(core == 0, mine, their), jnp.where(core == 0, their, mine)]
    trained = jnp.concatenate(rows).T
    return (trained, scores)


def solution(mesh):
    placed = (P("clip", "feat"), P("clip", "feat"), P("feat"), P("feat", "clip"), P("clip", None))
    return jax.shard_map(
        per_device,
        mesh=mesh,
        in_specs=placed,
        out_specs=(P("feat", "clip"), P("clip", "feat")),
        check_vma=False,
    )
```

time: 333 us -> 129 us (0.39)
  waiting for transfers between devices: 228 us -> 48.9 us
  blocking collectives: 55.9 us -> 0 us
  starting transfers between devices: 0.46 us -> 48 us
  matrix products: 29.6 us -> 4.87 us
  between operations: 14.2 us -> 1.14 us
  Pallas kernels: 0 us -> 10.9 us
  local copies, waits for them, and re-layouts: 0.39 us -> 9 us
    all_gather x2 -> x0, waiting for transfers between devices: 89.5 us -> none  [the longest x1 53.4 us: per_device(): lax.all_gather(embeds, 'feat', axis=1, tiled=True)]
    reduce_scatter x3 -> x0, waiting for transfers between devices: 76.3 us -> none  [the longest x2 45.2 us: per_device(): lax.psum_scatter(grad_part, 'clip', scatter_dimension=1, tiled=True)]
    unnamed x9 -> x0, waiting for transfers between devices: 61.8 us -> none
    all_gather x5 -> x0, blocking collectives: 55.9 us -> none  [the longest x2 28.4 us: per_device(): residual = lax.all_gather(residual_share, 'feat', axis=1, tiled=True)]
    ppermute x0 -> x38, waiting for transfers between devices: none -> 48.9 us  [the longest x17 26.7 us: line_swap(): return lax.ppermute(x, 'feat', [(i, i ^ 2 * k) for i in range(n)])]
    ppermute x0 -> x38, starting transfers between devices: none -> 48 us  [the longest x17 29.5 us: line_swap(): return lax.ppermute(x, 'feat', [(i, i ^ 2 * k) for i in range(n)])]
    dot_general x4 -> x10, matrix products: 26.9 us -> 4.87 us  [the longest x6 2.84 us: mix(): return jnp.dot(a, b, preferred_element_type=jnp.float32)]
    pallas_call x0 -> x2, Pallas kernels: none -> 10.9 us  [the longest x1 7.42 us: phi_by_kernels(): pl.pallas_call(functools.partial(early_kernel, slabs=slabs, columns=colum...]
  transfers between devices with their start and end apart: 7 -> 38, of which waited for: 7 -> 22; matrix products, arithmetic and copies ran while one was open for 0% -> 6% of each run, Pallas kernels for 0% -> 9%
where the time goes in v2:
time: 129 us; the launch traced here: 128 us
  waiting for transfers between devices  48.9 us (38%)
  starting transfers between devices  48 us (37%)
  Pallas kernels  10.9 us (8%)
  local copies, waits for them, and re-layouts  9 us (7%)
  other arithmetic  5.66 us (4%)
  matrix products  4.87 us (4%)
    ppermute x17, starting transfers between devices, line_swap(): return lax.ppermute(x, 'feat', [(i, i ^ 2 * k) for i in range(n)])  29.5 us
    ppermute x17, waiting for transfers between devices, line_swap(): return lax.ppermute(x, 'feat', [(i, i ^ 2 * k) for i in range(n)])  26.7 us
    ppermute x12, waiting for transfers between devices, clip_swap(): return lax.ppermute(x, 'clip', [(i, i ^ k) for i in range(n)])  16.3 us
    ppermute x12, starting transfers between devices, clip_swap(): return lax.ppermute(x, 'clip', [(i, i ^ k) for i in range(n)])  15.8 us
    pallas_call x1, Pallas kernels, phi_by_kernels(): pl.pallas_call(functools.partial(early_kernel, slabs=slabs, columns=colum...  7.42 us
    ppermute x2, waiting for transfers between devices, line_move(): lax.ppermute(x, 'feat', [(2 * a + c, 2 * b + c) for a, b in pairs for c i...  4.26 us
    unnamed x23, local copies, waits for them, and re-layouts  3.71 us
    pallas_call x1, Pallas kernels, phi_by_kernels(): pl.pallas_call(functools.partial(late_kernel, columns=columns, scale=scal...  3.5 us
  transfers between devices with their start and end apart: 38, of which 22 were waited for; matrix products, arithmetic and copies ran while one was open for 6% of the time, Pallas kernels for 9%

profile of v2, /device:TPU:0, one launch (start us, length us, event | category | flops | bytes accessed | tf_op | source)
XLA Modules:
  0.0 128.4 jit_solution(1897751167119484277)
XLA Ops:
  0.7 1.3 fusion.refs_0_
  1.9 4.1 %collective-permute-start.6 = (s16[144,1024]{1,0:T(8,128)(2,1)S(1)}, s16[144,1024]{1,0:T(8,128)(2,1)S(1)}, u32[]{:S(2)}, u32[]{:S(2)}) collective-permute-start(s16[144,1024]{1,0:T(8,128)(2,1)S(1)} %fusion.refs_0_), channel_id=1, source_target_pairs={{0,4},{1,5},{2,6},{3,7},{4,0},{5,1},{6,2},{7,3},{8,12},{9,13},{10,... | collective-permute-start | bytes 884744 | tf_op jit(solution)/shard_map/ppermute | solution.py:59
  6.0 1.6 %collective-permute-start.4 = (s16[144,1024]{1,0:T(8,128)(2,1)S(1)}, s16[144,1024]{1,0:T(8,128)(2,1)}, u32[]{:S(2)}, u32[]{:S(2)}) collective-permute-start(s16[144,1024]{1,0:T(8,128)(2,1)S(1)} %fusion.refs_0_), channel_id=1, source_target_pairs={{0,2},{1,3},{2,0},{3,1},{4,6},{5,7},{6,4},{7,5},{8,10},{9,11},{10,... | collective-permute-start | bytes 884744 | tf_op jit(solution)/shard_map/ppermute | solution.py:59
  7.6 0.7 collective-permute-start.11
  8.3 11.9 %collective-permute-done.6.refs_4_ = s16[144,1024]{1,0:T(8,128)(2,1)S(1)} collective-permute-done((s16[144,1024]{1,0:T(8,128)(2,1)S(1)}, s16[144,1024]{1,0:T(8,128)(2,1)S(1)}, u32[]{:S(2)}, u32[]{:S(2)}) %collective-permute-start.6) | collective-permute-done | bytes 294944 | tf_op jit(solution)/shard_map/ppermute | solution.py:59
  20.2 1.3 collective-permute-start.12
  21.7 1.9 %collective-permute-start.8 = (s16[288,640]{1,0:T(8,128)(2,1)S(1)}, s16[288,640]{1,0:T(8,128)(2,1)S(1)}, u32[]{:S(2)}, u32[]{:S(2)}) collective-permute-start(s16[288,640]{1,0:T(8,128)(2,1)S(1)} %round-nearest-even_convert_fusion.refs_6_), channel_id=1, source_target_pairs={{0,8},{8,0},{16,24},{24,16},{1,9},{9,1},{17,25},{25,17},{2,10},{10... | collective-permute-start | bytes 1105928 | tf_op jit(solution)/shard_map/ppermute | solution.py:68
  23.6 1.5 %collective-permute-start.9 = (s16[288,640]{1,0:T(8,128)(2,1)S(1)}, s16[288,640]{1,0:T(8,128)(2,1)S(1)}, u32[]{:S(2)}, u32[]{:S(2)}) collective-permute-start(s16[288,640]{1,0:T(8,128)(2,1)S(1)} %round-nearest-even_convert_fusion.refs_6_), channel_id=1, source_target_pairs={{0,16},{8,24},{16,0},{24,8},{1,17},{9,25},{17,1},{25,9},{2,18},{10... | collective-permute-start | bytes 1105928 | tf_op jit(solution)/shard_map/ppermute | solution.py:68
  25.2 4.3 %collective-permute-done.12 = s16[144,1024]{1,0:T(8,128)(2,1)S(1)} collective-permute-done((s16[144,1024]{1,0:T(8,128)(2,1)S(1)}, s16[144,1024]{1,0:T(8,128)(2,1)S(1)}, u32[]{:S(2)}, u32[]{:S(2)}) %collective-permute-start.12) | collective-permute-done | bytes 294944 | tf_op jit(solution)/shard_map/ppermute | solution.py:63
  29.5 0.7 copy-done.8
  30.5 1.0 broadcast_select_fusion.own_ref
  31.6 1.7 %collective-permute-done.8.refs_7_ = s16[288,640]{1,0:T(8,128)(2,1)S(1)} collective-permute-done((s16[288,640]{1,0:T(8,128)(2,1)S(1)}, s16[288,640]{1,0:T(8,128)(2,1)S(1)}, u32[]{:S(2)}, u32[]{:S(2)}) %collective-permute-start.8) | collective-permute-done | bytes 368672 | tf_op jit(solution)/shard_map/ppermute | solution.py:68
  33.2 1.8 %collective-permute-start = (f32[32,640]{1,0:T(8,128)}, f32[32,640]{1,0:T(8,128)}, u32[]{:S(2)}, u32[]{:S(2)}) collective-permute-start(f32[32,640]{1,0:T(8,128)} %bitcast.66), channel_id=1, source_target_pairs={{0,8},{8,0},{16,24},{24,16},{1,9},{9,1},{17,25},{25,17},{2,10},{10... | collective-permute-start | bytes 245768 | tf_op jit(solution)/shard_map/ppermute | solution.py:68
  35.1 4.4 %collective-permute-done.9.refs_8_ = s16[288,640]{1,0:T(8,128)(2,1)S(1)} collective-permute-done((s16[288,640]{1,0:T(8,128)(2,1)S(1)}, s16[288,640]{1,0:T(8,128)(2,1)S(1)}, u32[]{:S(2)}, u32[]{:S(2)}) %collective-permute-start.9) | collective-permute-done | bytes 368672 | tf_op jit(solution)/shard_map/ppermute | solution.py:68
  39.5 3.3 %collective-permute-start.1 = (f32[32,640]{1,0:T(8,128)}, f32[32,640]{1,0:T(8,128)}, u32[]{:S(2)}, u32[]{:S(2)}) collective-permute-start(f32[32,640]{1,0:T(8,128)} %bitcast.67), channel_id=1, source_target_pairs={{0,16},{8,24},{16,0},{24,8},{1,17},{9,25},{17,1},{25,9},{2,18},{10... | collective-permute-start | bytes 245768 | tf_op jit(solution)/shard_map/ppermute | solution.py:68
  42.9 7.4 %early_angles.1 = (f32[640,1024]{1,0:T(8,128)}, bf16[640,288]{1,0:T(8,128)(2,1)S(1)}, bf16[640,288]{1,0:T(8,128)(2,1)S(1)}) custom-call(s32[8]{0:T(128)S(1)} %stack.35.at_ref, s16[144,1024]{1,0:T(8,128)(2,1)S(1)} %fusion.refs_0_, s16[144,1024]{1,0:T(8,128)(2,1)S(1)} %collective-permute-done.3.refs_1_, s16[144,1024]{1,0:T(8,128)(2,1)} %collective-permute-done.4.refs_2_, ...), custom_call_target="tpu_custom_call" | custom-call | flops 3523215360 | bytes 5242880 | tf_op jit(solution)/shard_map/early_angles/pallas_call | solution.py:148
  50.3 1.7 %copy-done.1 = f32[640,1024]{1,0:T(8,128)S(1)} copy-done((f32[640,1024]{1,0:T(8,128)S(1)}, f32[640,1024]{1,0:T(8,128)}, u32[]{:S(2)}) %copy-start.1) | copy-done | bytes 2621464
  52.0 3.5 %late_angles.1 = bf16[640,1024]{1,0:T(8,128)(2,1)S(1)} custom-call(f32[640,1024]{1,0:T(8,128)S(1)} %copy-done.1, s16[144,1024]{1,0:T(8,128)(2,1)S(1)} %broadcast_select_fusion.own_ref, s16[144,1024]{1,0:T(8,128)(2,1)S(1)} %collective-permute-done.13.other_ref, bf16[640,288]{1,0:T(8,128)(2,1)S(1)} %get-tuple-element.6.high_ref, ...), custom_call_target="tpu_custom_call" | custom-call | flops 1132462080 | bytes 3932160 | tf_op jit(solution)/shard_map/late_angles/pallas_call | solution.py:170
  55.6 0.6 collective-permute-start.15
  56.3 0.9 bitcast_dynamic-update-slice_fusion.3
  57.2 0.9 bitcast_dynamic-update-slice_fusion.2
  58.1 0.9 bitcast_dynamic-update-slice_fusion.1
  59.0 0.7 dynamic-slice_bitcast_fusion.7
  59.6 0.7 pad_maximum_fusion.3
  60.3 1.6 %collective-permute-done.14 = f32[64,640]{1,0:T(8,128)S(1)} collective-permute-done((f32[64,640]{1,0:T(8,128)}, f32[64,640]{1,0:T(8,128)S(1)}, u32[]{:S(2)}, u32[]{:S(2)}) %collective-permute-start.14) | collective-permute-done | bytes 163872 | tf_op jit(solution)/shard_map/ppermute | solution.py:54
  62.3 1.1 fusion.51
  63.4 0.6 fusion.50
  64.0 2.4 %collective-permute-start.18 = (bf16[16,1024]{1,0:T(8,128)(2,1)}, bf16[16,1024]{1,0:T(8,128)(2,1)}, u32[]{:S(2)}, u32[]{:S(2)}) collective-permute-start(bf16[16,1024]{1,0:T(8,128)(2,1)} %get-tuple-element.27), channel_id=1, source_target_pairs={{0,2},{1,3},{2,0},{3,1},{4,6},{5,7},{6,4},{7,5},{8,10},{9,11},{10,... | collective-permute-start | bytes 98312 | tf_op jit(solution)/shard_map/ppermute | solution.py:59
  66.4 2.2 %collective-permute-start.17 = (bf16[16,1024]{1,0:T(8,128)(2,1)}, bf16[16,1024]{1,0:T(8,128)(2,1)}, u32[]{:S(2)}, u32[]{:S(2)}) collective-permute-start(bf16[16,1024]{1,0:T(8,128)(2,1)} %get-tuple-element.28), channel_id=1, source_target_pairs={{0,4},{1,5},{2,6},{3,7},{4,0},{5,1},{6,2},{7,3},{8,12},{9,13},{10,... | collective-permute-start | bytes 98312 | tf_op jit(solution)/shard_map/ppermute | solution.py:59
  68.6 1.5 %collective-permute-start.16 = (bf16[16,1024]{1,0:T(8,128)(2,1)}, bf16[16,1024]{1,0:T(8,128)(2,1)}, u32[]{:S(2)}, u32[]{:S(2)}) collective-permute-start(bf16[16,1024]{1,0:T(8,128)(2,1)} %get-tuple-element.26), channel_id=1, source_target_pairs={{0,6},{1,7},{2,4},{3,5},{4,2},{5,3},{6,0},{7,1},{8,14},{9,15},{10,... | collective-permute-start | bytes 98312 | tf_op jit(solution)/shard_map/ppermute | solution.py:59
  70.0 1.0 constant_dynamic-slice_fusion
  71.0 1.2 copy.10
  72.3 2.3 %collective-permute-done.16 = bf16[16,1024]{1,0:T(8,128)(2,1)} collective-permute-done((bf16[16,1024]{1,0:T(8,128)(2,1)}, bf16[16,1024]{1,0:T(8,128)(2,1)}, u32[]{:S(2)}, u32[]{:S(2)}) %collective-permute-start.16) | collective-permute-done | bytes 32800 | tf_op jit(solution)/shard_map/ppermute | solution.py:59
  74.6 0.9 fusion.34
  75.6 1.6 %collective-permute-start.21 = (bf16[16,1024]{1,0:T(8,128)(2,1)S(1)}, bf16[16,1024]{1,0:T(8,128)(2,1)S(1)}, u32[]{:S(2)}, u32[]{:S(2)}) collective-permute-start(bf16[16,1024]{1,0:T(8,128)(2,1)S(1)} %fusion.34), channel_id=1, source_target_pairs={{0,6},{1,7},{2,4},{3,5},{4,2},{5,3},{6,0},{7,1},{8,14},{9,15},{10,... | collective-permute-start | bytes 98312 | tf_op jit(solution)/shard_map/ppermute | solution.py:59
  77.3 2.7 %collective-permute-start.19 = (bf16[16,1024]{1,0:T(8,128)(2,1)S(1)}, bf16[16,1024]{1,0:T(8,128)(2,1)S(1)}, u32[]{:S(2)}, u32[]{:S(2)}) collective-permute-start(bf16[16,1024]{1,0:T(8,128)(2,1)S(1)} %fusion.34), channel_id=1, source_target_pairs={{0,2},{1,3},{2,0},{3,1},{4,6},{5,7},{6,4},{7,5},{8,10},{9,11},{10,... | collective-permute-start | bytes 98312 | tf_op jit(solution)/shard_map/ppermute | solution.py:59
  80.0 1.3 %collective-permute-done.21 = bf16[16,1024]{1,0:T(8,128)(2,1)S(1)} collective-permute-done((bf16[16,1024]{1,0:T(8,128)(2,1)S(1)}, bf16[16,1024]{1,0:T(8,128)(2,1)S(1)}, u32[]{:S(2)}, u32[]{:S(2)}) %collective-permute-start.21) | collective-permute-done | bytes 32800 | tf_op jit(solution)/shard_map/ppermute | solution.py:59
  81.3 0.8 collective-permute-done.20
  83.3 1.5 %collective-permute-start.24 = (bf16[64,1280]{1,0:T(8,128)(2,1)S(1)}, bf16[64,1280]{1,0:T(8,128)(2,1)S(1)}, u32[]{:S(2)}, u32[]{:S(2)}) collective-permute-start(bf16[64,1280]{1,0:T(8,128)(2,1)S(1)} %fusion.2), channel_id=1, source_target_pairs={{0,8},{8,0},{16,24},{24,16},{1,9},{9,1},{17,25},{25,17},{2,10},{10... | collective-permute-start | bytes 491528 | tf_op jit(solution)/shard_map/ppermute | solution.py:68
  84.8 2.0 %collective-permute-start.23 = (bf16[64,1280]{1,0:T(8,128)(2,1)S(1)}, bf16[64,1280]{1,0:T(8,128)(2,1)S(1)}, u32[]{:S(2)}, u32[]{:S(2)}) collective-permute-start(bf16[64,1280]{1,0:T(8,128)(2,1)S(1)} %fusion.2), channel_id=1, source_target_pairs={{0,16},{8,24},{16,0},{24,8},{1,17},{9,25},{17,1},{25,9},{2,18},{10... | collective-permute-start | bytes 491528 | tf_op jit(solution)/shard_map/ppermute | solution.py:68
  86.9 2.9 %collective-permute-done.24 = bf16[64,1280]{1,0:T(8,128)(2,1)S(1)} collective-permute-done((bf16[64,1280]{1,0:T(8,128)(2,1)S(1)}, bf16[64,1280]{1,0:T(8,128)(2,1)S(1)}, u32[]{:S(2)}, u32[]{:S(2)}) %collective-permute-start.24) | collective-permute-done | bytes 163872 | tf_op jit(solution)/shard_map/ppermute | solution.py:68
  89.8 1.7 %collective-permute-done.23 = bf16[64,1280]{1,0:T(8,128)(2,1)S(1)} collective-permute-done((bf16[64,1280]{1,0:T(8,128)(2,1)S(1)}, bf16[64,1280]{1,0:T(8,128)(2,1)S(1)}, u32[]{:S(2)}, u32[]{:S(2)}) %collective-permute-start.23) | collective-permute-done | bytes 163872 | tf_op jit(solution)/shard_map/ppermute | solution.py:68
  91.5 1.5 %collective-permute-done.22 = bf16[64,1280]{1,0:T(8,128)(2,1)S(1)} collective-permute-done((bf16[64,1280]{1,0:T(8,128)(2,1)S(1)}, bf16[64,1280]{1,0:T(8,128)(2,1)S(1)}, u32[]{:S(2)}, u32[]{:S(2)}) %collective-permute-start.22) | collective-permute-done | bytes 163872 | tf_op jit(solution)/shard_map/ppermute | solution.py:68
  93.8 1.7 %collective-permute-start.27 = (bf16[16,1024]{1,0:T(8,128)(2,1)S(1)}, bf16[16,1024]{1,0:T(8,128)(2,1)S(1)}, u32[]{:S(2)}, u32[]{:S(2)}) collective-permute-start(bf16[16,1024]{1,0:T(8,128)(2,1)S(1)} %get-tuple-element.24), channel_id=1, source_target_pairs={{0,2},{1,3},{2,0},{3,1},{4,6},{5,7},{6,4},{7,5},{8,10},{9,11},{10,... | collective-permute-start | bytes 98312 | tf_op jit(solution)/shard_map/ppermute | solution.py:59
  95.6 0.9 collective-permute-start.26
  96.5 1.8 %collective-permute-start.25 = (bf16[16,1024]{1,0:T(8,128)(2,1)S(1)}, bf16[16,1024]{1,0:T(8,128)(2,1)S(1)}, u32[]{:S(2)}, u32[]{:S(2)}) collective-permute-start(bf16[16,1024]{1,0:T(8,128)(2,1)S(1)} %get-tuple-element.23), channel_id=1, source_target_pairs={{0,6},{1,7},{2,4},{3,5},{4,2},{5,3},{6,0},{7,1},{8,14},{9,15},{10,... | collective-permute-start | bytes 98312 | tf_op jit(solution)/shard_map/ppermute | solution.py:59
  98.3 2.2 %collective-permute-done.26 = bf16[16,1024]{1,0:T(8,128)(2,1)S(1)} collective-permute-done((bf16[16,1024]{1,0:T(8,128)(2,1)S(1)}, bf16[16,1024]{1,0:T(8,128)(2,1)S(1)}, u32[]{:S(2)}, u32[]{:S(2)}) %collective-permute-start.26) | collective-permute-done | bytes 32800 | tf_op jit(solution)/shard_map/ppermute | solution.py:59
  100.5 2.0 %collective-permute-done.25 = bf16[16,1024]{1,0:T(8,128)(2,1)S(1)} collective-permute-done((bf16[16,1024]{1,0:T(8,128)(2,1)S(1)}, bf16[16,1024]{1,0:T(8,128)(2,1)S(1)}, u32[]{:S(2)}, u32[]{:S(2)}) %collective-permute-start.25) | collective-permute-done | bytes 32800 | tf_op jit(solution)/shard_map/ppermute | solution.py:59
  102.6 1.5 %collective-permute-start.30 = (bf16[16,1024]{1,0:T(8,128)(2,1)S(1)}, bf16[16,1024]{1,0:T(8,128)(2,1)S(1)}, u32[]{:S(2)}, u32[]{:S(2)}) collective-permute-start(bf16[16,1024]{1,0:T(8,128)(2,1)S(1)} %fusion.35), channel_id=1, source_target_pairs={{0,6},{1,7},{2,4},{3,5},{4,2},{5,3},{6,0},{7,1},{8,14},{9,15},{10,... | collective-permute-start | bytes 98312 | tf_op jit(solution)/shard_map/ppermute | solution.py:59
  104.1 2.9 %collective-permute-start.28 = (bf16[16,1024]{1,0:T(8,128)(2,1)S(1)}, bf16[16,1024]{1,0:T(8,128)(2,1)S(1)}, u32[]{:S(2)}, u32[]{:S(2)}) collective-permute-start(bf16[16,1024]{1,0:T(8,128)(2,1)S(1)} %fusion.35), channel_id=1, source_target_pairs={{0,2},{1,3},{2,0},{3,1},{4,6},{5,7},{6,4},{7,5},{8,10},{9,11},{10,... | collective-permute-start | bytes 98312 | tf_op jit(solution)/shard_map/ppermute | solution.py:59
  107.0 1.3 %collective-permute-done.30 = bf16[16,1024]{1,0:T(8,128)(2,1)S(1)} collective-permute-done((bf16[16,1024]{1,0:T(8,128)(2,1)S(1)}, bf16[16,1024]{1,0:T(8,128)(2,1)S(1)}, u32[]{:S(2)}, u32[]{:S(2)}) %collective-permute-start.30) | collective-permute-done | bytes 32800 | tf_op jit(solution)/shard_map/ppermute | solution.py:59
  108.4 0.8 collective-permute-done.29
  110.4 0.6 collective-permute-start.33
  110.9 0.8 collective-permute-start.32
  111.7 2.2 %collective-permute-start.31 = (bf16[64,1280]{1,0:T(8,128)(2,1)S(1)}, bf16[64,1280]{1,0:T(8,128)(2,1)S(1)}, u32[]{:S(2)}, u32[]{:S(2)}) collective-permute-start(bf16[64,1280]{1,0:T(8,128)(2,1)S(1)} %fusion.1), channel_id=1, source_target_pairs={{0,24},{8,16},{16,8},{24,0},{1,25},{9,17},{17,9},{25,1},{2,26},{10... | collective-permute-start | bytes 491528 | tf_op jit(solution)/shard_map/ppermute | solution.py:68
  113.9 1.8 %collective-permute-done.33 = bf16[64,1280]{1,0:T(8,128)(2,1)S(1)} collective-permute-done((bf16[64,1280]{1,0:T(8,128)(2,1)S(1)}, bf16[64,1280]{1,0:T(8,128)(2,1)S(1)}, u32[]{:S(2)}, u32[]{:S(2)}) %collective-permute-start.33) | collective-permute-done | bytes 163872 | tf_op jit(solution)/shard_map/ppermute | solution.py:68
  116.3 1.7 %collective-permute-done.31 = bf16[64,1280]{1,0:T(8,128)(2,1)S(1)} collective-permute-done((bf16[64,1280]{1,0:T(8,128)(2,1)S(1)}, bf16[64,1280]{1,0:T(8,128)(2,1)S(1)}, u32[]{:S(2)}, u32[]{:S(2)}) %collective-permute-start.31) | collective-permute-done | bytes 163872 | tf_op jit(solution)/shard_map/ppermute | solution.py:68
  119.0 1.3 %collective-permute-start.37 = (bf16[16,1024]{1,0:T(8,128)(2,1)S(1)}, bf16[16,1024]{1,0:T(8,128)(2,1)S(1)}, u32[]{:S(2)}, u32[]{:S(2)}) collective-permute-start(bf16[16,1024]{1,0:T(8,128)(2,1)S(1)} %get-tuple-element.21), channel_id=1, source_target_pairs={{0,2},{1,3},{2,0},{3,1},{4,6},{5,7},{6,4},{7,5},{8,10},{9,11},{10,... | collective-permute-start | bytes 98312 | tf_op jit(solution)/shard_map/ppermute | solution.py:59
  120.3 1.1 collective-permute-start.36
  121.4 2.0 %collective-permute-start.35 = (bf16[16,1024]{1,0:T(8,128)(2,1)S(1)}, bf16[16,1024]{1,0:T(8,128)(2,1)S(1)}, u32[]{:S(2)}, u32[]{:S(2)}) collective-permute-start(bf16[16,1024]{1,0:T(8,128)(2,1)S(1)} %get-tuple-element.20), channel_id=1, source_target_pairs={{0,6},{1,7},{2,4},{3,5},{4,2},{5,3},{6,0},{7,1},{8,14},{9,15},{10,... | collective-permute-start | bytes 98312 | tf_op jit(solution)/shard_map/ppermute | solution.py:59
  123.4 2.0 %collective-permute-done.36 = bf16[16,1024]{1,0:T(8,128)(2,1)S(1)} collective-permute-done((bf16[16,1024]{1,0:T(8,128)(2,1)S(1)}, bf16[16,1024]{1,0:T(8,128)(2,1)S(1)}, u32[]{:S(2)}, u32[]{:S(2)}) %collective-permute-start.36) | collective-permute-done | bytes 32800 | tf_op jit(solution)/shard_map/ppermute | solution.py:59
  125.4 1.7 %collective-permute-done.35 = bf16[16,1024]{1,0:T(8,128)(2,1)S(1)} collective-permute-done((bf16[16,1024]{1,0:T(8,128)(2,1)S(1)}, bf16[16,1024]{1,0:T(8,128)(2,1)S(1)}, u32[]{:S(2)}, u32[]{:S(2)}) %collective-permute-start.35) | collective-permute-done | bytes 32800 | tf_op jit(solution)/shard_map/ppermute | solution.py:59
  127.1 0.6 fusion.19
  127.8 0.6 maximum_bitcast_fusion
  (74 shorter events, 5.8 us)
Async XLA Ops:
  0.6 69.4 %copy-start = (s32[1024,128]{1,0:T(8,128)S(1)}, s32[1024,128]{1,0:T(8,128)}, u32[]{:S(2)}) copy-start(s32[1024,128]{1,0:T(8,128)} %param.9) | copy-start | bytes 1572868
  0.6 20.9 %copy-start.2 = (f32[288,640]{1,0:T(8,128)S(1)}, f32[288,640]{1,0:T(8,128)}, u32[]{:S(2)}) copy-start(f32[288,640]{1,0:T(8,128)} %param.6) | copy-start | bytes 2211844
  0.7 29.6 %copy-start.10 = (f32[640]{0:T(1024)S(1)}, f32[640]{0:T(1024)}, u32[]{:S(2)}) copy-start(f32[640]{0:T(1024)} %param.7) | copy-start | bytes 7684
  1.9 18.3 %collective-permute-start.6 = (s16[144,1024]{1,0:T(8,128)(2,1)S(1)}, s16[144,1024]{1,0:T(8,128)(2,1)S(1)}, u32[]{:S(2)}, u32[]{:S(2)}) collective-permute-start(s16[144,1024]{1,0:T(8,128)(2,1)S(1)} %fusion.refs_0_), channel_id=1, source_target_pairs={{0,4},{1,5},{2,6},{3,7},{4,0},{5,1},{6,2},{7,3},{8,12},{9,13},{10,... | collective-permute-start | bytes 884744 | tf_op jit(solution)/shard_map/ppermute | solution.py:59
  6.0 17.5 %collective-permute-start.3 = (s16[144,1024]{1,0:T(8,128)(2,1)S(1)}, s16[144,1024]{1,0:T(8,128)(2,1)S(1)}, u32[]{:S(2)}, u32[]{:S(2)}) collective-permute-start(s16[144,1024]{1,0:T(8,128)(2,1)S(1)} %fusion.refs_0_), channel_id=1, source_target_pairs={{0,1},{1,0},{2,3},{3,2},{4,5},{5,4},{6,7},{7,6},{8,9},{9,8},{10,11... | collective-permute-start | bytes 884744 | tf_op jit(solution)/shard_map/ppermute | solution.py:54
  6.0 19.1 %collective-permute-start.4 = (s16[144,1024]{1,0:T(8,128)(2,1)S(1)}, s16[144,1024]{1,0:T(8,128)(2,1)}, u32[]{:S(2)}, u32[]{:S(2)}) collective-permute-start(s16[144,1024]{1,0:T(8,128)(2,1)S(1)} %fusion.refs_0_), channel_id=1, source_target_pairs={{0,2},{1,3},{2,0},{3,1},{4,6},{5,7},{6,4},{7,5},{8,10},{9,11},{10,... | collective-permute-start | bytes 884744 | tf_op jit(solution)/shard_map/ppermute | solution.py:59
  7.6 17.6 %collective-permute-start.11 = (s16[144,1024]{1,0:T(8,128)(2,1)S(1)}, s16[144,1024]{1,0:T(8,128)(2,1)S(1)}, u32[]{:S(2)}, u32[]{:S(2)}) collective-permute-start(s16[144,1024]{1,0:T(8,128)(2,1)S(1)} %fusion.refs_0_), channel_id=1, source_target_pairs={{2,4},{3,5},{4,2},{5,3},{10,12},{11,13},{12,10},{13,11},{18,20},{1... | collective-permute-start | bytes 884744 | tf_op jit(solution)/shard_map/ppermute | solution.py:63
  20.2 9.2 %collective-permute-start.12 = (s16[144,1024]{1,0:T(8,128)(2,1)S(1)}, s16[144,1024]{1,0:T(8,128)(2,1)S(1)}, u32[]{:S(2)}, u32[]{:S(2)}) collective-permute-start(s16[144,1024]{1,0:T(8,128)(2,1)S(1)} %collective-permute-done.6.refs_4_), channel_id=1, source_target_pairs={{2,0},{3,1},{4,6},{5,7},{10,8},{11,9},{12,14},{13,15},{18,16},{19,... | collective-permute-start | bytes 884744 | tf_op jit(solution)/shard_map/ppermute | solution.py:63
  21.7 11.6 %collective-permute-start.8 = (s16[288,640]{1,0:T(8,128)(2,1)S(1)}, s16[288,640]{1,0:T(8,128)(2,1)S(1)}, u32[]{:S(2)}, u32[]{:S(2)}) collective-permute-start(s16[288,640]{1,0:T(8,128)(2,1)S(1)} %round-nearest-even_convert_fusion.refs_6_), channel_id=1, source_target_pairs={{0,8},{8,0},{16,24},{24,16},{1,9},{9,1},{17,25},{25,17},{2,10},{10... | collective-permute-start | bytes 1105928 | tf_op jit(solution)/shard_map/ppermute | solution.py:68
  23.6 15.9 %collective-permute-start.9 = (s16[288,640]{1,0:T(8,128)(2,1)S(1)}, s16[288,640]{1,0:T(8,128)(2,1)S(1)}, u32[]{:S(2)}, u32[]{:S(2)}) collective-permute-start(s16[288,640]{1,0:T(8,128)(2,1)S(1)} %round-nearest-even_convert_fusion.refs_6_), channel_id=1, source_target_pairs={{0,16},{8,24},{16,0},{24,8},{1,17},{9,25},{17,1},{25,9},{2,18},{10... | collective-permute-start | bytes 1105928 | tf_op jit(solution)/shard_map/ppermute | solution.py:68
  25.1 17.7 %collective-permute-start.10 = (s16[288,640]{1,0:T(8,128)(2,1)S(1)}, s16[288,640]{1,0:T(8,128)(2,1)S(1)}, u32[]{:S(2)}, u32[]{:S(2)}) collective-permute-start(s16[288,640]{1,0:T(8,128)(2,1)S(1)} %round-nearest-even_convert_fusion.refs_6_), channel_id=1, source_target_pairs={{0,24},{8,16},{16,8},{24,0},{1,25},{9,17},{17,9},{25,1},{2,26},{10... | collective-permute-start | bytes 1105928 | tf_op jit(solution)/shard_map/ppermute | solution.py:68
  25.2 17.7 %collective-permute-start.7 = (s16[144,1024]{1,0:T(8,128)(2,1)S(1)}, s16[144,1024]{1,0:T(8,128)(2,1)}, u32[]{:S(2)}, u32[]{:S(2)}) collective-permute-start(s16[144,1024]{1,0:T(8,128)(2,1)S(1)} %collective-permute-done.6.refs_4_), channel_id=1, source_target_pairs={{0,1},{1,0},{2,3},{3,2},{4,5},{5,4},{6,7},{7,6},{8,9},{9,8},{10,11... | collective-permute-start | bytes 884744 | tf_op jit(solution)/shard_map/ppermute | solution.py:54
  29.5 0.7 copy-start.8
  30.2 12.6 %collective-permute-start.5 = (s16[144,1024]{1,0:T(8,128)(2,1)}, s16[144,1024]{1,0:T(8,128)(2,1)}, u32[]{:S(2)}, u32[]{:S(2)}) collective-permute-start(s16[144,1024]{1,0:T(8,128)(2,1)} %collective-permute-done.4.refs_2_), channel_id=1, source_target_pairs={{0,1},{1,0},{2,3},{3,2},{4,5},{5,4},{6,7},{7,6},{8,9},{9,8},{10,11... | collective-permute-start | bytes 884744 | tf_op jit(solution)/shard_map/ppermute | solution.py:54
  33.2 23.0 %collective-permute-start = (f32[32,640]{1,0:T(8,128)}, f32[32,640]{1,0:T(8,128)}, u32[]{:S(2)}, u32[]{:S(2)}) collective-permute-start(f32[32,640]{1,0:T(8,128)} %bitcast.66), channel_id=1, source_target_pairs={{0,8},{8,0},{16,24},{24,16},{1,9},{9,1},{17,25},{25,17},{2,10},{10... | collective-permute-start | bytes 245768 | tf_op jit(solution)/shard_map/ppermute | solution.py:68
  39.5 17.7 %collective-permute-start.1 = (f32[32,640]{1,0:T(8,128)}, f32[32,640]{1,0:T(8,128)}, u32[]{:S(2)}, u32[]{:S(2)}) collective-permute-start(f32[32,640]{1,0:T(8,128)} %bitcast.67), channel_id=1, source_target_pairs={{0,16},{8,24},{16,0},{24,8},{1,17},{9,25},{17,1},{25,9},{2,18},{10... | collective-permute-start | bytes 245768 | tf_op jit(solution)/shard_map/ppermute | solution.py:68
  42.8 15.3 %collective-permute-start.2 = (f32[32,640]{1,0:T(8,128)}, f32[32,640]{1,0:T(8,128)}, u32[]{:S(2)}, u32[]{:S(2)}) collective-permute-start(f32[32,640]{1,0:T(8,128)} %bitcast.68), channel_id=1, source_target_pairs={{0,24},{8,16},{16,8},{24,0},{1,25},{9,17},{17,9},{25,1},{2,26},{10... | collective-permute-start | bytes 245768 | tf_op jit(solution)/shard_map/ppermute | solution.py:68
  42.8 7.5 %collective-permute-start.13 = (s16[144,1024]{1,0:T(8,128)(2,1)S(1)}, s16[144,1024]{1,0:T(8,128)(2,1)S(1)}, u32[]{:S(2)}, u32[]{:S(2)}) collective-permute-start(s16[144,1024]{1,0:T(8,128)(2,1)S(1)} %broadcast_select_fusion.own_ref), channel_id=1, source_target_pairs={{0,1},{1,0},{2,3},{3,2},{4,5},{5,4},{6,7},{7,6},{8,9},{9,8},{10,11... | collective-permute-start | bytes 884744 | tf_op jit(solution)/shard_map/ppermute | solution.py:54
  50.3 1.7 %copy-start.1 = (f32[640,1024]{1,0:T(8,128)S(1)}, f32[640,1024]{1,0:T(8,128)}, u32[]{:S(2)}) copy-start(f32[640,1024]{1,0:T(8,128)} %get-tuple-element.5.sum_ref) | copy-start | bytes 7864324
  52.0 4.1 %copy-start.9 = (f32[640,32]{0,1:T(8,128)S(1)}, f32[640,32]{0,1:T(8,128)}, u32[]{:S(2)}) copy-start(f32[640,32]{0,1:T(8,128)} %param.8) | copy-start | bytes 245764
  55.6 6.4 %collective-permute-start.15 = (bf16[640,1024]{1,0:T(8,128)(2,1)S(1)}, bf16[640,1024]{1,0:T(8,128)(2,1)S(1)}, u32[]{:S(2)}, u32[]{:S(2)}) collective-permute-start(bf16[640,1024]{1,0:T(8,128)(2,1)S(1)} %late_angles.1), channel_id=1, source_target_pairs={{0,1},{1,0},{2,3},{3,2},{4,5},{5,4},{6,7},{7,6},{8,9},{9,8},{10,11... | collective-permute-start | bytes 3932168 | tf_op jit(solution)/shard_map/ppermute | solution.py:54
  59.6 2.7 %copy-start.4 = (f32[16,640]{1,0:T(8,128)S(1)}, f32[16,640]{1,0:T(8,128)}, u32[]{:S(2)}) copy-start(f32[16,640]{1,0:T(8,128)} %get-tuple-element.18) | copy-start | bytes 122884
  59.6 2.7 %copy-start.6 = (f32[16,640]{1,0:T(8,128)S(1)}, f32[16,640]{1,0:T(8,128)}, u32[]{:S(2)}) copy-start(f32[16,640]{1,0:T(8,128)} %get-tuple-element.19) | copy-start | bytes 122884
  60.3 1.6 %collective-permute-start.14 = (f32[64,640]{1,0:T(8,128)}, f32[64,640]{1,0:T(8,128)S(1)}, u32[]{:S(2)}, u32[]{:S(2)}) collective-permute-start(f32[64,640]{1,0:T(8,128)} %pad_maximum_fusion.3), channel_id=1, source_target_pairs={{0,1},{1,0},{2,3},{3,2},{4,5},{5,4},{6,7},{7,6},{8,9},{9,8},{10,11... | collective-permute-start | bytes 491528 | tf_op jit(solution)/shard_map/ppermute | solution.py:54
  64.0 8.3 %collective-permute-start.18 = (bf16[16,1024]{1,0:T(8,128)(2,1)}, bf16[16,1024]{1,0:T(8,128)(2,1)}, u32[]{:S(2)}, u32[]{:S(2)}) collective-permute-start(bf16[16,1024]{1,0:T(8,128)(2,1)} %get-tuple-element.27), channel_id=1, source_target_pairs={{0,2},{1,3},{2,0},{3,1},{4,6},{5,7},{6,4},{7,5},{8,10},{9,11},{10,... | collective-permute-start | bytes 98312 | tf_op jit(solution)/shard_map/ppermute | solution.py:59
  66.4 5.9 %collective-permute-start.17 = (bf16[16,1024]{1,0:T(8,128)(2,1)}, bf16[16,1024]{1,0:T(8,128)(2,1)}, u32[]{:S(2)}, u32[]{:S(2)}) collective-permute-start(bf16[16,1024]{1,0:T(8,128)(2,1)} %get-tuple-element.28), channel_id=1, source_target_pairs={{0,4},{1,5},{2,6},{3,7},{4,0},{5,1},{6,2},{7,3},{8,12},{9,13},{10,... | collective-permute-start | bytes 98312 | tf_op jit(solution)/shard_map/ppermute | solution.py:59
  68.6 6.0 %collective-permute-start.16 = (bf16[16,1024]{1,0:T(8,128)(2,1)}, bf16[16,1024]{1,0:T(8,128)(2,1)}, u32[]{:S(2)}, u32[]{:S(2)}) collective-permute-start(bf16[16,1024]{1,0:T(8,128)(2,1)} %get-tuple-element.26), channel_id=1, source_target_pairs={{0,6},{1,7},{2,4},{3,5},{4,2},{5,3},{6,0},{7,1},{8,14},{9,15},{10,... | collective-permute-start | bytes 98312 | tf_op jit(solution)/shard_map/ppermute | solution.py:59
  75.6 5.8 %collective-permute-start.21 = (bf16[16,1024]{1,0:T(8,128)(2,1)S(1)}, bf16[16,1024]{1,0:T(8,128)(2,1)S(1)}, u32[]{:S(2)}, u32[]{:S(2)}) collective-permute-start(bf16[16,1024]{1,0:T(8,128)(2,1)S(1)} %fusion.34), channel_id=1, source_target_pairs={{0,6},{1,7},{2,4},{3,5},{4,2},{5,3},{6,0},{7,1},{8,14},{9,15},{10,... | collective-permute-start | bytes 98312 | tf_op jit(solution)/shard_map/ppermute | solution.py:59
  77.2 5.0 %collective-permute-start.20 = (bf16[16,1024]{1,0:T(8,128)(2,1)S(1)}, bf16[16,1024]{1,0:T(8,128)(2,1)S(1)}, u32[]{:S(2)}, u32[]{:S(2)}) collective-permute-start(bf16[16,1024]{1,0:T(8,128)(2,1)S(1)} %fusion.34), channel_id=1, source_target_pairs={{0,4},{1,5},{2,6},{3,7},{4,0},{5,1},{6,2},{7,3},{8,12},{9,13},{10,... | collective-permute-start | bytes 98312 | tf_op jit(solution)/shard_map/ppermute | solution.py:59
  77.3 4.9 %collective-permute-start.19 = (bf16[16,1024]{1,0:T(8,128)(2,1)S(1)}, bf16[16,1024]{1,0:T(8,128)(2,1)S(1)}, u32[]{:S(2)}, u32[]{:S(2)}) collective-permute-start(bf16[16,1024]{1,0:T(8,128)(2,1)S(1)} %fusion.34), channel_id=1, source_target_pairs={{0,2},{1,3},{2,0},{3,1},{4,6},{5,7},{6,4},{7,5},{8,10},{9,11},{10,... | collective-permute-start | bytes 98312 | tf_op jit(solution)/shard_map/ppermute | solution.py:59
  83.3 6.4 %collective-permute-start.24 = (bf16[64,1280]{1,0:T(8,128)(2,1)S(1)}, bf16[64,1280]{1,0:T(8,128)(2,1)S(1)}, u32[]{:S(2)}, u32[]{:S(2)}) collective-permute-start(bf16[64,1280]{1,0:T(8,128)(2,1)S(1)} %fusion.2), channel_id=1, source_target_pairs={{0,8},{8,0},{16,24},{24,16},{1,9},{9,1},{17,25},{25,17},{2,10},{10... | collective-permute-start | bytes 491528 | tf_op jit(solution)/shard_map/ppermute | solution.py:68
  84.8 6.7 %collective-permute-start.23 = (bf16[64,1280]{1,0:T(8,128)(2,1)S(1)}, bf16[64,1280]{1,0:T(8,128)(2,1)S(1)}, u32[]{:S(2)}, u32[]{:S(2)}) collective-permute-start(bf16[64,1280]{1,0:T(8,128)(2,1)S(1)} %fusion.2), channel_id=1, source_target_pairs={{0,16},{8,24},{16,0},{24,8},{1,17},{9,25},{17,1},{25,9},{2,18},{10... | collective-permute-start | bytes 491528 | tf_op jit(solution)/shard_map/ppermute | solution.py:68
  86.8 6.2 %collective-permute-start.22 = (bf16[64,1280]{1,0:T(8,128)(2,1)S(1)}, bf16[64,1280]{1,0:T(8,128)(2,1)S(1)}, u32[]{:S(2)}, u32[]{:S(2)}) collective-permute-start(bf16[64,1280]{1,0:T(8,128)(2,1)S(1)} %fusion.2), channel_id=1, source_target_pairs={{0,24},{8,16},{16,8},{24,0},{1,25},{9,17},{17,9},{25,1},{2,26},{10... | collective-permute-start | bytes 491528 | tf_op jit(solution)/shard_map/ppermute | solution.py:68
  93.8 4.5 %collective-permute-start.27 = (bf16[16,1024]{1,0:T(8,128)(2,1)S(1)}, bf16[16,1024]{1,0:T(8,128)(2,1)S(1)}, u32[]{:S(2)}, u32[]{:S(2)}) collective-permute-start(bf16[16,1024]{1,0:T(8,128)(2,1)S(1)} %get-tuple-element.24), channel_id=1, source_target_pairs={{0,2},{1,3},{2,0},{3,1},{4,6},{5,7},{6,4},{7,5},{8,10},{9,11},{10,... | collective-permute-start | bytes 98312 | tf_op jit(solution)/shard_map/ppermute | solution.py:59
  95.6 5.0 %collective-permute-start.26 = (bf16[16,1024]{1,0:T(8,128)(2,1)S(1)}, bf16[16,1024]{1,0:T(8,128)(2,1)S(1)}, u32[]{:S(2)}, u32[]{:S(2)}) collective-permute-start(bf16[16,1024]{1,0:T(8,128)(2,1)S(1)} %get-tuple-element.25), channel_id=1, source_target_pairs={{0,4},{1,5},{2,6},{3,7},{4,0},{5,1},{6,2},{7,3},{8,12},{9,13},{10,... | collective-permute-start | bytes 98312 | tf_op jit(solution)/shard_map/ppermute | solution.py:59
  96.5 6.1 %collective-permute-start.25 = (bf16[16,1024]{1,0:T(8,128)(2,1)S(1)}, bf16[16,1024]{1,0:T(8,128)(2,1)S(1)}, u32[]{:S(2)}, u32[]{:S(2)}) collective-permute-start(bf16[16,1024]{1,0:T(8,128)(2,1)S(1)} %get-tuple-element.23), channel_id=1, source_target_pairs={{0,6},{1,7},{2,4},{3,5},{4,2},{5,3},{6,0},{7,1},{8,14},{9,15},{10,... | collective-permute-start | bytes 98312 | tf_op jit(solution)/shard_map/ppermute | solution.py:59
  102.6 5.8 %collective-permute-start.30 = (bf16[16,1024]{1,0:T(8,128)(2,1)S(1)}, bf16[16,1024]{1,0:T(8,128)(2,1)S(1)}, u32[]{:S(2)}, u32[]{:S(2)}) collective-permute-start(bf16[16,1024]{1,0:T(8,128)(2,1)S(1)} %fusion.35), channel_id=1, source_target_pairs={{0,6},{1,7},{2,4},{3,5},{4,2},{5,3},{6,0},{7,1},{8,14},{9,15},{10,... | collective-permute-start | bytes 98312 | tf_op jit(solution)/shard_map/ppermute | solution.py:59
  104.1 5.1 %collective-permute-start.29 = (bf16[16,1024]{1,0:T(8,128)(2,1)S(1)}, bf16[16,1024]{1,0:T(8,128)(2,1)S(1)}, u32[]{:S(2)}, u32[]{:S(2)}) collective-permute-start(bf16[16,1024]{1,0:T(8,128)(2,1)S(1)} %fusion.35), channel_id=1, source_target_pairs={{0,4},{1,5},{2,6},{3,7},{4,0},{5,1},{6,2},{7,3},{8,12},{9,13},{10,... | collective-permute-start | bytes 98312 | tf_op jit(solution)/shard_map/ppermute | solution.py:59
  104.1 5.2 %collective-permute-start.28 = (bf16[16,1024]{1,0:T(8,128)(2,1)S(1)}, bf16[16,1024]{1,0:T(8,128)(2,1)S(1)}, u32[]{:S(2)}, u32[]{:S(2)}) collective-permute-start(bf16[16,1024]{1,0:T(8,128)(2,1)S(1)} %fusion.35), channel_id=1, source_target_pairs={{0,2},{1,3},{2,0},{3,1},{4,6},{5,7},{6,4},{7,5},{8,10},{9,11},{10,... | collective-permute-start | bytes 98312 | tf_op jit(solution)/shard_map/ppermute | solution.py:59
  109.8 8.3 %copy-start.5 = (f32[16,640]{1,0:T(8,128)S(1)}, f32[16,640]{1,0:T(8,128)}, u32[]{:S(2)}) copy-start(f32[16,640]{1,0:T(8,128)} %get-tuple-element.18) | copy-start | bytes 122884
  109.8 8.3 %copy-start.7 = (f32[16,640]{1,0:T(8,128)S(1)}, f32[16,640]{1,0:T(8,128)}, u32[]{:S(2)}) copy-start(f32[16,640]{1,0:T(8,128)} %get-tuple-element.19) | copy-start | bytes 122884
  110.4 5.4 %collective-permute-start.33 = (bf16[64,1280]{1,0:T(8,128)(2,1)S(1)}, bf16[64,1280]{1,0:T(8,128)(2,1)S(1)}, u32[]{:S(2)}, u32[]{:S(2)}) collective-permute-start(bf16[64,1280]{1,0:T(8,128)(2,1)S(1)} %fusion.1), channel_id=1, source_target_pairs={{0,8},{8,0},{16,24},{24,16},{1,9},{9,1},{17,25},{25,17},{2,10},{10... | collective-permute-start | bytes 491528 | tf_op jit(solution)/shard_map/ppermute | solution.py:68
  110.9 5.3 %collective-permute-start.32 = (bf16[64,1280]{1,0:T(8,128)(2,1)S(1)}, bf16[64,1280]{1,0:T(8,128)(2,1)S(1)}, u32[]{:S(2)}, u32[]{:S(2)}) collective-permute-start(bf16[64,1280]{1,0:T(8,128)(2,1)S(1)} %fusion.1), channel_id=1, source_target_pairs={{0,16},{8,24},{16,0},{24,8},{1,17},{9,25},{17,1},{25,9},{2,18},{10... | collective-permute-start | bytes 491528 | tf_op jit(solution)/shard_map/ppermute | solution.py:68
  111.7 6.3 %collective-permute-start.31 = (bf16[64,1280]{1,0:T(8,128)(2,1)S(1)}, bf16[64,1280]{1,0:T(8,128)(2,1)S(1)}, u32[]{:S(2)}, u32[]{:S(2)}) collective-permute-start(bf16[64,1280]{1,0:T(8,128)(2,1)S(1)} %fusion.1), channel_id=1, source_target_pairs={{0,24},{8,16},{16,8},{24,0},{1,25},{9,17},{17,9},{25,1},{2,26},{10... | collective-permute-start | bytes 491528 | tf_op jit(solution)/shard_map/ppermute | solution.py:68
  118.2 0.7 copy-start.3
  119.0 4.5 %collective-permute-start.37 = (bf16[16,1024]{1,0:T(8,128)(2,1)S(1)}, bf16[16,1024]{1,0:T(8,128)(2,1)S(1)}, u32[]{:S(2)}, u32[]{:S(2)}) collective-permute-start(bf16[16,1024]{1,0:T(8,128)(2,1)S(1)} %get-tuple-element.21), channel_id=1, source_target_pairs={{0,2},{1,3},{2,0},{3,1},{4,6},{5,7},{6,4},{7,5},{8,10},{9,11},{10,... | collective-permute-start | bytes 98312 | tf_op jit(solution)/shard_map/ppermute | solution.py:59
  120.3 5.2 %collective-permute-start.36 = (bf16[16,1024]{1,0:T(8,128)(2,1)S(1)}, bf16[16,1024]{1,0:T(8,128)(2,1)S(1)}, u32[]{:S(2)}, u32[]{:S(2)}) collective-permute-start(bf16[16,1024]{1,0:T(8,128)(2,1)S(1)} %get-tuple-element.22), channel_id=1, source_target_pairs={{0,4},{1,5},{2,6},{3,7},{4,0},{5,1},{6,2},{7,3},{8,12},{9,13},{10,... | collective-permute-start | bytes 98312 | tf_op jit(solution)/shard_map/ppermute | solution.py:59
  121.4 5.7 %collective-permute-start.35 = (bf16[16,1024]{1,0:T(8,128)(2,1)S(1)}, bf16[16,1024]{1,0:T(8,128)(2,1)S(1)}, u32[]{:S(2)}, u32[]{:S(2)}) collective-permute-start(bf16[16,1024]{1,0:T(8,128)(2,1)S(1)} %get-tuple-element.20), channel_id=1, source_target_pairs={{0,6},{1,7},{2,4},{3,5},{4,2},{5,3},{6,0},{7,1},{8,14},{9,15},{10,... | collective-permute-start | bytes 98312 | tf_op jit(solution)/shard_map/ppermute | solution.py:59
  123.4 4.4 %collective-permute-start.34 = (f32[64,640]{1,0:T(8,128)}, f32[64,640]{1,0:T(8,128)S(1)}, u32[]{:S(2)}, u32[]{:S(2)}) collective-permute-start(f32[64,640]{1,0:T(8,128)} %copy-done.3), channel_id=1, source_target_pairs={{0,1},{1,0},{2,3},{3,2},{4,5},{5,4},{6,7},{7,6},{8,9},{9,8},{10,11... | collective-permute-start | bytes 491528 | tf_op jit(solution)/shard_map/ppermute | solution.py:54

commit v3 on v2

v3 whole, which is shorter than its diff:
```python
import functools
import math

import jax
import jax.numpy as jnp
from jax import lax
from jax.experimental import pallas as pl
from jax.experimental.pallas import tpu as pltpu
from jax.sharding import PartitionSpec as P

STEPS = 2
EMBED_BOUND = 6.0
FREQ_BOUND = 0.5
CODE_MAX = 32766.0
LANES = 128
VMEM_BYTES = 13 * 1024 * 1024
COS_TURNS = (
    0.9999999890590243,
    -19.739204499454,
    64.93911745989858,
    -85.45013953092679,
    60.16763095123224,
    -25.967599249288032,
    6.528658162158786,
)
PER_TURN = EMBED_BOUND * FREQ_BOUND / (CODE_MAX * CODE_MAX * 2.0 * math.pi)


def encode(x, bound):
    return jnp.round(x * (CODE_MAX / bound)).astype(jnp.int16)


def split(code):
    wide = code.astype(jnp.float32)
    high = jnp.round(wide * (1.0 / 256.0)) * 256.0
    return high.astype(jnp.bfloat16), (wide - high).astype(jnp.bfloat16)


def scaled_cos(turns, scale):
    turns = turns - jnp.round(turns)
    square = turns * turns
    value = COS_TURNS[-1] * scale
    for coefficient in COS_TURNS[-2::-1]:
        value = value * square + coefficient * scale
    return value.astype(jnp.bfloat16)


def mix(a, b):
    return jnp.dot(a, b, preferred_element_type=jnp.float32)


def core_swap(x):
    n = lax.axis_size("feat")
    return lax.ppermute(x, "feat", [(i, i ^ 1) for i in range(n)])


def line_swap(x, k):
    n = lax.axis_size("feat")
    return lax.ppermute(x, "feat", [(i, i ^ (2 * k)) for i in range(n)])


def line_move(x, pairs):
    return lax.ppermute(x, "feat", [(2 * a + c, 2 * b + c) for a, b in pairs for c in range(2)])


def clip_swap(x, k):
    n = lax.axis_size("clip")
    return lax.ppermute(x, "clip", [(i, i ^ k) for i in range(n)])


def farthest_first(n):
    return range(n - 1, 0, -1)


def halves(x):
    high = jnp.round(x * (1.0 / 256.0)) * 256.0
    return high.astype(jnp.bfloat16), (x - high).astype(jnp.bfloat16)


def copied(sources, places, sem):
    copies = [pltpu.make_async_copy(a, b, sem.at[i]) for i, (a, b) in enumerate(zip(sources, places))]
    for copy in copies:
        copy.start()
    return copies


def tiles_of(ref):
    tile = 256 if ref.shape[1] % 256 == 0 else ref.shape[1]
    return [slice(start, start + tile) for start in range(0, ref.shape[1], tile)]


def early_kernel(
    at_ref, *refs, n_embeds, n_freqs, columns
):
    embeds, freqs = refs[:n_embeds], refs[n_embeds : n_embeds + n_freqs]
    (
        sum_ref, high_ref, low_ref, freq_code, embed_code, f_high, f_low, e_high, e_low, sem_f, sem_e,
    ) = refs[n_embeds + n_freqs :]
    depth = e_high.shape[0]
    used = n_embeds * columns
    rows = [pl.ds(pl.multiple_of(at_ref[i], 16), columns) for i in range(2 * n_freqs)]
    pieces = [ref.at[h * columns : (h + 1) * columns, :] for ref in freqs for h in range(2)]
    of_freqs = copied(pieces, [freq_code.at[r, :] for r in rows], sem_f)
    of_embeds = copied(embeds, [embed_code.at[i * columns : (i + 1) * columns, :] for i in range(n_embeds)], sem_e)
    if depth > used:
        freq_code[used:depth, :] = jnp.zeros((depth - used, freq_code.shape[1]), jnp.int16)
        embed_code[used:depth, :] = jnp.zeros((depth - used, embed_code.shape[1]), jnp.int16)
    for copy in of_embeds:
        copy.wait()
    e_high[...], e_low[...] = halves(embed_code[...].astype(jnp.float32))
    for copy in of_freqs:
        copy.wait()
    for start in range(0, depth, LANES):
        f_high[:, start : start + LANES], f_low[:, start : start + LANES] = halves(
            freq_code[start : start + LANES, :].astype(jnp.float32).T
        )
    high_ref[...], low_ref[...] = halves(freq_code[depth:, :].astype(jnp.float32).T)
    for at in tiles_of(sum_ref):
        sum_ref[:, at] = mix(f_high[...], e_high[:, at]) + (
            mix(f_high[...], e_low[:, at]) + mix(f_low[...], e_high[:, at])
        )


def late_kernel(
    pick_ref, sum_ref, own_a, own_b, other_a, other_b, high_ref, low_ref, phase_ref,
    phi_ref, embed_code, e_high, e_low, sem_e, *, columns, scale,
):
    @pl.when(pick_ref[0] == 1)
    def _():
        copied((own_a, other_a), (embed_code.at[:columns], embed_code.at[columns:]), sem_e)

    @pl.when(pick_ref[0] != 1)
    def _():
        copied((own_b, other_b), (embed_code.at[:columns], embed_code.at[columns:]), sem_e)

    for i in range(2):
        half = embed_code.at[i * columns : (i + 1) * columns]
        pltpu.make_async_copy(own_a, half, sem_e.at[i]).wait()
    e_high[...], e_low[...] = halves(embed_code[...].astype(jnp.float32))
    for at in tiles_of(sum_ref):
        total = sum_ref[:, at] + (
            mix(high_ref[...], e_high[:, at])
            + (mix(high_ref[...], e_low[:, at]) + mix(low_ref[...], e_high[:, at]))
        )
        phi_ref[:, at] = scaled_cos(total * PER_TURN + phase_ref[...], scale)


def phi_by_kernels(embed_code, frequencies, scale, line, core, clip, weights_in):
    slabs = 4
    columns, clips = embed_code.shape
    features = frequencies.shape[1]
    tie = lax.optimization_barrier
    freq = encode(frequencies, FREQ_BOUND)
    second = line_swap(embed_code, 2)
    first = line_swap(embed_code, 1)
    freq_xy, freq_x, freq_y = [clip_swap(freq, k) for k in (3, 1, 2)]
    second, first, freq_xy, freq_x, freq_y, embed_again = tie((second, first, freq_xy, freq_x, freq_y, embed_code))
    passed = line_move(second, [(1, 0), (2, 3)])
    middle = line_move(embed_again, [(1, 2), (2, 1)])
    own = [embed_again, first, second]
    other = tie(tuple(core_swap(x) for x in own) + (weights_in[2],))
    early = [y for pair in zip(own, other) for y in pair]
    beta, targets, column = weights_in[1](weights_in[0](other[-1]))
    freqs = [freq, freq_x, freq_y, freq_xy]
    used = len(early) * columns
    depth = -(-used // LANES) * LANES
    at = []
    for m in range(slabs):
        k = m ^ line ^ clip
        base = k * 2 * columns + jnp.where(k == slabs - 1, depth - used, 0)
        at += [base + core * columns, base + (1 - core) * columns]
    vmem = pl.BlockSpec(memory_space=pltpu.VMEM)
    smem = pl.BlockSpec(memory_space=pltpu.SMEM)
    anywhere = pl.BlockSpec(memory_space=pl.ANY)
    params = pltpu.CompilerParams(vmem_limit_bytes=VMEM_BYTES)
    summed, high, low = pl.pallas_call(
        functools.partial(early_kernel, n_embeds=len(early), n_freqs=len(freqs), columns=columns),
        out_shape=(
            jax.ShapeDtypeStruct((features, clips), jnp.float32),
            jax.ShapeDtypeStruct((features, 2 * columns), jnp.bfloat16),
            jax.ShapeDtypeStruct((features, 2 * columns), jnp.bfloat16),
        ),
        in_specs=[smem] + [anywhere] * (len(early) + len(freqs)),
        out_specs=(vmem, vmem, vmem),
        scratch_shapes=[
            pltpu.VMEM((depth + 2 * columns, features), jnp.int16),
            pltpu.VMEM((depth, clips), jnp.int16),
            pltpu.VMEM((features, depth), jnp.bfloat16),
            pltpu.VMEM((features, depth), jnp.bfloat16),
            pltpu.VMEM((depth, clips), jnp.bfloat16),
            pltpu.VMEM((depth, clips), jnp.bfloat16),
            pltpu.SemaphoreType.DMA((2 * len(freqs),)),
            pltpu.SemaphoreType.DMA((len(early),)),
        ],
        compiler_params=params,
        cost_estimate=pl.CostEstimate(
            flops=6 * features * depth * clips, bytes_accessed=8 * features * clips, transcendentals=0
        ),
        name="early_angles",
    )(jnp.stack(at).astype(jnp.int32), *early, *freqs)
    pick = jnp.where((line == 1) | (line == 2), 1, 0).astype(jnp.int32)[None]
    phi = pl.pallas_call(
        functools.partial(late_kernel, columns=columns, scale=scale),
        out_shape=jax.ShapeDtypeStruct((features, clips), jnp.bfloat16),
        in_specs=[smem, vmem] + [anywhere] * 4 + [vmem] * 3,
        out_specs=vmem,
        scratch_shapes=[
            pltpu.VMEM((2 * columns, clips), jnp.int16),
            pltpu.VMEM((2 * columns, clips), jnp.bfloat16),
            pltpu.VMEM((2 * columns, clips), jnp.bfloat16),
            pltpu.SemaphoreType.DMA((2,)),
        ],
        compiler_params=params,
        cost_estimate=pl.CostEstimate(
            flops=6 * features * 2 * columns * clips, bytes_accessed=6 * features * clips, transcendentals=0
        ),
        name="late_angles",
    )(pick, summed, middle, passed, core_swap(middle), core_swap(passed), high, low, column)
    return phi, beta, targets


def phi_by_ring(embed_code, frequencies, scale, line, core, clip, weights_in):
    freq_code = encode(frequencies, FREQ_BOUND)
    places, n_clip = lax.axis_size("feat") // 2, lax.axis_size("clip")
    columns, clips = embed_code.shape
    slab, features = freq_code.shape
    freq_all = jnp.zeros((n_clip * slab, features), jnp.int16)
    for k in range(n_clip):
        piece = freq_code if k == 0 else clip_swap(freq_code, k)
        freq_all = lax.dynamic_update_slice_in_dim(freq_all, piece, (clip ^ k) * slab, 0)
    embed_all = jnp.zeros((2 * places * columns, clips), jnp.int16)
    piece = embed_code
    ring = [(i, (i + 1) % places) for i in range(places)]
    for step in range(places):
        if step:
            piece = line_move(piece, ring)
        base = 2 * ((line - step) % places)
        embed_all = lax.dynamic_update_slice_in_dim(embed_all, piece, (base + core) * columns, 0)
        embed_all = lax.dynamic_update_slice_in_dim(
            embed_all, core_swap(piece), (base + 1 - core) * columns, 0
        )

    def dot0(a, b):
        return lax.dot_general(a, b, (((0,), (0,)), ((), ())), preferred_element_type=jnp.float32)

    embed_high, embed_low = split(embed_all)
    freq_high, freq_low = split(freq_all)
    total = dot0(freq_high, embed_high) + (dot0(freq_high, embed_low) + dot0(freq_low, embed_high))
    beta, targets, column = weights_in[1](weights_in[0](weights_in[2]))
    return scaled_cos(total * PER_TURN + column, scale), beta, targets


def per_device(embeds, frequencies, phases, weights, labels):
    n_feat, n_clip = lax.axis_size("feat"), lax.axis_size("clip")
    feat, clip = lax.axis_index("feat"), lax.axis_index("clip")
    places, line, core = n_feat // 2, feat // 2, feat % 2
    columns = embeds.shape[1]
    features = frequencies.shape[1]
    outputs = labels.shape[1]
    block = outputs // n_feat
    scale = math.sqrt(2.0 / (features * n_feat))

    embed_code = encode(embeds.T, EMBED_BOUND)
    phase_turns = phases * (0.5 / math.pi)
    by_kernels = places == 4 and n_clip == 4 and columns % 16 == 0 and frequencies.shape[0] == 2 * columns
    per_clip = places // n_clip

    def weights_in(weights):
        piece = weights.T
        return [piece] + [clip_swap(piece, k) for k in range(1, n_clip)]

    def weights_of(pieces):
        stacked = jnp.concatenate(pieces).reshape(n_clip * per_clip, 2, block, features)

        def ordered(side):
            rows = lax.dynamic_index_in_dim(stacked, side, 1, keepdims=False)
            found = []
            for k in range(places):
                place = line ^ k
                at = ((place // per_clip) ^ clip) * per_clip + place % per_clip
                found.append(lax.dynamic_index_in_dim(rows, at, 0, keepdims=False))
            return jnp.concatenate(found)

        beta_own, beta_sent = ordered(core), ordered(1 - core)
        targets = lax.dynamic_slice_in_dim(labels.T, feat * block, block, 0).astype(jnp.float32)
        return (beta_own, beta_sent, core_swap(beta_sent)), targets, phase_turns[:, None]

    def share_of(parts):
        parts = parts.reshape(places, block, -1)
        half = parts.astype(jnp.bfloat16)
        total = parts[0]
        found = [line_swap(half[k], k) for k in farthest_first(places)]
        return total, found

    def add_up(total, found):
        for x in found:
            total = total + x.astype(jnp.float32)
        return total

    def gradient_of(residual, phi):
        return lax.dot_general(residual, phi, (((1,), (1,)), ((), ())), preferred_element_type=jnp.float32)

    phi_of = phi_by_kernels if by_kernels else phi_by_ring
    phi, beta, targets = phi_of(
        embed_code, frequencies, scale, line, core, clip, (weights_in, weights_of, weights)
    )
    beta_own, beta_sent, beta_other = beta
    there = core_swap(mix(beta_sent.astype(jnp.bfloat16), phi).astype(jnp.bfloat16))
    parts = mix(beta_own.astype(jnp.bfloat16), phi) + there.astype(jnp.float32)
    phi_other = core_swap(phi)
    for step in range(STEPS):
        share = (jax.nn.sigmoid(add_up(*share_of(parts))) - targets).astype(jnp.bfloat16)
        found = {k: line_swap(share, k) for k in farthest_first(places)}
        residual = jnp.concatenate([share] + [found[k] for k in range(1, places)])
        grad = jnp.concatenate([gradient_of(residual, phi), gradient_of(residual, phi_other)], axis=1)
        sent = grad.astype(jnp.bfloat16)
        for k in farthest_first(n_clip):
            grad = grad + clip_swap(sent, k).astype(jnp.float32)
        beta_own = beta_own - 0.25 * grad[:, :features]
        beta_other = beta_other - 0.25 * grad[:, features:]
        parts = mix(beta_own.astype(jnp.bfloat16), phi) + mix(beta_other.astype(jnp.bfloat16), phi_other)
    total, found = share_of(parts)
    ours = beta_own.reshape(places, block, features)
    theirs = core_swap(beta_other).reshape(places, block, features)
    rows = []
    for b in range(per_clip):
        k = line ^ (clip * per_clip + b)
        mine = lax.dynamic_index_in_dim(ours, k, 0, keepdims=False)
        their = lax.dynamic_index_in_dim(theirs, k, 0, keepdims=False)
        rows += [jnp.where(core == 0, mine, their), jnp.where(core == 0, their, mine)]
    trained, total = lax.optimization_barrier((jnp.concatenate(rows).T, total))
    return (trained, add_up(total, found).T)


def solution(mesh):
    placed = (P("clip", "feat"), P("clip", "feat"), P("feat"), P("feat", "clip"), P("clip", None))
    return jax.shard_map(
        per_device,
        mesh=mesh,
        in_specs=placed,
        out_specs=(P("feat", "clip"), P("clip", "feat")),
        check_vma=False,
    )
```

time: 129 us -> 123 us (0.953)
  local copies, waits for them, and re-layouts: 9 us -> 4.01 us
  waiting for transfers between devices: 48.9 us -> 44.8 us
  Pallas kernels: 10.9 us -> 13.7 us
  starting transfers between devices: 48 us -> 45.3 us
  matrix products: 4.87 us -> 6.45 us
    ppermute x12, waiting for transfers between devices: 16.3 us -> 10.4 us  [clip_swap(): return lax.ppermute(x, 'clip', [(i, i ^ k) for i in range(n)])]
    ppermute x2, waiting for transfers between devices: 4.26 us -> 7.92 us  [line_move(): lax.ppermute(x, 'feat', [(2 * a + c, 2 * b + c) for a, b in pairs for c i...]
    dynamic_update_slice x4 -> x0, local copies, waits for them, and re-layouts: 2.71 us -> none  [per_device(): by_clip = lax.dynamic_update_slice_in_dim(by_clip, piece[None], clip ^ k, 0)]
    ppermute x17, starting transfers between devices: 29.5 us -> 26.8 us  [line_swap(): return lax.ppermute(x, 'feat', [(i, i ^ 2 * k) for i in range(n)])]
    pallas_call x1, Pallas kernels: 7.42 us -> 9.85 us  [phi_by_kernels(): pl.pallas_call(functools.partial(early_kernel, n_embeds=len(early), n_fre...]
    ppermute x17, waiting for transfers between devices: 26.7 us -> 24.4 us  [line_swap(): return lax.ppermute(x, 'feat', [(i, i ^ 2 * k) for i in range(n)])]
    unnamed x23 -> x37, local copies, waits for them, and re-layouts: 3.71 us -> 2.07 us
    dot_general x6, matrix products: 2.84 us -> 4.42 us  [mix(): return jnp.dot(a, b, preferred_element_type=jnp.float32)]
  transfers between devices with their start and end apart: 38 -> 40, of which waited for: 22 -> 19; matrix products, arithmetic and copies ran while one was open for 6% -> 7% of each run, Pallas kernels for 9% -> 8%
where the time goes in v3:
time: 123 us; the launch traced here: 122 us
  starting transfers between devices  45.3 us (37%)
  waiting for transfers between devices  44.8 us (36%)
  Pallas kernels  13.7 us (11%)
  other arithmetic  6.84 us (6%)
  matrix products  6.45 us (5%)
  local copies, waits for them, and re-layouts  4.01 us (3%)
  between operations  1.25 us (1%)
    ppermute x17, starting transfers between devices, line_swap(): return lax.ppermute(x, 'feat', [(i, i ^ 2 * k) for i in range(n)])  26.8 us
    ppermute x17, waiting for transfers between devices, line_swap(): return lax.ppermute(x, 'feat', [(i, i ^ 2 * k) for i in range(n)])  24.4 us
    ppermute x12, starting transfers between devices, clip_swap(): return lax.ppermute(x, 'clip', [(i, i ^ k) for i in range(n)])  15.2 us
    ppermute x12, waiting for transfers between devices, clip_swap(): return lax.ppermute(x, 'clip', [(i, i ^ k) for i in range(n)])  10.4 us
    pallas_call x1, Pallas kernels, phi_by_kernels(): pl.pallas_call(functools.partial(early_kernel, n_embeds=len(early), n_fre...  9.85 us
    ppermute x2, waiting for transfers between devices, line_move(): lax.ppermute(x, 'feat', [(2 * a + c, 2 * b + c) for a, b in pairs for c i...  7.92 us
    dot_general x6, matrix products, mix(): return jnp.dot(a, b, preferred_element_type=jnp.float32)  4.42 us
    pallas_call x1, Pallas kernels, phi_by_kernels(): pl.pallas_call(functools.partial(late_kernel, columns=columns, scale=scal...  3.87 us
  transfers between devices with their start and end apart: 40, of which 19 were waited for; matrix products, arithmetic and copies ran while one was open for 7% of the time, Pallas kernels for 8%

profile of v3, /device:TPU:0, one launch (start us, length us, event | category | flops | bytes accessed | tf_op | source)
XLA Modules:
  0.0 122.4 jit_solution(6181715157321794186)
XLA Ops:
  0.7 1.3 %round-nearest-even_convert_fusion.refs_6_ = s16[288,640]{1,0:T(8,128)(2,1)S(1)} fusion(f32[288,640]{1,0:T(8,128)} %param.6), kind=kLoop, calls=%fused_computation.4 | loop fusion | flops 552960 | bytes 1105920 | tf_op jit(solution)/shard_map/convert_element_type | solution.py:30
  2.0 4.0 %collective-permute-start.2 = (s16[288,640]{1,0:T(8,128)(2,1)S(1)}, s16[288,640]{1,0:T(8,128)(2,1)S(1)}, u32[]{:S(2)}, u32[]{:S(2)}) collective-permute-start(s16[288,640]{1,0:T(8,128)(2,1)S(1)} %round-nearest-even_convert_fusion.refs_6_), channel_id=1, source_target_pairs={{0,24},{8,16},{16,8},{24,0},{1,25},{9,17},{17,9},{25,1},{2,26},{10... | collective-permute-start | bytes 1105928 | tf_op jit(solution)/shard_map/ppermute | solution.py:68
  5.9 0.5 collective-permute-start.3
  6.7 3.1 %collective-permute-start = (s16[144,1024]{1,0:T(8,128)(2,1)S(1)}, s16[144,1024]{1,0:T(8,128)(2,1)}, u32[]{:S(2)}, u32[]{:S(2)}) collective-permute-start(s16[144,1024]{1,0:T(8,128)(2,1)S(1)} %fusion.refs_0_), channel_id=1, source_target_pairs={{0,4},{1,5},{2,6},{3,7},{4,0},{5,1},{6,2},{7,3},{8,12},{9,13},{10,... | collective-permute-start | bytes 884744 | tf_op jit(solution)/shard_map/ppermute | solution.py:59
  9.7 1.6 %collective-permute-start.1 = (s16[144,1024]{1,0:T(8,128)(2,1)S(1)}, s16[144,1024]{1,0:T(8,128)(2,1)}, u32[]{:S(2)}, u32[]{:S(2)}) collective-permute-start(s16[144,1024]{1,0:T(8,128)(2,1)S(1)} %fusion.refs_0_), channel_id=1, source_target_pairs={{0,2},{1,3},{2,0},{3,1},{4,6},{5,7},{6,4},{7,5},{8,10},{9,11},{10,... | collective-permute-start | bytes 884744 | tf_op jit(solution)/shard_map/ppermute | solution.py:59
  11.3 11.1 %collective-permute-done.refs_4_ = s16[144,1024]{1,0:T(8,128)(2,1)} collective-permute-done((s16[144,1024]{1,0:T(8,128)(2,1)S(1)}, s16[144,1024]{1,0:T(8,128)(2,1)}, u32[]{:S(2)}, u32[]{:S(2)}) %collective-permute-start) | collective-permute-done | bytes 294944 | tf_op jit(solution)/shard_map/ppermute | solution.py:59
  22.7 0.5 collective-permute-start.6
  23.3 0.7 collective-permute-start.11
  24.0 1.3 %collective-permute-start.12 = (s16[144,1024]{1,0:T(8,128)(2,1)}, s16[144,1024]{1,0:T(8,128)(2,1)S(1)}, u32[]{:S(2)}, u32[]{:S(2)}) collective-permute-start(s16[144,1024]{1,0:T(8,128)(2,1)} %collective-permute-done.refs_4_), channel_id=1, source_target_pairs={{2,0},{3,1},{4,6},{5,7},{10,8},{11,9},{12,14},{13,15},{18,16},{19,... | collective-permute-start | bytes 884744 | tf_op jit(solution)/shard_map/ppermute | solution.py:63
  25.7 2.6 %collective-permute-start.10 = (f32[32,640]{1,0:T(8,128)}, f32[32,640]{1,0:T(8,128)S(1)}, u32[]{:S(2)}, u32[]{:S(2)}) collective-permute-start(f32[32,640]{1,0:T(8,128)} %bitcast.58), channel_id=1, source_target_pairs={{0,24},{8,16},{16,8},{24,0},{1,25},{9,17},{17,9},{25,1},{2,26},{10... | collective-permute-start | bytes 245768 | tf_op jit(solution)/shard_map/ppermute | solution.py:68
  28.3 0.5 collective-permute-start.9
  28.8 0.5 collective-permute-start.8
  29.3 7.9 %collective-permute-done.12.own_b = s16[144,1024]{1,0:T(8,128)(2,1)S(1)} collective-permute-done((s16[144,1024]{1,0:T(8,128)(2,1)}, s16[144,1024]{1,0:T(8,128)(2,1)S(1)}, u32[]{:S(2)}, u32[]{:S(2)}) %collective-permute-start.12) | collective-permute-done | bytes 294944 | tf_op jit(solution)/shard_map/ppermute | solution.py:63
  37.2 9.8 %early_angles.1 = (f32[640,1024]{1,0:T(8,128)S(1)}, bf16[640,288]{1,0:T(8,128)(2,1)S(1)}, bf16[640,288]{1,0:T(8,128)(2,1)S(1)}) custom-call(s32[8]{0:T(128)S(1)} %stack.35.at_ref, s16[144,1024]{1,0:T(8,128)(2,1)S(1)} %fusion.refs_0_, s16[144,1024]{1,0:T(8,128)(2,1)} %collective-permute-done.5.refs_1_, s16[144,1024]{1,0:T(8,128)(2,1)} %collective-permute-done.1.refs_2_, ...), custom_call_target="tpu_custom_call" | custom-call | flops 3523215360 | bytes 5242880 | tf_op jit(solution)/shard_map/early_angles/pallas_call | solution.py:176
  47.2 3.9 %late_angles.1 = bf16[640,1024]{1,0:T(8,128)(2,1)S(1)} custom-call(s32[1]{0:T(128)} %bitcast.7.pick_ref, f32[640,1024]{1,0:T(8,128)S(1)} %get-tuple-element.27.sum_ref, s16[144,1024]{1,0:T(8,128)(2,1)S(1)} %collective-permute-done.11.own_a, s16[144,1024]{1,0:T(8,128)(2,1)S(1)} %collective-permute-done.12.own_b, ...), custom_call_target="tpu_custom_call" | custom-call | flops 1132462080 | bytes 3932160 | tf_op jit(solution)/shard_map/late_angles/pallas_call | solution.py:202
  51.1 0.6 collective-permute-start.22
  51.7 1.0 convolution_convert_fusion
  52.7 2.0 %collective-permute-done.15 = bf16[64,1024]{1,0:T(8,128)(2,1)S(1)} collective-permute-done((bf16[64,1024]{1,0:T(8,128)(2,1)}, bf16[64,1024]{1,0:T(8,128)(2,1)S(1)}, u32[]{:S(2)}, u32[]{:S(2)}) %collective-permute-start.15) | collective-permute-done | bytes 131104 | tf_op jit(solution)/shard_map/ppermute | solution.py:54
  54.7 0.6 copy-done.15
  55.4 2.0 %fusion.47 = (bf16[64,1024]{1,0:T(8,128)(2,1)S(1)}, f32[64,1024]{1,0:T(8,128)}) fusion(bf16[64,1024]{1,0:T(8,128)(2,1)} %copy-done.15, bf16[640,1024]{1,0:T(8,128)(2,1)S(1)} %late_angles.1, f32[16,640]{1,0:T(8,128)S(1)} %get-tuple-element.41, f32[16,640]{1,0:T(8,128)S(1)} %get-tuple-element.42, f32[16,640]{1,0:T(8,128)S(1)} %get-tuple-element.43, ...), kind=kOutput, calls=%fused_computation.79 | convolution fusion | flops 84410368 | bytes 1998848 | tf_op jit(solution)/shard_map/dot_general | solution.py:49
  57.4 0.6 fusion.46
  58.0 2.4 %collective-permute-start.17 = (bf16[16,1024]{1,0:T(8,128)(2,1)}, bf16[16,1024]{1,0:T(8,128)(2,1)S(1)}, u32[]{:S(2)}, u32[]{:S(2)}) collective-permute-start(bf16[16,1024]{1,0:T(8,128)(2,1)} %get-tuple-element.52), channel_id=1, source_target_pairs={{0,4},{1,5},{2,6},{3,7},{4,0},{5,1},{6,2},{7,3},{8,12},{9,13},{10,... | collective-permute-start | bytes 98312 | tf_op jit(solution)/shard_map/ppermute | solution.py:59
  60.4 2.0 %collective-permute-start.16 = (bf16[16,1024]{1,0:T(8,128)(2,1)S(1)}, bf16[16,1024]{1,0:T(8,128)(2,1)S(1)}, u32[]{:S(2)}, u32[]{:S(2)}) collective-permute-start(bf16[16,1024]{1,0:T(8,128)(2,1)S(1)} %get-tuple-element.50), channel_id=1, source_target_pairs={{0,6},{1,7},{2,4},{3,5},{4,2},{5,3},{6,0},{7,1},{8,14},{9,15},{10,... | collective-permute-start | bytes 98312 | tf_op jit(solution)/shard_map/ppermute | solution.py:59
  62.4 1.0 constant_dynamic-slice_fusion
  63.4 1.2 copy.10
  64.6 1.5 %collective-permute-done.16 = bf16[16,1024]{1,0:T(8,128)(2,1)S(1)} collective-permute-done((bf16[16,1024]{1,0:T(8,128)(2,1)S(1)}, bf16[16,1024]{1,0:T(8,128)(2,1)S(1)}, u32[]{:S(2)}, u32[]{:S(2)}) %collective-permute-start.16) | collective-permute-done | bytes 32800 | tf_op jit(solution)/shard_map/ppermute | solution.py:59
  66.2 0.9 fusion.30
  67.0 2.0 %collective-permute-start.21 = (bf16[16,1024]{1,0:T(8,128)(2,1)S(1)}, bf16[16,1024]{1,0:T(8,128)(2,1)S(1)}, u32[]{:S(2)}, u32[]{:S(2)}) collective-permute-start(bf16[16,1024]{1,0:T(8,128)(2,1)S(1)} %fusion.30), channel_id=1, source_target_pairs={{0,6},{1,7},{2,4},{3,5},{4,2},{5,3},{6,0},{7,1},{8,14},{9,15},{10,... | collective-permute-start | bytes 98312 | tf_op jit(solution)/shard_map/ppermute | solution.py:59
  69.1 2.4 %collective-permute-start.19 = (bf16[16,1024]{1,0:T(8,128)(2,1)S(1)}, bf16[16,1024]{1,0:T(8,128)(2,1)S(1)}, u32[]{:S(2)}, u32[]{:S(2)}) collective-permute-start(bf16[16,1024]{1,0:T(8,128)(2,1)S(1)} %fusion.30), channel_id=1, source_target_pairs={{0,2},{1,3},{2,0},{3,1},{4,6},{5,7},{6,4},{7,5},{8,10},{9,11},{10,... | collective-permute-start | bytes 98312 | tf_op jit(solution)/shard_map/ppermute | solution.py:59
  71.5 1.3 %collective-permute-done.21 = bf16[16,1024]{1,0:T(8,128)(2,1)S(1)} collective-permute-done((bf16[16,1024]{1,0:T(8,128)(2,1)S(1)}, bf16[16,1024]{1,0:T(8,128)(2,1)S(1)}, u32[]{:S(2)}, u32[]{:S(2)}) %collective-permute-start.21) | collective-permute-done | bytes 32800 | tf_op jit(solution)/shard_map/ppermute | solution.py:59
  72.8 1.1 collective-permute-done.20
  73.9 0.5 fusion.36
  74.4 0.5 fusion.35
  75.0 1.6 %collective-permute-start.25 = (bf16[64,1280]{1,0:T(8,128)(2,1)S(1)}, bf16[64,1280]{1,0:T(8,128)(2,1)S(1)}, u32[]{:S(2)}, u32[]{:S(2)}) collective-permute-start(bf16[64,1280]{1,0:T(8,128)(2,1)S(1)} %fusion.2), channel_id=1, source_target_pairs={{0,8},{8,0},{16,24},{24,16},{1,9},{9,1},{17,25},{25,17},{2,10},{10... | collective-permute-start | bytes 491528 | tf_op jit(solution)/shard_map/ppermute | solution.py:68
  76.5 1.4 %collective-permute-start.24 = (bf16[64,1280]{1,0:T(8,128)(2,1)S(1)}, bf16[64,1280]{1,0:T(8,128)(2,1)S(1)}, u32[]{:S(2)}, u32[]{:S(2)}) collective-permute-start(bf16[64,1280]{1,0:T(8,128)(2,1)S(1)} %fusion.2), channel_id=1, source_target_pairs={{0,16},{8,24},{16,0},{24,8},{1,17},{9,25},{17,1},{25,9},{2,18},{10... | collective-permute-start | bytes 491528 | tf_op jit(solution)/shard_map/ppermute | solution.py:68
  78.0 0.6 collective-permute-start.23
  78.7 2.2 %collective-permute-done.25 = bf16[64,1280]{1,0:T(8,128)(2,1)S(1)} collective-permute-done((bf16[64,1280]{1,0:T(8,128)(2,1)S(1)}, bf16[64,1280]{1,0:T(8,128)(2,1)S(1)}, u32[]{:S(2)}, u32[]{:S(2)}) %collective-permute-start.25) | collective-permute-done | bytes 163872 | tf_op jit(solution)/shard_map/ppermute | solution.py:68
  80.8 1.1 collective-permute-done.24
  81.9 2.3 %collective-permute-done.23 = bf16[64,1280]{1,0:T(8,128)(2,1)S(1)} collective-permute-done((bf16[64,1280]{1,0:T(8,128)(2,1)S(1)}, bf16[64,1280]{1,0:T(8,128)(2,1)S(1)}, u32[]{:S(2)}, u32[]{:S(2)}) %collective-permute-start.23) | collective-permute-done | bytes 163872 | tf_op jit(solution)/shard_map/ppermute | solution.py:68
  85.1 1.6 %collective-permute-start.29 = (bf16[16,1024]{1,0:T(8,128)(2,1)S(1)}, bf16[16,1024]{1,0:T(8,128)(2,1)S(1)}, u32[]{:S(2)}, u32[]{:S(2)}) collective-permute-start(bf16[16,1024]{1,0:T(8,128)(2,1)S(1)} %get-tuple-element.48), channel_id=1, source_target_pairs={{0,2},{1,3},{2,0},{3,1},{4,6},{5,7},{6,4},{7,5},{8,10},{9,11},{10,... | collective-permute-start | bytes 98312 | tf_op jit(solution)/shard_map/ppermute | solution.py:59
  86.6 0.9 collective-permute-start.28
  87.5 2.0 %collective-permute-start.27 = (bf16[16,1024]{1,0:T(8,128)(2,1)S(1)}, bf16[16,1024]{1,0:T(8,128)(2,1)S(1)}, u32[]{:S(2)}, u32[]{:S(2)}) collective-permute-start(bf16[16,1024]{1,0:T(8,128)(2,1)S(1)} %get-tuple-element.47), channel_id=1, source_target_pairs={{0,6},{1,7},{2,4},{3,5},{4,2},{5,3},{6,0},{7,1},{8,14},{9,15},{10,... | collective-permute-start | bytes 98312 | tf_op jit(solution)/shard_map/ppermute | solution.py:59
  89.5 2.2 %collective-permute-done.28 = bf16[16,1024]{1,0:T(8,128)(2,1)S(1)} collective-permute-done((bf16[16,1024]{1,0:T(8,128)(2,1)S(1)}, bf16[16,1024]{1,0:T(8,128)(2,1)S(1)}, u32[]{:S(2)}, u32[]{:S(2)}) %collective-permute-start.28) | collective-permute-done | bytes 32800 | tf_op jit(solution)/shard_map/ppermute | solution.py:59
  91.8 1.5 %collective-permute-done.27 = bf16[16,1024]{1,0:T(8,128)(2,1)S(1)} collective-permute-done((bf16[16,1024]{1,0:T(8,128)(2,1)S(1)}, bf16[16,1024]{1,0:T(8,128)(2,1)S(1)}, u32[]{:S(2)}, u32[]{:S(2)}) %collective-permute-start.27) | collective-permute-done | bytes 32800 | tf_op jit(solution)/shard_map/ppermute | solution.py:59
  93.3 2.0 %collective-permute-start.32 = (bf16[16,1024]{1,0:T(8,128)(2,1)S(1)}, bf16[16,1024]{1,0:T(8,128)(2,1)S(1)}, u32[]{:S(2)}, u32[]{:S(2)}) collective-permute-start(bf16[16,1024]{1,0:T(8,128)(2,1)S(1)} %fusion.31), channel_id=1, source_target_pairs={{0,6},{1,7},{2,4},{3,5},{4,2},{5,3},{6,0},{7,1},{8,14},{9,15},{10,... | collective-permute-start | bytes 98312 | tf_op jit(solution)/shard_map/ppermute | solution.py:59
  95.8 2.0 %collective-permute-start.30 = (bf16[16,1024]{1,0:T(8,128)(2,1)S(1)}, bf16[16,1024]{1,0:T(8,128)(2,1)S(1)}, u32[]{:S(2)}, u32[]{:S(2)}) collective-permute-start(bf16[16,1024]{1,0:T(8,128)(2,1)S(1)} %fusion.31), channel_id=1, source_target_pairs={{0,2},{1,3},{2,0},{3,1},{4,6},{5,7},{6,4},{7,5},{8,10},{9,11},{10,... | collective-permute-start | bytes 98312 | tf_op jit(solution)/shard_map/ppermute | solution.py:59
  97.8 1.3 %collective-permute-done.32 = bf16[16,1024]{1,0:T(8,128)(2,1)S(1)} collective-permute-done((bf16[16,1024]{1,0:T(8,128)(2,1)S(1)}, bf16[16,1024]{1,0:T(8,128)(2,1)S(1)}, u32[]{:S(2)}, u32[]{:S(2)}) %collective-permute-start.32) | collective-permute-done | bytes 32800 | tf_op jit(solution)/shard_map/ppermute | solution.py:59
  99.1 1.1 collective-permute-done.31
  100.2 0.5 fusion.33
  100.7 0.5 fusion.34
  101.3 0.7 fusion.1
  102.1 0.9 collective-permute-start.35
  103.5 2.1 %collective-permute-start.33 = (bf16[64,1280]{1,0:T(8,128)(2,1)}, bf16[64,1280]{1,0:T(8,128)(2,1)}, u32[]{:S(2)}, u32[]{:S(2)}) collective-permute-start(bf16[64,1280]{1,0:T(8,128)(2,1)} %fusion.1), channel_id=1, source_target_pairs={{0,24},{8,16},{16,8},{24,0},{1,25},{9,17},{17,9},{25,1},{2,26},{10... | collective-permute-start | bytes 491528 | tf_op jit(solution)/shard_map/ppermute | solution.py:68
  105.6 2.1 %collective-permute-done.35 = bf16[64,1280]{1,0:T(8,128)(2,1)} collective-permute-done((bf16[64,1280]{1,0:T(8,128)(2,1)}, bf16[64,1280]{1,0:T(8,128)(2,1)}, u32[]{:S(2)}, u32[]{:S(2)}) %collective-permute-start.35) | collective-permute-done | bytes 163872 | tf_op jit(solution)/shard_map/ppermute | solution.py:68
  107.7 2.7 %collective-permute-done.34 = bf16[64,1280]{1,0:T(8,128)(2,1)} collective-permute-done((bf16[64,1280]{1,0:T(8,128)(2,1)}, bf16[64,1280]{1,0:T(8,128)(2,1)}, u32[]{:S(2)}, u32[]{:S(2)}) %collective-permute-start.34) | collective-permute-done | bytes 163872 | tf_op jit(solution)/shard_map/ppermute | solution.py:68
  110.4 1.3 %convert_add_fusion = f32[64,1280]{1,0:T(8,128)S(1)} fusion(bf16[64,1280]{1,0:T(8,128)(2,1)} %collective-permute-done.35, bf16[64,1280]{1,0:T(8,128)(2,1)} %collective-permute-done.34, bf16[64,1280]{1,0:T(8,128)(2,1)} %collective-permute-done.33, f32[64,640]{1,0:T(8,128)} %copy-done.1, f32[64,640]{1,0:T(8,128)} %copy-done.2), kind=kLoop, calls=%fused_computation.9 | loop fusion | flops 573440 | bytes 1146880 | tf_op jit(solution)/shard_map/add | solution.py:318
  111.7 1.0 fusion.4
  113.6 1.6 %collective-permute-start.39 = (bf16[16,1024]{1,0:T(8,128)(2,1)S(1)}, bf16[16,1024]{1,0:T(8,128)(2,1)S(1)}, u32[]{:S(2)}, u32[]{:S(2)}) collective-permute-start(bf16[16,1024]{1,0:T(8,128)(2,1)S(1)} %get-tuple-element.45), channel_id=1, source_target_pairs={{0,2},{1,3},{2,0},{3,1},{4,6},{5,7},{6,4},{7,5},{8,10},{9,11},{10,... | collective-permute-start | bytes 98312 | tf_op jit(solution)/shard_map/ppermute | solution.py:59
  115.1 0.9 collective-permute-start.38
  116.0 2.0 %collective-permute-start.37 = (bf16[16,1024]{1,0:T(8,128)(2,1)S(1)}, bf16[16,1024]{1,0:T(8,128)(2,1)S(1)}, u32[]{:S(2)}, u32[]{:S(2)}) collective-permute-start(bf16[16,1024]{1,0:T(8,128)(2,1)S(1)} %get-tuple-element.44), channel_id=1, source_target_pairs={{0,6},{1,7},{2,4},{3,5},{4,2},{5,3},{6,0},{7,1},{8,14},{9,15},{10,... | collective-permute-start | bytes 98312 | tf_op jit(solution)/shard_map/ppermute | solution.py:59
  118.0 0.6 maximum_bitcast_fusion
  118.7 2.3 %collective-permute-done.38 = bf16[16,1024]{1,0:T(8,128)(2,1)S(1)} collective-permute-done((bf16[16,1024]{1,0:T(8,128)(2,1)S(1)}, bf16[16,1024]{1,0:T(8,128)(2,1)S(1)}, u32[]{:S(2)}, u32[]{:S(2)}) %collective-permute-start.38) | collective-permute-done | bytes 32800 | tf_op jit(solution)/shard_map/ppermute | solution.py:59
  121.0 0.8 collective-permute-done.37
  121.8 0.6 add_bitcast_fusion
  (88 shorter events, 3.9 us)
Async XLA Ops:
  0.6 61.8 %copy-start = (s32[1024,128]{1,0:T(8,128)S(1)}, s32[1024,128]{1,0:T(8,128)}, u32[]{:S(2)}) copy-start(s32[1024,128]{1,0:T(8,128)} %param.9) | copy-start | bytes 1572868
  0.6 5.9 %copy-start.8 = (f32[1024,144]{0,1:T(8,128)S(1)}, f32[1024,144]{0,1:T(8,128)}, u32[]{:S(2)}) copy-start(f32[1024,144]{0,1:T(8,128)} %param.5) | copy-start | bytes 1769476
  0.7 24.7 %copy-start.17 = (f32[640]{0:T(1024)S(1)}, f32[640]{0:T(1024)}, u32[]{:S(2)}) copy-start(f32[640]{0:T(1024)} %param.7) | copy-start | bytes 7684
  2.0 20.7 %collective-permute-start.2 = (s16[288,640]{1,0:T(8,128)(2,1)S(1)}, s16[288,640]{1,0:T(8,128)(2,1)S(1)}, u32[]{:S(2)}, u32[]{:S(2)}) collective-permute-start(s16[288,640]{1,0:T(8,128)(2,1)S(1)} %round-nearest-even_convert_fusion.refs_6_), channel_id=1, source_target_pairs={{0,24},{8,16},{16,8},{24,0},{1,25},{9,17},{17,9},{25,1},{2,26},{10... | collective-permute-start | bytes 1105928 | tf_op jit(solution)/shard_map/ppermute | solution.py:68
  5.9 16.8 %collective-permute-start.3 = (s16[288,640]{1,0:T(8,128)(2,1)S(1)}, s16[288,640]{1,0:T(8,128)(2,1)S(1)}, u32[]{:S(2)}, u32[]{:S(2)}) collective-permute-start(s16[288,640]{1,0:T(8,128)(2,1)S(1)} %round-nearest-even_convert_fusion.refs_6_), channel_id=1, source_target_pairs={{0,8},{8,0},{16,24},{24,16},{1,9},{9,1},{17,25},{25,17},{2,10},{10... | collective-permute-start | bytes 1105928 | tf_op jit(solution)/shard_map/ppermute | solution.py:68
  6.5 16.2 %collective-permute-start.4 = (s16[288,640]{1,0:T(8,128)(2,1)S(1)}, s16[288,640]{1,0:T(8,128)(2,1)S(1)}, u32[]{:S(2)}, u32[]{:S(2)}) collective-permute-start(s16[288,640]{1,0:T(8,128)(2,1)S(1)} %round-nearest-even_convert_fusion.refs_6_), channel_id=1, source_target_pairs={{0,16},{8,24},{16,0},{24,8},{1,17},{9,25},{17,1},{25,9},{2,18},{10... | collective-permute-start | bytes 1105928 | tf_op jit(solution)/shard_map/ppermute | solution.py:68
  6.7 15.8 %collective-permute-start = (s16[144,1024]{1,0:T(8,128)(2,1)S(1)}, s16[144,1024]{1,0:T(8,128)(2,1)}, u32[]{:S(2)}, u32[]{:S(2)}) collective-permute-start(s16[144,1024]{1,0:T(8,128)(2,1)S(1)} %fusion.refs_0_), channel_id=1, source_target_pairs={{0,4},{1,5},{2,6},{3,7},{4,0},{5,1},{6,2},{7,3},{8,12},{9,13},{10,... | collective-permute-start | bytes 884744 | tf_op jit(solution)/shard_map/ppermute | solution.py:59
  9.7 12.9 %collective-permute-start.1 = (s16[144,1024]{1,0:T(8,128)(2,1)S(1)}, s16[144,1024]{1,0:T(8,128)(2,1)}, u32[]{:S(2)}, u32[]{:S(2)}) collective-permute-start(s16[144,1024]{1,0:T(8,128)(2,1)S(1)} %fusion.refs_0_), channel_id=1, source_target_pairs={{0,2},{1,3},{2,0},{3,1},{4,6},{5,7},{6,4},{7,5},{8,10},{9,11},{10,... | collective-permute-start | bytes 884744 | tf_op jit(solution)/shard_map/ppermute | solution.py:59
  22.7 2.9 %collective-permute-start.5 = (s16[144,1024]{1,0:T(8,128)(2,1)S(1)}, s16[144,1024]{1,0:T(8,128)(2,1)}, u32[]{:S(2)}, u32[]{:S(2)}) collective-permute-start(s16[144,1024]{1,0:T(8,128)(2,1)S(1)} %fusion.refs_0_), channel_id=1, source_target_pairs={{0,1},{1,0},{2,3},{3,2},{4,5},{5,4},{6,7},{7,6},{8,9},{9,8},{10,11... | collective-permute-start | bytes 884744 | tf_op jit(solution)/shard_map/ppermute | solution.py:54
  22.7 2.9 %collective-permute-start.6 = (s16[144,1024]{1,0:T(8,128)(2,1)}, s16[144,1024]{1,0:T(8,128)(2,1)}, u32[]{:S(2)}, u32[]{:S(2)}) collective-permute-start(s16[144,1024]{1,0:T(8,128)(2,1)} %collective-permute-done.1.refs_2_), channel_id=1, source_target_pairs={{0,1},{1,0},{2,3},{3,2},{4,5},{5,4},{6,7},{7,6},{8,9},{9,8},{10,11... | collective-permute-start | bytes 884744 | tf_op jit(solution)/shard_map/ppermute | solution.py:54
  23.2 2.5 %collective-permute-start.7 = (s16[144,1024]{1,0:T(8,128)(2,1)}, s16[144,1024]{1,0:T(8,128)(2,1)}, u32[]{:S(2)}, u32[]{:S(2)}) collective-permute-start(s16[144,1024]{1,0:T(8,128)(2,1)} %collective-permute-done.refs_4_), channel_id=1, source_target_pairs={{0,1},{1,0},{2,3},{3,2},{4,5},{5,4},{6,7},{7,6},{8,9},{9,8},{10,11... | collective-permute-start | bytes 884744 | tf_op jit(solution)/shard_map/ppermute | solution.py:54
  23.3 6.0 %collective-permute-start.11 = (s16[144,1024]{1,0:T(8,128)(2,1)S(1)}, s16[144,1024]{1,0:T(8,128)(2,1)S(1)}, u32[]{:S(2)}, u32[]{:S(2)}) collective-permute-start(s16[144,1024]{1,0:T(8,128)(2,1)S(1)} %fusion.refs_0_), channel_id=1, source_target_pairs={{2,4},{3,5},{4,2},{5,3},{10,12},{11,13},{12,10},{13,11},{18,20},{1... | collective-permute-start | bytes 884744 | tf_op jit(solution)/shard_map/ppermute | solution.py:63
  24.0 13.2 %collective-permute-start.12 = (s16[144,1024]{1,0:T(8,128)(2,1)}, s16[144,1024]{1,0:T(8,128)(2,1)S(1)}, u32[]{:S(2)}, u32[]{:S(2)}) collective-permute-start(s16[144,1024]{1,0:T(8,128)(2,1)} %collective-permute-done.refs_4_), channel_id=1, source_target_pairs={{2,0},{3,1},{4,6},{5,7},{10,8},{11,9},{12,14},{13,15},{18,16},{19,... | collective-permute-start | bytes 884744 | tf_op jit(solution)/shard_map/ppermute | solution.py:63
  25.7 21.4 %copy-start.16 = (f32[640,32]{0,1:T(8,128)S(1)}, f32[640,32]{0,1:T(8,128)}, u32[]{:S(2)}) copy-start(f32[640,32]{0,1:T(8,128)} %param.8) | copy-start | bytes 245764
  25.7 21.3 %collective-permute-start.10 = (f32[32,640]{1,0:T(8,128)}, f32[32,640]{1,0:T(8,128)S(1)}, u32[]{:S(2)}, u32[]{:S(2)}) collective-permute-start(f32[32,640]{1,0:T(8,128)} %bitcast.58), channel_id=1, source_target_pairs={{0,24},{8,16},{16,8},{24,0},{1,25},{9,17},{17,9},{25,1},{2,26},{10... | collective-permute-start | bytes 245768 | tf_op jit(solution)/shard_map/ppermute | solution.py:68
  28.3 18.8 %collective-permute-start.9 = (f32[32,640]{1,0:T(8,128)}, f32[32,640]{1,0:T(8,128)S(1)}, u32[]{:S(2)}, u32[]{:S(2)}) collective-permute-start(f32[32,640]{1,0:T(8,128)} %bitcast.59), channel_id=1, source_target_pairs={{0,16},{8,24},{16,0},{24,8},{1,17},{9,25},{17,1},{25,9},{2,18},{10... | collective-permute-start | bytes 245768 | tf_op jit(solution)/shard_map/ppermute | solution.py:68
  28.8 18.3 %collective-permute-start.8 = (f32[32,640]{1,0:T(8,128)}, f32[32,640]{1,0:T(8,128)S(1)}, u32[]{:S(2)}, u32[]{:S(2)}) collective-permute-start(f32[32,640]{1,0:T(8,128)} %bitcast.60), channel_id=1, source_target_pairs={{0,8},{8,0},{16,24},{24,16},{1,9},{9,1},{17,25},{25,17},{2,10},{10... | collective-permute-start | bytes 245768 | tf_op jit(solution)/shard_map/ppermute | solution.py:68
  29.3 17.9 %collective-permute-start.13 = (s16[144,1024]{1,0:T(8,128)(2,1)S(1)}, s16[144,1024]{1,0:T(8,128)(2,1)S(1)}, u32[]{:S(2)}, u32[]{:S(2)}) collective-permute-start(s16[144,1024]{1,0:T(8,128)(2,1)S(1)} %collective-permute-done.11.own_a), channel_id=1, source_target_pairs={{0,1},{1,0},{2,3},{3,2},{4,5},{5,4},{6,7},{7,6},{8,9},{9,8},{10,11... | collective-permute-start | bytes 884744 | tf_op jit(solution)/shard_map/ppermute | solution.py:54
  37.2 10.0 %collective-permute-start.14 = (s16[144,1024]{1,0:T(8,128)(2,1)S(1)}, s16[144,1024]{1,0:T(8,128)(2,1)S(1)}, u32[]{:S(2)}, u32[]{:S(2)}) collective-permute-start(s16[144,1024]{1,0:T(8,128)(2,1)S(1)} %collective-permute-done.12.own_b), channel_id=1, source_target_pairs={{0,1},{1,0},{2,3},{3,2},{4,5},{5,4},{6,7},{7,6},{8,9},{9,8},{10,11... | collective-permute-start | bytes 884744 | tf_op jit(solution)/shard_map/ppermute | solution.py:54
  47.2 4.5 %copy-start.11 = (f32[16,640]{1,0:T(8,128)}, f32[16,640]{1,0:T(8,128)S(1)}, u32[]{:S(2)}) copy-start(f32[16,640]{1,0:T(8,128)S(1)} %get-tuple-element.39) | copy-start | bytes 122884
  47.2 4.5 %copy-start.13 = (f32[16,640]{1,0:T(8,128)}, f32[16,640]{1,0:T(8,128)S(1)}, u32[]{:S(2)}) copy-start(f32[16,640]{1,0:T(8,128)S(1)} %get-tuple-element.40) | copy-start | bytes 122884
  47.2 8.2 %copy-start.4 = (f32[16,640]{1,0:T(8,128)}, f32[16,640]{1,0:T(8,128)S(1)}, u32[]{:S(2)}) copy-start(f32[16,640]{1,0:T(8,128)S(1)} %get-tuple-element.42) | copy-start | bytes 122884
  47.2 8.2 %copy-start.6 = (f32[16,640]{1,0:T(8,128)}, f32[16,640]{1,0:T(8,128)S(1)}, u32[]{:S(2)}) copy-start(f32[16,640]{1,0:T(8,128)S(1)} %get-tuple-element.43) | copy-start | bytes 122884
  51.1 23.3 %collective-permute-start.22 = (bf16[640,1024]{1,0:T(8,128)(2,1)S(1)}, bf16[640,1024]{1,0:T(8,128)(2,1)S(1)}, u32[]{:S(2)}, u32[]{:S(2)}) collective-permute-start(bf16[640,1024]{1,0:T(8,128)(2,1)S(1)} %late_angles.1), channel_id=1, source_target_pairs={{0,1},{1,0},{2,3},{3,2},{4,5},{5,4},{6,7},{7,6},{8,9},{9,8},{10,11... | collective-permute-start | bytes 3932168 | tf_op jit(solution)/shard_map/ppermute | solution.py:54
  52.7 2.0 %collective-permute-start.15 = (bf16[64,1024]{1,0:T(8,128)(2,1)}, bf16[64,1024]{1,0:T(8,128)(2,1)S(1)}, u32[]{:S(2)}, u32[]{:S(2)}) collective-permute-start(bf16[64,1024]{1,0:T(8,128)(2,1)} %convolution_convert_fusion), channel_id=1, source_target_pairs={{0,1},{1,0},{2,3},{3,2},{4,5},{5,4},{6,7},{7,6},{8,9},{9,8},{10,11... | collective-permute-start | bytes 393224 | tf_op jit(solution)/shard_map/ppermute | solution.py:54
  54.7 0.6 copy-start.15
  58.0 6.6 %collective-permute-start.18 = (bf16[16,1024]{1,0:T(8,128)(2,1)}, bf16[16,1024]{1,0:T(8,128)(2,1)S(1)}, u32[]{:S(2)}, u32[]{:S(2)}) collective-permute-start(bf16[16,1024]{1,0:T(8,128)(2,1)} %get-tuple-element.51), channel_id=1, source_target_pairs={{0,2},{1,3},{2,0},{3,1},{4,6},{5,7},{6,4},{7,5},{8,10},{9,11},{10,... | collective-permute-start | bytes 98312 | tf_op jit(solution)/shard_map/ppermute | solution.py:59
  58.0 6.6 %collective-permute-start.17 = (bf16[16,1024]{1,0:T(8,128)(2,1)}, bf16[16,1024]{1,0:T(8,128)(2,1)S(1)}, u32[]{:S(2)}, u32[]{:S(2)}) collective-permute-start(bf16[16,1024]{1,0:T(8,128)(2,1)} %get-tuple-element.52), channel_id=1, source_target_pairs={{0,4},{1,5},{2,6},{3,7},{4,0},{5,1},{6,2},{7,3},{8,12},{9,13},{10,... | collective-permute-start | bytes 98312 | tf_op jit(solution)/shard_map/ppermute | solution.py:59
  60.4 5.7 %collective-permute-start.16 = (bf16[16,1024]{1,0:T(8,128)(2,1)S(1)}, bf16[16,1024]{1,0:T(8,128)(2,1)S(1)}, u32[]{:S(2)}, u32[]{:S(2)}) collective-permute-start(bf16[16,1024]{1,0:T(8,128)(2,1)S(1)} %get-tuple-element.50), channel_id=1, source_target_pairs={{0,6},{1,7},{2,4},{3,5},{4,2},{5,3},{6,0},{7,1},{8,14},{9,15},{10,... | collective-permute-start | bytes 98312 | tf_op jit(solution)/shard_map/ppermute | solution.py:59
  64.6 10.3 %copy-start.9 = (s32[1024,16]{0,1:T(8,128)}, s32[1024,16]{0,1:T(8,128)S(1)}, u32[]{:S(2)}) copy-start(s32[1024,16]{0,1:T(8,128)S(1)} %copy.10) | copy-start | bytes 196612
  67.0 5.8 %collective-permute-start.21 = (bf16[16,1024]{1,0:T(8,128)(2,1)S(1)}, bf16[16,1024]{1,0:T(8,128)(2,1)S(1)}, u32[]{:S(2)}, u32[]{:S(2)}) collective-permute-start(bf16[16,1024]{1,0:T(8,128)(2,1)S(1)} %fusion.30), channel_id=1, source_target_pairs={{0,6},{1,7},{2,4},{3,5},{4,2},{5,3},{6,0},{7,1},{8,14},{9,15},{10,... | collective-permute-start | bytes 98312 | tf_op jit(solution)/shard_map/ppermute | solution.py:59
  69.1 4.8 %collective-permute-start.20 = (bf16[16,1024]{1,0:T(8,128)(2,1)S(1)}, bf16[16,1024]{1,0:T(8,128)(2,1)S(1)}, u32[]{:S(2)}, u32[]{:S(2)}) collective-permute-start(bf16[16,1024]{1,0:T(8,128)(2,1)S(1)} %fusion.30), channel_id=1, source_target_pairs={{0,4},{1,5},{2,6},{3,7},{4,0},{5,1},{6,2},{7,3},{8,12},{9,13},{10,... | collective-permute-start | bytes 98312 | tf_op jit(solution)/shard_map/ppermute | solution.py:59
  69.1 4.8 %collective-permute-start.19 = (bf16[16,1024]{1,0:T(8,128)(2,1)S(1)}, bf16[16,1024]{1,0:T(8,128)(2,1)S(1)}, u32[]{:S(2)}, u32[]{:S(2)}) collective-permute-start(bf16[16,1024]{1,0:T(8,128)(2,1)S(1)} %fusion.30), channel_id=1, source_target_pairs={{0,2},{1,3},{2,0},{3,1},{4,6},{5,7},{6,4},{7,5},{8,10},{9,11},{10,... | collective-permute-start | bytes 98312 | tf_op jit(solution)/shard_map/ppermute | solution.py:59
  74.4 4.1 %copy-start.12 = (f32[16,640]{1,0:T(8,128)S(1)}, f32[16,640]{1,0:T(8,128)}, u32[]{:S(2)}) copy-start(f32[16,640]{1,0:T(8,128)} %copy-done.11) | copy-start | bytes 122884
  74.4 4.1 %copy-start.14 = (f32[16,640]{1,0:T(8,128)S(1)}, f32[16,640]{1,0:T(8,128)}, u32[]{:S(2)}) copy-start(f32[16,640]{1,0:T(8,128)} %copy-done.13) | copy-start | bytes 122884
  75.0 5.8 %collective-permute-start.25 = (bf16[64,1280]{1,0:T(8,128)(2,1)S(1)}, bf16[64,1280]{1,0:T(8,128)(2,1)S(1)}, u32[]{:S(2)}, u32[]{:S(2)}) collective-permute-start(bf16[64,1280]{1,0:T(8,128)(2,1)S(1)} %fusion.2), channel_id=1, source_target_pairs={{0,8},{8,0},{16,24},{24,16},{1,9},{9,1},{17,25},{25,17},{2,10},{10... | collective-permute-start | bytes 491528 | tf_op jit(solution)/shard_map/ppermute | solution.py:68
  76.5 5.4 %collective-permute-start.24 = (bf16[64,1280]{1,0:T(8,128)(2,1)S(1)}, bf16[64,1280]{1,0:T(8,128)(2,1)S(1)}, u32[]{:S(2)}, u32[]{:S(2)}) collective-permute-start(bf16[64,1280]{1,0:T(8,128)(2,1)S(1)} %fusion.2), channel_id=1, source_target_pairs={{0,16},{8,24},{16,0},{24,8},{1,17},{9,25},{17,1},{25,9},{2,18},{10... | collective-permute-start | bytes 491528 | tf_op jit(solution)/shard_map/ppermute | solution.py:68
  78.0 6.2 %collective-permute-start.23 = (bf16[64,1280]{1,0:T(8,128)(2,1)S(1)}, bf16[64,1280]{1,0:T(8,128)(2,1)S(1)}, u32[]{:S(2)}, u32[]{:S(2)}) collective-permute-start(bf16[64,1280]{1,0:T(8,128)(2,1)S(1)} %fusion.2), channel_id=1, source_target_pairs={{0,24},{8,16},{16,8},{24,0},{1,25},{9,17},{17,9},{25,1},{2,26},{10... | collective-permute-start | bytes 491528 | tf_op jit(solution)/shard_map/ppermute | solution.py:68
  78.6 6.1 %copy-start.5 = (f32[16,640]{1,0:T(8,128)S(1)}, f32[16,640]{1,0:T(8,128)}, u32[]{:S(2)}) copy-start(f32[16,640]{1,0:T(8,128)} %copy-done.4) | copy-start | bytes 122884
  78.6 6.1 %copy-start.7 = (f32[16,640]{1,0:T(8,128)S(1)}, f32[16,640]{1,0:T(8,128)}, u32[]{:S(2)}) copy-start(f32[16,640]{1,0:T(8,128)} %copy-done.6) | copy-start | bytes 122884
  78.6 5.7 %collective-permute-start.26 = (f32[64,640]{1,0:T(8,128)S(1)}, f32[64,640]{1,0:T(8,128)S(1)}, u32[]{:S(2)}, u32[]{:S(2)}) collective-permute-start(f32[64,640]{1,0:T(8,128)S(1)} %pad_maximum_fusion.4), channel_id=1, source_target_pairs={{0,1},{1,0},{2,3},{3,2},{4,5},{5,4},{6,7},{7,6},{8,9},{9,8},{10,11... | collective-permute-start | bytes 491528 | tf_op jit(solution)/shard_map/ppermute | solution.py:54
  84.3 15.9 %copy-start.3 = (f32[64,640]{1,0:T(8,128)}, f32[64,640]{1,0:T(8,128)S(1)}, u32[]{:S(2)}) copy-start(f32[64,640]{1,0:T(8,128)S(1)} %collective-permute-done.26) | copy-start | bytes 491524
  84.7 8.6 %copy-start.10 = (s32[1024,16]{0,1:T(8,128)S(1)}, s32[1024,16]{0,1:T(8,128)}, u32[]{:S(2)}) copy-start(s32[1024,16]{0,1:T(8,128)} %copy-done.9) | copy-start | bytes 196612
  85.1 4.5 %collective-permute-start.29 = (bf16[16,1024]{1,0:T(8,128)(2,1)S(1)}, bf16[16,1024]{1,0:T(8,128)(2,1)S(1)}, u32[]{:S(2)}, u32[]{:S(2)}) collective-permute-start(bf16[16,1024]{1,0:T(8,128)(2,1)S(1)} %get-tuple-element.48), channel_id=1, source_target_pairs={{0,2},{1,3},{2,0},{3,1},{4,6},{5,7},{6,4},{7,5},{8,10},{9,11},{10,... | collective-permute-start | bytes 98312 | tf_op jit(solution)/shard_map/ppermute | solution.py:59
  86.6 5.1 %collective-permute-start.28 = (bf16[16,1024]{1,0:T(8,128)(2,1)S(1)}, bf16[16,1024]{1,0:T(8,128)(2,1)S(1)}, u32[]{:S(2)}, u32[]{:S(2)}) collective-permute-start(bf16[16,1024]{1,0:T(8,128)(2,1)S(1)} %get-tuple-element.49), channel_id=1, source_target_pairs={{0,4},{1,5},{2,6},{3,7},{4,0},{5,1},{6,2},{7,3},{8,12},{9,13},{10,... | collective-permute-start | bytes 98312 | tf_op jit(solution)/shard_map/ppermute | solution.py:59
  87.5 5.7 %collective-permute-start.27 = (bf16[16,1024]{1,0:T(8,128)(2,1)S(1)}, bf16[16,1024]{1,0:T(8,128)(2,1)S(1)}, u32[]{:S(2)}, u32[]{:S(2)}) collective-permute-start(bf16[16,1024]{1,0:T(8,128)(2,1)S(1)} %get-tuple-element.47), channel_id=1, source_target_pairs={{0,6},{1,7},{2,4},{3,5},{4,2},{5,3},{6,0},{7,1},{8,14},{9,15},{10,... | collective-permute-start | bytes 98312 | tf_op jit(solution)/shard_map/ppermute | solution.py:59
  93.3 5.8 %collective-permute-start.32 = (bf16[16,1024]{1,0:T(8,128)(2,1)S(1)}, bf16[16,1024]{1,0:T(8,128)(2,1)S(1)}, u32[]{:S(2)}, u32[]{:S(2)}) collective-permute-start(bf16[16,1024]{1,0:T(8,128)(2,1)S(1)} %fusion.31), channel_id=1, source_target_pairs={{0,6},{1,7},{2,4},{3,5},{4,2},{5,3},{6,0},{7,1},{8,14},{9,15},{10,... | collective-permute-start | bytes 98312 | tf_op jit(solution)/shard_map/ppermute | solution.py:59
  95.3 4.8 %collective-permute-start.31 = (bf16[16,1024]{1,0:T(8,128)(2,1)S(1)}, bf16[16,1024]{1,0:T(8,128)(2,1)S(1)}, u32[]{:S(2)}, u32[]{:S(2)}) collective-permute-start(bf16[16,1024]{1,0:T(8,128)(2,1)S(1)} %fusion.31), channel_id=1, source_target_pairs={{0,4},{1,5},{2,6},{3,7},{4,0},{5,1},{6,2},{7,3},{8,12},{9,13},{10,... | collective-permute-start | bytes 98312 | tf_op jit(solution)/shard_map/ppermute | solution.py:59
  95.8 4.4 %collective-permute-start.30 = (bf16[16,1024]{1,0:T(8,128)(2,1)S(1)}, bf16[16,1024]{1,0:T(8,128)(2,1)S(1)}, u32[]{:S(2)}, u32[]{:S(2)}) collective-permute-start(bf16[16,1024]{1,0:T(8,128)(2,1)S(1)} %fusion.31), channel_id=1, source_target_pairs={{0,2},{1,3},{2,0},{3,1},{4,6},{5,7},{6,4},{7,5},{8,10},{9,11},{10,... | collective-permute-start | bytes 98312 | tf_op jit(solution)/shard_map/ppermute | solution.py:59
  100.7 0.7 copy-start.1
  101.3 0.7 copy-start.2
  102.1 5.6 %collective-permute-start.35 = (bf16[64,1280]{1,0:T(8,128)(2,1)}, bf16[64,1280]{1,0:T(8,128)(2,1)}, u32[]{:S(2)}, u32[]{:S(2)}) collective-permute-start(bf16[64,1280]{1,0:T(8,128)(2,1)} %fusion.1), channel_id=1, source_target_pairs={{0,8},{8,0},{16,24},{24,16},{1,9},{9,1},{17,25},{25,17},{2,10},{10... | collective-permute-start | bytes 491528 | tf_op jit(solution)/shard_map/ppermute | solution.py:68
  103.0 7.4 %collective-permute-start.34 = (bf16[64,1280]{1,0:T(8,128)(2,1)}, bf16[64,1280]{1,0:T(8,128)(2,1)}, u32[]{:S(2)}, u32[]{:S(2)}) collective-permute-start(bf16[64,1280]{1,0:T(8,128)(2,1)} %fusion.1), channel_id=1, source_target_pairs={{0,16},{8,24},{16,0},{24,8},{1,17},{9,25},{17,1},{25,9},{2,18},{10... | collective-permute-start | bytes 491528 | tf_op jit(solution)/shard_map/ppermute | solution.py:68
  103.5 6.9 %collective-permute-start.33 = (bf16[64,1280]{1,0:T(8,128)(2,1)}, bf16[64,1280]{1,0:T(8,128)(2,1)}, u32[]{:S(2)}, u32[]{:S(2)}) collective-permute-start(bf16[64,1280]{1,0:T(8,128)(2,1)} %fusion.1), channel_id=1, source_target_pairs={{0,24},{8,16},{16,8},{24,0},{1,25},{9,17},{17,9},{25,1},{2,26},{10... | collective-permute-start | bytes 491528 | tf_op jit(solution)/shard_map/ppermute | solution.py:68
  112.7 5.3 %collective-permute-start.36 = (f32[64,640]{1,0:T(8,128)S(1)}, f32[64,640]{1,0:T(8,128)S(1)}, u32[]{:S(2)}, u32[]{:S(2)}) collective-permute-start(f32[64,640]{1,0:T(8,128)S(1)} %get-tuple-element.33), channel_id=1, source_target_pairs={{0,1},{1,0},{2,3},{3,2},{4,5},{5,4},{6,7},{7,6},{8,9},{9,8},{10,11... | collective-permute-start | bytes 491528 | tf_op jit(solution)/shard_map/ppermute | solution.py:54
  113.6 5.1 %collective-permute-start.39 = (bf16[16,1024]{1,0:T(8,128)(2,1)S(1)}, bf16[16,1024]{1,0:T(8,128)(2,1)S(1)}, u32[]{:S(2)}, u32[]{:S(2)}) collective-permute-start(bf16[16,1024]{1,0:T(8,128)(2,1)S(1)} %get-tuple-element.45), channel_id=1, source_target_pairs={{0,2},{1,3},{2,0},{3,1},{4,6},{5,7},{6,4},{7,5},{8,10},{9,11},{10,... | collective-permute-start | bytes 98312 | tf_op jit(solution)/shard_map/ppermute | solution.py:59
  115.1 5.8 %collective-permute-start.38 = (bf16[16,1024]{1,0:T(8,128)(2,1)S(1)}, bf16[16,1024]{1,0:T(8,128)(2,1)S(1)}, u32[]{:S(2)}, u32[]{:S(2)}) collective-permute-start(bf16[16,1024]{1,0:T(8,128)(2,1)S(1)} %get-tuple-element.46), channel_id=1, source_target_pairs={{0,4},{1,5},{2,6},{3,7},{4,0},{5,1},{6,2},{7,3},{8,12},{9,13},{10,... | collective-permute-start | bytes 98312 | tf_op jit(solution)/shard_map/ppermute | solution.py:59
  116.0 5.7 %collective-permute-start.37 = (bf16[16,1024]{1,0:T(8,128)(2,1)S(1)}, bf16[16,1024]{1,0:T(8,128)(2,1)S(1)}, u32[]{:S(2)}, u32[]{:S(2)}) collective-permute-start(bf16[16,1024]{1,0:T(8,128)(2,1)S(1)} %get-tuple-element.44), channel_id=1, source_target_pairs={{0,6},{1,7},{2,4},{3,5},{4,2},{5,3},{6,0},{7,1},{8,14},{9,15},{10,... | collective-permute-start | bytes 98312 | tf_op jit(solution)/shard_map/ppermute | solution.py:59

commit v4 on v3

v4 whole, which is shorter than its diff:
```python
import functools
import math

import jax
import jax.numpy as jnp
from jax import lax
from jax.experimental import pallas as pl
from jax.experimental.pallas import tpu as pltpu
from jax.sharding import PartitionSpec as P

STEPS = 2
EMBED_BOUND = 6.0
FREQ_BOUND = 0.5
CODE_MAX = 32766.0
LANES = 128
VMEM_BYTES = 16 * 1024 * 1024
EARLY_VMEM_BYTES = 56 * 1024 * 1024
WEIGHT_BOUND = 6.0
COS_TURNS = (
    0.9999999890590243,
    -19.739204499454,
    64.93911745989858,
    -85.45013953092679,
    60.16763095123224,
    -25.967599249288032,
    6.528658162158786,
)
PER_TURN = EMBED_BOUND * FREQ_BOUND / (CODE_MAX * CODE_MAX * 2.0 * math.pi)


def encode(x, bound):
    return jnp.round(x * (CODE_MAX / bound)).astype(jnp.int16)


def split(code):
    wide = code.astype(jnp.float32)
    high = jnp.round(wide * (1.0 / 256.0)) * 256.0
    return high.astype(jnp.bfloat16), (wide - high).astype(jnp.bfloat16)


def scaled_cos(turns, scale):
    turns = turns - jnp.round(turns)
    square = turns * turns
    value = COS_TURNS[-1] * scale
    for coefficient in COS_TURNS[-2::-1]:
        value = value * square + coefficient * scale
    return value.astype(jnp.bfloat16)


def mix(a, b):
    return jnp.dot(a, b, preferred_element_type=jnp.float32)


def core_swap(x):
    n = lax.axis_size("feat")
    return lax.ppermute(x, "feat", [(i, i ^ 1) for i in range(n)])


def line_swap(x, k):
    n = lax.axis_size("feat")
    return lax.ppermute(x, "feat", [(i, i ^ (2 * k)) for i in range(n)])


def line_move(x, pairs):
    return lax.ppermute(x, "feat", [(2 * a + c, 2 * b + c) for a, b in pairs for c in range(2)])


def clip_swap(x, k):
    n = lax.axis_size("clip")
    return lax.ppermute(x, "clip", [(i, i ^ k) for i in range(n)])


def farthest_first(n):
    return range(n - 1, 0, -1)


def halves(x):
    high = jnp.round(x * (1.0 / 256.0)) * 256.0
    return high.astype(jnp.bfloat16), (x - high).astype(jnp.bfloat16)


def copied(sources, places, sem):
    copies = [pltpu.make_async_copy(a, b, sem.at[i]) for i, (a, b) in enumerate(zip(sources, places))]
    for copy in copies:
        copy.start()
    return copies


def tiles_of(ref):
    tile = 256 if ref.shape[1] % 256 == 0 else ref.shape[1]
    return [slice(start, start + tile) for start in range(0, ref.shape[1], tile)]


def early_kernel(
    at_ref, *refs, n_embeds, n_freqs, columns
):
    embeds, freqs = refs[:n_embeds], refs[n_embeds : n_embeds + n_freqs]
    (
        sum_ref, high_ref, low_ref, freq_code, embed_code, f_high, f_low, e_high, e_low, sem_f, sem_e,
    ) = refs[n_embeds + n_freqs :]
    depth = e_high.shape[0]
    used = n_embeds * columns
    line, clip, core = at_ref[0], at_ref[1], at_ref[2]

    def on_ring(place):
        return jnp.where(place == 0, 0, jnp.where(place == 1, 3, place - 1))

    rows = []
    for m in range(n_freqs // 2):
        step = (on_ring(line) - on_ring(clip ^ m)) & 3
        base = step * 2 * columns + jnp.where(step == 3, depth - used, 0)
        rows += [pl.ds(pl.multiple_of(base + h * columns, 16), columns) for h in (core, 1 - core)]
    pieces = [ref.at[:columns, :] for ref in freqs]
    of_freqs = copied(pieces, [freq_code.at[r, :] for r in rows], sem_f)
    of_embeds = copied(embeds, [embed_code.at[i * columns : (i + 1) * columns, :] for i in range(n_embeds)], sem_e)
    if depth > used:
        freq_code[used:depth, :] = jnp.zeros((depth - used, freq_code.shape[1]), jnp.int16)
        embed_code[used:depth, :] = jnp.zeros((depth - used, embed_code.shape[1]), jnp.int16)
    for copy in of_embeds:
        copy.wait()
    e_high[...], e_low[...] = halves(embed_code[...].astype(jnp.float32))
    for copy in of_freqs:
        copy.wait()
    for start in range(0, depth, LANES):
        f_high[:, start : start + LANES], f_low[:, start : start + LANES] = halves(
            freq_code[start : start + LANES, :].T.astype(jnp.float32)
        )
    high_ref[...], low_ref[...] = halves(freq_code[depth:, :].T.astype(jnp.float32))
    for at in tiles_of(sum_ref):
        sum_ref[:, at] = mix(f_high[...], e_high[:, at]) + (
            mix(f_high[...], e_low[:, at]) + mix(f_low[...], e_high[:, at])
        )


def late_kernel(
    sum_ref, own_ref, other_ref, high_ref, low_ref, phase_ref,
    phi_ref, sums, embed_code, e_high, e_low, sem_s, sem_e, *, columns, scale,
):
    of_embeds = copied((own_ref, other_ref), (embed_code.at[:columns], embed_code.at[columns:]), sem_e)
    of_sums = copied((sum_ref,), (sums,), sem_s)
    for copy in of_embeds:
        copy.wait()
    e_high[...], e_low[...] = halves(embed_code[...].astype(jnp.float32))
    for copy in of_sums:
        copy.wait()
    for at in tiles_of(sums):
        total = sums[:, at] + (
            mix(high_ref[...], e_high[:, at])
            + (mix(high_ref[...], e_low[:, at]) + mix(low_ref[...], e_high[:, at]))
        )
        phi_ref[:, at] = scaled_cos(total * PER_TURN + phase_ref[...], scale)


def phi_by_kernels(embed_code, freq_code, column, scale, line, core, clip, prepare):
    slabs = 4
    columns, clips = embed_code.shape
    features = freq_code[0].shape[1]
    tie = lax.optimization_barrier
    x_low, y_high = clip_swap(freq_code[0], 1), clip_swap(freq_code[1], 2)
    x_high, y_low = clip_swap(freq_code[1], 1), clip_swap(freq_code[0], 2)
    freqs = [*freq_code, x_low, x_high, y_low, y_high, clip_swap(x_low, 2), clip_swap(y_high, 1)]
    ring = [(0, 2), (2, 3), (3, 1), (1, 0)]
    own = [embed_code]
    for _ in range(slabs - 1):
        own.append(line_move(own[-1], ring))
    other = [core_swap(own[0]), core_swap(own[1])]
    *freqs, turn = tie((*freqs, own[2]))
    other.append(core_swap(turn))
    rest = prepare(freqs)
    early = [x for pair in zip(own[:3], other) for x in pair]
    used = len(early) * columns
    depth = -(-used // LANES) * LANES
    vmem = pl.BlockSpec(memory_space=pltpu.VMEM)
    smem = pl.BlockSpec(memory_space=pltpu.SMEM)
    anywhere = pl.BlockSpec(memory_space=pl.ANY)
    summed, high, low = pl.pallas_call(
        functools.partial(early_kernel, n_embeds=len(early), n_freqs=len(freqs), columns=columns),
        out_shape=(
            jax.ShapeDtypeStruct((features, clips), jnp.float32),
            jax.ShapeDtypeStruct((features, 2 * columns), jnp.bfloat16),
            jax.ShapeDtypeStruct((features, 2 * columns), jnp.bfloat16),
        ),
        in_specs=[smem] + [anywhere] * (len(early) + len(freqs)),
        out_specs=(vmem, vmem, vmem),
        scratch_shapes=[
            pltpu.VMEM((depth + 2 * columns, features), jnp.int16),
            pltpu.VMEM((depth, clips), jnp.int16),
            pltpu.VMEM((features, depth), jnp.bfloat16),
            pltpu.VMEM((features, depth), jnp.bfloat16),
            pltpu.VMEM((depth, clips), jnp.bfloat16),
            pltpu.VMEM((depth, clips), jnp.bfloat16),
            pltpu.SemaphoreType.DMA((len(freqs),)),
            pltpu.SemaphoreType.DMA((len(early),)),
        ],
        compiler_params=pltpu.CompilerParams(vmem_limit_bytes=EARLY_VMEM_BYTES),
        cost_estimate=pl.CostEstimate(
            flops=6 * features * depth * clips, bytes_accessed=8 * features * clips, transcendentals=0
        ),
        name="early_angles",
    )(jnp.stack([line, clip, core]).astype(jnp.int32), *early, *freqs)
    last, high = tie((own[3], high))
    phi = pl.pallas_call(
        functools.partial(late_kernel, columns=columns, scale=scale),
        out_shape=jax.ShapeDtypeStruct((features, clips), jnp.bfloat16),
        in_specs=[anywhere] * 3 + [vmem] * 3,
        out_specs=vmem,
        scratch_shapes=[
            pltpu.VMEM((features, clips), jnp.float32),
            pltpu.VMEM((2 * columns, clips), jnp.int16),
            pltpu.VMEM((2 * columns, clips), jnp.bfloat16),
            pltpu.VMEM((2 * columns, clips), jnp.bfloat16),
            pltpu.SemaphoreType.DMA((1,)),
            pltpu.SemaphoreType.DMA((2,)),
        ],
        compiler_params=pltpu.CompilerParams(vmem_limit_bytes=VMEM_BYTES),
        cost_estimate=pl.CostEstimate(
            flops=6 * features * 2 * columns * clips, bytes_accessed=6 * features * clips, transcendentals=0
        ),
        name="late_angles",
    )(summed, last, core_swap(last), high, low, column)
    return phi, rest


def phi_by_ring(embed_code, freq_code, column, scale, line, core, clip, prepare):
    places, n_clip = lax.axis_size("feat") // 2, lax.axis_size("clip")
    columns, clips = embed_code.shape
    slab, features = 2 * places * columns // n_clip, freq_code[0].shape[1]
    freqs = [y for k in range(n_clip) for y in (x if k == 0 else clip_swap(x, k) for x in freq_code)]
    freq_all = jnp.zeros((n_clip * slab, features), jnp.int16)
    for i, piece in enumerate(freqs):
        at = (clip ^ (i // 2)) * slab + (i % 2) * (slab // 2)
        freq_all = lax.dynamic_update_slice_in_dim(freq_all, piece[: slab // 2], at, 0)
    embed_all = jnp.zeros((2 * places * columns, clips), jnp.int16)
    piece = embed_code
    ring = [(i, (i + 1) % places) for i in range(places)]
    for step in range(places):
        if step:
            piece = line_move(piece, ring)
        base = 2 * ((line - step) % places)
        embed_all = lax.dynamic_update_slice_in_dim(embed_all, piece, (base + core) * columns, 0)
        embed_all = lax.dynamic_update_slice_in_dim(
            embed_all, core_swap(piece), (base + 1 - core) * columns, 0
        )

    def dot0(a, b):
        return lax.dot_general(a, b, (((0,), (0,)), ((), ())), preferred_element_type=jnp.float32)

    embed_high, embed_low = split(embed_all)
    freq_high, freq_low = split(freq_all)
    total = dot0(freq_high, embed_high) + (dot0(freq_high, embed_low) + dot0(freq_low, embed_high))
    return scaled_cos(total * PER_TURN + column, scale), prepare(freqs)


def per_device(embeds, frequencies, phases, weights, labels):
    n_feat, n_clip = lax.axis_size("feat"), lax.axis_size("clip")
    feat, clip = lax.axis_index("feat"), lax.axis_index("clip")
    places, line, core = n_feat // 2, feat // 2, feat % 2
    columns = embeds.shape[1]
    slab, features = frequencies.shape
    outputs = labels.shape[1]
    block = outputs // n_feat
    per_clip = places // n_clip
    scale = math.sqrt(2.0 / (features * n_feat))

    embed_code = encode(embeds.T, EMBED_BOUND)
    weight_rows = weights.T.reshape(per_clip, 2, block, features)
    freq_code = [
        jnp.concatenate(
            [
                encode(frequencies[h * (slab // 2) : (h + 1) * (slab // 2)], FREQ_BOUND),
                encode(weight_rows[:, h].reshape(-1, features), WEIGHT_BOUND),
            ]
        )
        for h in range(2)
    ]
    column = (phases * (0.5 / math.pi))[:, None]

    def prepare(codes):
        stacked = jnp.concatenate([code[slab // 2 :] for code in codes]).reshape(n_clip, 2, per_clip, block, features)

        def ordered(side):
            rows = lax.dynamic_index_in_dim(stacked, side, 1, keepdims=False).reshape(-1, block, features)
            found = []
            for k in range(places):
                place = line ^ k
                at = ((place // per_clip) ^ clip) * per_clip + place % per_clip
                found.append(lax.dynamic_index_in_dim(rows, at, 0, keepdims=False))
            return jnp.concatenate(found)

        def decode(code):
            return code.astype(jnp.float32) * (WEIGHT_BOUND / CODE_MAX)

        own, sent = lax.optimization_barrier((ordered(core), ordered(1 - core)))
        casts = lax.optimization_barrier((decode(own).astype(jnp.bfloat16), decode(sent).astype(jnp.bfloat16)))
        targets = lax.dynamic_slice_in_dim(labels.T, feat * block, block, 0).astype(jnp.float32)
        return decode(own), decode(core_swap(sent)), casts, targets

    def share_of(parts):
        parts = parts.reshape(places, block, -1)
        half = parts.astype(jnp.bfloat16)
        total = parts[0]
        found = [line_swap(half[k], k) for k in farthest_first(places)]
        return total, found

    def add_up(total, found):
        for x in found:
            total = total + x.astype(jnp.float32)
        return total

    def gradient_of(residual, phi):
        return lax.dot_general(residual, phi, (((1,), (1,)), ((), ())), preferred_element_type=jnp.float32)

    by_kernels = places == 4 and n_clip == 4 and columns % 16 == 0 and slab == 2 * columns
    phi_of = phi_by_kernels if by_kernels else phi_by_ring
    phi, (beta_own, beta_other, casts, targets) = phi_of(
        embed_code, freq_code, column, scale, line, core, clip, prepare
    )
    there = core_swap(mix(casts[1], phi).astype(jnp.bfloat16))
    parts = lax.optimization_barrier(mix(casts[0], phi)) + there.astype(jnp.float32)
    phi_other = core_swap(lax.optimization_barrier((phi, there))[0])
    moved_own = moved_other = 0.0
    for step in range(STEPS):
        share = (jax.nn.sigmoid(add_up(*share_of(parts))) - targets).astype(jnp.bfloat16)
        found = {k: line_swap(share, k) for k in farthest_first(places)}
        residual = jnp.concatenate([share] + [found[k] for k in range(1, places)])
        grad = jnp.concatenate([gradient_of(residual, phi), gradient_of(residual, phi_other)], axis=1)
        sent = grad.astype(jnp.bfloat16)
        for k in farthest_first(n_clip):
            grad = grad + clip_swap(sent, k).astype(jnp.float32)
        moved_own = moved_own + 0.25 * grad[:, :features]
        moved_other = moved_other + 0.25 * grad[:, features:]
        parts = mix((beta_own - moved_own).astype(jnp.bfloat16), phi) + mix(
            (beta_other - moved_other).astype(jnp.bfloat16), phi_other
        )
    total, found = share_of(parts)
    ours = moved_own.reshape(places, block, features)
    theirs = core_swap(moved_other).reshape(places, block, features)
    rows = []
    for b in range(per_clip):
        k = line ^ (clip * per_clip + b)
        mine = lax.dynamic_index_in_dim(ours, k, 0, keepdims=False)
        their = lax.dynamic_index_in_dim(theirs, k, 0, keepdims=False)
        rows += [jnp.where(core == 0, mine, their), jnp.where(core == 0, their, mine)]
    trained, total = lax.optimization_barrier((weights - jnp.concatenate(rows).T, total))
    return (trained, add_up(total, found).T)


def solution(mesh):
    placed = (P("clip", "feat"), P("clip", "feat"), P("feat"), P("feat", "clip"), P("clip", None))
    return jax.shard_map(
        per_device,
        mesh=mesh,
        in_specs=placed,
        out_specs=(P("feat", "clip"), P("clip", "feat")),
        check_vma=False,
    )
```

time: 123 us -> 114 us (0.927)
  waiting for transfers between devices: 44.8 us -> 31.4 us
  local copies, waits for them, and re-layouts: 4.01 us -> 8.63 us
  matrix products: 6.45 us -> 4.09 us
  other arithmetic: 6.84 us -> 8.82 us
    ppermute x17 -> x15, waiting for transfers between devices: 24.4 us -> 12.2 us  [line_swap(): return lax.ppermute(x, 'feat', [(i, i ^ 2 * k) for i in range(n)])]
    ppermute x2 -> x3, waiting for transfers between devices: 7.92 us -> 1.12 us  [line_move(): lax.ppermute(x, 'feat', [(2 * a + c, 2 * b + c) for a, b in pairs for c i...]
    ppermute x2 -> x3, starting transfers between devices: 1.96 us -> 8.14 us  [line_move(): lax.ppermute(x, 'feat', [(2 * a + c, 2 * b + c) for a, b in pairs for c i...]
    ppermute x12, waiting for transfers between devices: 10.4 us -> 16.5 us  [clip_swap(): return lax.ppermute(x, 'clip', [(i, i ^ k) for i in range(n)])]
    unnamed x37 -> x64, local copies, waits for them, and re-layouts: 2.07 us -> 7.37 us
    ppermute x17 -> x15, starting transfers between devices: 26.8 us -> 22.3 us  [line_swap(): return lax.ppermute(x, 'feat', [(i, i ^ 2 * k) for i in range(n)])]
    dot_general x6, matrix products: 4.42 us -> 2.06 us  [mix(): return jnp.dot(a, b, preferred_element_type=jnp.float32)]
    convert_element_type x0 -> x3, other arithmetic: none -> 1.71 us  [the longest x1 0.92 us: prepare(): decode(sent).astype(jnp.bfloat16)]
  transfers between devices with their start and end apart: 40 -> 38, of which waited for: 19 -> 19; matrix products, arithmetic and copies ran while one was open for 7% -> 8% of each run, Pallas kernels for 8% -> 9%
where the time goes in v4:
time: 114 us
  starting transfers between devices  45.4 us (40%)
  waiting for transfers between devices  31.4 us (28%)
  Pallas kernels  14.4 us (13%)
  other arithmetic  8.82 us (8%)
  local copies, waits for them, and re-layouts  8.63 us (8%)
  matrix products  4.09 us (4%)
  between operations  1.16 us (1%)
    ppermute x15, starting transfers between devices, line_swap(): return lax.ppermute(x, 'feat', [(i, i ^ 2 * k) for i in range(n)])  22.3 us
    ppermute x12, waiting for transfers between devices, clip_swap(): return lax.ppermute(x, 'clip', [(i, i ^ k) for i in range(n)])  16.5 us
    ppermute x12, starting transfers between devices, clip_swap(): return lax.ppermute(x, 'clip', [(i, i ^ k) for i in range(n)])  14.2 us
    ppermute x15, waiting for transfers between devices, line_swap(): return lax.ppermute(x, 'feat', [(i, i ^ 2 * k) for i in range(n)])  12.2 us
    pallas_call x1, Pallas kernels, phi_by_kernels(): pl.pallas_call(functools.partial(early_kernel, n_embeds=len(early), n_fre...  10.2 us
    ppermute x3, starting transfers between devices, line_move(): lax.ppermute(x, 'feat', [(2 * a + c, 2 * b + c) for a, b in pairs for c i...  8.14 us
    unnamed x64, local copies, waits for them, and re-layouts  7.37 us
    pallas_call x1, Pallas kernels, phi_by_kernels(): pl.pallas_call(functools.partial(late_kernel, columns=columns, scale=scal...  4.15 us
  transfers between devices with their start and end apart: 38, of which 19 were waited for; matrix products, arithmetic and copies ran while one was open for 8% of the time, Pallas kernels for 9%

profile of v4, /device:TPU:0, one launch (start us, length us, event | category | flops | bytes accessed | tf_op | source)
XLA Modules:
  0.0 113.9 jit_solution(7408430143155749587)
XLA Ops:
  0.7 1.3 %fusion.refs_0_ = s16[144,1024]{1,0:T(8,128)(2,1)S(1)} fusion(f32[1024,144]{0,1:T(8,128)} %param.5), kind=kLoop, calls=%fused_computation.10 | loop fusion | flops 442368 | bytes 884736 | tf_op jit(solution)/shard_map/convert_element_type | solution.py:32
  1.9 4.1 %collective-permute-start.6 = (s16[144,1024]{1,0:T(8,128)(2,1)S(1)}, s16[144,1024]{1,0:T(8,128)(2,1)S(1)}, u32[]{:S(2)}, u32[]{:S(2)}) collective-permute-start(s16[144,1024]{1,0:T(8,128)(2,1)S(1)} %fusion.refs_0_), channel_id=1, source_target_pairs={{0,4},{1,5},{4,6},{5,7},{6,2},{7,3},{2,0},{3,1},{8,12},{9,13},{12,... | collective-permute-start | bytes 884744 | tf_op jit(solution)/shard_map/ppermute | solution.py:65
  6.2 1.6 %collective-permute-start = (s16[160,640]{1,0:T(8,128)(2,1)S(1)}, s16[160,640]{1,0:T(8,128)(2,1)S(1)}, u32[]{:S(2)}, u32[]{:S(2)}) collective-permute-start(s16[160,640]{1,0:T(8,128)(2,1)S(1)} %pad_add_fusion.refs_6_), channel_id=1, source_target_pairs={{0,8},{8,0},{16,24},{24,16},{1,9},{9,1},{17,25},{25,17},{2,10},{10... | collective-permute-start | bytes 614408 | tf_op jit(solution)/shard_map/ppermute | solution.py:70
  7.8 1.6 %collective-permute-start.3 = (s16[160,640]{1,0:T(8,128)(2,1)S(1)}, s16[160,640]{1,0:T(8,128)(2,1)S(1)}, u32[]{:S(2)}, u32[]{:S(2)}) collective-permute-start(s16[160,640]{1,0:T(8,128)(2,1)S(1)} %pad_add_fusion.1.refs_7_), channel_id=1, source_target_pairs={{0,16},{8,24},{16,0},{24,8},{1,17},{9,25},{17,1},{25,9},{2,18},{10... | collective-permute-start | bytes 614408 | tf_op jit(solution)/shard_map/ppermute | solution.py:70
  9.4 0.5 collective-permute-start.1
  10.5 3.9 %collective-permute-done.refs_8_ = s16[160,640]{1,0:T(8,128)(2,1)S(1)} collective-permute-done((s16[160,640]{1,0:T(8,128)(2,1)S(1)}, s16[160,640]{1,0:T(8,128)(2,1)S(1)}, u32[]{:S(2)}, u32[]{:S(2)}) %collective-permute-start) | collective-permute-done | bytes 204832 | tf_op jit(solution)/shard_map/ppermute | solution.py:70
  14.3 1.5 %collective-permute-start.4 = (s16[160,640]{1,0:T(8,128)(2,1)S(1)}, s16[160,640]{1,0:T(8,128)(2,1)S(1)}, u32[]{:S(2)}, u32[]{:S(2)}) collective-permute-start(s16[160,640]{1,0:T(8,128)(2,1)S(1)} %collective-permute-done.refs_8_), channel_id=1, source_target_pairs={{0,16},{8,24},{16,0},{24,8},{1,17},{9,25},{17,1},{25,9},{2,18},{10... | collective-permute-start | bytes 614408 | tf_op jit(solution)/shard_map/ppermute | solution.py:70
  15.9 1.4 %collective-permute-start.5 = (s16[160,640]{1,0:T(8,128)(2,1)S(1)}, s16[160,640]{1,0:T(8,128)(2,1)S(1)}, u32[]{:S(2)}, u32[]{:S(2)}) collective-permute-start(s16[160,640]{1,0:T(8,128)(2,1)S(1)} %collective-permute-done.3.refs_11_), channel_id=1, source_target_pairs={{0,8},{8,0},{16,24},{24,16},{1,9},{9,1},{17,25},{25,17},{2,10},{10... | collective-permute-start | bytes 614408 | tf_op jit(solution)/shard_map/ppermute | solution.py:70
  17.3 1.6 %collective-permute-start.7 = (s16[144,1024]{1,0:T(8,128)(2,1)S(1)}, s16[144,1024]{1,0:T(8,128)(2,1)S(1)}, u32[]{:S(2)}, u32[]{:S(2)}) collective-permute-start(s16[144,1024]{1,0:T(8,128)(2,1)S(1)} %collective-permute-done.6.refs_2_), channel_id=1, source_target_pairs={{0,4},{1,5},{4,6},{5,7},{6,2},{7,3},{2,0},{3,1},{8,12},{9,13},{12,... | collective-permute-start | bytes 884744 | tf_op jit(solution)/shard_map/ppermute | solution.py:65
  19.1 0.6 pad_add_fusion.4.at_ref
  19.6 0.7 collective-permute-done.2.refs_10_
  20.3 2.6 %collective-permute-done.4.refs_12_ = s16[160,640]{1,0:T(8,128)(2,1)S(1)} collective-permute-done((s16[160,640]{1,0:T(8,128)(2,1)S(1)}, s16[160,640]{1,0:T(8,128)(2,1)S(1)}, u32[]{:S(2)}, u32[]{:S(2)}) %collective-permute-start.4) | collective-permute-done | bytes 204832 | tf_op jit(solution)/shard_map/ppermute | solution.py:70
  22.9 1.1 collective-permute-done.7.refs_4_
  24.2 0.7 pad_add_fusion.2
  24.9 2.5 %collective-permute-start.11 = (s16[144,1024]{1,0:T(8,128)(2,1)S(1)}, s16[144,1024]{1,0:T(8,128)(2,1)S(1)}, u32[]{:S(2)}, u32[]{:S(2)}) collective-permute-start(s16[144,1024]{1,0:T(8,128)(2,1)S(1)} %collective-permute-done.7.refs_4_), channel_id=1, source_target_pairs={{0,4},{1,5},{4,6},{5,7},{6,2},{7,3},{2,0},{3,1},{8,12},{9,13},{12,... | collective-permute-start | bytes 884744 | tf_op jit(solution)/shard_map/ppermute | solution.py:65
  27.5 0.6 copy-done.25
  28.2 0.7 copy-done.27
  28.9 10.2 %early_angles.1 = (f32[640,1024]{1,0:T(8,128)}, bf16[640,288]{1,0:T(8,128)(2,1)}, bf16[640,288]{1,0:T(8,128)(2,1)}) custom-call(s32[3]{0:T(128)} %pad_add_fusion.4.at_ref, s16[144,1024]{1,0:T(8,128)(2,1)} %copy-done.13, s16[144,1024]{1,0:T(8,128)(2,1)} %copy-done.25, s16[144,1024]{1,0:T(8,128)(2,1)} %copy-done.23, s16[144,1024]{1,0:T(8,128)(2,1)} %copy-done.26, ...), custom_call_target="tpu_custom_call" | custom-call | flops 3523215360 | bytes 5242880 | tf_op jit(solution)/shard_map/early_angles/pallas_call | solution.py:176
  39.5 0.9 multiply_convert_fusion
  40.8 1.7 %copy-done.1 = f32[640,1024]{1,0:T(8,128)S(1)} copy-done((f32[640,1024]{1,0:T(8,128)S(1)}, f32[640,1024]{1,0:T(8,128)}, u32[]{:S(2)}) %copy-start.1) | copy-done | bytes 2621464
  42.6 1.0 copy-done.2
  43.6 1.0 copy-done.3
  44.6 4.1 %late_angles.1 = bf16[640,1024]{1,0:T(8,128)(2,1)S(1)} custom-call(f32[640,1024]{1,0:T(8,128)S(1)} %copy-done.1, s16[144,1024]{1,0:T(8,128)(2,1)S(1)} %collective-permute-done.11.own_ref, s16[144,1024]{1,0:T(8,128)(2,1)S(1)} %collective-permute-done.12.other_ref, bf16[640,288]{1,0:T(8,128)(2,1)S(1)} %copy-done.2, bf16[640,288]{1,0:T(8,128)(2,1)S(1)} %copy-done.3, ...), custom_call_target="tpu_custom_call" | custom-call | flops 1132462080 | bytes 3932160 | tf_op jit(solution)/shard_map/late_angles/pallas_call | solution.py:202
  49.4 1.1 collective-permute-done.13
  51.1 0.8 fusion.51
  52.2 0.8 collective-permute-start.15
  52.9 3.4 %collective-permute-start.16 = (bf16[16,1024]{1,0:T(8,128)(2,1)S(1)}, bf16[16,1024]{1,0:T(8,128)(2,1)S(1)}, u32[]{:S(2)}, u32[]{:S(2)}) collective-permute-start(bf16[16,1024]{1,0:T(8,128)(2,1)S(1)} %get-tuple-element.67), channel_id=1, source_target_pairs={{0,2},{1,3},{2,0},{3,1},{4,6},{5,7},{6,4},{7,5},{8,10},{9,11},{10,... | collective-permute-start | bytes 98312 | tf_op jit(solution)/shard_map/ppermute | solution.py:61
  56.3 1.0 constant_dynamic-slice_fusion
  57.4 1.2 %copy.10 = s32[1024,16]{0,1:T(8,128)S(1)} copy(s32[1024,16]{1,0:T(8,128)} %constant_dynamic-slice_fusion) | data formatting | bytes 131072
  58.6 0.9 fusion.29
  59.5 1.7 %collective-permute-start.17 = (bf16[16,1024]{1,0:T(8,128)(2,1)S(1)}, bf16[16,1024]{1,0:T(8,128)(2,1)S(1)}, u32[]{:S(2)}, u32[]{:S(2)}) collective-permute-start(bf16[16,1024]{1,0:T(8,128)(2,1)S(1)} %fusion.29), channel_id=1, source_target_pairs={{0,2},{1,3},{2,0},{3,1},{4,6},{5,7},{6,4},{7,5},{8,10},{9,11},{10,... | collective-permute-start | bytes 98312 | tf_op jit(solution)/shard_map/ppermute | solution.py:61
  61.2 0.9 collective-permute-start.18
  62.1 1.9 %collective-permute-start.19 = (bf16[16,1024]{1,0:T(8,128)(2,1)S(1)}, bf16[16,1024]{1,0:T(8,128)(2,1)S(1)}, u32[]{:S(2)}, u32[]{:S(2)}) collective-permute-start(bf16[16,1024]{1,0:T(8,128)(2,1)S(1)} %fusion.29), channel_id=1, source_target_pairs={{0,6},{1,7},{2,4},{3,5},{4,2},{5,3},{6,0},{7,1},{8,14},{9,15},{10,... | collective-permute-start | bytes 98312 | tf_op jit(solution)/shard_map/ppermute | solution.py:61
  64.0 2.2 %collective-permute-done.18 = bf16[16,1024]{1,0:T(8,128)(2,1)S(1)} collective-permute-done((bf16[16,1024]{1,0:T(8,128)(2,1)S(1)}, bf16[16,1024]{1,0:T(8,128)(2,1)S(1)}, u32[]{:S(2)}, u32[]{:S(2)}) %collective-permute-start.18) | collective-permute-done | bytes 32800 | tf_op jit(solution)/shard_map/ppermute | solution.py:61
  66.2 1.6 %collective-permute-done.19 = bf16[16,1024]{1,0:T(8,128)(2,1)S(1)} collective-permute-done((bf16[16,1024]{1,0:T(8,128)(2,1)S(1)}, bf16[16,1024]{1,0:T(8,128)(2,1)S(1)}, u32[]{:S(2)}, u32[]{:S(2)}) %collective-permute-start.19) | collective-permute-done | bytes 32800 | tf_op jit(solution)/shard_map/ppermute | solution.py:61
  68.3 0.5 fusion.37
  68.9 1.6 %collective-permute-start.21 = (bf16[64,1280]{1,0:T(8,128)(2,1)S(1)}, bf16[64,1280]{1,0:T(8,128)(2,1)S(1)}, u32[]{:S(2)}, u32[]{:S(2)}) collective-permute-start(bf16[64,1280]{1,0:T(8,128)(2,1)S(1)} %fusion.2), channel_id=1, source_target_pairs={{0,24},{8,16},{16,8},{24,0},{1,25},{9,17},{17,9},{25,1},{2,26},{10... | collective-permute-start | bytes 491528 | tf_op jit(solution)/shard_map/ppermute | solution.py:70
  71.0 1.4 %collective-permute-start.23 = (bf16[64,1280]{1,0:T(8,128)(2,1)S(1)}, bf16[64,1280]{1,0:T(8,128)(2,1)S(1)}, u32[]{:S(2)}, u32[]{:S(2)}) collective-permute-start(bf16[64,1280]{1,0:T(8,128)(2,1)S(1)} %fusion.2), channel_id=1, source_target_pairs={{0,8},{8,0},{16,24},{24,16},{1,9},{9,1},{17,25},{25,17},{2,10},{10... | collective-permute-start | bytes 491528 | tf_op jit(solution)/shard_map/ppermute | solution.py:70
  72.5 2.8 %collective-permute-done.21 = bf16[64,1280]{1,0:T(8,128)(2,1)S(1)} collective-permute-done((bf16[64,1280]{1,0:T(8,128)(2,1)S(1)}, bf16[64,1280]{1,0:T(8,128)(2,1)S(1)}, u32[]{:S(2)}, u32[]{:S(2)}) %collective-permute-start.21) | collective-permute-done | bytes 163872 | tf_op jit(solution)/shard_map/ppermute | solution.py:70
  75.3 1.7 %collective-permute-done.22 = bf16[64,1280]{1,0:T(8,128)(2,1)S(1)} collective-permute-done((bf16[64,1280]{1,0:T(8,128)(2,1)S(1)}, bf16[64,1280]{1,0:T(8,128)(2,1)S(1)}, u32[]{:S(2)}, u32[]{:S(2)}) %collective-permute-start.22) | collective-permute-done | bytes 163872 | tf_op jit(solution)/shard_map/ppermute | solution.py:70
  77.0 0.6 copy-done.9
  78.4 2.4 %collective-permute-start.25 = (bf16[16,1024]{1,0:T(8,128)(2,1)S(1)}, bf16[16,1024]{1,0:T(8,128)(2,1)S(1)}, u32[]{:S(2)}, u32[]{:S(2)}) collective-permute-start(bf16[16,1024]{1,0:T(8,128)(2,1)S(1)} %get-tuple-element.63), channel_id=1, source_target_pairs={{0,6},{1,7},{2,4},{3,5},{4,2},{5,3},{6,0},{7,1},{8,14},{9,15},{10,... | collective-permute-start | bytes 98312 | tf_op jit(solution)/shard_map/ppermute | solution.py:61
  80.7 2.1 %collective-permute-start.27 = (bf16[16,1024]{1,0:T(8,128)(2,1)S(1)}, bf16[16,1024]{1,0:T(8,128)(2,1)S(1)}, u32[]{:S(2)}, u32[]{:S(2)}) collective-permute-start(bf16[16,1024]{1,0:T(8,128)(2,1)S(1)} %get-tuple-element.64), channel_id=1, source_target_pairs={{0,2},{1,3},{2,0},{3,1},{4,6},{5,7},{6,4},{7,5},{8,10},{9,11},{10,... | collective-permute-start | bytes 98312 | tf_op jit(solution)/shard_map/ppermute | solution.py:61
  82.8 1.3 %collective-permute-done.25 = bf16[16,1024]{1,0:T(8,128)(2,1)S(1)} collective-permute-done((bf16[16,1024]{1,0:T(8,128)(2,1)S(1)}, bf16[16,1024]{1,0:T(8,128)(2,1)S(1)}, u32[]{:S(2)}, u32[]{:S(2)}) %collective-permute-start.25) | collective-permute-done | bytes 32800 | tf_op jit(solution)/shard_map/ppermute | solution.py:61
  84.2 1.4 %collective-permute-done.26 = bf16[16,1024]{1,0:T(8,128)(2,1)S(1)} collective-permute-done((bf16[16,1024]{1,0:T(8,128)(2,1)S(1)}, bf16[16,1024]{1,0:T(8,128)(2,1)S(1)}, u32[]{:S(2)}, u32[]{:S(2)}) %collective-permute-start.26) | collective-permute-done | bytes 32800 | tf_op jit(solution)/shard_map/ppermute | solution.py:61
  85.6 1.3 %collective-permute-start.28 = (bf16[16,1024]{1,0:T(8,128)(2,1)S(1)}, bf16[16,1024]{1,0:T(8,128)(2,1)S(1)}, u32[]{:S(2)}, u32[]{:S(2)}) collective-permute-start(bf16[16,1024]{1,0:T(8,128)(2,1)S(1)} %fusion.30), channel_id=1, source_target_pairs={{0,2},{1,3},{2,0},{3,1},{4,6},{5,7},{6,4},{7,5},{8,10},{9,11},{10,... | collective-permute-start | bytes 98312 | tf_op jit(solution)/shard_map/ppermute | solution.py:61
  86.9 1.2 %collective-permute-start.29 = (bf16[16,1024]{1,0:T(8,128)(2,1)S(1)}, bf16[16,1024]{1,0:T(8,128)(2,1)S(1)}, u32[]{:S(2)}, u32[]{:S(2)}) collective-permute-start(bf16[16,1024]{1,0:T(8,128)(2,1)S(1)} %fusion.30), channel_id=1, source_target_pairs={{0,4},{1,5},{2,6},{3,7},{4,0},{5,1},{6,2},{7,3},{8,12},{9,13},{10,... | collective-permute-start | bytes 98312 | tf_op jit(solution)/shard_map/ppermute | solution.py:61
  88.0 2.0 %collective-permute-start.30 = (bf16[16,1024]{1,0:T(8,128)(2,1)S(1)}, bf16[16,1024]{1,0:T(8,128)(2,1)S(1)}, u32[]{:S(2)}, u32[]{:S(2)}) collective-permute-start(bf16[16,1024]{1,0:T(8,128)(2,1)S(1)} %fusion.30), channel_id=1, source_target_pairs={{0,6},{1,7},{2,4},{3,5},{4,2},{5,3},{6,0},{7,1},{8,14},{9,15},{10,... | collective-permute-start | bytes 98312 | tf_op jit(solution)/shard_map/ppermute | solution.py:61
  90.1 1.6 %collective-permute-done.29 = bf16[16,1024]{1,0:T(8,128)(2,1)S(1)} collective-permute-done((bf16[16,1024]{1,0:T(8,128)(2,1)S(1)}, bf16[16,1024]{1,0:T(8,128)(2,1)S(1)}, u32[]{:S(2)}, u32[]{:S(2)}) %collective-permute-start.29) | collective-permute-done | bytes 32800 | tf_op jit(solution)/shard_map/ppermute | solution.py:61
  91.7 2.1 %collective-permute-done.30 = bf16[16,1024]{1,0:T(8,128)(2,1)S(1)} collective-permute-done((bf16[16,1024]{1,0:T(8,128)(2,1)S(1)}, bf16[16,1024]{1,0:T(8,128)(2,1)S(1)}, u32[]{:S(2)}, u32[]{:S(2)}) %collective-permute-start.30) | collective-permute-done | bytes 32800 | tf_op jit(solution)/shard_map/ppermute | solution.py:61
  94.3 0.5 fusion.35
  94.9 0.7 fusion.1
  95.7 1.6 %collective-permute-start.31 = (bf16[64,1280]{1,0:T(8,128)(2,1)}, bf16[64,1280]{1,0:T(8,128)(2,1)}, u32[]{:S(2)}, u32[]{:S(2)}) collective-permute-start(bf16[64,1280]{1,0:T(8,128)(2,1)} %fusion.1), channel_id=1, source_target_pairs={{0,24},{8,16},{16,8},{24,0},{1,25},{9,17},{17,9},{25,1},{2,26},{10... | collective-permute-start | bytes 491528 | tf_op jit(solution)/shard_map/ppermute | solution.py:70
  97.3 0.6 collective-permute-start.32
  97.9 1.3 %collective-permute-start.33 = (bf16[64,1280]{1,0:T(8,128)(2,1)}, bf16[64,1280]{1,0:T(8,128)(2,1)}, u32[]{:S(2)}, u32[]{:S(2)}) collective-permute-start(bf16[64,1280]{1,0:T(8,128)(2,1)} %fusion.1), channel_id=1, source_target_pairs={{0,8},{8,0},{16,24},{24,16},{1,9},{9,1},{17,25},{25,17},{2,10},{10... | collective-permute-start | bytes 491528 | tf_op jit(solution)/shard_map/ppermute | solution.py:70
  99.2 3.1 %collective-permute-done.31 = bf16[64,1280]{1,0:T(8,128)(2,1)} collective-permute-done((bf16[64,1280]{1,0:T(8,128)(2,1)}, bf16[64,1280]{1,0:T(8,128)(2,1)}, u32[]{:S(2)}, u32[]{:S(2)}) %collective-permute-start.31) | collective-permute-done | bytes 163872 | tf_op jit(solution)/shard_map/ppermute | solution.py:70
  102.3 1.7 %collective-permute-done.32 = bf16[64,1280]{1,0:T(8,128)(2,1)} collective-permute-done((bf16[64,1280]{1,0:T(8,128)(2,1)}, bf16[64,1280]{1,0:T(8,128)(2,1)}, u32[]{:S(2)}, u32[]{:S(2)}) %collective-permute-start.32) | collective-permute-done | bytes 163872 | tf_op jit(solution)/shard_map/ppermute | solution.py:70
  104.0 1.3 %convert_add_fusion = f32[64,1280]{1,0:T(8,128)S(1)} fusion(bf16[64,1280]{1,0:T(8,128)(2,1)} %collective-permute-done.33, bf16[64,1280]{1,0:T(8,128)(2,1)} %collective-permute-done.32, bf16[64,1280]{1,0:T(8,128)(2,1)} %collective-permute-done.31, f32[64,640]{1,0:T(8,128)} %copy-done.5, f32[64,640]{1,0:T(8,128)} %copy-done.4), kind=kLoop, calls=%fused_computation.8 | loop fusion | flops 573440 | bytes 1146880 | tf_op jit(solution)/shard_map/add | solution.py:329
  106.2 2.1 %collective-permute-start.35 = (bf16[16,1024]{1,0:T(8,128)(2,1)S(1)}, bf16[16,1024]{1,0:T(8,128)(2,1)S(1)}, u32[]{:S(2)}, u32[]{:S(2)}) collective-permute-start(bf16[16,1024]{1,0:T(8,128)(2,1)S(1)} %get-tuple-element.60), channel_id=1, source_target_pairs={{0,6},{1,7},{2,4},{3,5},{4,2},{5,3},{6,0},{7,1},{8,14},{9,15},{10,... | collective-permute-start | bytes 98312 | tf_op jit(solution)/shard_map/ppermute | solution.py:61
  108.2 2.4 %collective-permute-start.37 = (bf16[16,1024]{1,0:T(8,128)(2,1)S(1)}, bf16[16,1024]{1,0:T(8,128)(2,1)S(1)}, u32[]{:S(2)}, u32[]{:S(2)}) collective-permute-start(bf16[16,1024]{1,0:T(8,128)(2,1)S(1)} %get-tuple-element.61), channel_id=1, source_target_pairs={{0,2},{1,3},{2,0},{3,1},{4,6},{5,7},{6,4},{7,5},{8,10},{9,11},{10,... | collective-permute-start | bytes 98312 | tf_op jit(solution)/shard_map/ppermute | solution.py:61
  110.7 0.6 fusion.8
  111.3 0.9 collective-permute-done.35
  112.2 1.0 collective-permute-done.36
  113.2 0.6 add_bitcast_fusion
  (117 shorter events, 6.9 us)
Async XLA Ops:
  0.6 55.7 %copy-start = (s32[1024,128]{1,0:T(8,128)S(1)}, s32[1024,128]{1,0:T(8,128)}, u32[]{:S(2)}) copy-start(s32[1024,128]{1,0:T(8,128)} %param.9) | copy-start | bytes 1572868
  0.6 5.4 %copy-start.6 = (f32[288,640]{1,0:T(8,128)S(1)}, f32[288,640]{1,0:T(8,128)}, u32[]{:S(2)}) copy-start(f32[288,640]{1,0:T(8,128)} %param.6) | copy-start | bytes 2211844
  0.7 5.5 %copy-start.11 = (f32[640,32]{0,1:T(8,128)S(1)}, f32[640,32]{0,1:T(8,128)}, u32[]{:S(2)}) copy-start(f32[640,32]{0,1:T(8,128)} %param.8) | copy-start | bytes 245764
  0.7 18.2 %copy-start.16 = (f32[640]{0:T(1024)S(1)}, f32[640]{0:T(1024)}, u32[]{:S(2)}) copy-start(f32[640]{0:T(1024)} %param.7) | copy-start | bytes 7684
  1.9 22.2 %copy-start.13 = (s16[144,1024]{1,0:T(8,128)(2,1)}, s16[144,1024]{1,0:T(8,128)(2,1)S(1)}, u32[]{:S(2)}) copy-start(s16[144,1024]{1,0:T(8,128)(2,1)S(1)} %fusion.refs_0_) | copy-start | bytes 884740
  1.9 15.4 %collective-permute-start.6 = (s16[144,1024]{1,0:T(8,128)(2,1)S(1)}, s16[144,1024]{1,0:T(8,128)(2,1)S(1)}, u32[]{:S(2)}, u32[]{:S(2)}) collective-permute-start(s16[144,1024]{1,0:T(8,128)(2,1)S(1)} %fusion.refs_0_), channel_id=1, source_target_pairs={{0,4},{1,5},{4,6},{5,7},{6,2},{7,3},{2,0},{3,1},{8,12},{9,13},{12,... | collective-permute-start | bytes 884744 | tf_op jit(solution)/shard_map/ppermute | solution.py:65
  6.2 21.1 %copy-start.14 = (s16[160,640]{1,0:T(8,128)(2,1)}, s16[160,640]{1,0:T(8,128)(2,1)S(1)}, u32[]{:S(2)}) copy-start(s16[160,640]{1,0:T(8,128)(2,1)S(1)} %pad_add_fusion.refs_6_) | copy-start | bytes 614404
  6.2 8.1 %collective-permute-start = (s16[160,640]{1,0:T(8,128)(2,1)S(1)}, s16[160,640]{1,0:T(8,128)(2,1)S(1)}, u32[]{:S(2)}, u32[]{:S(2)}) collective-permute-start(s16[160,640]{1,0:T(8,128)(2,1)S(1)} %pad_add_fusion.refs_6_), channel_id=1, source_target_pairs={{0,8},{8,0},{16,24},{24,16},{1,9},{9,1},{17,25},{25,17},{2,10},{10... | collective-permute-start | bytes 614408 | tf_op jit(solution)/shard_map/ppermute | solution.py:70
  7.8 19.6 %copy-start.15 = (s16[160,640]{1,0:T(8,128)(2,1)}, s16[160,640]{1,0:T(8,128)(2,1)S(1)}, u32[]{:S(2)}) copy-start(s16[160,640]{1,0:T(8,128)(2,1)S(1)} %pad_add_fusion.1.refs_7_) | copy-start | bytes 614404
  7.8 8.1 %collective-permute-start.3 = (s16[160,640]{1,0:T(8,128)(2,1)S(1)}, s16[160,640]{1,0:T(8,128)(2,1)S(1)}, u32[]{:S(2)}, u32[]{:S(2)}) collective-permute-start(s16[160,640]{1,0:T(8,128)(2,1)S(1)} %pad_add_fusion.1.refs_7_), channel_id=1, source_target_pairs={{0,16},{8,24},{16,0},{24,8},{1,17},{9,25},{17,1},{25,9},{2,18},{10... | collective-permute-start | bytes 614408 | tf_op jit(solution)/shard_map/ppermute | solution.py:70
  9.4 10.2 %collective-permute-start.1 = (s16[160,640]{1,0:T(8,128)(2,1)S(1)}, s16[160,640]{1,0:T(8,128)(2,1)S(1)}, u32[]{:S(2)}, u32[]{:S(2)}) collective-permute-start(s16[160,640]{1,0:T(8,128)(2,1)S(1)} %pad_add_fusion.1.refs_7_), channel_id=1, source_target_pairs={{0,8},{8,0},{16,24},{24,16},{1,9},{9,1},{17,25},{25,17},{2,10},{10... | collective-permute-start | bytes 614408 | tf_op jit(solution)/shard_map/ppermute | solution.py:70
  9.9 10.4 %collective-permute-start.2 = (s16[160,640]{1,0:T(8,128)(2,1)S(1)}, s16[160,640]{1,0:T(8,128)(2,1)S(1)}, u32[]{:S(2)}, u32[]{:S(2)}) collective-permute-start(s16[160,640]{1,0:T(8,128)(2,1)S(1)} %pad_add_fusion.refs_6_), channel_id=1, source_target_pairs={{0,16},{8,24},{16,0},{24,8},{1,17},{9,25},{17,1},{25,9},{2,18},{10... | collective-permute-start | bytes 614408 | tf_op jit(solution)/shard_map/ppermute | solution.py:70
  14.3 13.1 %copy-start.17 = (s16[160,640]{1,0:T(8,128)(2,1)}, s16[160,640]{1,0:T(8,128)(2,1)S(1)}, u32[]{:S(2)}) copy-start(s16[160,640]{1,0:T(8,128)(2,1)S(1)} %collective-permute-done.refs_8_) | copy-start | bytes 614404
  14.3 8.6 %collective-permute-start.4 = (s16[160,640]{1,0:T(8,128)(2,1)S(1)}, s16[160,640]{1,0:T(8,128)(2,1)S(1)}, u32[]{:S(2)}, u32[]{:S(2)}) collective-permute-start(s16[160,640]{1,0:T(8,128)(2,1)S(1)} %collective-permute-done.refs_8_), channel_id=1, source_target_pairs={{0,16},{8,24},{16,0},{24,8},{1,17},{9,25},{17,1},{25,9},{2,18},{10... | collective-permute-start | bytes 614408 | tf_op jit(solution)/shard_map/ppermute | solution.py:70
  15.9 11.5 %copy-start.18 = (s16[160,640]{1,0:T(8,128)(2,1)}, s16[160,640]{1,0:T(8,128)(2,1)S(1)}, u32[]{:S(2)}) copy-start(s16[160,640]{1,0:T(8,128)(2,1)S(1)} %collective-permute-done.3.refs_11_) | copy-start | bytes 614404
  15.9 7.0 %collective-permute-start.5 = (s16[160,640]{1,0:T(8,128)(2,1)S(1)}, s16[160,640]{1,0:T(8,128)(2,1)S(1)}, u32[]{:S(2)}, u32[]{:S(2)}) collective-permute-start(s16[160,640]{1,0:T(8,128)(2,1)S(1)} %collective-permute-done.3.refs_11_), channel_id=1, source_target_pairs={{0,8},{8,0},{16,24},{24,16},{1,9},{9,1},{17,25},{25,17},{2,10},{10... | collective-permute-start | bytes 614408 | tf_op jit(solution)/shard_map/ppermute | solution.py:70
  17.3 10.1 %copy-start.23 = (s16[144,1024]{1,0:T(8,128)(2,1)}, s16[144,1024]{1,0:T(8,128)(2,1)S(1)}, u32[]{:S(2)}) copy-start(s16[144,1024]{1,0:T(8,128)(2,1)S(1)} %collective-permute-done.6.refs_2_) | copy-start | bytes 884740
  17.3 6.7 %collective-permute-start.7 = (s16[144,1024]{1,0:T(8,128)(2,1)S(1)}, s16[144,1024]{1,0:T(8,128)(2,1)S(1)}, u32[]{:S(2)}, u32[]{:S(2)}) collective-permute-start(s16[144,1024]{1,0:T(8,128)(2,1)S(1)} %collective-permute-done.6.refs_2_), channel_id=1, source_target_pairs={{0,4},{1,5},{4,6},{5,7},{6,2},{7,3},{2,0},{3,1},{8,12},{9,13},{12,... | collective-permute-start | bytes 884744 | tf_op jit(solution)/shard_map/ppermute | solution.py:65
  19.6 7.8 %copy-start.19 = (s16[160,640]{1,0:T(8,128)(2,1)}, s16[160,640]{1,0:T(8,128)(2,1)S(1)}, u32[]{:S(2)}) copy-start(s16[160,640]{1,0:T(8,128)(2,1)S(1)} %collective-permute-done.1.refs_9_) | copy-start | bytes 614404
  19.6 7.7 %collective-permute-start.8 = (s16[144,1024]{1,0:T(8,128)(2,1)S(1)}, s16[144,1024]{1,0:T(8,128)(2,1)S(1)}, u32[]{:S(2)}, u32[]{:S(2)}) collective-permute-start(s16[144,1024]{1,0:T(8,128)(2,1)S(1)} %fusion.refs_0_), channel_id=1, source_target_pairs={{0,1},{1,0},{2,3},{3,2},{4,5},{5,4},{6,7},{7,6},{8,9},{9,8},{10,11... | collective-permute-start | bytes 884744 | tf_op jit(solution)/shard_map/ppermute | solution.py:56
  20.3 7.1 %copy-start.20 = (s16[160,640]{1,0:T(8,128)(2,1)}, s16[160,640]{1,0:T(8,128)(2,1)S(1)}, u32[]{:S(2)}) copy-start(s16[160,640]{1,0:T(8,128)(2,1)S(1)} %collective-permute-done.2.refs_10_) | copy-start | bytes 614404
  20.3 7.0 %collective-permute-start.9 = (s16[144,1024]{1,0:T(8,128)(2,1)S(1)}, s16[144,1024]{1,0:T(8,128)(2,1)S(1)}, u32[]{:S(2)}, u32[]{:S(2)}) collective-permute-start(s16[144,1024]{1,0:T(8,128)(2,1)S(1)} %collective-permute-done.6.refs_2_), channel_id=1, source_target_pairs={{0,1},{1,0},{2,3},{3,2},{4,5},{5,4},{6,7},{7,6},{8,9},{9,8},{10,11... | collective-permute-start | bytes 884744 | tf_op jit(solution)/shard_map/ppermute | solution.py:56
  22.9 4.5 %copy-start.21 = (s16[160,640]{1,0:T(8,128)(2,1)}, s16[160,640]{1,0:T(8,128)(2,1)S(1)}, u32[]{:S(2)}) copy-start(s16[160,640]{1,0:T(8,128)(2,1)S(1)} %collective-permute-done.4.refs_12_) | copy-start | bytes 614404
  22.9 4.5 %copy-start.22 = (s16[160,640]{1,0:T(8,128)(2,1)}, s16[160,640]{1,0:T(8,128)(2,1)S(1)}, u32[]{:S(2)}) copy-start(s16[160,640]{1,0:T(8,128)(2,1)S(1)} %collective-permute-done.5.refs_13_) | copy-start | bytes 614404
  24.1 3.4 %copy-start.24 = (s16[144,1024]{1,0:T(8,128)(2,1)}, s16[144,1024]{1,0:T(8,128)(2,1)S(1)}, u32[]{:S(2)}) copy-start(s16[144,1024]{1,0:T(8,128)(2,1)S(1)} %collective-permute-done.7.refs_4_) | copy-start | bytes 884740
  24.1 3.3 %collective-permute-start.10 = (s16[144,1024]{1,0:T(8,128)(2,1)S(1)}, s16[144,1024]{1,0:T(8,128)(2,1)S(1)}, u32[]{:S(2)}, u32[]{:S(2)}) collective-permute-start(s16[144,1024]{1,0:T(8,128)(2,1)S(1)} %collective-permute-done.7.refs_4_), channel_id=1, source_target_pairs={{0,1},{1,0},{2,3},{3,2},{4,5},{5,4},{6,7},{7,6},{8,9},{9,8},{10,11... | collective-permute-start | bytes 884744 | tf_op jit(solution)/shard_map/ppermute | solution.py:56
  24.9 14.3 %collective-permute-start.11 = (s16[144,1024]{1,0:T(8,128)(2,1)S(1)}, s16[144,1024]{1,0:T(8,128)(2,1)S(1)}, u32[]{:S(2)}, u32[]{:S(2)}) collective-permute-start(s16[144,1024]{1,0:T(8,128)(2,1)S(1)} %collective-permute-done.7.refs_4_), channel_id=1, source_target_pairs={{0,4},{1,5},{4,6},{5,7},{6,2},{7,3},{2,0},{3,1},{8,12},{9,13},{12,... | collective-permute-start | bytes 884744 | tf_op jit(solution)/shard_map/ppermute | solution.py:65
  27.3 0.7 copy-start.25
  27.3 0.8 copy-start.26
  28.2 0.7 copy-start.27
  39.2 1.6 %collective-permute-start.12 = (s16[144,1024]{1,0:T(8,128)(2,1)S(1)}, s16[144,1024]{1,0:T(8,128)(2,1)S(1)}, u32[]{:S(2)}, u32[]{:S(2)}) collective-permute-start(s16[144,1024]{1,0:T(8,128)(2,1)S(1)} %collective-permute-done.11.own_ref), channel_id=1, source_target_pairs={{0,1},{1,0},{2,3},{3,2},{4,5},{5,4},{6,7},{7,6},{8,9},{9,8},{10,11... | collective-permute-start | bytes 884744 | tf_op jit(solution)/shard_map/ppermute | solution.py:56
  40.8 1.7 %copy-start.1 = (f32[640,1024]{1,0:T(8,128)S(1)}, f32[640,1024]{1,0:T(8,128)}, u32[]{:S(2)}) copy-start(f32[640,1024]{1,0:T(8,128)} %get-tuple-element.35.sum_ref) | copy-start | bytes 7864324
  42.6 1.0 copy-start.2
  43.6 1.0 copy-start.3
  49.1 1.4 %collective-permute-start.13 = (bf16[64,1024]{1,0:T(8,128)(2,1)S(1)}, bf16[64,1024]{1,0:T(8,128)(2,1)S(1)}, u32[]{:S(2)}, u32[]{:S(2)}) collective-permute-start(bf16[64,1024]{1,0:T(8,128)(2,1)S(1)} %convolution_convert_fusion), channel_id=1, source_target_pairs={{0,1},{1,0},{2,3},{3,2},{4,5},{5,4},{6,7},{7,6},{8,9},{9,8},{10,11... | collective-permute-start | bytes 393224 | tf_op jit(solution)/shard_map/ppermute | solution.py:56
  50.5 17.8 %collective-permute-start.20 = (bf16[640,1024]{1,0:T(8,128)(2,1)S(1)}, bf16[640,1024]{1,0:T(8,128)(2,1)S(1)}, u32[]{:S(2)}, u32[]{:S(2)}) collective-permute-start(bf16[640,1024]{1,0:T(8,128)(2,1)S(1)} %late_angles.1), channel_id=1, source_target_pairs={{0,1},{1,0},{2,3},{3,2},{4,5},{5,4},{6,7},{7,6},{8,9},{9,8},{10,11... | collective-permute-start | bytes 3932168 | tf_op jit(solution)/shard_map/ppermute | solution.py:56
  51.9 6.7 %collective-permute-start.14 = (bf16[16,1024]{1,0:T(8,128)(2,1)S(1)}, bf16[16,1024]{1,0:T(8,128)(2,1)S(1)}, u32[]{:S(2)}, u32[]{:S(2)}) collective-permute-start(bf16[16,1024]{1,0:T(8,128)(2,1)S(1)} %get-tuple-element.66), channel_id=1, source_target_pairs={{0,6},{1,7},{2,4},{3,5},{4,2},{5,3},{6,0},{7,1},{8,14},{9,15},{10,... | collective-permute-start | bytes 98312 | tf_op jit(solution)/shard_map/ppermute | solution.py:61
  52.2 6.4 %collective-permute-start.15 = (bf16[16,1024]{1,0:T(8,128)(2,1)S(1)}, bf16[16,1024]{1,0:T(8,128)(2,1)S(1)}, u32[]{:S(2)}, u32[]{:S(2)}) collective-permute-start(bf16[16,1024]{1,0:T(8,128)(2,1)S(1)} %get-tuple-element.68), channel_id=1, source_target_pairs={{0,4},{1,5},{2,6},{3,7},{4,0},{5,1},{6,2},{7,3},{8,12},{9,13},{10,... | collective-permute-start | bytes 98312 | tf_op jit(solution)/shard_map/ppermute | solution.py:61
  52.9 5.7 %collective-permute-start.16 = (bf16[16,1024]{1,0:T(8,128)(2,1)S(1)}, bf16[16,1024]{1,0:T(8,128)(2,1)S(1)}, u32[]{:S(2)}, u32[]{:S(2)}) collective-permute-start(bf16[16,1024]{1,0:T(8,128)(2,1)S(1)} %get-tuple-element.67), channel_id=1, source_target_pairs={{0,2},{1,3},{2,0},{3,1},{4,6},{5,7},{6,4},{7,5},{8,10},{9,11},{10,... | collective-permute-start | bytes 98312 | tf_op jit(solution)/shard_map/ppermute | solution.py:61
  58.6 10.3 %copy-start.7 = (s32[1024,16]{0,1:T(8,128)}, s32[1024,16]{0,1:T(8,128)S(1)}, u32[]{:S(2)}) copy-start(s32[1024,16]{0,1:T(8,128)S(1)} %copy.10) | copy-start | bytes 196612
  59.5 4.5 %collective-permute-start.17 = (bf16[16,1024]{1,0:T(8,128)(2,1)S(1)}, bf16[16,1024]{1,0:T(8,128)(2,1)S(1)}, u32[]{:S(2)}, u32[]{:S(2)}) collective-permute-start(bf16[16,1024]{1,0:T(8,128)(2,1)S(1)} %fusion.29), channel_id=1, source_target_pairs={{0,2},{1,3},{2,0},{3,1},{4,6},{5,7},{6,4},{7,5},{8,10},{9,11},{10,... | collective-permute-start | bytes 98312 | tf_op jit(solution)/shard_map/ppermute | solution.py:61
  61.2 5.0 %collective-permute-start.18 = (bf16[16,1024]{1,0:T(8,128)(2,1)S(1)}, bf16[16,1024]{1,0:T(8,128)(2,1)S(1)}, u32[]{:S(2)}, u32[]{:S(2)}) collective-permute-start(bf16[16,1024]{1,0:T(8,128)(2,1)S(1)} %fusion.29), channel_id=1, source_target_pairs={{0,4},{1,5},{2,6},{3,7},{4,0},{5,1},{6,2},{7,3},{8,12},{9,13},{10,... | collective-permute-start | bytes 98312 | tf_op jit(solution)/shard_map/ppermute | solution.py:61
  62.1 5.7 %collective-permute-start.19 = (bf16[16,1024]{1,0:T(8,128)(2,1)S(1)}, bf16[16,1024]{1,0:T(8,128)(2,1)S(1)}, u32[]{:S(2)}, u32[]{:S(2)}) collective-permute-start(bf16[16,1024]{1,0:T(8,128)(2,1)S(1)} %fusion.29), channel_id=1, source_target_pairs={{0,6},{1,7},{2,4},{3,5},{4,2},{5,3},{6,0},{7,1},{8,14},{9,15},{10,... | collective-permute-start | bytes 98312 | tf_op jit(solution)/shard_map/ppermute | solution.py:61
  68.9 6.4 %collective-permute-start.21 = (bf16[64,1280]{1,0:T(8,128)(2,1)S(1)}, bf16[64,1280]{1,0:T(8,128)(2,1)S(1)}, u32[]{:S(2)}, u32[]{:S(2)}) collective-permute-start(bf16[64,1280]{1,0:T(8,128)(2,1)S(1)} %fusion.2), channel_id=1, source_target_pairs={{0,24},{8,16},{16,8},{24,0},{1,25},{9,17},{17,9},{25,1},{2,26},{10... | collective-permute-start | bytes 491528 | tf_op jit(solution)/shard_map/ppermute | solution.py:70
  70.5 6.4 %collective-permute-start.22 = (bf16[64,1280]{1,0:T(8,128)(2,1)S(1)}, bf16[64,1280]{1,0:T(8,128)(2,1)S(1)}, u32[]{:S(2)}, u32[]{:S(2)}) collective-permute-start(bf16[64,1280]{1,0:T(8,128)(2,1)S(1)} %fusion.2), channel_id=1, source_target_pairs={{0,16},{8,24},{16,0},{24,8},{1,17},{9,25},{17,1},{25,9},{2,18},{10... | collective-permute-start | bytes 491528 | tf_op jit(solution)/shard_map/ppermute | solution.py:70
  71.0 5.9 %collective-permute-start.23 = (bf16[64,1280]{1,0:T(8,128)(2,1)S(1)}, bf16[64,1280]{1,0:T(8,128)(2,1)S(1)}, u32[]{:S(2)}, u32[]{:S(2)}) collective-permute-start(bf16[64,1280]{1,0:T(8,128)(2,1)S(1)} %fusion.2), channel_id=1, source_target_pairs={{0,8},{8,0},{16,24},{24,16},{1,9},{9,1},{17,25},{25,17},{2,10},{10... | collective-permute-start | bytes 491528 | tf_op jit(solution)/shard_map/ppermute | solution.py:70
  72.4 4.6 %collective-permute-start.24 = (s16[64,640]{1,0:T(8,128)(2,1)}, s16[64,640]{1,0:T(8,128)(2,1)S(1)}, u32[]{:S(2)}, u32[]{:S(2)}) collective-permute-start(s16[64,640]{1,0:T(8,128)(2,1)} %get-tuple-element.32), channel_id=1, source_target_pairs={{0,1},{1,0},{2,3},{3,2},{4,5},{5,4},{6,7},{7,6},{8,9},{9,8},{10,11... | collective-permute-start | bytes 245768 | tf_op jit(solution)/shard_map/ppermute | solution.py:56
  78.0 7.5 %copy-start.8 = (s32[1024,16]{0,1:T(8,128)S(1)}, s32[1024,16]{0,1:T(8,128)}, u32[]{:S(2)}) copy-start(s32[1024,16]{0,1:T(8,128)} %copy-done.7) | copy-start | bytes 196612
  78.4 5.8 %collective-permute-start.25 = (bf16[16,1024]{1,0:T(8,128)(2,1)S(1)}, bf16[16,1024]{1,0:T(8,128)(2,1)S(1)}, u32[]{:S(2)}, u32[]{:S(2)}) collective-permute-start(bf16[16,1024]{1,0:T(8,128)(2,1)S(1)} %get-tuple-element.63), channel_id=1, source_target_pairs={{0,6},{1,7},{2,4},{3,5},{4,2},{5,3},{6,0},{7,1},{8,14},{9,15},{10,... | collective-permute-start | bytes 98312 | tf_op jit(solution)/shard_map/ppermute | solution.py:61
  80.7 4.8 %collective-permute-start.26 = (bf16[16,1024]{1,0:T(8,128)(2,1)S(1)}, bf16[16,1024]{1,0:T(8,128)(2,1)S(1)}, u32[]{:S(2)}, u32[]{:S(2)}) collective-permute-start(bf16[16,1024]{1,0:T(8,128)(2,1)S(1)} %get-tuple-element.65), channel_id=1, source_target_pairs={{0,4},{1,5},{2,6},{3,7},{4,0},{5,1},{6,2},{7,3},{8,12},{9,13},{10,... | collective-permute-start | bytes 98312 | tf_op jit(solution)/shard_map/ppermute | solution.py:61
  80.7 4.8 %collective-permute-start.27 = (bf16[16,1024]{1,0:T(8,128)(2,1)S(1)}, bf16[16,1024]{1,0:T(8,128)(2,1)S(1)}, u32[]{:S(2)}, u32[]{:S(2)}) collective-permute-start(bf16[16,1024]{1,0:T(8,128)(2,1)S(1)} %get-tuple-element.64), channel_id=1, source_target_pairs={{0,2},{1,3},{2,0},{3,1},{4,6},{5,7},{6,4},{7,5},{8,10},{9,11},{10,... | collective-permute-start | bytes 98312 | tf_op jit(solution)/shard_map/ppermute | solution.py:61
  85.6 4.5 %collective-permute-start.28 = (bf16[16,1024]{1,0:T(8,128)(2,1)S(1)}, bf16[16,1024]{1,0:T(8,128)(2,1)S(1)}, u32[]{:S(2)}, u32[]{:S(2)}) collective-permute-start(bf16[16,1024]{1,0:T(8,128)(2,1)S(1)} %fusion.30), channel_id=1, source_target_pairs={{0,2},{1,3},{2,0},{3,1},{4,6},{5,7},{6,4},{7,5},{8,10},{9,11},{10,... | collective-permute-start | bytes 98312 | tf_op jit(solution)/shard_map/ppermute | solution.py:61
  86.9 4.8 %collective-permute-start.29 = (bf16[16,1024]{1,0:T(8,128)(2,1)S(1)}, bf16[16,1024]{1,0:T(8,128)(2,1)S(1)}, u32[]{:S(2)}, u32[]{:S(2)}) collective-permute-start(bf16[16,1024]{1,0:T(8,128)(2,1)S(1)} %fusion.30), channel_id=1, source_target_pairs={{0,4},{1,5},{2,6},{3,7},{4,0},{5,1},{6,2},{7,3},{8,12},{9,13},{10,... | collective-permute-start | bytes 98312 | tf_op jit(solution)/shard_map/ppermute | solution.py:61
  88.0 5.7 %collective-permute-start.30 = (bf16[16,1024]{1,0:T(8,128)(2,1)S(1)}, bf16[16,1024]{1,0:T(8,128)(2,1)S(1)}, u32[]{:S(2)}, u32[]{:S(2)}) collective-permute-start(bf16[16,1024]{1,0:T(8,128)(2,1)S(1)} %fusion.30), channel_id=1, source_target_pairs={{0,6},{1,7},{2,4},{3,5},{4,2},{5,3},{6,0},{7,1},{8,14},{9,15},{10,... | collective-permute-start | bytes 98312 | tf_op jit(solution)/shard_map/ppermute | solution.py:61
  94.9 0.7 copy-start.5
  95.7 6.6 %collective-permute-start.31 = (bf16[64,1280]{1,0:T(8,128)(2,1)}, bf16[64,1280]{1,0:T(8,128)(2,1)}, u32[]{:S(2)}, u32[]{:S(2)}) collective-permute-start(bf16[64,1280]{1,0:T(8,128)(2,1)} %fusion.1), channel_id=1, source_target_pairs={{0,24},{8,16},{16,8},{24,0},{1,25},{9,17},{17,9},{25,1},{2,26},{10... | collective-permute-start | bytes 491528 | tf_op jit(solution)/shard_map/ppermute | solution.py:70
  97.3 6.7 %collective-permute-start.32 = (bf16[64,1280]{1,0:T(8,128)(2,1)}, bf16[64,1280]{1,0:T(8,128)(2,1)}, u32[]{:S(2)}, u32[]{:S(2)}) collective-permute-start(bf16[64,1280]{1,0:T(8,128)(2,1)} %fusion.1), channel_id=1, source_target_pairs={{0,16},{8,24},{16,0},{24,8},{1,17},{9,25},{17,1},{25,9},{2,18},{10... | collective-permute-start | bytes 491528 | tf_op jit(solution)/shard_map/ppermute | solution.py:70
  97.9 6.1 %collective-permute-start.33 = (bf16[64,1280]{1,0:T(8,128)(2,1)}, bf16[64,1280]{1,0:T(8,128)(2,1)}, u32[]{:S(2)}, u32[]{:S(2)}) collective-permute-start(bf16[64,1280]{1,0:T(8,128)(2,1)} %fusion.1), channel_id=1, source_target_pairs={{0,8},{8,0},{16,24},{24,16},{1,9},{9,1},{17,25},{25,17},{2,10},{10... | collective-permute-start | bytes 491528 | tf_op jit(solution)/shard_map/ppermute | solution.py:70
  99.2 6.3 %copy-start.10 = (s16[64,640]{1,0:T(8,128)(2,1)S(1)}, s16[64,640]{1,0:T(8,128)(2,1)}, u32[]{:S(2)}) copy-start(s16[64,640]{1,0:T(8,128)(2,1)} %copy-done.9) | copy-start | bytes 245764
  105.3 5.3 %collective-permute-start.34 = (f32[64,640]{1,0:T(8,128)S(1)}, f32[64,640]{1,0:T(8,128)S(1)}, u32[]{:S(2)}, u32[]{:S(2)}) collective-permute-start(f32[64,640]{1,0:T(8,128)S(1)} %get-tuple-element.49), channel_id=1, source_target_pairs={{0,1},{1,0},{2,3},{3,2},{4,5},{5,4},{6,7},{7,6},{8,9},{9,8},{10,11... | collective-permute-start | bytes 491528 | tf_op jit(solution)/shard_map/ppermute | solution.py:56
  105.8 4.9 %copy-start.12 = (f32[640,32]{0,1:T(8,128)S(1)}, f32[640,32]{0,1:T(8,128)}, u32[]{:S(2)}) copy-start(f32[640,32]{0,1:T(8,128)} %param.8) | copy-start | bytes 245764
  106.2 6.0 %collective-permute-start.35 = (bf16[16,1024]{1,0:T(8,128)(2,1)S(1)}, bf16[16,1024]{1,0:T(8,128)(2,1)S(1)}, u32[]{:S(2)}, u32[]{:S(2)}) collective-permute-start(bf16[16,1024]{1,0:T(8,128)(2,1)S(1)} %get-tuple-element.60), channel_id=1, source_target_pairs={{0,6},{1,7},{2,4},{3,5},{4,2},{5,3},{6,0},{7,1},{8,14},{9,15},{10,... | collective-permute-start | bytes 98312 | tf_op jit(solution)/shard_map/ppermute | solution.py:61
  108.2 5.0 %collective-permute-start.36 = (bf16[16,1024]{1,0:T(8,128)(2,1)S(1)}, bf16[16,1024]{1,0:T(8,128)(2,1)S(1)}, u32[]{:S(2)}, u32[]{:S(2)}) collective-permute-start(bf16[16,1024]{1,0:T(8,128)(2,1)S(1)} %get-tuple-element.62), channel_id=1, source_target_pairs={{0,4},{1,5},{2,6},{3,7},{4,0},{5,1},{6,2},{7,3},{8,12},{9,13},{10,... | collective-permute-start | bytes 98312 | tf_op jit(solution)/shard_map/ppermute | solution.py:61
  108.2 5.0 %collective-permute-start.37 = (bf16[16,1024]{1,0:T(8,128)(2,1)S(1)}, bf16[16,1024]{1,0:T(8,128)(2,1)S(1)}, u32[]{:S(2)}, u32[]{:S(2)}) collective-permute-start(bf16[16,1024]{1,0:T(8,128)(2,1)S(1)} %get-tuple-element.61), channel_id=1, source_target_pairs={{0,2},{1,3},{2,0},{3,1},{4,6},{5,7},{6,4},{7,5},{8,10},{9,11},{10,... | collective-permute-start | bytes 98312 | tf_op jit(solution)/shard_map/ppermute | solution.py:61
  (2 other events, 1.3 us)

commit v5 on v4

--- a/solution.py
+++ b/solution.py
@@ -79,76 +79,59 @@
     return high.astype(jnp.bfloat16), (x - high).astype(jnp.bfloat16)
 
 
-def copied(sources, places, sem):
-    copies = [pltpu.make_async_copy(a, b, sem.at[i]) for i, (a, b) in enumerate(zip(sources, places))]
-    for copy in copies:
-        copy.start()
-    return copies
-
-
-def tiles_of(ref):
-    tile = 256 if ref.shape[1] % 256 == 0 else ref.shape[1]
-    return [slice(start, start + tile) for start in range(0, ref.shape[1], tile)]
-
-
-def early_kernel(
-    at_ref, *refs, n_embeds, n_freqs, columns
+def early_kernel(at_ref, *refs, n_embeds, n_freqs, columns):
+    embeds, freqs = refs[:n_embeds], refs[n_embeds : n_embeds + n_freqs]
+    sum_ref, last_ref, freq_code, f_all, e_all = refs[n_embeds + n_freqs :]
+    used = n_embeds * columns
+    depth = e_all.shape[0] // 3
+
+    @pl.when(pl.program_id(0) == 0)
+    def _():
+        line, clip, core = at_ref[0], at_ref[1], at_ref[2]
+
+        def on_ring(place):
+            return jnp.where(place == 0, 0, jnp.where(place == 1, 3, place - 1))
+
+        for m in range(n_freqs // 2):
+            step = (on_ring(line) - on_ring(clip ^ m)) & 3
+            base = step * 2 * columns + jnp.where(step == 3, depth - used, 0)
+            for h, side in enumerate((core, 1 - core)):
+                row = pl.multiple_of(base + side * columns, 16)
+                freq_code[pl.ds(row, columns), :] = freqs[2 * m + h][:columns, :]
+        if depth > used:
+            freq_code[used:depth, :] = jnp.zeros((depth - used, freq_code.shape[1]), jnp.int16)
+            for start in range(0, 3 * depth, depth):
+                e_all[start + used : start + depth, :] = jnp.zeros((depth - used, e_all.shape[1]), jnp.bfloat16)
+        for start in range(0, depth, LANES):
+            high, low = halves(freq_code[start : start + LANES, :].T.astype(jnp.float32))
+            f_all[:, start : start + LANES] = high
+            f_all[:, depth + start : depth + start + LANES] = high
+            f_all[:, 2 * depth + start : 2 * depth + start + LANES] = low
+        last_ref[0], last_ref[1] = halves(freq_code[depth:, :].T.astype(jnp.float32))
+
+    for i, ref in enumerate(embeds):
+        high, low = halves(ref[...].astype(jnp.float32))
+        for start, value in ((0, high), (depth, low), (2 * depth, high)):
+            e_all[start + i * columns : start + (i + 1) * columns, :] = value
+    sum_ref[...] = mix(f_all[...], e_all[...])
+
+
+def late_kernel(
+    sum_ref, own_ref, other_ref, last_ref, phase_ref, beta_ref, phi_ref, keep_ref, send_ref, e_high, e_low, *, scale
 ):
-    embeds, freqs = refs[:n_embeds], refs[n_embeds : n_embeds + n_freqs]
-    (
-        sum_ref, high_ref, low_ref, freq_code, embed_code, f_high, f_low, e_high, e_low, sem_f, sem_e,
-    ) = refs[n_embeds + n_freqs :]
-    depth = e_high.shape[0]
-    used = n_embeds * columns
-    line, clip, core = at_ref[0], at_ref[1], at_ref[2]
-
-    def on_ring(place):
-        return jnp.where(place == 0, 0, jnp.where(place == 1, 3, place - 1))
-
-    rows = []
-    for m in range(n_freqs // 2):
-        step = (on_ring(line) - on_ring(clip ^ m)) & 3
-        base = step * 2 * columns + jnp.where(step == 3, depth - used, 0)
-        rows += [pl.ds(pl.multiple_of(base + h * columns, 16), columns) for h in (core, 1 - core)]
-    pieces = [ref.at[:columns, :] for ref in freqs]
-    of_freqs = copied(pieces, [freq_code.at[r, :] for r in rows], sem_f)
-    of_embeds = copied(embeds, [embed_code.at[i * columns : (i + 1) * columns, :] for i in range(n_embeds)], sem_e)
-    if depth > used:
-        freq_code[used:depth, :] = jnp.zeros((depth - used, freq_code.shape[1]), jnp.int16)
-        embed_code[used:depth, :] = jnp.zeros((depth - used, embed_code.shape[1]), jnp.int16)
-    for copy in of_embeds:
-        copy.wait()
-    e_high[...], e_low[...] = halves(embed_code[...].astype(jnp.float32))
-    for copy in of_freqs:
-        copy.wait()
-    for start in range(0, depth, LANES):
-        f_high[:, start : start + LANES], f_low[:, start : start + LANES] = halves(
-            freq_code[start : start + LANES, :].T.astype(jnp.float32)
-        )
-    high_ref[...], low_ref[...] = halves(freq_code[depth:, :].T.astype(jnp.float32))
-    for at in tiles_of(sum_ref):
-        sum_ref[:, at] = mix(f_high[...], e_high[:, at]) + (
-            mix(f_high[...], e_low[:, at]) + mix(f_low[...], e_high[:, at])
-        )
-
-
-def late_kernel(
-    sum_ref, own_ref, other_ref, high_ref, low_ref, phase_ref,
-    phi_ref, sums, embed_code, e_high, e_low, sem_s, sem_e, *, columns, scale,
-):
-    of_embeds = copied((own_ref, other_ref), (embed_code.at[:columns], embed_code.at[columns:]), sem_e)
-    of_sums = copied((sum_ref,), (sums,), sem_s)
-    for copy in of_embeds:
-        copy.wait()
-    e_high[...], e_low[...] = halves(embed_code[...].astype(jnp.float32))
-    for copy in of_sums:
-        copy.wait()
-    for at in tiles_of(sums):
-        total = sums[:, at] + (
-            mix(high_ref[...], e_high[:, at])
-            + (mix(high_ref[...], e_low[:, at]) + mix(low_ref[...], e_high[:, at]))
-        )
-        phi_ref[:, at] = scaled_cos(total * PER_TURN + phase_ref[...], scale)
+    columns = own_ref.shape[0]
+    for i, ref in enumerate((own_ref, other_ref)):
+        rows = slice(i * columns, (i + 1) * columns)
+        e_high[rows, :], e_low[rows, :] = halves(ref[...].astype(jnp.float32))
+    total = sum_ref[...] + (
+        mix(last_ref[0], e_high[...]) + (mix(last_ref[0], e_low[...]) + mix(last_ref[1], e_high[...]))
+    )
+    phi = scaled_cos(total * PER_TURN + phase_ref[...], scale)
+    phi_ref[...] = phi
+    logits = mix(beta_ref[...], phi)
+    half = keep_ref.shape[0]
+    keep_ref[...] = logits[:half]
+    send_ref[...] = logits[half:].astype(jnp.bfloat16)
 
 
 def phi_by_kernels(embed_code, freq_code, column, scale, line, core, clip, prepare):
@@ -166,31 +149,33 @@
     other = [core_swap(own[0]), core_swap(own[1])]
     *freqs, turn = tie((*freqs, own[2]))
     other.append(core_swap(turn))
-    rest = prepare(freqs)
+    betas, cast = prepare(freqs)
     early = [x for pair in zip(own[:3], other) for x in pair]
     used = len(early) * columns
     depth = -(-used // LANES) * LANES
-    vmem = pl.BlockSpec(memory_space=pltpu.VMEM)
-    smem = pl.BlockSpec(memory_space=pltpu.SMEM)
-    anywhere = pl.BlockSpec(memory_space=pl.ANY)
-    summed, high, low = pl.pallas_call(
+    tile = 256 if clips % 256 == 0 else clips
+
+    def whole(*shape):
+        return pl.BlockSpec(shape, lambda i: (0,) * len(shape))
+
+    def by_clips(rows):
+        return pl.BlockSpec((rows, tile), lambda i: (0, i))
+
+    summed, freq_last = pl.pallas_call(
         functools.partial(early_kernel, n_embeds=len(early), n_freqs=len(freqs), columns=columns),
+        grid=(clips // tile,),
         out_shape=(
             jax.ShapeDtypeStruct((features, clips), jnp.float32),
-            jax.ShapeDtypeStruct((features, 2 * columns), jnp.bfloat16),
-            jax.ShapeDtypeStruct((features, 2 * columns), jnp.bfloat16),
+            jax.ShapeDtypeStruct((2, features, 2 * columns), jnp.bfloat16),
         ),
-        in_specs=[smem] + [anywhere] * (len(early) + len(freqs)),
-        out_specs=(vmem, vmem, vmem),
+        in_specs=[pl.BlockSpec(memory_space=pltpu.SMEM)]
+        + [by_clips(columns)] * len(early)
+        + [whole(*x.shape) for x in freqs],
+        out_specs=(by_clips(features), whole(2, features, 2 * columns)),
         scratch_shapes=[
             pltpu.VMEM((depth + 2 * columns, features), jnp.int16),
-            pltpu.VMEM((depth, clips), jnp.int16),
-            pltpu.VMEM((features, depth), jnp.bfloat16),
-            pltpu.VMEM((features, depth), jnp.bfloat16),
-            pltpu.VMEM((depth, clips), jnp.bfloat16),
-            pltpu.VMEM((depth, clips), jnp.bfloat16),
-            pltpu.SemaphoreType.DMA((len(freqs),)),
-            pltpu.SemaphoreType.DMA((len(early),)),
+            pltpu.VMEM((features, 3 * depth), jnp.bfloat16),
+            pltpu.VMEM((3 * depth, tile), jnp.bfloat16),
         ],
         compiler_params=pltpu.CompilerParams(vmem_limit_bytes=EARLY_VMEM_BYTES),
         cost_estimate=pl.CostEstimate(
@@ -198,27 +183,33 @@
         ),
         name="early_angles",
     )(jnp.stack([line, clip, core]).astype(jnp.int32), *early, *freqs)
-    last, high = tie((own[3], high))
-    phi = pl.pallas_call(
-        functools.partial(late_kernel, columns=columns, scale=scale),
-        out_shape=jax.ShapeDtypeStruct((features, clips), jnp.bfloat16),
-        in_specs=[anywhere] * 3 + [vmem] * 3,
-        out_specs=vmem,
-        scratch_shapes=[
-            pltpu.VMEM((features, clips), jnp.float32),
-            pltpu.VMEM((2 * columns, clips), jnp.int16),
-            pltpu.VMEM((2 * columns, clips), jnp.bfloat16),
-            pltpu.VMEM((2 * columns, clips), jnp.bfloat16),
-            pltpu.SemaphoreType.DMA((1,)),
-            pltpu.SemaphoreType.DMA((2,)),
+    last, freq_last = tie((own[3], freq_last))
+    outputs = cast.shape[0]
+    phi, keep, send = pl.pallas_call(
+        functools.partial(late_kernel, scale=scale),
+        grid=(clips // tile,),
+        out_shape=(
+            jax.ShapeDtypeStruct((features, clips), jnp.bfloat16),
+            jax.ShapeDtypeStruct((outputs // 2, clips), jnp.float32),
+            jax.ShapeDtypeStruct((outputs // 2, clips), jnp.bfloat16),
+        ),
+        in_specs=[
+            by_clips(features),
+            by_clips(columns),
+            by_clips(columns),
+            whole(2, features, 2 * columns),
+            whole(features, 1),
+            whole(outputs, features),
         ],
+        out_specs=(by_clips(features), by_clips(outputs // 2), by_clips(outputs // 2)),
+        scratch_shapes=[pltpu.VMEM((2 * columns, tile), jnp.bfloat16)] * 2,
         compiler_params=pltpu.CompilerParams(vmem_limit_bytes=VMEM_BYTES),
         cost_estimate=pl.CostEstimate(
             flops=6 * features * 2 * columns * clips, bytes_accessed=6 * features * clips, transcendentals=0
         ),
         name="late_angles",
-    )(summed, last, core_swap(last), high, low, column)
-    return phi, rest
+    )(summed, last, core_swap(last), freq_last, column, cast)
+    return phi, keep, send, betas
 
 
 def phi_by_ring(embed_code, freq_code, column, scale, line, core, clip, prepare):
@@ -248,7 +239,11 @@
     embed_high, embed_low = split(embed_all)
     freq_high, freq_low = split(freq_all)
     total = dot0(freq_high, embed_high) + (dot0(freq_high, embed_low) + dot0(freq_low, embed_high))
-    return scaled_cos(total * PER_TURN + column, scale), prepare(freqs)
+    phi = scaled_cos(total * PER_TURN + column, scale)
+    betas, cast = prepare(freqs)
+    logits = mix(cast, phi)
+    half = logits.shape[0] // 2
+    return phi, logits[:half], logits[half:].astype(jnp.bfloat16), betas
 
 
 def per_device(embeds, frequencies, phases, weights, labels):
@@ -291,9 +286,8 @@
             return code.astype(jnp.float32) * (WEIGHT_BOUND / CODE_MAX)
 
         own, sent = lax.optimization_barrier((ordered(core), ordered(1 - core)))
-        casts = lax.optimization_barrier((decode(own).astype(jnp.bfloat16), decode(sent).astype(jnp.bfloat16)))
-        targets = lax.dynamic_slice_in_dim(labels.T, feat * block, block, 0).astype(jnp.float32)
-        return decode(own), decode(core_swap(sent)), casts, targets
+        cast = lax.optimization_barrier(decode(jnp.concatenate([own, sent])).astype(jnp.bfloat16))
+        return (decode(own), decode(core_swap(sent))), cast
 
     def share_of(parts):
         parts = parts.reshape(places, block, -1)
@@ -312,29 +306,30 @@
 
     by_kernels = places == 4 and n_clip == 4 and columns % 16 == 0 and slab == 2 * columns
     phi_of = phi_by_kernels if by_kernels else phi_by_ring
-    phi, (beta_own, beta_other, casts, targets) = phi_of(
+    phi, keep, send, (beta_own, beta_other) = phi_of(
         embed_code, freq_code, column, scale, line, core, clip, prepare
     )
-    there = core_swap(mix(casts[1], phi).astype(jnp.bfloat16))
-    parts = lax.optimization_barrier(mix(casts[0], phi)) + there.astype(jnp.float32)
+    targets = lax.dynamic_slice_in_dim(labels.T, feat * block, block, 0).astype(jnp.float32)
+    there = core_swap(send)
+    parts = keep + there.astype(jnp.float32)
     phi_other = core_swap(lax.optimization_barrier((phi, there))[0])
-    moved_own = moved_other = 0.0
+    phi_both = lax.optimization_barrier(jnp.concatenate([phi, phi_other]))
+    beta = jnp.concatenate([beta_own, beta_other], axis=1)
+    moved = 0.0
     for step in range(STEPS):
         share = (jax.nn.sigmoid(add_up(*share_of(parts))) - targets).astype(jnp.bfloat16)
         found = {k: line_swap(share, k) for k in farthest_first(places)}
         residual = jnp.concatenate([share] + [found[k] for k in range(1, places)])
-        grad = jnp.concatenate([gradient_of(residual, phi), gradient_of(residual, phi_other)], axis=1)
+        grad = gradient_of(residual, phi_both)
         sent = grad.astype(jnp.bfloat16)
         for k in farthest_first(n_clip):
             grad = grad + clip_swap(sent, k).astype(jnp.float32)
-        moved_own = moved_own + 0.25 * grad[:, :features]
-        moved_other = moved_other + 0.25 * grad[:, features:]
-        parts = mix((beta_own - moved_own).astype(jnp.bfloat16), phi) + mix(
-            (beta_other - moved_other).astype(jnp.bfloat16), phi_other
-        )
+        moved = moved + 0.25 * grad
+        cast = lax.optimization_barrier((beta - moved).astype(jnp.bfloat16))
+        parts = mix(cast, phi_both)
     total, found = share_of(parts)
-    ours = moved_own.reshape(places, block, features)
-    theirs = core_swap(moved_other).reshape(places, block, features)
+    ours = moved[:, :features].reshape(places, block, features)
+    theirs = core_swap(moved[:, features:]).reshape(places, block, features)
     rows = []
     for b in range(per_clip):
         k = line ^ (clip * per_clip + b)

time: 114 us -> 111 us (0.974)
  local copies, waits for them, and re-layouts: 8.63 us -> 5.11 us
  other arithmetic: 8.82 us -> 7.29 us
    unnamed x64 -> x48, local copies, waits for them, and re-layouts: 7.37 us -> 4.68 us
    convert_element_type x3, other arithmetic: 1.39 us -> 3.26 us  [encode(): return jnp.round(x * (CODE_MAX / bound)).astype(jnp.int16)]
    pallas_call x1, Pallas kernels: 10.2 us -> 8.61 us  [phi_by_kernels(): pl.pallas_call(functools.partial(early_kernel, n_embeds=len(early), n_fre...]
    concatenate x0 -> x1, other arithmetic: none -> 1.56 us  [per_device(): phi_both = lax.optimization_barrier(jnp.concatenate([phi, phi_other]))]
    add x3 -> x0, other arithmetic: 1.44 us -> none  [the longest x2 1.38 us: per_device(): grad = grad + clip_swap(sent, k).astype(jnp.float32)]
    convert_element_type x4 -> x3, other arithmetic: 1.71 us -> 0.34 us  [the longest x2 0.28 us: per_device(): cast = lax.optimization_barrier((beta - moved).astype(jnp.bfloat16))]
    dot_general x6 -> x2, matrix products: 2.06 us -> 2.91 us  [mix(): return jnp.dot(a, b, preferred_element_type=jnp.float32)]
  transfers between devices with their start and end apart: 38 -> 38, of which waited for: 19 -> 23; matrix products, arithmetic and copies ran while one was open for 8% -> 6% of each run, Pallas kernels for 9% -> 8%
where the time goes in v5:
time: 111 us; the launch traced here: 110 us
  starting transfers between devices  45.9 us (41%)
  waiting for transfers between devices  32.5 us (29%)
  Pallas kernels  13.5 us (12%)
  other arithmetic  7.29 us (7%)
  local copies, waits for them, and re-layouts  5.11 us (5%)
  matrix products  4.75 us (4%)
    ppermute x15, starting transfers between devices, line_swap(): return lax.ppermute(x, 'feat', [(i, i ^ 2 * k) for i in range(n)])  22.3 us
    ppermute x12, waiting for transfers between devices, clip_swap(): return lax.ppermute(x, 'clip', [(i, i ^ k) for i in range(n)])  16.4 us
    ppermute x12, starting transfers between devices, clip_swap(): return lax.ppermute(x, 'clip', [(i, i ^ k) for i in range(n)])  14.2 us
    ppermute x15, waiting for transfers between devices, line_swap(): return lax.ppermute(x, 'feat', [(i, i ^ 2 * k) for i in range(n)])  12.6 us
    pallas_call x1, Pallas kernels, phi_by_kernels(): pl.pallas_call(functools.partial(early_kernel, n_embeds=len(early), n_fre...  8.61 us
    ppermute x3, starting transfers between devices, line_move(): lax.ppermute(x, 'feat', [(2 * a + c, 2 * b + c) for a, b in pairs for c i...  8.19 us
    pallas_call x1, Pallas kernels, phi_by_kernels(): pl.pallas_call(functools.partial(late_kernel, scale=scale), grid=(clips /...  4.93 us
    unnamed x48, local copies, waits for them, and re-layouts  4.68 us
  transfers between devices with their start and end apart: 38, of which 23 were waited for; matrix products, arithmetic and copies ran while one was open for 6% of the time, Pallas kernels for 8%

profile of v5, /device:TPU:0, one launch (start us, length us, event | category | flops | bytes accessed | tf_op | source)
XLA Modules:
  0.0 110.0 jit_solution(1896567069977879068)
XLA Ops:
  0.7 1.2 %fusion.refs_0_ = s16[144,1024]{1,0:T(8,128)(2,1)S(1)} fusion(f32[1024,144]{0,1:T(8,128)} %param.5), kind=kLoop, calls=%fused_computation.10 | loop fusion | flops 442368 | bytes 884736 | tf_op jit(solution)/shard_map/convert_element_type | solution.py:32
  1.9 4.1 %collective-permute-start.1 = (s16[144,1024]{1,0:T(8,128)(2,1)S(1)}, s16[144,1024]{1,0:T(8,128)(2,1)S(1)}, u32[]{:S(2)}, u32[]{:S(2)}) collective-permute-start(s16[144,1024]{1,0:T(8,128)(2,1)S(1)} %fusion.refs_0_), channel_id=1, source_target_pairs={{0,4},{1,5},{4,6},{5,7},{6,2},{7,3},{2,0},{3,1},{8,12},{9,13},{12,... | collective-permute-start | bytes 884744 | tf_op jit(solution)/shard_map/ppermute | solution.py:65
  6.0 1.2 %round-nearest-even_convert_fusion.1 = (s16[144,640]{1,0:T(8,128)(2,1)S(1)}, s16[144,640]{1,0:T(8,128)(2,1)S(1)}) fusion(f32[288,640]{1,0:T(8,128)} %param.6), kind=kLoop, calls=%fused_computation.2 | loop fusion | flops 552960 | bytes 1105920 | tf_op jit(solution)/shard_map/convert_element_type | solution.py:32
  7.2 0.8 fusion.39
  8.1 1.6 %collective-permute-start.4 = (s16[160,640]{1,0:T(8,128)(2,1)S(1)}, s16[160,640]{1,0:T(8,128)(2,1)S(1)}, u32[]{:S(2)}, u32[]{:S(2)}) collective-permute-start(s16[160,640]{1,0:T(8,128)(2,1)S(1)} %pad_add_fusion.refs_6_), channel_id=1, source_target_pairs={{0,8},{8,0},{16,24},{24,16},{1,9},{9,1},{17,25},{25,17},{2,10},{10... | collective-permute-start | bytes 614408 | tf_op jit(solution)/shard_map/ppermute | solution.py:70
  9.6 1.6 %collective-permute-start.7 = (s16[160,640]{1,0:T(8,128)(2,1)S(1)}, s16[160,640]{1,0:T(8,128)(2,1)S(1)}, u32[]{:S(2)}, u32[]{:S(2)}) collective-permute-start(s16[160,640]{1,0:T(8,128)(2,1)S(1)} %pad_add_fusion.1.refs_7_), channel_id=1, source_target_pairs={{0,16},{8,24},{16,0},{24,8},{1,17},{9,25},{17,1},{25,9},{2,18},{10... | collective-permute-start | bytes 614408 | tf_op jit(solution)/shard_map/ppermute | solution.py:70
  11.2 0.5 collective-permute-start.5
  11.8 0.5 collective-permute-start.6
  12.3 3.9 %collective-permute-done.4.refs_8_ = s16[160,640]{1,0:T(8,128)(2,1)S(1)} collective-permute-done((s16[160,640]{1,0:T(8,128)(2,1)S(1)}, s16[160,640]{1,0:T(8,128)(2,1)S(1)}, u32[]{:S(2)}, u32[]{:S(2)}) %collective-permute-start.4) | collective-permute-done | bytes 204832 | tf_op jit(solution)/shard_map/ppermute | solution.py:70
  16.1 1.5 %collective-permute-start.8 = (s16[160,640]{1,0:T(8,128)(2,1)S(1)}, s16[160,640]{1,0:T(8,128)(2,1)S(1)}, u32[]{:S(2)}, u32[]{:S(2)}) collective-permute-start(s16[160,640]{1,0:T(8,128)(2,1)S(1)} %collective-permute-done.4.refs_8_), channel_id=1, source_target_pairs={{0,16},{8,24},{16,0},{24,8},{1,17},{9,25},{17,1},{25,9},{2,18},{10... | collective-permute-start | bytes 614408 | tf_op jit(solution)/shard_map/ppermute | solution.py:70
  17.7 1.4 %collective-permute-start.9 = (s16[160,640]{1,0:T(8,128)(2,1)S(1)}, s16[160,640]{1,0:T(8,128)(2,1)S(1)}, u32[]{:S(2)}, u32[]{:S(2)}) collective-permute-start(s16[160,640]{1,0:T(8,128)(2,1)S(1)} %collective-permute-done.7.refs_11_), channel_id=1, source_target_pairs={{0,8},{8,0},{16,24},{24,16},{1,9},{9,1},{17,25},{25,17},{2,10},{10... | collective-permute-start | bytes 614408 | tf_op jit(solution)/shard_map/ppermute | solution.py:70
  19.2 1.6 %collective-permute-start.3 = (s16[144,1024]{1,0:T(8,128)(2,1)S(1)}, s16[144,1024]{1,0:T(8,128)(2,1)S(1)}, u32[]{:S(2)}, u32[]{:S(2)}) collective-permute-start(s16[144,1024]{1,0:T(8,128)(2,1)S(1)} %collective-permute-done.1.refs_2_), channel_id=1, source_target_pairs={{0,4},{1,5},{4,6},{5,7},{6,2},{7,3},{2,0},{3,1},{8,12},{9,13},{12,... | collective-permute-start | bytes 884744 | tf_op jit(solution)/shard_map/ppermute | solution.py:65
  20.9 0.6 pad_add_fusion.4.at_ref
  21.5 0.6 collective-permute-done.6.refs_10_
  22.1 2.6 %collective-permute-done.8.refs_12_ = s16[160,640]{1,0:T(8,128)(2,1)S(1)} collective-permute-done((s16[160,640]{1,0:T(8,128)(2,1)S(1)}, s16[160,640]{1,0:T(8,128)(2,1)S(1)}, u32[]{:S(2)}, u32[]{:S(2)}) %collective-permute-start.8) | collective-permute-done | bytes 204832 | tf_op jit(solution)/shard_map/ppermute | solution.py:70
  24.8 1.1 %collective-permute-done.3.refs_4_ = s16[144,1024]{1,0:T(8,128)(2,1)S(1)} collective-permute-done((s16[144,1024]{1,0:T(8,128)(2,1)S(1)}, s16[144,1024]{1,0:T(8,128)(2,1)S(1)}, u32[]{:S(2)}, u32[]{:S(2)}) %collective-permute-start.3) | collective-permute-done | bytes 294944 | tf_op jit(solution)/shard_map/ppermute | solution.py:65
  26.0 2.5 %collective-permute-start.11 = (s16[144,1024]{1,0:T(8,128)(2,1)S(1)}, s16[144,1024]{1,0:T(8,128)(2,1)S(1)}, u32[]{:S(2)}, u32[]{:S(2)}) collective-permute-start(s16[144,1024]{1,0:T(8,128)(2,1)S(1)} %collective-permute-done.3.refs_4_), channel_id=1, source_target_pairs={{0,4},{1,5},{4,6},{5,7},{6,2},{7,3},{2,0},{3,1},{8,12},{9,13},{12,... | collective-permute-start | bytes 884744 | tf_op jit(solution)/shard_map/ppermute | solution.py:65
  28.6 0.6 copy-done.17
  29.4 0.7 copy-done.19
  30.1 8.6 %early_angles.1 = (f32[640,1024]{1,0:T(8,128)}, bf16[2,640,288]{2,1,0:T(8,128)(2,1)}) custom-call(s32[3]{0:T(128)} %pad_add_fusion.4.at_ref, s16[144,1024]{1,0:T(8,128)(2,1)} %copy-done.5, s16[144,1024]{1,0:T(8,128)(2,1)} %copy-done.17, s16[144,1024]{1,0:T(8,128)(2,1)} %copy-done.15, s16[144,1024]{1,0:T(8,128)(2,1)} %copy-done.18, ...), custom_call_target="tpu_custom_call" | custom-call | flops 3523215360 | bytes 5242880 | tf_op jit(solution)/shard_map/early_angles/pallas_call | solution.py:164
  39.1 1.3 %collective-permute-done.12.other_ref = s16[144,1024]{1,0:T(8,128)(2,1)S(1)} collective-permute-done((s16[144,1024]{1,0:T(8,128)(2,1)S(1)}, s16[144,1024]{1,0:T(8,128)(2,1)S(1)}, u32[]{:S(2)}, u32[]{:S(2)}) %collective-permute-start.12) | collective-permute-done | bytes 294944 | tf_op jit(solution)/shard_map/ppermute | solution.py:56
  40.4 1.7 %copy-done.1 = f32[640,1024]{1,0:T(8,128)S(1)} copy-done((f32[640,1024]{1,0:T(8,128)S(1)}, f32[640,1024]{1,0:T(8,128)}, u32[]{:S(2)}) %copy-start.1) | copy-done | bytes 2621464
  42.1 1.2 %copy-done.2 = bf16[2,640,288]{2,1,0:T(8,128)(2,1)S(1)} copy-done((bf16[2,640,288]{2,1,0:T(8,128)(2,1)S(1)}, bf16[2,640,288]{2,1,0:T(8,128)(2,1)}, u32[]{:S(2)}) %copy-start.2) | copy-done | bytes 737304
  43.3 4.9 %late_angles.1 = (bf16[640,1024]{1,0:T(8,128)(2,1)S(1)}, f32[64,1024]{1,0:T(8,128)S(1)}, bf16[64,1024]{1,0:T(8,128)(2,1)S(1)}) custom-call(f32[640,1024]{1,0:T(8,128)S(1)} %copy-done.1, s16[144,1024]{1,0:T(8,128)(2,1)S(1)} %collective-permute-done.11.own_ref, s16[144,1024]{1,0:T(8,128)(2,1)S(1)} %collective-permute-done.12.other_ref, ...), custom_call_target="tpu_custom_call" | custom-call | flops 1132462080 | bytes 3932160 | tf_op jit(solution)/shard_map/late_angles/pallas_call | solution.py:188
  48.5 1.1 %collective-permute-done.13 = bf16[64,1024]{1,0:T(8,128)(2,1)S(1)} collective-permute-done((bf16[64,1024]{1,0:T(8,128)(2,1)S(1)}, bf16[64,1024]{1,0:T(8,128)(2,1)S(1)}, u32[]{:S(2)}, u32[]{:S(2)}) %collective-permute-start.13) | collective-permute-done | bytes 131104 | tf_op jit(solution)/shard_map/ppermute | solution.py:56
  50.2 0.3 collective-permute-start.24
  50.9 0.8 collective-permute-start.15
  51.7 3.4 %collective-permute-start.16 = (bf16[16,1024]{1,0:T(8,128)(2,1)S(1)}, bf16[16,1024]{1,0:T(8,128)(2,1)S(1)}, u32[]{:S(2)}, u32[]{:S(2)}) collective-permute-start(bf16[16,1024]{1,0:T(8,128)(2,1)S(1)} %get-tuple-element.69), channel_id=1, source_target_pairs={{0,2},{1,3},{2,0},{3,1},{4,6},{5,7},{6,4},{7,5},{8,10},{9,11},{10,... | collective-permute-start | bytes 98312 | tf_op jit(solution)/shard_map/ppermute | solution.py:61
  55.1 1.6 %collective-permute-done.14 = bf16[16,1024]{1,0:T(8,128)(2,1)S(1)} collective-permute-done((bf16[16,1024]{1,0:T(8,128)(2,1)S(1)}, bf16[16,1024]{1,0:T(8,128)(2,1)S(1)}, u32[]{:S(2)}, u32[]{:S(2)}) %collective-permute-start.14) | collective-permute-done | bytes 32800 | tf_op jit(solution)/shard_map/ppermute | solution.py:61
  57.1 2.0 %collective-permute-start.17 = (bf16[16,1024]{1,0:T(8,128)(2,1)S(1)}, bf16[16,1024]{1,0:T(8,128)(2,1)S(1)}, u32[]{:S(2)}, u32[]{:S(2)}) collective-permute-start(bf16[16,1024]{1,0:T(8,128)(2,1)S(1)} %fusion.32), channel_id=1, source_target_pairs={{0,2},{1,3},{2,0},{3,1},{4,6},{5,7},{6,4},{7,5},{8,10},{9,11},{10,... | collective-permute-start | bytes 98312 | tf_op jit(solution)/shard_map/ppermute | solution.py:61
  59.1 0.9 collective-permute-start.18
  60.0 1.5 %collective-permute-start.19 = (bf16[16,1024]{1,0:T(8,128)(2,1)S(1)}, bf16[16,1024]{1,0:T(8,128)(2,1)S(1)}, u32[]{:S(2)}, u32[]{:S(2)}) collective-permute-start(bf16[16,1024]{1,0:T(8,128)(2,1)S(1)} %fusion.32), channel_id=1, source_target_pairs={{0,6},{1,7},{2,4},{3,5},{4,2},{5,3},{6,0},{7,1},{8,14},{9,15},{10,... | collective-permute-start | bytes 98312 | tf_op jit(solution)/shard_map/ppermute | solution.py:61
  61.6 1.6 %pad_maximum_fusion = bf16[1280,1024]{1,0:T(8,128)(2,1)S(1)} fusion(bf16[640,1024]{1,0:T(8,128)(2,1)} %collective-permute-done.20, bf16[640,1024]{1,0:T(8,128)(2,1)S(1)} %get-tuple-element.41), kind=kLoop, calls=%fused_computation | loop fusion | flops 5242880 | bytes 5242880 | tf_op jit(solution)/shard_map/concatenate | solution.py:316
  63.1 0.8 collective-permute-done.18
  63.9 1.8 %collective-permute-done.19 = bf16[16,1024]{1,0:T(8,128)(2,1)S(1)} collective-permute-done((bf16[16,1024]{1,0:T(8,128)(2,1)S(1)}, bf16[16,1024]{1,0:T(8,128)(2,1)S(1)}, u32[]{:S(2)}, u32[]{:S(2)}) %collective-permute-start.19) | collective-permute-done | bytes 32800 | tf_op jit(solution)/shard_map/ppermute | solution.py:61
  65.7 0.9 fusion.47
  66.6 1.6 %collective-permute-start.21 = (bf16[64,1280]{1,0:T(8,128)(2,1)S(1)}, bf16[64,1280]{1,0:T(8,128)(2,1)S(1)}, u32[]{:S(2)}, u32[]{:S(2)}) collective-permute-start(bf16[64,1280]{1,0:T(8,128)(2,1)S(1)} %get-tuple-element.73), channel_id=1, source_target_pairs={{0,24},{8,16},{16,8},{24,0},{1,25},{9,17},{17,9},{25,1},{2,26},{10... | collective-permute-start | bytes 491528 | tf_op jit(solution)/shard_map/ppermute | solution.py:70
  68.3 0.5 collective-permute-start.22
  68.8 1.4 %collective-permute-start.23 = (bf16[64,1280]{1,0:T(8,128)(2,1)S(1)}, bf16[64,1280]{1,0:T(8,128)(2,1)S(1)}, u32[]{:S(2)}, u32[]{:S(2)}) collective-permute-start(bf16[64,1280]{1,0:T(8,128)(2,1)S(1)} %get-tuple-element.73), channel_id=1, source_target_pairs={{0,8},{8,0},{16,24},{24,16},{1,9},{9,1},{17,25},{25,17},{2,10},{10... | collective-permute-start | bytes 491528 | tf_op jit(solution)/shard_map/ppermute | solution.py:70
  70.2 2.8 %collective-permute-done.21 = bf16[64,1280]{1,0:T(8,128)(2,1)S(1)} collective-permute-done((bf16[64,1280]{1,0:T(8,128)(2,1)S(1)}, bf16[64,1280]{1,0:T(8,128)(2,1)S(1)}, u32[]{:S(2)}, u32[]{:S(2)}) %collective-permute-start.21) | collective-permute-done | bytes 163872 | tf_op jit(solution)/shard_map/ppermute | solution.py:70
  73.0 1.7 %collective-permute-done.22 = bf16[64,1280]{1,0:T(8,128)(2,1)S(1)} collective-permute-done((bf16[64,1280]{1,0:T(8,128)(2,1)S(1)}, bf16[64,1280]{1,0:T(8,128)(2,1)S(1)}, u32[]{:S(2)}, u32[]{:S(2)}) %collective-permute-start.22) | collective-permute-done | bytes 163872 | tf_op jit(solution)/shard_map/ppermute | solution.py:70
  74.8 0.6 fusion.48
  75.4 1.9 %collective-permute-start.25 = (bf16[16,1024]{1,0:T(8,128)(2,1)S(1)}, bf16[16,1024]{1,0:T(8,128)(2,1)S(1)}, u32[]{:S(2)}, u32[]{:S(2)}) collective-permute-start(bf16[16,1024]{1,0:T(8,128)(2,1)S(1)} %get-tuple-element.65), channel_id=1, source_target_pairs={{0,6},{1,7},{2,4},{3,5},{4,2},{5,3},{6,0},{7,1},{8,14},{9,15},{10,... | collective-permute-start | bytes 98312 | tf_op jit(solution)/shard_map/ppermute | solution.py:61
  77.3 2.6 %collective-permute-start.27 = (bf16[16,1024]{1,0:T(8,128)(2,1)S(1)}, bf16[16,1024]{1,0:T(8,128)(2,1)S(1)}, u32[]{:S(2)}, u32[]{:S(2)}) collective-permute-start(bf16[16,1024]{1,0:T(8,128)(2,1)S(1)} %get-tuple-element.66), channel_id=1, source_target_pairs={{0,2},{1,3},{2,0},{3,1},{4,6},{5,7},{6,4},{7,5},{8,10},{9,11},{10,... | collective-permute-start | bytes 98312 | tf_op jit(solution)/shard_map/ppermute | solution.py:61
  79.8 1.3 %collective-permute-done.25 = bf16[16,1024]{1,0:T(8,128)(2,1)S(1)} collective-permute-done((bf16[16,1024]{1,0:T(8,128)(2,1)S(1)}, bf16[16,1024]{1,0:T(8,128)(2,1)S(1)}, u32[]{:S(2)}, u32[]{:S(2)}) %collective-permute-start.25) | collective-permute-done | bytes 32800 | tf_op jit(solution)/shard_map/ppermute | solution.py:61
  81.2 1.2 %collective-permute-done.26 = bf16[16,1024]{1,0:T(8,128)(2,1)S(1)} collective-permute-done((bf16[16,1024]{1,0:T(8,128)(2,1)S(1)}, bf16[16,1024]{1,0:T(8,128)(2,1)S(1)}, u32[]{:S(2)}, u32[]{:S(2)}) %collective-permute-start.26) | collective-permute-done | bytes 32800 | tf_op jit(solution)/shard_map/ppermute | solution.py:61
  82.5 1.4 %collective-permute-start.28 = (bf16[16,1024]{1,0:T(8,128)(2,1)S(1)}, bf16[16,1024]{1,0:T(8,128)(2,1)S(1)}, u32[]{:S(2)}, u32[]{:S(2)}) collective-permute-start(bf16[16,1024]{1,0:T(8,128)(2,1)S(1)} %fusion.33), channel_id=1, source_target_pairs={{0,2},{1,3},{2,0},{3,1},{4,6},{5,7},{6,4},{7,5},{8,10},{9,11},{10,... | collective-permute-start | bytes 98312 | tf_op jit(solution)/shard_map/ppermute | solution.py:61
  83.9 0.9 collective-permute-start.29
  84.8 2.2 %collective-permute-start.30 = (bf16[16,1024]{1,0:T(8,128)(2,1)S(1)}, bf16[16,1024]{1,0:T(8,128)(2,1)S(1)}, u32[]{:S(2)}, u32[]{:S(2)}) collective-permute-start(bf16[16,1024]{1,0:T(8,128)(2,1)S(1)} %fusion.33), channel_id=1, source_target_pairs={{0,6},{1,7},{2,4},{3,5},{4,2},{5,3},{6,0},{7,1},{8,14},{9,15},{10,... | collective-permute-start | bytes 98312 | tf_op jit(solution)/shard_map/ppermute | solution.py:61
  86.9 2.1 %collective-permute-done.29 = bf16[16,1024]{1,0:T(8,128)(2,1)S(1)} collective-permute-done((bf16[16,1024]{1,0:T(8,128)(2,1)S(1)}, bf16[16,1024]{1,0:T(8,128)(2,1)S(1)}, u32[]{:S(2)}, u32[]{:S(2)}) %collective-permute-start.29) | collective-permute-done | bytes 32800 | tf_op jit(solution)/shard_map/ppermute | solution.py:61
  89.0 1.5 %collective-permute-done.30 = bf16[16,1024]{1,0:T(8,128)(2,1)S(1)} collective-permute-done((bf16[16,1024]{1,0:T(8,128)(2,1)S(1)}, bf16[16,1024]{1,0:T(8,128)(2,1)S(1)}, u32[]{:S(2)}, u32[]{:S(2)}) %collective-permute-start.30) | collective-permute-done | bytes 32800 | tf_op jit(solution)/shard_map/ppermute | solution.py:61
  90.5 0.9 fusion.49
  91.4 1.6 %collective-permute-start.31 = (bf16[64,1280]{1,0:T(8,128)(2,1)S(1)}, bf16[64,1280]{1,0:T(8,128)(2,1)S(1)}, u32[]{:S(2)}, u32[]{:S(2)}) collective-permute-start(bf16[64,1280]{1,0:T(8,128)(2,1)S(1)} %get-tuple-element.77), channel_id=1, source_target_pairs={{0,24},{8,16},{16,8},{24,0},{1,25},{9,17},{17,9},{25,1},{2,26},{10... | collective-permute-start | bytes 491528 | tf_op jit(solution)/shard_map/ppermute | solution.py:70
  93.0 1.3 %collective-permute-start.32 = (bf16[64,1280]{1,0:T(8,128)(2,1)S(1)}, bf16[64,1280]{1,0:T(8,128)(2,1)S(1)}, u32[]{:S(2)}, u32[]{:S(2)}) collective-permute-start(bf16[64,1280]{1,0:T(8,128)(2,1)S(1)} %get-tuple-element.77), channel_id=1, source_target_pairs={{0,16},{8,24},{16,0},{24,8},{1,17},{9,25},{17,1},{25,9},{2,18},{10... | collective-permute-start | bytes 491528 | tf_op jit(solution)/shard_map/ppermute | solution.py:70
  94.3 0.6 collective-permute-start.33
  94.9 2.8 %collective-permute-done.31 = bf16[64,1280]{1,0:T(8,128)(2,1)S(1)} collective-permute-done((bf16[64,1280]{1,0:T(8,128)(2,1)S(1)}, bf16[64,1280]{1,0:T(8,128)(2,1)S(1)}, u32[]{:S(2)}, u32[]{:S(2)}) %collective-permute-start.31) | collective-permute-done | bytes 163872 | tf_op jit(solution)/shard_map/ppermute | solution.py:70
  97.8 1.7 %collective-permute-done.32 = bf16[64,1280]{1,0:T(8,128)(2,1)S(1)} collective-permute-done((bf16[64,1280]{1,0:T(8,128)(2,1)S(1)}, bf16[64,1280]{1,0:T(8,128)(2,1)S(1)}, u32[]{:S(2)}, u32[]{:S(2)}) %collective-permute-start.32) | collective-permute-done | bytes 163872 | tf_op jit(solution)/shard_map/ppermute | solution.py:70
  99.9 2.3 %fusion.50 = (bf16[64,1024]{1,0:T(8,128)(2,1)S(1)}, f32[64,1024]{1,0:T(8,128)S(1)}) fusion(bf16[64,1280]{1,0:T(8,128)(2,1)S(1)} %get-tuple-element.44, bf16[1280,1024]{1,0:T(8,128)(2,1)} %copy-done.3), kind=kOutput, calls=%fused_computation.94 | convolution fusion | flops 167837696 | bytes 3178496 | tf_op jit(solution)/shard_map/dot_general | solution.py:51
  102.3 2.0 %collective-permute-start.35 = (bf16[16,1024]{1,0:T(8,128)(2,1)S(1)}, bf16[16,1024]{1,0:T(8,128)(2,1)S(1)}, u32[]{:S(2)}, u32[]{:S(2)}) collective-permute-start(bf16[16,1024]{1,0:T(8,128)(2,1)S(1)} %get-tuple-element.62), channel_id=1, source_target_pairs={{0,6},{1,7},{2,4},{3,5},{4,2},{5,3},{6,0},{7,1},{8,14},{9,15},{10,... | collective-permute-start | bytes 98312 | tf_op jit(solution)/shard_map/ppermute | solution.py:61
  104.3 2.5 %collective-permute-start.37 = (bf16[16,1024]{1,0:T(8,128)(2,1)S(1)}, bf16[16,1024]{1,0:T(8,128)(2,1)S(1)}, u32[]{:S(2)}, u32[]{:S(2)}) collective-permute-start(bf16[16,1024]{1,0:T(8,128)(2,1)S(1)} %get-tuple-element.63), channel_id=1, source_target_pairs={{0,2},{1,3},{2,0},{3,1},{4,6},{5,7},{6,4},{7,5},{8,10},{9,11},{10,... | collective-permute-start | bytes 98312 | tf_op jit(solution)/shard_map/ppermute | solution.py:61
  106.8 0.6 fusion.17
  107.5 0.9 collective-permute-done.35
  108.4 1.0 collective-permute-done.36
  109.4 0.6 add_bitcast_fusion
  (95 shorter events, 3.4 us)
Async XLA Ops:
  0.6 49.2 %copy-start = (s32[1024,128]{1,0:T(8,128)S(1)}, s32[1024,128]{1,0:T(8,128)}, u32[]{:S(2)}) copy-start(s32[1024,128]{1,0:T(8,128)} %param.9) | copy-start | bytes 1572868
  0.6 20.1 %copy-start.8 = (f32[640]{0:T(1024)S(1)}, f32[640]{0:T(1024)}, u32[]{:S(2)}) copy-start(f32[640]{0:T(1024)} %param.7) | copy-start | bytes 7684
  1.9 26.7 %copy-start.5 = (s16[144,1024]{1,0:T(8,128)(2,1)}, s16[144,1024]{1,0:T(8,128)(2,1)S(1)}, u32[]{:S(2)}) copy-start(s16[144,1024]{1,0:T(8,128)(2,1)S(1)} %fusion.refs_0_) | copy-start | bytes 884740
  1.9 17.3 %collective-permute-start.1 = (s16[144,1024]{1,0:T(8,128)(2,1)S(1)}, s16[144,1024]{1,0:T(8,128)(2,1)S(1)}, u32[]{:S(2)}, u32[]{:S(2)}) collective-permute-start(s16[144,1024]{1,0:T(8,128)(2,1)S(1)} %fusion.refs_0_), channel_id=1, source_target_pairs={{0,4},{1,5},{4,6},{5,7},{6,2},{7,3},{2,0},{3,1},{8,12},{9,13},{12,... | collective-permute-start | bytes 884744 | tf_op jit(solution)/shard_map/ppermute | solution.py:65
  8.0 20.5 %copy-start.6 = (s16[160,640]{1,0:T(8,128)(2,1)}, s16[160,640]{1,0:T(8,128)(2,1)S(1)}, u32[]{:S(2)}) copy-start(s16[160,640]{1,0:T(8,128)(2,1)S(1)} %pad_add_fusion.refs_6_) | copy-start | bytes 614404
  8.1 8.1 %collective-permute-start.4 = (s16[160,640]{1,0:T(8,128)(2,1)S(1)}, s16[160,640]{1,0:T(8,128)(2,1)S(1)}, u32[]{:S(2)}, u32[]{:S(2)}) collective-permute-start(s16[160,640]{1,0:T(8,128)(2,1)S(1)} %pad_add_fusion.refs_6_), channel_id=1, source_target_pairs={{0,8},{8,0},{16,24},{24,16},{1,9},{9,1},{17,25},{25,17},{2,10},{10... | collective-permute-start | bytes 614408 | tf_op jit(solution)/shard_map/ppermute | solution.py:70
  9.6 18.9 %copy-start.7 = (s16[160,640]{1,0:T(8,128)(2,1)}, s16[160,640]{1,0:T(8,128)(2,1)S(1)}, u32[]{:S(2)}) copy-start(s16[160,640]{1,0:T(8,128)(2,1)S(1)} %pad_add_fusion.1.refs_7_) | copy-start | bytes 614404
  9.6 8.1 %collective-permute-start.7 = (s16[160,640]{1,0:T(8,128)(2,1)S(1)}, s16[160,640]{1,0:T(8,128)(2,1)S(1)}, u32[]{:S(2)}, u32[]{:S(2)}) collective-permute-start(s16[160,640]{1,0:T(8,128)(2,1)S(1)} %pad_add_fusion.1.refs_7_), channel_id=1, source_target_pairs={{0,16},{8,24},{16,0},{24,8},{1,17},{9,25},{17,1},{25,9},{2,18},{10... | collective-permute-start | bytes 614408 | tf_op jit(solution)/shard_map/ppermute | solution.py:70
  11.2 10.2 %collective-permute-start.5 = (s16[160,640]{1,0:T(8,128)(2,1)S(1)}, s16[160,640]{1,0:T(8,128)(2,1)S(1)}, u32[]{:S(2)}, u32[]{:S(2)}) collective-permute-start(s16[160,640]{1,0:T(8,128)(2,1)S(1)} %pad_add_fusion.1.refs_7_), channel_id=1, source_target_pairs={{0,8},{8,0},{16,24},{24,16},{1,9},{9,1},{17,25},{25,17},{2,10},{10... | collective-permute-start | bytes 614408 | tf_op jit(solution)/shard_map/ppermute | solution.py:70
  11.8 10.4 %collective-permute-start.6 = (s16[160,640]{1,0:T(8,128)(2,1)S(1)}, s16[160,640]{1,0:T(8,128)(2,1)S(1)}, u32[]{:S(2)}, u32[]{:S(2)}) collective-permute-start(s16[160,640]{1,0:T(8,128)(2,1)S(1)} %pad_add_fusion.refs_6_), channel_id=1, source_target_pairs={{0,16},{8,24},{16,0},{24,8},{1,17},{9,25},{17,1},{25,9},{2,18},{10... | collective-permute-start | bytes 614408 | tf_op jit(solution)/shard_map/ppermute | solution.py:70
  16.1 12.4 %copy-start.9 = (s16[160,640]{1,0:T(8,128)(2,1)}, s16[160,640]{1,0:T(8,128)(2,1)S(1)}, u32[]{:S(2)}) copy-start(s16[160,640]{1,0:T(8,128)(2,1)S(1)} %collective-permute-done.4.refs_8_) | copy-start | bytes 614404
  16.1 8.6 %collective-permute-start.8 = (s16[160,640]{1,0:T(8,128)(2,1)S(1)}, s16[160,640]{1,0:T(8,128)(2,1)S(1)}, u32[]{:S(2)}, u32[]{:S(2)}) collective-permute-start(s16[160,640]{1,0:T(8,128)(2,1)S(1)} %collective-permute-done.4.refs_8_), channel_id=1, source_target_pairs={{0,16},{8,24},{16,0},{24,8},{1,17},{9,25},{17,1},{25,9},{2,18},{10... | collective-permute-start | bytes 614408 | tf_op jit(solution)/shard_map/ppermute | solution.py:70
  17.7 10.8 %copy-start.10 = (s16[160,640]{1,0:T(8,128)(2,1)}, s16[160,640]{1,0:T(8,128)(2,1)S(1)}, u32[]{:S(2)}) copy-start(s16[160,640]{1,0:T(8,128)(2,1)S(1)} %collective-permute-done.7.refs_11_) | copy-start | bytes 614404
  17.7 7.0 %collective-permute-start.9 = (s16[160,640]{1,0:T(8,128)(2,1)S(1)}, s16[160,640]{1,0:T(8,128)(2,1)S(1)}, u32[]{:S(2)}, u32[]{:S(2)}) collective-permute-start(s16[160,640]{1,0:T(8,128)(2,1)S(1)} %collective-permute-done.7.refs_11_), channel_id=1, source_target_pairs={{0,8},{8,0},{16,24},{24,16},{1,9},{9,1},{17,25},{25,17},{2,10},{10... | collective-permute-start | bytes 614408 | tf_op jit(solution)/shard_map/ppermute | solution.py:70
  19.1 9.4 %copy-start.15 = (s16[144,1024]{1,0:T(8,128)(2,1)}, s16[144,1024]{1,0:T(8,128)(2,1)S(1)}, u32[]{:S(2)}) copy-start(s16[144,1024]{1,0:T(8,128)(2,1)S(1)} %collective-permute-done.1.refs_2_) | copy-start | bytes 884740
  19.2 6.7 %collective-permute-start.3 = (s16[144,1024]{1,0:T(8,128)(2,1)S(1)}, s16[144,1024]{1,0:T(8,128)(2,1)S(1)}, u32[]{:S(2)}, u32[]{:S(2)}) collective-permute-start(s16[144,1024]{1,0:T(8,128)(2,1)S(1)} %collective-permute-done.1.refs_2_), channel_id=1, source_target_pairs={{0,4},{1,5},{4,6},{5,7},{6,2},{7,3},{2,0},{3,1},{8,12},{9,13},{12,... | collective-permute-start | bytes 884744 | tf_op jit(solution)/shard_map/ppermute | solution.py:65
  21.5 7.1 %copy-start.11 = (s16[160,640]{1,0:T(8,128)(2,1)}, s16[160,640]{1,0:T(8,128)(2,1)S(1)}, u32[]{:S(2)}) copy-start(s16[160,640]{1,0:T(8,128)(2,1)S(1)} %collective-permute-done.5.refs_9_) | copy-start | bytes 614404
  21.5 7.0 %collective-permute-start = (s16[144,1024]{1,0:T(8,128)(2,1)S(1)}, s16[144,1024]{1,0:T(8,128)(2,1)S(1)}, u32[]{:S(2)}, u32[]{:S(2)}) collective-permute-start(s16[144,1024]{1,0:T(8,128)(2,1)S(1)} %fusion.refs_0_), channel_id=1, source_target_pairs={{0,1},{1,0},{2,3},{3,2},{4,5},{5,4},{6,7},{7,6},{8,9},{9,8},{10,11... | collective-permute-start | bytes 884744 | tf_op jit(solution)/shard_map/ppermute | solution.py:56
  22.1 6.5 %copy-start.12 = (s16[160,640]{1,0:T(8,128)(2,1)}, s16[160,640]{1,0:T(8,128)(2,1)S(1)}, u32[]{:S(2)}) copy-start(s16[160,640]{1,0:T(8,128)(2,1)S(1)} %collective-permute-done.6.refs_10_) | copy-start | bytes 614404
  22.1 6.4 %collective-permute-start.2 = (s16[144,1024]{1,0:T(8,128)(2,1)S(1)}, s16[144,1024]{1,0:T(8,128)(2,1)S(1)}, u32[]{:S(2)}, u32[]{:S(2)}) collective-permute-start(s16[144,1024]{1,0:T(8,128)(2,1)S(1)} %collective-permute-done.1.refs_2_), channel_id=1, source_target_pairs={{0,1},{1,0},{2,3},{3,2},{4,5},{5,4},{6,7},{7,6},{8,9},{9,8},{10,11... | collective-permute-start | bytes 884744 | tf_op jit(solution)/shard_map/ppermute | solution.py:56
  24.7 3.9 %copy-start.13 = (s16[160,640]{1,0:T(8,128)(2,1)}, s16[160,640]{1,0:T(8,128)(2,1)S(1)}, u32[]{:S(2)}) copy-start(s16[160,640]{1,0:T(8,128)(2,1)S(1)} %collective-permute-done.8.refs_12_) | copy-start | bytes 614404
  24.8 3.9 %copy-start.14 = (s16[160,640]{1,0:T(8,128)(2,1)}, s16[160,640]{1,0:T(8,128)(2,1)S(1)}, u32[]{:S(2)}) copy-start(s16[160,640]{1,0:T(8,128)(2,1)S(1)} %collective-permute-done.9.refs_13_) | copy-start | bytes 614404
  25.9 2.8 %copy-start.16 = (s16[144,1024]{1,0:T(8,128)(2,1)}, s16[144,1024]{1,0:T(8,128)(2,1)S(1)}, u32[]{:S(2)}) copy-start(s16[144,1024]{1,0:T(8,128)(2,1)S(1)} %collective-permute-done.3.refs_4_) | copy-start | bytes 884740
  25.9 2.7 %collective-permute-start.10 = (s16[144,1024]{1,0:T(8,128)(2,1)S(1)}, s16[144,1024]{1,0:T(8,128)(2,1)S(1)}, u32[]{:S(2)}, u32[]{:S(2)}) collective-permute-start(s16[144,1024]{1,0:T(8,128)(2,1)S(1)} %collective-permute-done.3.refs_4_), channel_id=1, source_target_pairs={{0,1},{1,0},{2,3},{3,2},{4,5},{5,4},{6,7},{7,6},{8,9},{9,8},{10,11... | collective-permute-start | bytes 884744 | tf_op jit(solution)/shard_map/ppermute | solution.py:56
  26.0 12.7 %collective-permute-start.11 = (s16[144,1024]{1,0:T(8,128)(2,1)S(1)}, s16[144,1024]{1,0:T(8,128)(2,1)S(1)}, u32[]{:S(2)}, u32[]{:S(2)}) collective-permute-start(s16[144,1024]{1,0:T(8,128)(2,1)S(1)} %collective-permute-done.3.refs_4_), channel_id=1, source_target_pairs={{0,4},{1,5},{4,6},{5,7},{6,2},{7,3},{2,0},{3,1},{8,12},{9,13},{12,... | collective-permute-start | bytes 884744 | tf_op jit(solution)/shard_map/ppermute | solution.py:65
  28.5 0.7 copy-start.17
  28.5 0.8 copy-start.18
  29.4 0.7 copy-start.19
  38.7 1.6 %collective-permute-start.12 = (s16[144,1024]{1,0:T(8,128)(2,1)S(1)}, s16[144,1024]{1,0:T(8,128)(2,1)S(1)}, u32[]{:S(2)}, u32[]{:S(2)}) collective-permute-start(s16[144,1024]{1,0:T(8,128)(2,1)S(1)} %collective-permute-done.11.own_ref), channel_id=1, source_target_pairs={{0,1},{1,0},{2,3},{3,2},{4,5},{5,4},{6,7},{7,6},{8,9},{9,8},{10,11... | collective-permute-start | bytes 884744 | tf_op jit(solution)/shard_map/ppermute | solution.py:56
  40.4 1.7 %copy-start.1 = (f32[640,1024]{1,0:T(8,128)S(1)}, f32[640,1024]{1,0:T(8,128)}, u32[]{:S(2)}) copy-start(f32[640,1024]{1,0:T(8,128)} %get-tuple-element.32.sum_ref) | copy-start | bytes 7864324
  42.1 1.2 %copy-start.2 = (bf16[2,640,288]{2,1,0:T(8,128)(2,1)S(1)}, bf16[2,640,288]{2,1,0:T(8,128)(2,1)}, u32[]{:S(2)}) copy-start(bf16[2,640,288]{2,1,0:T(8,128)(2,1)} %get-tuple-element.35.last_ref) | copy-start | bytes 2211844
  48.2 1.4 %collective-permute-start.13 = (bf16[64,1024]{1,0:T(8,128)(2,1)S(1)}, bf16[64,1024]{1,0:T(8,128)(2,1)S(1)}, u32[]{:S(2)}, u32[]{:S(2)}) collective-permute-start(bf16[64,1024]{1,0:T(8,128)(2,1)S(1)} %get-tuple-element.39), channel_id=1, source_target_pairs={{0,1},{1,0},{2,3},{3,2},{4,5},{5,4},{6,7},{7,6},{8,9},{9,8},{10,11... | collective-permute-start | bytes 393224 | tf_op jit(solution)/shard_map/ppermute | solution.py:56
  49.7 11.9 %collective-permute-start.20 = (bf16[640,1024]{1,0:T(8,128)(2,1)S(1)}, bf16[640,1024]{1,0:T(8,128)(2,1)}, u32[]{:S(2)}, u32[]{:S(2)}) collective-permute-start(bf16[640,1024]{1,0:T(8,128)(2,1)S(1)} %get-tuple-element.41), channel_id=1, source_target_pairs={{0,1},{1,0},{2,3},{3,2},{4,5},{5,4},{6,7},{7,6},{8,9},{9,8},{10,11... | collective-permute-start | bytes 3932168 | tf_op jit(solution)/shard_map/ppermute | solution.py:56
  50.2 20.0 %collective-permute-start.24 = (s16[64,640]{1,0:T(8,128)(2,1)S(1)}, s16[64,640]{1,0:T(8,128)(2,1)S(1)}, u32[]{:S(2)}, u32[]{:S(2)}) collective-permute-start(s16[64,640]{1,0:T(8,128)(2,1)S(1)} %get-tuple-element.37), channel_id=1, source_target_pairs={{0,1},{1,0},{2,3},{3,2},{4,5},{5,4},{6,7},{7,6},{8,9},{9,8},{10,11... | collective-permute-start | bytes 245768 | tf_op jit(solution)/shard_map/ppermute | solution.py:56
  50.6 6.1 %collective-permute-start.14 = (bf16[16,1024]{1,0:T(8,128)(2,1)S(1)}, bf16[16,1024]{1,0:T(8,128)(2,1)S(1)}, u32[]{:S(2)}, u32[]{:S(2)}) collective-permute-start(bf16[16,1024]{1,0:T(8,128)(2,1)S(1)} %get-tuple-element.68), channel_id=1, source_target_pairs={{0,6},{1,7},{2,4},{3,5},{4,2},{5,3},{6,0},{7,1},{8,14},{9,15},{10,... | collective-permute-start | bytes 98312 | tf_op jit(solution)/shard_map/ppermute | solution.py:61
  50.9 5.8 %collective-permute-start.15 = (bf16[16,1024]{1,0:T(8,128)(2,1)S(1)}, bf16[16,1024]{1,0:T(8,128)(2,1)S(1)}, u32[]{:S(2)}, u32[]{:S(2)}) collective-permute-start(bf16[16,1024]{1,0:T(8,128)(2,1)S(1)} %get-tuple-element.70), channel_id=1, source_target_pairs={{0,4},{1,5},{2,6},{3,7},{4,0},{5,1},{6,2},{7,3},{8,12},{9,13},{10,... | collective-permute-start | bytes 98312 | tf_op jit(solution)/shard_map/ppermute | solution.py:61
  51.7 5.3 %collective-permute-start.16 = (bf16[16,1024]{1,0:T(8,128)(2,1)S(1)}, bf16[16,1024]{1,0:T(8,128)(2,1)S(1)}, u32[]{:S(2)}, u32[]{:S(2)}) collective-permute-start(bf16[16,1024]{1,0:T(8,128)(2,1)S(1)} %get-tuple-element.69), channel_id=1, source_target_pairs={{0,2},{1,3},{2,0},{3,1},{4,6},{5,7},{6,4},{7,5},{8,10},{9,11},{10,... | collective-permute-start | bytes 98312 | tf_op jit(solution)/shard_map/ppermute | solution.py:61
  57.1 6.0 %collective-permute-start.17 = (bf16[16,1024]{1,0:T(8,128)(2,1)S(1)}, bf16[16,1024]{1,0:T(8,128)(2,1)S(1)}, u32[]{:S(2)}, u32[]{:S(2)}) collective-permute-start(bf16[16,1024]{1,0:T(8,128)(2,1)S(1)} %fusion.32), channel_id=1, source_target_pairs={{0,2},{1,3},{2,0},{3,1},{4,6},{5,7},{6,4},{7,5},{8,10},{9,11},{10,... | collective-permute-start | bytes 98312 | tf_op jit(solution)/shard_map/ppermute | solution.py:61
  59.1 4.8 %collective-permute-start.18 = (bf16[16,1024]{1,0:T(8,128)(2,1)S(1)}, bf16[16,1024]{1,0:T(8,128)(2,1)S(1)}, u32[]{:S(2)}, u32[]{:S(2)}) collective-permute-start(bf16[16,1024]{1,0:T(8,128)(2,1)S(1)} %fusion.32), channel_id=1, source_target_pairs={{0,4},{1,5},{2,6},{3,7},{4,0},{5,1},{6,2},{7,3},{8,12},{9,13},{10,... | collective-permute-start | bytes 98312 | tf_op jit(solution)/shard_map/ppermute | solution.py:61
  60.0 5.7 %collective-permute-start.19 = (bf16[16,1024]{1,0:T(8,128)(2,1)S(1)}, bf16[16,1024]{1,0:T(8,128)(2,1)S(1)}, u32[]{:S(2)}, u32[]{:S(2)}) collective-permute-start(bf16[16,1024]{1,0:T(8,128)(2,1)S(1)} %fusion.32), channel_id=1, source_target_pairs={{0,6},{1,7},{2,4},{3,5},{4,2},{5,3},{6,0},{7,1},{8,14},{9,15},{10,... | collective-permute-start | bytes 98312 | tf_op jit(solution)/shard_map/ppermute | solution.py:61
  63.1 27.4 %copy-start.3 = (bf16[1280,1024]{1,0:T(8,128)(2,1)}, bf16[1280,1024]{1,0:T(8,128)(2,1)S(1)}, u32[]{:S(2)}) copy-start(bf16[1280,1024]{1,0:T(8,128)(2,1)S(1)} %pad_maximum_fusion) | copy-start | bytes 7864324
  66.6 6.4 %collective-permute-start.21 = (bf16[64,1280]{1,0:T(8,128)(2,1)S(1)}, bf16[64,1280]{1,0:T(8,128)(2,1)S(1)}, u32[]{:S(2)}, u32[]{:S(2)}) collective-permute-start(bf16[64,1280]{1,0:T(8,128)(2,1)S(1)} %get-tuple-element.73), channel_id=1, source_target_pairs={{0,24},{8,16},{16,8},{24,0},{1,25},{9,17},{17,9},{25,1},{2,26},{10... | collective-permute-start | bytes 491528 | tf_op jit(solution)/shard_map/ppermute | solution.py:70
  68.3 6.4 %collective-permute-start.22 = (bf16[64,1280]{1,0:T(8,128)(2,1)S(1)}, bf16[64,1280]{1,0:T(8,128)(2,1)S(1)}, u32[]{:S(2)}, u32[]{:S(2)}) collective-permute-start(bf16[64,1280]{1,0:T(8,128)(2,1)S(1)} %get-tuple-element.73), channel_id=1, source_target_pairs={{0,16},{8,24},{16,0},{24,8},{1,17},{9,25},{17,1},{25,9},{2,18},{10... | collective-permute-start | bytes 491528 | tf_op jit(solution)/shard_map/ppermute | solution.py:70
  68.8 5.9 %collective-permute-start.23 = (bf16[64,1280]{1,0:T(8,128)(2,1)S(1)}, bf16[64,1280]{1,0:T(8,128)(2,1)S(1)}, u32[]{:S(2)}, u32[]{:S(2)}) collective-permute-start(bf16[64,1280]{1,0:T(8,128)(2,1)S(1)} %get-tuple-element.73), channel_id=1, source_target_pairs={{0,8},{8,0},{16,24},{24,16},{1,9},{9,1},{17,25},{25,17},{2,10},{10... | collective-permute-start | bytes 491528 | tf_op jit(solution)/shard_map/ppermute | solution.py:70
  75.4 5.8 %collective-permute-start.25 = (bf16[16,1024]{1,0:T(8,128)(2,1)S(1)}, bf16[16,1024]{1,0:T(8,128)(2,1)S(1)}, u32[]{:S(2)}, u32[]{:S(2)}) collective-permute-start(bf16[16,1024]{1,0:T(8,128)(2,1)S(1)} %get-tuple-element.65), channel_id=1, source_target_pairs={{0,6},{1,7},{2,4},{3,5},{4,2},{5,3},{6,0},{7,1},{8,14},{9,15},{10,... | collective-permute-start | bytes 98312 | tf_op jit(solution)/shard_map/ppermute | solution.py:61
  77.3 5.1 %collective-permute-start.26 = (bf16[16,1024]{1,0:T(8,128)(2,1)S(1)}, bf16[16,1024]{1,0:T(8,128)(2,1)S(1)}, u32[]{:S(2)}, u32[]{:S(2)}) collective-permute-start(bf16[16,1024]{1,0:T(8,128)(2,1)S(1)} %get-tuple-element.67), channel_id=1, source_target_pairs={{0,4},{1,5},{2,6},{3,7},{4,0},{5,1},{6,2},{7,3},{8,12},{9,13},{10,... | collective-permute-start | bytes 98312 | tf_op jit(solution)/shard_map/ppermute | solution.py:61
  77.3 5.2 %collective-permute-start.27 = (bf16[16,1024]{1,0:T(8,128)(2,1)S(1)}, bf16[16,1024]{1,0:T(8,128)(2,1)S(1)}, u32[]{:S(2)}, u32[]{:S(2)}) collective-permute-start(bf16[16,1024]{1,0:T(8,128)(2,1)S(1)} %get-tuple-element.66), channel_id=1, source_target_pairs={{0,2},{1,3},{2,0},{3,1},{4,6},{5,7},{6,4},{7,5},{8,10},{9,11},{10,... | collective-permute-start | bytes 98312 | tf_op jit(solution)/shard_map/ppermute | solution.py:61
  82.5 4.5 %collective-permute-start.28 = (bf16[16,1024]{1,0:T(8,128)(2,1)S(1)}, bf16[16,1024]{1,0:T(8,128)(2,1)S(1)}, u32[]{:S(2)}, u32[]{:S(2)}) collective-permute-start(bf16[16,1024]{1,0:T(8,128)(2,1)S(1)} %fusion.33), channel_id=1, source_target_pairs={{0,2},{1,3},{2,0},{3,1},{4,6},{5,7},{6,4},{7,5},{8,10},{9,11},{10,... | collective-permute-start | bytes 98312 | tf_op jit(solution)/shard_map/ppermute | solution.py:61
  83.9 5.2 %collective-permute-start.29 = (bf16[16,1024]{1,0:T(8,128)(2,1)S(1)}, bf16[16,1024]{1,0:T(8,128)(2,1)S(1)}, u32[]{:S(2)}, u32[]{:S(2)}) collective-permute-start(bf16[16,1024]{1,0:T(8,128)(2,1)S(1)} %fusion.33), channel_id=1, source_target_pairs={{0,4},{1,5},{2,6},{3,7},{4,0},{5,1},{6,2},{7,3},{8,12},{9,13},{10,... | collective-permute-start | bytes 98312 | tf_op jit(solution)/shard_map/ppermute | solution.py:61
  84.8 5.7 %collective-permute-start.30 = (bf16[16,1024]{1,0:T(8,128)(2,1)S(1)}, bf16[16,1024]{1,0:T(8,128)(2,1)S(1)}, u32[]{:S(2)}, u32[]{:S(2)}) collective-permute-start(bf16[16,1024]{1,0:T(8,128)(2,1)S(1)} %fusion.33), channel_id=1, source_target_pairs={{0,6},{1,7},{2,4},{3,5},{4,2},{5,3},{6,0},{7,1},{8,14},{9,15},{10,... | collective-permute-start | bytes 98312 | tf_op jit(solution)/shard_map/ppermute | solution.py:61
  91.4 6.4 %collective-permute-start.31 = (bf16[64,1280]{1,0:T(8,128)(2,1)S(1)}, bf16[64,1280]{1,0:T(8,128)(2,1)S(1)}, u32[]{:S(2)}, u32[]{:S(2)}) collective-permute-start(bf16[64,1280]{1,0:T(8,128)(2,1)S(1)} %get-tuple-element.77), channel_id=1, source_target_pairs={{0,24},{8,16},{16,8},{24,0},{1,25},{9,17},{17,9},{25,1},{2,26},{10... | collective-permute-start | bytes 491528 | tf_op jit(solution)/shard_map/ppermute | solution.py:70
  93.0 6.4 %collective-permute-start.32 = (bf16[64,1280]{1,0:T(8,128)(2,1)S(1)}, bf16[64,1280]{1,0:T(8,128)(2,1)S(1)}, u32[]{:S(2)}, u32[]{:S(2)}) collective-permute-start(bf16[64,1280]{1,0:T(8,128)(2,1)S(1)} %get-tuple-element.77), channel_id=1, source_target_pairs={{0,16},{8,24},{16,0},{24,8},{1,17},{9,25},{17,1},{25,9},{2,18},{10... | collective-permute-start | bytes 491528 | tf_op jit(solution)/shard_map/ppermute | solution.py:70
  94.3 5.3 %collective-permute-start.33 = (bf16[64,1280]{1,0:T(8,128)(2,1)S(1)}, bf16[64,1280]{1,0:T(8,128)(2,1)S(1)}, u32[]{:S(2)}, u32[]{:S(2)}) collective-permute-start(bf16[64,1280]{1,0:T(8,128)(2,1)S(1)} %get-tuple-element.77), channel_id=1, source_target_pairs={{0,8},{8,0},{16,24},{24,16},{1,9},{9,1},{17,25},{25,17},{2,10},{10... | collective-permute-start | bytes 491528 | tf_op jit(solution)/shard_map/ppermute | solution.py:70
  99.9 7.0 %copy-start.4 = (f32[640,32]{0,1:T(8,128)S(1)}, f32[640,32]{0,1:T(8,128)}, u32[]{:S(2)}) copy-start(f32[640,32]{0,1:T(8,128)} %param.8) | copy-start | bytes 245764
  102.2 4.6 %collective-permute-start.34 = (f32[64,640]{1,0:T(8,128)S(1)}, f32[64,640]{1,0:T(8,128)S(1)}, u32[]{:S(2)}, u32[]{:S(2)}) collective-permute-start(f32[64,640]{1,0:T(8,128)S(1)} %get-tuple-element.53), channel_id=1, source_target_pairs={{0,1},{1,0},{2,3},{3,2},{4,5},{5,4},{6,7},{7,6},{8,9},{9,8},{10,11... | collective-permute-start | bytes 491528 | tf_op jit(solution)/shard_map/ppermute | solution.py:56
  102.3 6.0 %collective-permute-start.35 = (bf16[16,1024]{1,0:T(8,128)(2,1)S(1)}, bf16[16,1024]{1,0:T(8,128)(2,1)S(1)}, u32[]{:S(2)}, u32[]{:S(2)}) collective-permute-start(bf16[16,1024]{1,0:T(8,128)(2,1)S(1)} %get-tuple-element.62), channel_id=1, source_target_pairs={{0,6},{1,7},{2,4},{3,5},{4,2},{5,3},{6,0},{7,1},{8,14},{9,15},{10,... | collective-permute-start | bytes 98312 | tf_op jit(solution)/shard_map/ppermute | solution.py:61
  104.3 5.1 %collective-permute-start.36 = (bf16[16,1024]{1,0:T(8,128)(2,1)S(1)}, bf16[16,1024]{1,0:T(8,128)(2,1)S(1)}, u32[]{:S(2)}, u32[]{:S(2)}) collective-permute-start(bf16[16,1024]{1,0:T(8,128)(2,1)S(1)} %get-tuple-element.64), channel_id=1, source_target_pairs={{0,4},{1,5},{2,6},{3,7},{4,0},{5,1},{6,2},{7,3},{8,12},{9,13},{10,... | collective-permute-start | bytes 98312 | tf_op jit(solution)/shard_map/ppermute | solution.py:61
  104.3 5.1 %collective-permute-start.37 = (bf16[16,1024]{1,0:T(8,128)(2,1)S(1)}, bf16[16,1024]{1,0:T(8,128)(2,1)S(1)}, u32[]{:S(2)}, u32[]{:S(2)}) collective-permute-start(bf16[16,1024]{1,0:T(8,128)(2,1)S(1)} %get-tuple-element.63), channel_id=1, source_target_pairs={{0,2},{1,3},{2,0},{3,1},{4,6},{5,7},{6,4},{7,5},{8,10},{9,11},{10,... | collective-permute-start | bytes 98312 | tf_op jit(solution)/shard_map/ppermute | solution.py:61

commit v6 on v5

--- a/solution.py
+++ b/solution.py
@@ -14,7 +14,7 @@
 CODE_MAX = 32766.0
 LANES = 128
 VMEM_BYTES = 16 * 1024 * 1024
-EARLY_VMEM_BYTES = 56 * 1024 * 1024
+EARLY_VMEM_BYTES = 36 * 1024 * 1024
 WEIGHT_BOUND = 6.0
 COS_TURNS = (
     0.9999999890590243,
@@ -107,7 +107,7 @@
             f_all[:, start : start + LANES] = high
             f_all[:, depth + start : depth + start + LANES] = high
             f_all[:, 2 * depth + start : 2 * depth + start + LANES] = low
-        last_ref[0], last_ref[1] = halves(freq_code[depth:, :].T.astype(jnp.float32))
+        last_ref[...] = freq_code[depth:, :].T
 
     for i, ref in enumerate(embeds):
         high, low = halves(ref[...].astype(jnp.float32))
@@ -117,15 +117,21 @@
 
 
 def late_kernel(
-    sum_ref, own_ref, other_ref, last_ref, phase_ref, beta_ref, phi_ref, keep_ref, send_ref, e_high, e_low, *, scale
+    sum_ref, own_ref, other_ref, last_ref, phase_ref, beta_ref, phi_ref, keep_ref, send_ref, e_all, f_all, *, scale
 ):
     columns = own_ref.shape[0]
+    depth = 2 * columns
     for i, ref in enumerate((own_ref, other_ref)):
-        rows = slice(i * columns, (i + 1) * columns)
-        e_high[rows, :], e_low[rows, :] = halves(ref[...].astype(jnp.float32))
-    total = sum_ref[...] + (
-        mix(last_ref[0], e_high[...]) + (mix(last_ref[0], e_low[...]) + mix(last_ref[1], e_high[...]))
-    )
+        high, low = halves(ref[...].astype(jnp.float32))
+        for start, value in ((0, high), (depth, low), (2 * depth, high)):
+            e_all[start + i * columns : start + (i + 1) * columns, :] = value
+
+    @pl.when(pl.program_id(0) == 0)
+    def _():
+        high, low = halves(last_ref[...].astype(jnp.float32))
+        f_all[:, :depth], f_all[:, depth : 2 * depth], f_all[:, 2 * depth :] = high, high, low
+
+    total = sum_ref[...] + mix(f_all[...], e_all[...])
     phi = scaled_cos(total * PER_TURN + phase_ref[...], scale)
     phi_ref[...] = phi
     logits = mix(beta_ref[...], phi)
@@ -153,7 +159,7 @@
     early = [x for pair in zip(own[:3], other) for x in pair]
     used = len(early) * columns
     depth = -(-used // LANES) * LANES
-    tile = 256 if clips % 256 == 0 else clips
+    tile = 512 if clips % 512 == 0 else clips
 
     def whole(*shape):
         return pl.BlockSpec(shape, lambda i: (0,) * len(shape))
@@ -166,12 +172,12 @@
         grid=(clips // tile,),
         out_shape=(
             jax.ShapeDtypeStruct((features, clips), jnp.float32),
-            jax.ShapeDtypeStruct((2, features, 2 * columns), jnp.bfloat16),
+            jax.ShapeDtypeStruct((features, 2 * columns), jnp.int16),
         ),
         in_specs=[pl.BlockSpec(memory_space=pltpu.SMEM)]
         + [by_clips(columns)] * len(early)
         + [whole(*x.shape) for x in freqs],
-        out_specs=(by_clips(features), whole(2, features, 2 * columns)),
+        out_specs=(by_clips(features), whole(features, 2 * columns)),
         scratch_shapes=[
             pltpu.VMEM((depth + 2 * columns, features), jnp.int16),
             pltpu.VMEM((features, 3 * depth), jnp.bfloat16),
@@ -197,12 +203,15 @@
             by_clips(features),
             by_clips(columns),
             by_clips(columns),
-            whole(2, features, 2 * columns),
+            whole(features, 2 * columns),
             whole(features, 1),
             whole(outputs, features),
         ],
         out_specs=(by_clips(features), by_clips(outputs // 2), by_clips(outputs // 2)),
-        scratch_shapes=[pltpu.VMEM((2 * columns, tile), jnp.bfloat16)] * 2,
+        scratch_shapes=[
+            pltpu.VMEM((6 * columns, tile), jnp.bfloat16),
+            pltpu.VMEM((features, 6 * columns), jnp.bfloat16),
+        ],
         compiler_params=pltpu.CompilerParams(vmem_limit_bytes=VMEM_BYTES),
         cost_estimate=pl.CostEstimate(
             flops=6 * features * 2 * columns * clips, bytes_accessed=6 * features * clips, transcendentals=0
@@ -277,7 +286,7 @@
             rows = lax.dynamic_index_in_dim(stacked, side, 1, keepdims=False).reshape(-1, block, features)
             found = []
             for k in range(places):
-                place = line ^ k
+                place = line ^ ((places - k) % places)
                 at = ((place // per_clip) ^ clip) * per_clip + place % per_clip
                 found.append(lax.dynamic_index_in_dim(rows, at, 0, keepdims=False))
             return jnp.concatenate(found)
@@ -293,7 +302,7 @@
         parts = parts.reshape(places, block, -1)
         half = parts.astype(jnp.bfloat16)
         total = parts[0]
-        found = [line_swap(half[k], k) for k in farthest_first(places)]
+        found = [line_swap(half[k], places - k) for k in range(1, places)]
         return total, found
 
     def add_up(total, found):
@@ -318,8 +327,7 @@
     moved = 0.0
     for step in range(STEPS):
         share = (jax.nn.sigmoid(add_up(*share_of(parts))) - targets).astype(jnp.bfloat16)
-        found = {k: line_swap(share, k) for k in farthest_first(places)}
-        residual = jnp.concatenate([share] + [found[k] for k in range(1, places)])
+        residual = jnp.concatenate([share] + [line_swap(share, places - k) for k in range(1, places)])
         grad = gradient_of(residual, phi_both)
         sent = grad.astype(jnp.bfloat16)
         for k in farthest_first(n_clip):
@@ -332,7 +340,7 @@
     theirs = core_swap(moved[:, features:]).reshape(places, block, features)
     rows = []
     for b in range(per_clip):
-        k = line ^ (clip * per_clip + b)
+        k = (places - (line ^ (clip * per_clip + b))) % places
         mine = lax.dynamic_index_in_dim(ours, k, 0, keepdims=False)
         their = lax.dynamic_index_in_dim(theirs, k, 0, keepdims=False)
         rows += [jnp.where(core == 0, mine, their), jnp.where(core == 0, their, mine)]

time: 111 us -> 103 us (0.928)
  local copies, waits for them, and re-layouts: 5.11 us -> 0.68 us
  Pallas kernels: 13.5 us -> 10.4 us
  waiting for transfers between devices: 32.5 us -> 34 us
    unnamed x48 -> x16, local copies, waits for them, and re-layouts: 4.68 us -> 0.25 us
    pallas_call x1, Pallas kernels: 8.61 us -> 5.97 us  [phi_by_kernels(): pl.pallas_call(functools.partial(early_kernel, n_embeds=len(early), n_fre...]
  transfers between devices with their start and end apart: 38 -> 38, of which waited for: 23 -> 22; matrix products, arithmetic and copies ran while one was open for 6% -> 6% of each run, Pallas kernels for 8% -> 6%
where the time goes in v6:
time: 103 us
  starting transfers between devices  45.5 us (44%)
  waiting for transfers between devices  34 us (33%)
  Pallas kernels  10.4 us (10%)
  other arithmetic  6.78 us (7%)
  matrix products  4.75 us (5%)
    ppermute x15, starting transfers between devices, line_swap(): return lax.ppermute(x, 'feat', [(i, i ^ 2 * k) for i in range(n)])  22.3 us
    ppermute x12, waiting for transfers between devices, clip_swap(): return lax.ppermute(x, 'clip', [(i, i ^ k) for i in range(n)])  16.6 us
    ppermute x12, starting transfers between devices, clip_swap(): return lax.ppermute(x, 'clip', [(i, i ^ k) for i in range(n)])  14.2 us
    ppermute x15, waiting for transfers between devices, line_swap(): return lax.ppermute(x, 'feat', [(i, i ^ 2 * k) for i in range(n)])  12.7 us
    ppermute x3, starting transfers between devices, line_move(): lax.ppermute(x, 'feat', [(2 * a + c, 2 * b + c) for a, b in pairs for c i...  8.19 us
    pallas_call x1, Pallas kernels, phi_by_kernels(): pl.pallas_call(functools.partial(early_kernel, n_embeds=len(early), n_fre...  5.97 us
    pallas_call x1, Pallas kernels, phi_by_kernels(): pl.pallas_call(functools.partial(late_kernel, scale=scale), grid=(clips /...  4.43 us
    convert_element_type x3, other arithmetic, encode(): return jnp.round(x * (CODE_MAX / bound)).astype(jnp.int16)  3.26 us
  transfers between devices with their start and end apart: 38, of which 22 were waited for; matrix products, arithmetic and copies ran while one was open for 6% of the time, Pallas kernels for 6%

profile of v6, /device:TPU:0, one launch (start us, length us, event | category | flops | bytes accessed | tf_op | source)
XLA Modules:
  0.0 103.1 jit_solution(14343962864108680943)
XLA Ops:
  0.7 1.2 %fusion.refs_0_ = s16[144,1024]{1,0:T(8,128)(2,1)S(1)} fusion(f32[1024,144]{0,1:T(8,128)} %param.5), kind=kLoop, calls=%fused_computation.10 | loop fusion | flops 442368 | bytes 884736 | tf_op jit(solution)/shard_map/convert_element_type | solution.py:32
  1.9 4.1 %collective-permute-start.1 = (s16[144,1024]{1,0:T(8,128)(2,1)S(1)}, s16[144,1024]{1,0:T(8,128)(2,1)S(1)}, u32[]{:S(2)}, u32[]{:S(2)}) collective-permute-start(s16[144,1024]{1,0:T(8,128)(2,1)S(1)} %fusion.refs_0_), channel_id=1, source_target_pairs={{0,4},{1,5},{4,6},{5,7},{6,2},{7,3},{2,0},{3,1},{8,12},{9,13},{12,... | collective-permute-start | bytes 884744 | tf_op jit(solution)/shard_map/ppermute | solution.py:65
  6.0 1.2 %round-nearest-even_convert_fusion.1 = (s16[144,640]{1,0:T(8,128)(2,1)S(1)}, s16[144,640]{1,0:T(8,128)(2,1)S(1)}) fusion(f32[288,640]{1,0:T(8,128)} %param.6), kind=kLoop, calls=%fused_computation.2 | loop fusion | flops 552960 | bytes 1105920 | tf_op jit(solution)/shard_map/convert_element_type | solution.py:32
  7.2 0.8 fusion.39
  8.0 1.6 %collective-permute-start.4 = (s16[160,640]{1,0:T(8,128)(2,1)S(1)}, s16[160,640]{1,0:T(8,128)(2,1)S(1)}, u32[]{:S(2)}, u32[]{:S(2)}) collective-permute-start(s16[160,640]{1,0:T(8,128)(2,1)S(1)} %pad_add_fusion.refs_6_), channel_id=1, source_target_pairs={{0,8},{8,0},{16,24},{24,16},{1,9},{9,1},{17,25},{25,17},{2,10},{10... | collective-permute-start | bytes 614408 | tf_op jit(solution)/shard_map/ppermute | solution.py:70
  9.6 1.6 %collective-permute-start.7 = (s16[160,640]{1,0:T(8,128)(2,1)S(1)}, s16[160,640]{1,0:T(8,128)(2,1)S(1)}, u32[]{:S(2)}, u32[]{:S(2)}) collective-permute-start(s16[160,640]{1,0:T(8,128)(2,1)S(1)} %pad_add_fusion.1.refs_7_), channel_id=1, source_target_pairs={{0,16},{8,24},{16,0},{24,8},{1,17},{9,25},{17,1},{25,9},{2,18},{10... | collective-permute-start | bytes 614408 | tf_op jit(solution)/shard_map/ppermute | solution.py:70
  11.2 0.5 collective-permute-start.5
  11.7 0.5 collective-permute-start.6
  12.2 3.9 %collective-permute-done.4.refs_8_ = s16[160,640]{1,0:T(8,128)(2,1)S(1)} collective-permute-done((s16[160,640]{1,0:T(8,128)(2,1)S(1)}, s16[160,640]{1,0:T(8,128)(2,1)S(1)}, u32[]{:S(2)}, u32[]{:S(2)}) %collective-permute-start.4) | collective-permute-done | bytes 204832 | tf_op jit(solution)/shard_map/ppermute | solution.py:70
  16.1 1.5 %collective-permute-start.8 = (s16[160,640]{1,0:T(8,128)(2,1)S(1)}, s16[160,640]{1,0:T(8,128)(2,1)S(1)}, u32[]{:S(2)}, u32[]{:S(2)}) collective-permute-start(s16[160,640]{1,0:T(8,128)(2,1)S(1)} %collective-permute-done.4.refs_8_), channel_id=1, source_target_pairs={{0,16},{8,24},{16,0},{24,8},{1,17},{9,25},{17,1},{25,9},{2,18},{10... | collective-permute-start | bytes 614408 | tf_op jit(solution)/shard_map/ppermute | solution.py:70
  17.7 1.4 %collective-permute-start.9 = (s16[160,640]{1,0:T(8,128)(2,1)S(1)}, s16[160,640]{1,0:T(8,128)(2,1)S(1)}, u32[]{:S(2)}, u32[]{:S(2)}) collective-permute-start(s16[160,640]{1,0:T(8,128)(2,1)S(1)} %collective-permute-done.7.refs_11_), channel_id=1, source_target_pairs={{0,8},{8,0},{16,24},{24,16},{1,9},{9,1},{17,25},{25,17},{2,10},{10... | collective-permute-start | bytes 614408 | tf_op jit(solution)/shard_map/ppermute | solution.py:70
  19.1 1.6 %collective-permute-start.3 = (s16[144,1024]{1,0:T(8,128)(2,1)S(1)}, s16[144,1024]{1,0:T(8,128)(2,1)S(1)}, u32[]{:S(2)}, u32[]{:S(2)}) collective-permute-start(s16[144,1024]{1,0:T(8,128)(2,1)S(1)} %collective-permute-done.1.refs_2_), channel_id=1, source_target_pairs={{0,4},{1,5},{4,6},{5,7},{6,2},{7,3},{2,0},{3,1},{8,12},{9,13},{12,... | collective-permute-start | bytes 884744 | tf_op jit(solution)/shard_map/ppermute | solution.py:65
  21.0 1.1 %collective-permute-done.6.refs_10_ = s16[160,640]{1,0:T(8,128)(2,1)S(1)} collective-permute-done((s16[160,640]{1,0:T(8,128)(2,1)S(1)}, s16[160,640]{1,0:T(8,128)(2,1)S(1)}, u32[]{:S(2)}, u32[]{:S(2)}) %collective-permute-start.6) | collective-permute-done | bytes 204832 | tf_op jit(solution)/shard_map/ppermute | solution.py:70
  22.1 2.6 %collective-permute-done.8.refs_12_ = s16[160,640]{1,0:T(8,128)(2,1)S(1)} collective-permute-done((s16[160,640]{1,0:T(8,128)(2,1)S(1)}, s16[160,640]{1,0:T(8,128)(2,1)S(1)}, u32[]{:S(2)}, u32[]{:S(2)}) %collective-permute-start.8) | collective-permute-done | bytes 204832 | tf_op jit(solution)/shard_map/ppermute | solution.py:70
  24.7 1.1 %collective-permute-done.3.refs_4_ = s16[144,1024]{1,0:T(8,128)(2,1)S(1)} collective-permute-done((s16[144,1024]{1,0:T(8,128)(2,1)S(1)}, s16[144,1024]{1,0:T(8,128)(2,1)S(1)}, u32[]{:S(2)}, u32[]{:S(2)}) %collective-permute-start.3) | collective-permute-done | bytes 294944 | tf_op jit(solution)/shard_map/ppermute | solution.py:65
  25.9 2.5 %collective-permute-start.11 = (s16[144,1024]{1,0:T(8,128)(2,1)S(1)}, s16[144,1024]{1,0:T(8,128)(2,1)S(1)}, u32[]{:S(2)}, u32[]{:S(2)}) collective-permute-start(s16[144,1024]{1,0:T(8,128)(2,1)S(1)} %collective-permute-done.3.refs_4_), channel_id=1, source_target_pairs={{0,4},{1,5},{4,6},{5,7},{6,2},{7,3},{2,0},{3,1},{8,12},{9,13},{12,... | collective-permute-start | bytes 884744 | tf_op jit(solution)/shard_map/ppermute | solution.py:65
  28.5 6.0 %early_angles.1 = (f32[640,1024]{1,0:T(8,128)S(1)}, s16[640,288]{1,0:T(8,128)(2,1)S(1)}) custom-call(s32[3]{0:T(128)S(1)} %pad_add_fusion.4.at_ref, s16[144,1024]{1,0:T(8,128)(2,1)S(1)} %fusion.refs_0_, s16[144,1024]{1,0:T(8,128)(2,1)S(1)} %collective-permute-done.refs_1_, s16[144,1024]{1,0:T(8,128)(2,1)S(1)} %collective-permute-done.1.refs_2_, ...), custom_call_target="tpu_custom_call" | custom-call | flops 3523215360 | bytes 5242880 | tf_op jit(solution)/shard_map/early_angles/pallas_call | solution.py:170
  34.5 0.9 collective-permute-done.11.own_ref
  35.5 1.5 %collective-permute-done.12.other_ref = s16[144,1024]{1,0:T(8,128)(2,1)S(1)} collective-permute-done((s16[144,1024]{1,0:T(8,128)(2,1)S(1)}, s16[144,1024]{1,0:T(8,128)(2,1)S(1)}, u32[]{:S(2)}, u32[]{:S(2)}) %collective-permute-start.12) | collective-permute-done | bytes 294944 | tf_op jit(solution)/shard_map/ppermute | solution.py:56
  37.0 4.4 %late_angles.1 = (bf16[640,1024]{1,0:T(8,128)(2,1)S(1)}, f32[64,1024]{1,0:T(8,128)S(1)}, bf16[64,1024]{1,0:T(8,128)(2,1)S(1)}) custom-call(f32[640,1024]{1,0:T(8,128)S(1)} %get-tuple-element.32.sum_ref, s16[144,1024]{1,0:T(8,128)(2,1)S(1)} %collective-permute-done.11.own_ref, s16[144,1024]{1,0:T(8,128)(2,1)S(1)} %collective-permute-done.12.other_ref, ...), custom_call_target="tpu_custom_call" | custom-call | flops 1132462080 | bytes 3932160 | tf_op jit(solution)/shard_map/late_angles/pallas_call | solution.py:194
  41.4 0.2 collective-permute-start.13
  41.6 1.2 %collective-permute-done.13 = bf16[64,1024]{1,0:T(8,128)(2,1)S(1)} collective-permute-done((bf16[64,1024]{1,0:T(8,128)(2,1)S(1)}, bf16[64,1024]{1,0:T(8,128)(2,1)S(1)}, u32[]{:S(2)}, u32[]{:S(2)}) %collective-permute-start.13) | collective-permute-done | bytes 131104 | tf_op jit(solution)/shard_map/ppermute | solution.py:56
  43.0 0.2 constant_dynamic-slice_fusion
  43.4 0.4 collective-permute-start.24
  43.8 2.3 %collective-permute-start.14 = (bf16[16,1024]{1,0:T(8,128)(2,1)S(1)}, bf16[16,1024]{1,0:T(8,128)(2,1)S(1)}, u32[]{:S(2)}, u32[]{:S(2)}) collective-permute-start(bf16[16,1024]{1,0:T(8,128)(2,1)S(1)} %get-tuple-element.68), channel_id=1, source_target_pairs={{0,6},{1,7},{2,4},{3,5},{4,2},{5,3},{6,0},{7,1},{8,14},{9,15},{10,... | collective-permute-start | bytes 98312 | tf_op jit(solution)/shard_map/ppermute | solution.py:61
  46.1 1.3 %collective-permute-start.15 = (bf16[16,1024]{1,0:T(8,128)(2,1)S(1)}, bf16[16,1024]{1,0:T(8,128)(2,1)S(1)}, u32[]{:S(2)}, u32[]{:S(2)}) collective-permute-start(bf16[16,1024]{1,0:T(8,128)(2,1)S(1)} %get-tuple-element.70), channel_id=1, source_target_pairs={{0,4},{1,5},{2,6},{3,7},{4,0},{5,1},{6,2},{7,3},{8,12},{9,13},{10,... | collective-permute-start | bytes 98312 | tf_op jit(solution)/shard_map/ppermute | solution.py:61
  47.3 0.9 collective-permute-start.16
  48.3 1.3 %collective-permute-done.14 = bf16[16,1024]{1,0:T(8,128)(2,1)S(1)} collective-permute-done((bf16[16,1024]{1,0:T(8,128)(2,1)S(1)}, bf16[16,1024]{1,0:T(8,128)(2,1)S(1)}, u32[]{:S(2)}, u32[]{:S(2)}) %collective-permute-start.14) | collective-permute-done | bytes 32800 | tf_op jit(solution)/shard_map/ppermute | solution.py:61
  49.6 1.7 %collective-permute-done.15 = bf16[16,1024]{1,0:T(8,128)(2,1)S(1)} collective-permute-done((bf16[16,1024]{1,0:T(8,128)(2,1)S(1)}, bf16[16,1024]{1,0:T(8,128)(2,1)S(1)}, u32[]{:S(2)}, u32[]{:S(2)}) %collective-permute-start.15) | collective-permute-done | bytes 32800 | tf_op jit(solution)/shard_map/ppermute | solution.py:61
  51.5 2.7 %collective-permute-start.17 = (bf16[16,1024]{1,0:T(8,128)(2,1)S(1)}, bf16[16,1024]{1,0:T(8,128)(2,1)S(1)}, u32[]{:S(2)}, u32[]{:S(2)}) collective-permute-start(bf16[16,1024]{1,0:T(8,128)(2,1)S(1)} %fusion.32), channel_id=1, source_target_pairs={{0,6},{1,7},{2,4},{3,5},{4,2},{5,3},{6,0},{7,1},{8,14},{9,15},{10,... | collective-permute-start | bytes 98312 | tf_op jit(solution)/shard_map/ppermute | solution.py:61
  54.2 1.7 %collective-permute-start.19 = (bf16[16,1024]{1,0:T(8,128)(2,1)S(1)}, bf16[16,1024]{1,0:T(8,128)(2,1)S(1)}, u32[]{:S(2)}, u32[]{:S(2)}) collective-permute-start(bf16[16,1024]{1,0:T(8,128)(2,1)S(1)} %fusion.32), channel_id=1, source_target_pairs={{0,2},{1,3},{2,0},{3,1},{4,6},{5,7},{6,4},{7,5},{8,10},{9,11},{10,... | collective-permute-start | bytes 98312 | tf_op jit(solution)/shard_map/ppermute | solution.py:61
  55.9 1.6 %pad_maximum_fusion = bf16[1280,1024]{1,0:T(8,128)(2,1)S(1)} fusion(bf16[640,1024]{1,0:T(8,128)(2,1)} %collective-permute-done.20, bf16[640,1024]{1,0:T(8,128)(2,1)S(1)} %get-tuple-element.41), kind=kLoop, calls=%fused_computation | loop fusion | flops 5242880 | bytes 5242880 | tf_op jit(solution)/shard_map/concatenate | solution.py:325
  57.5 1.5 %collective-permute-done.18 = bf16[16,1024]{1,0:T(8,128)(2,1)S(1)} collective-permute-done((bf16[16,1024]{1,0:T(8,128)(2,1)S(1)}, bf16[16,1024]{1,0:T(8,128)(2,1)S(1)}, u32[]{:S(2)}, u32[]{:S(2)}) %collective-permute-start.18) | collective-permute-done | bytes 32800 | tf_op jit(solution)/shard_map/ppermute | solution.py:61
  59.0 0.9 fusion.47
  59.9 1.6 %collective-permute-start.21 = (bf16[64,1280]{1,0:T(8,128)(2,1)S(1)}, bf16[64,1280]{1,0:T(8,128)(2,1)S(1)}, u32[]{:S(2)}, u32[]{:S(2)}) collective-permute-start(bf16[64,1280]{1,0:T(8,128)(2,1)S(1)} %get-tuple-element.73), channel_id=1, source_target_pairs={{0,24},{8,16},{16,8},{24,0},{1,25},{9,17},{17,9},{25,1},{2,26},{10... | collective-permute-start | bytes 491528 | tf_op jit(solution)/shard_map/ppermute | solution.py:70
  61.6 0.5 collective-permute-start.22
  62.1 1.4 %collective-permute-start.23 = (bf16[64,1280]{1,0:T(8,128)(2,1)S(1)}, bf16[64,1280]{1,0:T(8,128)(2,1)S(1)}, u32[]{:S(2)}, u32[]{:S(2)}) collective-permute-start(bf16[64,1280]{1,0:T(8,128)(2,1)S(1)} %get-tuple-element.73), channel_id=1, source_target_pairs={{0,8},{8,0},{16,24},{24,16},{1,9},{9,1},{17,25},{25,17},{2,10},{10... | collective-permute-start | bytes 491528 | tf_op jit(solution)/shard_map/ppermute | solution.py:70
  63.5 2.8 %collective-permute-done.21 = bf16[64,1280]{1,0:T(8,128)(2,1)S(1)} collective-permute-done((bf16[64,1280]{1,0:T(8,128)(2,1)S(1)}, bf16[64,1280]{1,0:T(8,128)(2,1)S(1)}, u32[]{:S(2)}, u32[]{:S(2)}) %collective-permute-start.21) | collective-permute-done | bytes 163872 | tf_op jit(solution)/shard_map/ppermute | solution.py:70
  66.3 1.7 %collective-permute-done.22 = bf16[64,1280]{1,0:T(8,128)(2,1)S(1)} collective-permute-done((bf16[64,1280]{1,0:T(8,128)(2,1)S(1)}, bf16[64,1280]{1,0:T(8,128)(2,1)S(1)}, u32[]{:S(2)}, u32[]{:S(2)}) %collective-permute-start.22) | collective-permute-done | bytes 163872 | tf_op jit(solution)/shard_map/ppermute | solution.py:70
  68.1 0.6 fusion.48
  68.7 1.9 %collective-permute-start.25 = (bf16[16,1024]{1,0:T(8,128)(2,1)S(1)}, bf16[16,1024]{1,0:T(8,128)(2,1)S(1)}, u32[]{:S(2)}, u32[]{:S(2)}) collective-permute-start(bf16[16,1024]{1,0:T(8,128)(2,1)S(1)} %get-tuple-element.65), channel_id=1, source_target_pairs={{0,6},{1,7},{2,4},{3,5},{4,2},{5,3},{6,0},{7,1},{8,14},{9,15},{10,... | collective-permute-start | bytes 98312 | tf_op jit(solution)/shard_map/ppermute | solution.py:61
  70.6 0.4 collective-permute-start.26
  71.0 2.1 %collective-permute-start.27 = (bf16[16,1024]{1,0:T(8,128)(2,1)S(1)}, bf16[16,1024]{1,0:T(8,128)(2,1)S(1)}, u32[]{:S(2)}, u32[]{:S(2)}) collective-permute-start(bf16[16,1024]{1,0:T(8,128)(2,1)S(1)} %get-tuple-element.66), channel_id=1, source_target_pairs={{0,2},{1,3},{2,0},{3,1},{4,6},{5,7},{6,4},{7,5},{8,10},{9,11},{10,... | collective-permute-start | bytes 98312 | tf_op jit(solution)/shard_map/ppermute | solution.py:61
  73.1 1.3 %collective-permute-done.25 = bf16[16,1024]{1,0:T(8,128)(2,1)S(1)} collective-permute-done((bf16[16,1024]{1,0:T(8,128)(2,1)S(1)}, bf16[16,1024]{1,0:T(8,128)(2,1)S(1)}, u32[]{:S(2)}, u32[]{:S(2)}) %collective-permute-start.25) | collective-permute-done | bytes 32800 | tf_op jit(solution)/shard_map/ppermute | solution.py:61
  74.4 2.2 %collective-permute-done.26 = bf16[16,1024]{1,0:T(8,128)(2,1)S(1)} collective-permute-done((bf16[16,1024]{1,0:T(8,128)(2,1)S(1)}, bf16[16,1024]{1,0:T(8,128)(2,1)S(1)}, u32[]{:S(2)}, u32[]{:S(2)}) %collective-permute-start.26) | collective-permute-done | bytes 32800 | tf_op jit(solution)/shard_map/ppermute | solution.py:61
  76.7 2.1 %collective-permute-start.28 = (bf16[16,1024]{1,0:T(8,128)(2,1)S(1)}, bf16[16,1024]{1,0:T(8,128)(2,1)S(1)}, u32[]{:S(2)}, u32[]{:S(2)}) collective-permute-start(bf16[16,1024]{1,0:T(8,128)(2,1)S(1)} %fusion.33), channel_id=1, source_target_pairs={{0,6},{1,7},{2,4},{3,5},{4,2},{5,3},{6,0},{7,1},{8,14},{9,15},{10,... | collective-permute-start | bytes 98312 | tf_op jit(solution)/shard_map/ppermute | solution.py:61
  78.8 2.3 %collective-permute-start.30 = (bf16[16,1024]{1,0:T(8,128)(2,1)S(1)}, bf16[16,1024]{1,0:T(8,128)(2,1)S(1)}, u32[]{:S(2)}, u32[]{:S(2)}) collective-permute-start(bf16[16,1024]{1,0:T(8,128)(2,1)S(1)} %fusion.33), channel_id=1, source_target_pairs={{0,2},{1,3},{2,0},{3,1},{4,6},{5,7},{6,4},{7,5},{8,10},{9,11},{10,... | collective-permute-start | bytes 98312 | tf_op jit(solution)/shard_map/ppermute | solution.py:61
  81.1 1.3 %collective-permute-done.28 = bf16[16,1024]{1,0:T(8,128)(2,1)S(1)} collective-permute-done((bf16[16,1024]{1,0:T(8,128)(2,1)S(1)}, bf16[16,1024]{1,0:T(8,128)(2,1)S(1)}, u32[]{:S(2)}, u32[]{:S(2)}) %collective-permute-start.28) | collective-permute-done | bytes 32800 | tf_op jit(solution)/shard_map/ppermute | solution.py:61
  82.4 1.2 %collective-permute-done.29 = bf16[16,1024]{1,0:T(8,128)(2,1)S(1)} collective-permute-done((bf16[16,1024]{1,0:T(8,128)(2,1)S(1)}, bf16[16,1024]{1,0:T(8,128)(2,1)S(1)}, u32[]{:S(2)}, u32[]{:S(2)}) %collective-permute-start.29) | collective-permute-done | bytes 32800 | tf_op jit(solution)/shard_map/ppermute | solution.py:61
  83.6 0.9 fusion.49
  84.5 1.6 %collective-permute-start.31 = (bf16[64,1280]{1,0:T(8,128)(2,1)S(1)}, bf16[64,1280]{1,0:T(8,128)(2,1)S(1)}, u32[]{:S(2)}, u32[]{:S(2)}) collective-permute-start(bf16[64,1280]{1,0:T(8,128)(2,1)S(1)} %get-tuple-element.77), channel_id=1, source_target_pairs={{0,24},{8,16},{16,8},{24,0},{1,25},{9,17},{17,9},{25,1},{2,26},{10... | collective-permute-start | bytes 491528 | tf_op jit(solution)/shard_map/ppermute | solution.py:70
  86.2 0.7 collective-permute-start.32
  86.8 1.3 %collective-permute-start.33 = (bf16[64,1280]{1,0:T(8,128)(2,1)S(1)}, bf16[64,1280]{1,0:T(8,128)(2,1)S(1)}, u32[]{:S(2)}, u32[]{:S(2)}) collective-permute-start(bf16[64,1280]{1,0:T(8,128)(2,1)S(1)} %get-tuple-element.77), channel_id=1, source_target_pairs={{0,8},{8,0},{16,24},{24,16},{1,9},{9,1},{17,25},{25,17},{2,10},{10... | collective-permute-start | bytes 491528 | tf_op jit(solution)/shard_map/ppermute | solution.py:70
  88.1 2.8 %collective-permute-done.31 = bf16[64,1280]{1,0:T(8,128)(2,1)S(1)} collective-permute-done((bf16[64,1280]{1,0:T(8,128)(2,1)S(1)}, bf16[64,1280]{1,0:T(8,128)(2,1)S(1)}, u32[]{:S(2)}, u32[]{:S(2)}) %collective-permute-start.31) | collective-permute-done | bytes 163872 | tf_op jit(solution)/shard_map/ppermute | solution.py:70
  90.9 1.7 %collective-permute-done.32 = bf16[64,1280]{1,0:T(8,128)(2,1)S(1)} collective-permute-done((bf16[64,1280]{1,0:T(8,128)(2,1)S(1)}, bf16[64,1280]{1,0:T(8,128)(2,1)S(1)}, u32[]{:S(2)}, u32[]{:S(2)}) %collective-permute-start.32) | collective-permute-done | bytes 163872 | tf_op jit(solution)/shard_map/ppermute | solution.py:70
  92.6 0.2 subtract_convert_fusion
  92.8 2.3 %fusion.50 = (bf16[64,1024]{1,0:T(8,128)(2,1)S(1)}, f32[64,1024]{1,0:T(8,128)S(1)}) fusion(bf16[64,1280]{1,0:T(8,128)(2,1)S(1)} %get-tuple-element.44, bf16[1280,1024]{1,0:T(8,128)(2,1)} %copy-done.1), kind=kOutput, calls=%fused_computation.94 | convolution fusion | flops 167837696 | bytes 3178496 | tf_op jit(solution)/shard_map/dot_general | solution.py:51
  95.3 1.9 %collective-permute-start.35 = (bf16[16,1024]{1,0:T(8,128)(2,1)S(1)}, bf16[16,1024]{1,0:T(8,128)(2,1)S(1)}, u32[]{:S(2)}, u32[]{:S(2)}) collective-permute-start(bf16[16,1024]{1,0:T(8,128)(2,1)S(1)} %get-tuple-element.62), channel_id=1, source_target_pairs={{0,6},{1,7},{2,4},{3,5},{4,2},{5,3},{6,0},{7,1},{8,14},{9,15},{10,... | collective-permute-start | bytes 98312 | tf_op jit(solution)/shard_map/ppermute | solution.py:61
  97.1 1.1 %collective-permute-start.36 = (bf16[16,1024]{1,0:T(8,128)(2,1)S(1)}, bf16[16,1024]{1,0:T(8,128)(2,1)S(1)}, u32[]{:S(2)}, u32[]{:S(2)}) collective-permute-start(bf16[16,1024]{1,0:T(8,128)(2,1)S(1)} %get-tuple-element.64), channel_id=1, source_target_pairs={{0,4},{1,5},{2,6},{3,7},{4,0},{5,1},{6,2},{7,3},{8,12},{9,13},{10,... | collective-permute-start | bytes 98312 | tf_op jit(solution)/shard_map/ppermute | solution.py:61
  98.2 1.5 %collective-permute-start.37 = (bf16[16,1024]{1,0:T(8,128)(2,1)S(1)}, bf16[16,1024]{1,0:T(8,128)(2,1)S(1)}, u32[]{:S(2)}, u32[]{:S(2)}) collective-permute-start(bf16[16,1024]{1,0:T(8,128)(2,1)S(1)} %get-tuple-element.63), channel_id=1, source_target_pairs={{0,2},{1,3},{2,0},{3,1},{4,6},{5,7},{6,4},{7,5},{8,10},{9,11},{10,... | collective-permute-start | bytes 98312 | tf_op jit(solution)/shard_map/ppermute | solution.py:61
  99.8 0.6 fusion.17
  100.4 0.7 collective-permute-done.35
  101.1 1.4 %collective-permute-done.36 = bf16[16,1024]{1,0:T(8,128)(2,1)S(1)} collective-permute-done((bf16[16,1024]{1,0:T(8,128)(2,1)S(1)}, bf16[16,1024]{1,0:T(8,128)(2,1)S(1)}, u32[]{:S(2)}, u32[]{:S(2)}) %collective-permute-start.36) | collective-permute-done | bytes 32800 | tf_op jit(solution)/shard_map/ppermute | solution.py:61
  102.4 0.6 add_bitcast_fusion
  (63 shorter events, 1.4 us)
Async XLA Ops:
  0.6 42.4 %copy-start = (s32[1024,128]{1,0:T(8,128)S(1)}, s32[1024,128]{1,0:T(8,128)}, u32[]{:S(2)}) copy-start(s32[1024,128]{1,0:T(8,128)} %param.9) | copy-start | bytes 1572868
  0.6 20.1 %copy-start.3 = (f32[640]{0:T(1024)S(1)}, f32[640]{0:T(1024)}, u32[]{:S(2)}) copy-start(f32[640]{0:T(1024)} %param.7) | copy-start | bytes 7684
  1.9 17.2 %collective-permute-start.1 = (s16[144,1024]{1,0:T(8,128)(2,1)S(1)}, s16[144,1024]{1,0:T(8,128)(2,1)S(1)}, u32[]{:S(2)}, u32[]{:S(2)}) collective-permute-start(s16[144,1024]{1,0:T(8,128)(2,1)S(1)} %fusion.refs_0_), channel_id=1, source_target_pairs={{0,4},{1,5},{4,6},{5,7},{6,2},{7,3},{2,0},{3,1},{8,12},{9,13},{12,... | collective-permute-start | bytes 884744 | tf_op jit(solution)/shard_map/ppermute | solution.py:65
  8.0 8.1 %collective-permute-start.4 = (s16[160,640]{1,0:T(8,128)(2,1)S(1)}, s16[160,640]{1,0:T(8,128)(2,1)S(1)}, u32[]{:S(2)}, u32[]{:S(2)}) collective-permute-start(s16[160,640]{1,0:T(8,128)(2,1)S(1)} %pad_add_fusion.refs_6_), channel_id=1, source_target_pairs={{0,8},{8,0},{16,24},{24,16},{1,9},{9,1},{17,25},{25,17},{2,10},{10... | collective-permute-start | bytes 614408 | tf_op jit(solution)/shard_map/ppermute | solution.py:70
  9.6 8.1 %collective-permute-start.7 = (s16[160,640]{1,0:T(8,128)(2,1)S(1)}, s16[160,640]{1,0:T(8,128)(2,1)S(1)}, u32[]{:S(2)}, u32[]{:S(2)}) collective-permute-start(s16[160,640]{1,0:T(8,128)(2,1)S(1)} %pad_add_fusion.1.refs_7_), channel_id=1, source_target_pairs={{0,16},{8,24},{16,0},{24,8},{1,17},{9,25},{17,1},{25,9},{2,18},{10... | collective-permute-start | bytes 614408 | tf_op jit(solution)/shard_map/ppermute | solution.py:70
  11.2 9.7 %collective-permute-start.5 = (s16[160,640]{1,0:T(8,128)(2,1)S(1)}, s16[160,640]{1,0:T(8,128)(2,1)S(1)}, u32[]{:S(2)}, u32[]{:S(2)}) collective-permute-start(s16[160,640]{1,0:T(8,128)(2,1)S(1)} %pad_add_fusion.1.refs_7_), channel_id=1, source_target_pairs={{0,8},{8,0},{16,24},{24,16},{1,9},{9,1},{17,25},{25,17},{2,10},{10... | collective-permute-start | bytes 614408 | tf_op jit(solution)/shard_map/ppermute | solution.py:70
  11.7 10.4 %collective-permute-start.6 = (s16[160,640]{1,0:T(8,128)(2,1)S(1)}, s16[160,640]{1,0:T(8,128)(2,1)S(1)}, u32[]{:S(2)}, u32[]{:S(2)}) collective-permute-start(s16[160,640]{1,0:T(8,128)(2,1)S(1)} %pad_add_fusion.refs_6_), channel_id=1, source_target_pairs={{0,16},{8,24},{16,0},{24,8},{1,17},{9,25},{17,1},{25,9},{2,18},{10... | collective-permute-start | bytes 614408 | tf_op jit(solution)/shard_map/ppermute | solution.py:70
  16.1 8.6 %collective-permute-start.8 = (s16[160,640]{1,0:T(8,128)(2,1)S(1)}, s16[160,640]{1,0:T(8,128)(2,1)S(1)}, u32[]{:S(2)}, u32[]{:S(2)}) collective-permute-start(s16[160,640]{1,0:T(8,128)(2,1)S(1)} %collective-permute-done.4.refs_8_), channel_id=1, source_target_pairs={{0,16},{8,24},{16,0},{24,8},{1,17},{9,25},{17,1},{25,9},{2,18},{10... | collective-permute-start | bytes 614408 | tf_op jit(solution)/shard_map/ppermute | solution.py:70
  17.7 7.0 %collective-permute-start.9 = (s16[160,640]{1,0:T(8,128)(2,1)S(1)}, s16[160,640]{1,0:T(8,128)(2,1)S(1)}, u32[]{:S(2)}, u32[]{:S(2)}) collective-permute-start(s16[160,640]{1,0:T(8,128)(2,1)S(1)} %collective-permute-done.7.refs_11_), channel_id=1, source_target_pairs={{0,8},{8,0},{16,24},{24,16},{1,9},{9,1},{17,25},{25,17},{2,10},{10... | collective-permute-start | bytes 614408 | tf_op jit(solution)/shard_map/ppermute | solution.py:70
  19.1 6.7 %collective-permute-start.3 = (s16[144,1024]{1,0:T(8,128)(2,1)S(1)}, s16[144,1024]{1,0:T(8,128)(2,1)S(1)}, u32[]{:S(2)}, u32[]{:S(2)}) collective-permute-start(s16[144,1024]{1,0:T(8,128)(2,1)S(1)} %collective-permute-done.1.refs_2_), channel_id=1, source_target_pairs={{0,4},{1,5},{4,6},{5,7},{6,2},{7,3},{2,0},{3,1},{8,12},{9,13},{12,... | collective-permute-start | bytes 884744 | tf_op jit(solution)/shard_map/ppermute | solution.py:65
  20.9 7.5 %collective-permute-start = (s16[144,1024]{1,0:T(8,128)(2,1)S(1)}, s16[144,1024]{1,0:T(8,128)(2,1)S(1)}, u32[]{:S(2)}, u32[]{:S(2)}) collective-permute-start(s16[144,1024]{1,0:T(8,128)(2,1)S(1)} %fusion.refs_0_), channel_id=1, source_target_pairs={{0,1},{1,0},{2,3},{3,2},{4,5},{5,4},{6,7},{7,6},{8,9},{9,8},{10,11... | collective-permute-start | bytes 884744 | tf_op jit(solution)/shard_map/ppermute | solution.py:56
  22.1 6.4 %collective-permute-start.2 = (s16[144,1024]{1,0:T(8,128)(2,1)S(1)}, s16[144,1024]{1,0:T(8,128)(2,1)S(1)}, u32[]{:S(2)}, u32[]{:S(2)}) collective-permute-start(s16[144,1024]{1,0:T(8,128)(2,1)S(1)} %collective-permute-done.1.refs_2_), channel_id=1, source_target_pairs={{0,1},{1,0},{2,3},{3,2},{4,5},{5,4},{6,7},{7,6},{8,9},{9,8},{10,11... | collective-permute-start | bytes 884744 | tf_op jit(solution)/shard_map/ppermute | solution.py:56
  25.8 2.6 %collective-permute-start.10 = (s16[144,1024]{1,0:T(8,128)(2,1)S(1)}, s16[144,1024]{1,0:T(8,128)(2,1)S(1)}, u32[]{:S(2)}, u32[]{:S(2)}) collective-permute-start(s16[144,1024]{1,0:T(8,128)(2,1)S(1)} %collective-permute-done.3.refs_4_), channel_id=1, source_target_pairs={{0,1},{1,0},{2,3},{3,2},{4,5},{5,4},{6,7},{7,6},{8,9},{9,8},{10,11... | collective-permute-start | bytes 884744 | tf_op jit(solution)/shard_map/ppermute | solution.py:56
  25.9 9.5 %collective-permute-start.11 = (s16[144,1024]{1,0:T(8,128)(2,1)S(1)}, s16[144,1024]{1,0:T(8,128)(2,1)S(1)}, u32[]{:S(2)}, u32[]{:S(2)}) collective-permute-start(s16[144,1024]{1,0:T(8,128)(2,1)S(1)} %collective-permute-done.3.refs_4_), channel_id=1, source_target_pairs={{0,4},{1,5},{4,6},{5,7},{6,2},{7,3},{2,0},{3,1},{8,12},{9,13},{12,... | collective-permute-start | bytes 884744 | tf_op jit(solution)/shard_map/ppermute | solution.py:65
  35.4 1.6 %collective-permute-start.12 = (s16[144,1024]{1,0:T(8,128)(2,1)S(1)}, s16[144,1024]{1,0:T(8,128)(2,1)S(1)}, u32[]{:S(2)}, u32[]{:S(2)}) collective-permute-start(s16[144,1024]{1,0:T(8,128)(2,1)S(1)} %collective-permute-done.11.own_ref), channel_id=1, source_target_pairs={{0,1},{1,0},{2,3},{3,2},{4,5},{5,4},{6,7},{7,6},{8,9},{9,8},{10,11... | collective-permute-start | bytes 884744 | tf_op jit(solution)/shard_map/ppermute | solution.py:56
  41.4 1.4 %collective-permute-start.13 = (bf16[64,1024]{1,0:T(8,128)(2,1)S(1)}, bf16[64,1024]{1,0:T(8,128)(2,1)S(1)}, u32[]{:S(2)}, u32[]{:S(2)}) collective-permute-start(bf16[64,1024]{1,0:T(8,128)(2,1)S(1)} %get-tuple-element.39), channel_id=1, source_target_pairs={{0,1},{1,0},{2,3},{3,2},{4,5},{5,4},{6,7},{7,6},{8,9},{9,8},{10,11... | collective-permute-start | bytes 393224 | tf_op jit(solution)/shard_map/ppermute | solution.py:56
  42.8 13.1 %collective-permute-start.20 = (bf16[640,1024]{1,0:T(8,128)(2,1)S(1)}, bf16[640,1024]{1,0:T(8,128)(2,1)}, u32[]{:S(2)}, u32[]{:S(2)}) collective-permute-start(bf16[640,1024]{1,0:T(8,128)(2,1)S(1)} %get-tuple-element.41), channel_id=1, source_target_pairs={{0,1},{1,0},{2,3},{3,2},{4,5},{5,4},{6,7},{7,6},{8,9},{9,8},{10,11... | collective-permute-start | bytes 3932168 | tf_op jit(solution)/shard_map/ppermute | solution.py:56
  43.4 20.1 %collective-permute-start.24 = (s16[64,640]{1,0:T(8,128)(2,1)S(1)}, s16[64,640]{1,0:T(8,128)(2,1)S(1)}, u32[]{:S(2)}, u32[]{:S(2)}) collective-permute-start(s16[64,640]{1,0:T(8,128)(2,1)S(1)} %get-tuple-element.37), channel_id=1, source_target_pairs={{0,1},{1,0},{2,3},{3,2},{4,5},{5,4},{6,7},{7,6},{8,9},{9,8},{10,11... | collective-permute-start | bytes 245768 | tf_op jit(solution)/shard_map/ppermute | solution.py:56
  43.8 5.8 %collective-permute-start.14 = (bf16[16,1024]{1,0:T(8,128)(2,1)S(1)}, bf16[16,1024]{1,0:T(8,128)(2,1)S(1)}, u32[]{:S(2)}, u32[]{:S(2)}) collective-permute-start(bf16[16,1024]{1,0:T(8,128)(2,1)S(1)} %get-tuple-element.68), channel_id=1, source_target_pairs={{0,6},{1,7},{2,4},{3,5},{4,2},{5,3},{6,0},{7,1},{8,14},{9,15},{10,... | collective-permute-start | bytes 98312 | tf_op jit(solution)/shard_map/ppermute | solution.py:61
  46.1 5.3 %collective-permute-start.15 = (bf16[16,1024]{1,0:T(8,128)(2,1)S(1)}, bf16[16,1024]{1,0:T(8,128)(2,1)S(1)}, u32[]{:S(2)}, u32[]{:S(2)}) collective-permute-start(bf16[16,1024]{1,0:T(8,128)(2,1)S(1)} %get-tuple-element.70), channel_id=1, source_target_pairs={{0,4},{1,5},{2,6},{3,7},{4,0},{5,1},{6,2},{7,3},{8,12},{9,13},{10,... | collective-permute-start | bytes 98312 | tf_op jit(solution)/shard_map/ppermute | solution.py:61
  47.3 4.1 %collective-permute-start.16 = (bf16[16,1024]{1,0:T(8,128)(2,1)S(1)}, bf16[16,1024]{1,0:T(8,128)(2,1)S(1)}, u32[]{:S(2)}, u32[]{:S(2)}) collective-permute-start(bf16[16,1024]{1,0:T(8,128)(2,1)S(1)} %get-tuple-element.69), channel_id=1, source_target_pairs={{0,2},{1,3},{2,0},{3,1},{4,6},{5,7},{6,4},{7,5},{8,10},{9,11},{10,... | collective-permute-start | bytes 98312 | tf_op jit(solution)/shard_map/ppermute | solution.py:61
  51.5 6.0 %collective-permute-start.17 = (bf16[16,1024]{1,0:T(8,128)(2,1)S(1)}, bf16[16,1024]{1,0:T(8,128)(2,1)S(1)}, u32[]{:S(2)}, u32[]{:S(2)}) collective-permute-start(bf16[16,1024]{1,0:T(8,128)(2,1)S(1)} %fusion.32), channel_id=1, source_target_pairs={{0,6},{1,7},{2,4},{3,5},{4,2},{5,3},{6,0},{7,1},{8,14},{9,15},{10,... | collective-permute-start | bytes 98312 | tf_op jit(solution)/shard_map/ppermute | solution.py:61
  54.2 4.8 %collective-permute-start.18 = (bf16[16,1024]{1,0:T(8,128)(2,1)S(1)}, bf16[16,1024]{1,0:T(8,128)(2,1)S(1)}, u32[]{:S(2)}, u32[]{:S(2)}) collective-permute-start(bf16[16,1024]{1,0:T(8,128)(2,1)S(1)} %fusion.32), channel_id=1, source_target_pairs={{0,4},{1,5},{2,6},{3,7},{4,0},{5,1},{6,2},{7,3},{8,12},{9,13},{10,... | collective-permute-start | bytes 98312 | tf_op jit(solution)/shard_map/ppermute | solution.py:61
  54.2 4.8 %collective-permute-start.19 = (bf16[16,1024]{1,0:T(8,128)(2,1)S(1)}, bf16[16,1024]{1,0:T(8,128)(2,1)S(1)}, u32[]{:S(2)}, u32[]{:S(2)}) collective-permute-start(bf16[16,1024]{1,0:T(8,128)(2,1)S(1)} %fusion.32), channel_id=1, source_target_pairs={{0,2},{1,3},{2,0},{3,1},{4,6},{5,7},{6,4},{7,5},{8,10},{9,11},{10,... | collective-permute-start | bytes 98312 | tf_op jit(solution)/shard_map/ppermute | solution.py:61
  57.5 26.1 %copy-start.1 = (bf16[1280,1024]{1,0:T(8,128)(2,1)}, bf16[1280,1024]{1,0:T(8,128)(2,1)S(1)}, u32[]{:S(2)}) copy-start(bf16[1280,1024]{1,0:T(8,128)(2,1)S(1)} %pad_maximum_fusion) | copy-start | bytes 7864324
  59.9 6.4 %collective-permute-start.21 = (bf16[64,1280]{1,0:T(8,128)(2,1)S(1)}, bf16[64,1280]{1,0:T(8,128)(2,1)S(1)}, u32[]{:S(2)}, u32[]{:S(2)}) collective-permute-start(bf16[64,1280]{1,0:T(8,128)(2,1)S(1)} %get-tuple-element.73), channel_id=1, source_target_pairs={{0,24},{8,16},{16,8},{24,0},{1,25},{9,17},{17,9},{25,1},{2,26},{10... | collective-permute-start | bytes 491528 | tf_op jit(solution)/shard_map/ppermute | solution.py:70
  61.6 6.4 %collective-permute-start.22 = (bf16[64,1280]{1,0:T(8,128)(2,1)S(1)}, bf16[64,1280]{1,0:T(8,128)(2,1)S(1)}, u32[]{:S(2)}, u32[]{:S(2)}) collective-permute-start(bf16[64,1280]{1,0:T(8,128)(2,1)S(1)} %get-tuple-element.73), channel_id=1, source_target_pairs={{0,16},{8,24},{16,0},{24,8},{1,17},{9,25},{17,1},{25,9},{2,18},{10... | collective-permute-start | bytes 491528 | tf_op jit(solution)/shard_map/ppermute | solution.py:70
  62.1 5.9 %collective-permute-start.23 = (bf16[64,1280]{1,0:T(8,128)(2,1)S(1)}, bf16[64,1280]{1,0:T(8,128)(2,1)S(1)}, u32[]{:S(2)}, u32[]{:S(2)}) collective-permute-start(bf16[64,1280]{1,0:T(8,128)(2,1)S(1)} %get-tuple-element.73), channel_id=1, source_target_pairs={{0,8},{8,0},{16,24},{24,16},{1,9},{9,1},{17,25},{25,17},{2,10},{10... | collective-permute-start | bytes 491528 | tf_op jit(solution)/shard_map/ppermute | solution.py:70
  68.7 5.8 %collective-permute-start.25 = (bf16[16,1024]{1,0:T(8,128)(2,1)S(1)}, bf16[16,1024]{1,0:T(8,128)(2,1)S(1)}, u32[]{:S(2)}, u32[]{:S(2)}) collective-permute-start(bf16[16,1024]{1,0:T(8,128)(2,1)S(1)} %get-tuple-element.65), channel_id=1, source_target_pairs={{0,6},{1,7},{2,4},{3,5},{4,2},{5,3},{6,0},{7,1},{8,14},{9,15},{10,... | collective-permute-start | bytes 98312 | tf_op jit(solution)/shard_map/ppermute | solution.py:61
  70.6 6.0 %collective-permute-start.26 = (bf16[16,1024]{1,0:T(8,128)(2,1)S(1)}, bf16[16,1024]{1,0:T(8,128)(2,1)S(1)}, u32[]{:S(2)}, u32[]{:S(2)}) collective-permute-start(bf16[16,1024]{1,0:T(8,128)(2,1)S(1)} %get-tuple-element.67), channel_id=1, source_target_pairs={{0,4},{1,5},{2,6},{3,7},{4,0},{5,1},{6,2},{7,3},{8,12},{9,13},{10,... | collective-permute-start | bytes 98312 | tf_op jit(solution)/shard_map/ppermute | solution.py:61
  71.0 5.6 %collective-permute-start.27 = (bf16[16,1024]{1,0:T(8,128)(2,1)S(1)}, bf16[16,1024]{1,0:T(8,128)(2,1)S(1)}, u32[]{:S(2)}, u32[]{:S(2)}) collective-permute-start(bf16[16,1024]{1,0:T(8,128)(2,1)S(1)} %get-tuple-element.66), channel_id=1, source_target_pairs={{0,2},{1,3},{2,0},{3,1},{4,6},{5,7},{6,4},{7,5},{8,10},{9,11},{10,... | collective-permute-start | bytes 98312 | tf_op jit(solution)/shard_map/ppermute | solution.py:61
  76.7 5.8 %collective-permute-start.28 = (bf16[16,1024]{1,0:T(8,128)(2,1)S(1)}, bf16[16,1024]{1,0:T(8,128)(2,1)S(1)}, u32[]{:S(2)}, u32[]{:S(2)}) collective-permute-start(bf16[16,1024]{1,0:T(8,128)(2,1)S(1)} %fusion.33), channel_id=1, source_target_pairs={{0,6},{1,7},{2,4},{3,5},{4,2},{5,3},{6,0},{7,1},{8,14},{9,15},{10,... | collective-permute-start | bytes 98312 | tf_op jit(solution)/shard_map/ppermute | solution.py:61
  78.8 4.8 %collective-permute-start.29 = (bf16[16,1024]{1,0:T(8,128)(2,1)S(1)}, bf16[16,1024]{1,0:T(8,128)(2,1)S(1)}, u32[]{:S(2)}, u32[]{:S(2)}) collective-permute-start(bf16[16,1024]{1,0:T(8,128)(2,1)S(1)} %fusion.33), channel_id=1, source_target_pairs={{0,4},{1,5},{2,6},{3,7},{4,0},{5,1},{6,2},{7,3},{8,12},{9,13},{10,... | collective-permute-start | bytes 98312 | tf_op jit(solution)/shard_map/ppermute | solution.py:61
  78.8 4.8 %collective-permute-start.30 = (bf16[16,1024]{1,0:T(8,128)(2,1)S(1)}, bf16[16,1024]{1,0:T(8,128)(2,1)S(1)}, u32[]{:S(2)}, u32[]{:S(2)}) collective-permute-start(bf16[16,1024]{1,0:T(8,128)(2,1)S(1)} %fusion.33), channel_id=1, source_target_pairs={{0,2},{1,3},{2,0},{3,1},{4,6},{5,7},{6,4},{7,5},{8,10},{9,11},{10,... | collective-permute-start | bytes 98312 | tf_op jit(solution)/shard_map/ppermute | solution.py:61
  84.5 6.4 %collective-permute-start.31 = (bf16[64,1280]{1,0:T(8,128)(2,1)S(1)}, bf16[64,1280]{1,0:T(8,128)(2,1)S(1)}, u32[]{:S(2)}, u32[]{:S(2)}) collective-permute-start(bf16[64,1280]{1,0:T(8,128)(2,1)S(1)} %get-tuple-element.77), channel_id=1, source_target_pairs={{0,24},{8,16},{16,8},{24,0},{1,25},{9,17},{17,9},{25,1},{2,26},{10... | collective-permute-start | bytes 491528 | tf_op jit(solution)/shard_map/ppermute | solution.py:70
  86.2 6.4 %collective-permute-start.32 = (bf16[64,1280]{1,0:T(8,128)(2,1)S(1)}, bf16[64,1280]{1,0:T(8,128)(2,1)S(1)}, u32[]{:S(2)}, u32[]{:S(2)}) collective-permute-start(bf16[64,1280]{1,0:T(8,128)(2,1)S(1)} %get-tuple-element.77), channel_id=1, source_target_pairs={{0,16},{8,24},{16,0},{24,8},{1,17},{9,25},{17,1},{25,9},{2,18},{10... | collective-permute-start | bytes 491528 | tf_op jit(solution)/shard_map/ppermute | solution.py:70
  86.8 5.7 %collective-permute-start.33 = (bf16[64,1280]{1,0:T(8,128)(2,1)S(1)}, bf16[64,1280]{1,0:T(8,128)(2,1)S(1)}, u32[]{:S(2)}, u32[]{:S(2)}) collective-permute-start(bf16[64,1280]{1,0:T(8,128)(2,1)S(1)} %get-tuple-element.77), channel_id=1, source_target_pairs={{0,8},{8,0},{16,24},{24,16},{1,9},{9,1},{17,25},{25,17},{2,10},{10... | collective-permute-start | bytes 491528 | tf_op jit(solution)/shard_map/ppermute | solution.py:70
  92.8 7.0 %copy-start.2 = (f32[640,32]{0,1:T(8,128)S(1)}, f32[640,32]{0,1:T(8,128)}, u32[]{:S(2)}) copy-start(f32[640,32]{0,1:T(8,128)} %param.8) | copy-start | bytes 245764
  95.2 4.6 %collective-permute-start.34 = (f32[64,640]{1,0:T(8,128)S(1)}, f32[64,640]{1,0:T(8,128)S(1)}, u32[]{:S(2)}, u32[]{:S(2)}) collective-permute-start(f32[64,640]{1,0:T(8,128)S(1)} %get-tuple-element.53), channel_id=1, source_target_pairs={{0,1},{1,0},{2,3},{3,2},{4,5},{5,4},{6,7},{7,6},{8,9},{9,8},{10,11... | collective-permute-start | bytes 491528 | tf_op jit(solution)/shard_map/ppermute | solution.py:56
  95.3 5.8 %collective-permute-start.35 = (bf16[16,1024]{1,0:T(8,128)(2,1)S(1)}, bf16[16,1024]{1,0:T(8,128)(2,1)S(1)}, u32[]{:S(2)}, u32[]{:S(2)}) collective-permute-start(bf16[16,1024]{1,0:T(8,128)(2,1)S(1)} %get-tuple-element.62), channel_id=1, source_target_pairs={{0,6},{1,7},{2,4},{3,5},{4,2},{5,3},{6,0},{7,1},{8,14},{9,15},{10,... | collective-permute-start | bytes 98312 | tf_op jit(solution)/shard_map/ppermute | solution.py:61
  97.1 5.3 %collective-permute-start.36 = (bf16[16,1024]{1,0:T(8,128)(2,1)S(1)}, bf16[16,1024]{1,0:T(8,128)(2,1)S(1)}, u32[]{:S(2)}, u32[]{:S(2)}) collective-permute-start(bf16[16,1024]{1,0:T(8,128)(2,1)S(1)} %get-tuple-element.64), channel_id=1, source_target_pairs={{0,4},{1,5},{2,6},{3,7},{4,0},{5,1},{6,2},{7,3},{8,12},{9,13},{10,... | collective-permute-start | bytes 98312 | tf_op jit(solution)/shard_map/ppermute | solution.py:61
  98.2 4.3 %collective-permute-start.37 = (bf16[16,1024]{1,0:T(8,128)(2,1)S(1)}, bf16[16,1024]{1,0:T(8,128)(2,1)S(1)}, u32[]{:S(2)}, u32[]{:S(2)}) collective-permute-start(bf16[16,1024]{1,0:T(8,128)(2,1)S(1)} %get-tuple-element.63), channel_id=1, source_target_pairs={{0,2},{1,3},{2,0},{3,1},{4,6},{5,7},{6,4},{7,5},{8,10},{9,11},{10,... | collective-permute-start | bytes 98312 | tf_op jit(solution)/shard_map/ppermute | solution.py:61

commit v7 on v6

--- a/solution.py
+++ b/solution.py
@@ -92,12 +92,14 @@
         def on_ring(place):
             return jnp.where(place == 0, 0, jnp.where(place == 1, 3, place - 1))
 
-        for m in range(n_freqs // 2):
+        rows = freqs[-1].shape[0]
+        pieces = [(ref, h * rows) for ref in freqs[:-2] for h in range(2)] + [(ref, 0) for ref in freqs[-2:]]
+        for m in range(len(pieces) // 2):
             step = (on_ring(line) - on_ring(clip ^ m)) & 3
             base = step * 2 * columns + jnp.where(step == 3, depth - used, 0)
-            for h, side in enumerate((core, 1 - core)):
+            for (ref, start), side in zip(pieces[2 * m : 2 * m + 2], (core, 1 - core)):
                 row = pl.multiple_of(base + side * columns, 16)
-                freq_code[pl.ds(row, columns), :] = freqs[2 * m + h][:columns, :]
+                freq_code[pl.ds(row, columns), :] = ref[start : start + columns, :]
         if depth > used:
             freq_code[used:depth, :] = jnp.zeros((depth - used, freq_code.shape[1]), jnp.int16)
             for start in range(0, 3 * depth, depth):
@@ -143,18 +145,19 @@
 def phi_by_kernels(embed_code, freq_code, column, scale, line, core, clip, prepare):
     slabs = 4
     columns, clips = embed_code.shape
-    features = freq_code[0].shape[1]
+    features = freq_code.shape[1]
     tie = lax.optimization_barrier
-    x_low, y_high = clip_swap(freq_code[0], 1), clip_swap(freq_code[1], 2)
-    x_high, y_low = clip_swap(freq_code[1], 1), clip_swap(freq_code[0], 2)
-    freqs = [*freq_code, x_low, x_high, y_low, y_high, clip_swap(x_low, 2), clip_swap(y_high, 1)]
+    rows = freq_code.shape[0] // 2
+    freq_x, freq_y = clip_swap(freq_code, 1), clip_swap(freq_code, 2)
     ring = [(0, 2), (2, 3), (3, 1), (1, 0)]
     own = [embed_code]
     for _ in range(slabs - 1):
         own.append(line_move(own[-1], ring))
     other = [core_swap(own[0]), core_swap(own[1])]
-    *freqs, turn = tie((*freqs, own[2]))
-    other.append(core_swap(turn))
+    x_again, y_again, other[1] = tie((freq_x, freq_y, other[1]))
+    freqs = [freq_code, freq_x, freq_y, clip_swap(x_again[:rows], 2), clip_swap(y_again[rows:], 1)]
+    other.append(core_swap(own[2]))
+    *freqs, own[2] = tie((*freqs, own[2]))
     betas, cast = prepare(freqs)
     early = [x for pair in zip(own[:3], other) for x in pair]
     used = len(early) * columns
@@ -224,12 +227,13 @@
 def phi_by_ring(embed_code, freq_code, column, scale, line, core, clip, prepare):
     places, n_clip = lax.axis_size("feat") // 2, lax.axis_size("clip")
     columns, clips = embed_code.shape
-    slab, features = 2 * places * columns // n_clip, freq_code[0].shape[1]
-    freqs = [y for k in range(n_clip) for y in (x if k == 0 else clip_swap(x, k) for x in freq_code)]
+    slab, features = 2 * places * columns // n_clip, freq_code.shape[1]
+    freqs = [freq_code] + [clip_swap(freq_code, k) for k in range(1, n_clip)]
     freq_all = jnp.zeros((n_clip * slab, features), jnp.int16)
-    for i, piece in enumerate(freqs):
-        at = (clip ^ (i // 2)) * slab + (i % 2) * (slab // 2)
-        freq_all = lax.dynamic_update_slice_in_dim(freq_all, piece[: slab // 2], at, 0)
+    for k, piece in enumerate(freqs):
+        for h in range(2):
+            half = piece[h * (piece.shape[0] // 2) :][: slab // 2]
+            freq_all = lax.dynamic_update_slice_in_dim(freq_all, half, (clip ^ k) * slab + h * (slab // 2), 0)
     embed_all = jnp.zeros((2 * places * columns, clips), jnp.int16)
     piece = embed_code
     ring = [(i, (i + 1) % places) for i in range(places)]
@@ -268,19 +272,23 @@
 
     embed_code = encode(embeds.T, EMBED_BOUND)
     weight_rows = weights.T.reshape(per_clip, 2, block, features)
-    freq_code = [
-        jnp.concatenate(
-            [
+    freq_code = jnp.concatenate(
+        [
+            part
+            for h in range(2)
+            for part in (
                 encode(frequencies[h * (slab // 2) : (h + 1) * (slab // 2)], FREQ_BOUND),
                 encode(weight_rows[:, h].reshape(-1, features), WEIGHT_BOUND),
-            ]
-        )
-        for h in range(2)
-    ]
+            )
+        ]
+    )
     column = (phases * (0.5 / math.pi))[:, None]
 
     def prepare(codes):
-        stacked = jnp.concatenate([code[slab // 2 :] for code in codes]).reshape(n_clip, 2, per_clip, block, features)
+        rows = (slab + weights.shape[1]) // 2
+        stacked = jnp.concatenate(
+            [code[start + slab // 2 : start + rows] for code in codes for start in range(0, code.shape[0], rows)]
+        ).reshape(n_clip, 2, per_clip, block, features)
 
         def ordered(side):
             rows = lax.dynamic_index_in_dim(stacked, side, 1, keepdims=False).reshape(-1, block, features)

time: 103 us -> 102 us (level)
  waiting for transfers between devices: 34 us -> 30.8 us
    ppermute x12 -> x10, starting transfers between devices: 14.2 us -> 12.3 us  [clip_swap(): return lax.ppermute(x, 'clip', [(i, i ^ k) for i in range(n)])]
    ppermute x3, starting transfers between devices: 8.19 us -> 10 us  [line_move(): lax.ppermute(x, 'feat', [(2 * a + c, 2 * b + c) for a, b in pairs for c i...]
    ppermute x15, waiting for transfers between devices: 12.7 us -> 11 us  [line_swap(): return lax.ppermute(x, 'feat', [(i, i ^ 2 * k) for i in range(n)])]
    ppermute x12 -> x10, waiting for transfers between devices: 16.6 us -> 16 us  [clip_swap(): return lax.ppermute(x, 'clip', [(i, i ^ k) for i in range(n)])]
  transfers between devices with their start and end apart: 38 -> 36, of which waited for: 22 -> 21; matrix products, arithmetic and copies ran while one was open for 6% -> 7% of each run, Pallas kernels for 6% -> 6%
where the time goes in v7:
time: 102 us; the launch traced here: 101 us
  starting transfers between devices  46 us (45%)
  waiting for transfers between devices  30.8 us (30%)
  Pallas kernels  10.7 us (10%)
  other arithmetic  6.77 us (7%)
  matrix products  4.75 us (5%)
  local copies, waits for them, and re-layouts  1.42 us (1%)
    ppermute x15, starting transfers between devices, line_swap(): return lax.ppermute(x, 'feat', [(i, i ^ 2 * k) for i in range(n)])  22.3 us
    ppermute x10, waiting for transfers between devices, clip_swap(): return lax.ppermute(x, 'clip', [(i, i ^ k) for i in range(n)])  16 us
    ppermute x10, starting transfers between devices, clip_swap(): return lax.ppermute(x, 'clip', [(i, i ^ k) for i in range(n)])  12.3 us
    ppermute x15, waiting for transfers between devices, line_swap(): return lax.ppermute(x, 'feat', [(i, i ^ 2 * k) for i in range(n)])  11 us
    ppermute x3, starting transfers between devices, line_move(): lax.ppermute(x, 'feat', [(2 * a + c, 2 * b + c) for a, b in pairs for c i...  10 us
    pallas_call x1, Pallas kernels, phi_by_kernels(): pl.pallas_call(functools.partial(early_kernel, n_embeds=len(early), n_fre...  6.26 us
    pallas_call x1, Pallas kernels, phi_by_kernels(): pl.pallas_call(functools.partial(late_kernel, scale=scale), grid=(clips /...  4.44 us
    convert_element_type x3, other arithmetic, encode(): return jnp.round(x * (CODE_MAX / bound)).astype(jnp.int16)  3.26 us
  transfers between devices with their start and end apart: 36, of which 21 were waited for; matrix products, arithmetic and copies ran while one was open for 7% of the time, Pallas kernels for 6%

profile of v7, /device:TPU:0, one launch (start us, length us, event | category | flops | bytes accessed | tf_op | source)
XLA Modules:
  0.0 101.4 jit_solution(4290718295038173942)
XLA Ops:
  0.7 1.2 %fusion.refs_0_ = s16[144,1024]{1,0:T(8,128)(2,1)S(1)} fusion(f32[1024,144]{0,1:T(8,128)} %param.5), kind=kLoop, calls=%fused_computation.11 | loop fusion | flops 442368 | bytes 884736 | tf_op jit(solution)/shard_map/convert_element_type | solution.py:32
  1.9 4.1 %collective-permute-start.1 = (s16[144,1024]{1,0:T(8,128)(2,1)S(1)}, s16[144,1024]{1,0:T(8,128)(2,1)S(1)}, u32[]{:S(2)}, u32[]{:S(2)}) collective-permute-start(s16[144,1024]{1,0:T(8,128)(2,1)S(1)} %fusion.refs_0_), channel_id=1, source_target_pairs={{0,4},{1,5},{4,6},{5,7},{6,2},{7,3},{2,0},{3,1},{8,12},{9,13},{12,... | collective-permute-start | bytes 884744 | tf_op jit(solution)/shard_map/ppermute | solution.py:65
  6.0 1.2 %round-nearest-even_convert_fusion.2 = (s16[144,640]{1,0:T(8,128)(2,1)S(1)}, s16[144,640]{1,0:T(8,128)(2,1)S(1)}) fusion(f32[288,640]{1,0:T(8,128)} %param.6), kind=kLoop, calls=%fused_computation.4 | loop fusion | flops 552960 | bytes 1105920 | tf_op jit(solution)/shard_map/convert_element_type | solution.py:32
  7.2 0.8 fusion.38
  8.1 1.6 %collective-permute-start.2 = (s16[320,640]{1,0:T(8,128)(2,1)S(1)}, s16[320,640]{1,0:T(8,128)(2,1)S(1)}, u32[]{:S(2)}, u32[]{:S(2)}) collective-permute-start(s16[320,640]{1,0:T(8,128)(2,1)S(1)} %pad_add_fusion.refs_6_), channel_id=1, source_target_pairs={{0,8},{8,0},{16,24},{24,16},{1,9},{9,1},{17,25},{25,17},{2,10},{10... | collective-permute-start | bytes 1228808 | tf_op jit(solution)/shard_map/ppermute | solution.py:70
  9.6 1.5 %collective-permute-start.3 = (s16[320,640]{1,0:T(8,128)(2,1)S(1)}, s16[320,640]{1,0:T(8,128)(2,1)S(1)}, u32[]{:S(2)}, u32[]{:S(2)}) collective-permute-start(s16[320,640]{1,0:T(8,128)(2,1)S(1)} %pad_add_fusion.refs_6_), channel_id=1, source_target_pairs={{0,16},{8,24},{16,0},{24,8},{1,17},{9,25},{17,1},{25,9},{2,18},{10... | collective-permute-start | bytes 1228808 | tf_op jit(solution)/shard_map/ppermute | solution.py:70
  11.1 1.1 %collective-permute-done.1.refs_2_ = s16[144,1024]{1,0:T(8,128)(2,1)S(1)} collective-permute-done((s16[144,1024]{1,0:T(8,128)(2,1)S(1)}, s16[144,1024]{1,0:T(8,128)(2,1)S(1)}, u32[]{:S(2)}, u32[]{:S(2)}) %collective-permute-start.1) | collective-permute-done | bytes 294944 | tf_op jit(solution)/shard_map/ppermute | solution.py:65
  12.2 0.5 collective-permute-start
  12.7 3.4 %collective-permute-start.7 = (s16[144,1024]{1,0:T(8,128)(2,1)S(1)}, s16[144,1024]{1,0:T(8,128)(2,1)S(1)}, u32[]{:S(2)}, u32[]{:S(2)}) collective-permute-start(s16[144,1024]{1,0:T(8,128)(2,1)S(1)} %collective-permute-done.1.refs_2_), channel_id=1, source_target_pairs={{0,4},{1,5},{4,6},{5,7},{6,2},{7,3},{2,0},{3,1},{8,12},{9,13},{12,... | collective-permute-start | bytes 884744 | tf_op jit(solution)/shard_map/ppermute | solution.py:65
  16.1 2.9 %collective-permute-done.2.refs_7_ = s16[320,640]{1,0:T(8,128)(2,1)S(1)} collective-permute-done((s16[320,640]{1,0:T(8,128)(2,1)S(1)}, s16[320,640]{1,0:T(8,128)(2,1)S(1)}, u32[]{:S(2)}, u32[]{:S(2)}) %collective-permute-start.2) | collective-permute-done | bytes 409632 | tf_op jit(solution)/shard_map/ppermute | solution.py:70
  19.0 1.2 %collective-permute-done.3.refs_8_ = s16[320,640]{1,0:T(8,128)(2,1)S(1)} collective-permute-done((s16[320,640]{1,0:T(8,128)(2,1)S(1)}, s16[320,640]{1,0:T(8,128)(2,1)S(1)}, u32[]{:S(2)}, u32[]{:S(2)}) %collective-permute-start.3) | collective-permute-done | bytes 409632 | tf_op jit(solution)/shard_map/ppermute | solution.py:70
  20.3 1.6 %collective-permute-start.5 = (s16[160,640]{1,0:T(8,128)(2,1)S(1)}, s16[160,640]{1,0:T(8,128)(2,1)S(1)}, u32[]{:S(2)}, u32[]{:S(2)}) collective-permute-start(s16[160,640]{1,0:T(8,128)(2,1)S(1)} %slice.100), channel_id=1, source_target_pairs={{0,16},{8,24},{16,0},{24,8},{1,17},{9,25},{17,1},{25,9},{2,18},{10... | collective-permute-start | bytes 614408 | tf_op jit(solution)/shard_map/ppermute | solution.py:70
  21.9 0.7 slice.101
  22.6 0.5 collective-permute-start.6
  23.4 2.6 %collective-permute-start.9 = (s16[144,1024]{1,0:T(8,128)(2,1)S(1)}, s16[144,1024]{1,0:T(8,128)(2,1)S(1)}, u32[]{:S(2)}, u32[]{:S(2)}) collective-permute-start(s16[144,1024]{1,0:T(8,128)(2,1)S(1)} %collective-permute-done.7.refs_4_), channel_id=1, source_target_pairs={{0,4},{1,5},{4,6},{5,7},{6,2},{7,3},{2,0},{3,1},{8,12},{9,13},{12,... | collective-permute-start | bytes 884744 | tf_op jit(solution)/shard_map/ppermute | solution.py:65
  26.1 2.4 %collective-permute-done.6.refs_10_ = s16[160,640]{1,0:T(8,128)(2,1)S(1)} collective-permute-done((s16[160,640]{1,0:T(8,128)(2,1)}, s16[160,640]{1,0:T(8,128)(2,1)S(1)}, u32[]{:S(2)}, u32[]{:S(2)}) %collective-permute-start.6) | collective-permute-done | bytes 204832 | tf_op jit(solution)/shard_map/ppermute | solution.py:70
  28.6 6.3 %early_angles.1 = (f32[640,1024]{1,0:T(8,128)S(1)}, s16[640,288]{1,0:T(8,128)(2,1)S(1)}) custom-call(s32[3]{0:T(128)S(1)} %pad_add_fusion.3.at_ref, s16[144,1024]{1,0:T(8,128)(2,1)S(1)} %fusion.refs_0_, s16[144,1024]{1,0:T(8,128)(2,1)} %collective-permute-done.refs_1_, s16[144,1024]{1,0:T(8,128)(2,1)S(1)} %collective-permute-done.1.refs_2_, ...), custom_call_target="tpu_custom_call" | custom-call | flops 3523215360 | bytes 5242880 | tf_op jit(solution)/shard_map/early_angles/pallas_call | solution.py:173
  35.1 1.4 %collective-permute-done.10.other_ref = s16[144,1024]{1,0:T(8,128)(2,1)S(1)} collective-permute-done((s16[144,1024]{1,0:T(8,128)(2,1)S(1)}, s16[144,1024]{1,0:T(8,128)(2,1)S(1)}, u32[]{:S(2)}, u32[]{:S(2)}) %collective-permute-start.10) | collective-permute-done | bytes 294944 | tf_op jit(solution)/shard_map/ppermute | solution.py:56
  36.6 4.4 %late_angles.1 = (bf16[640,1024]{1,0:T(8,128)(2,1)S(1)}, f32[64,1024]{1,0:T(8,128)S(1)}, bf16[64,1024]{1,0:T(8,128)(2,1)S(1)}) custom-call(f32[640,1024]{1,0:T(8,128)S(1)} %get-tuple-element.32.sum_ref, s16[144,1024]{1,0:T(8,128)(2,1)S(1)} %collective-permute-done.9.own_ref, s16[144,1024]{1,0:T(8,128)(2,1)S(1)} %collective-permute-done.10.other_ref, ...), custom_call_target="tpu_custom_call" | custom-call | flops 1132462080 | bytes 3932160 | tf_op jit(solution)/shard_map/late_angles/pallas_call | solution.py:197
  41.2 1.2 %collective-permute-done.11 = bf16[64,1024]{1,0:T(8,128)(2,1)S(1)} collective-permute-done((bf16[64,1024]{1,0:T(8,128)(2,1)S(1)}, bf16[64,1024]{1,0:T(8,128)(2,1)S(1)}, u32[]{:S(2)}, u32[]{:S(2)}) %collective-permute-start.11) | collective-permute-done | bytes 131104 | tf_op jit(solution)/shard_map/ppermute | solution.py:56
  42.6 0.2 constant_dynamic-slice_fusion
  43.0 0.4 collective-permute-start.22
  43.4 1.4 %collective-permute-start.12 = (bf16[16,1024]{1,0:T(8,128)(2,1)S(1)}, bf16[16,1024]{1,0:T(8,128)(2,1)S(1)}, u32[]{:S(2)}, u32[]{:S(2)}) collective-permute-start(bf16[16,1024]{1,0:T(8,128)(2,1)S(1)} %get-tuple-element.68), channel_id=1, source_target_pairs={{0,6},{1,7},{2,4},{3,5},{4,2},{5,3},{6,0},{7,1},{8,14},{9,15},{10,... | collective-permute-start | bytes 98312 | tf_op jit(solution)/shard_map/ppermute | solution.py:61
  44.8 0.4 collective-permute-start.13
  45.2 2.7 %collective-permute-start.14 = (bf16[16,1024]{1,0:T(8,128)(2,1)S(1)}, bf16[16,1024]{1,0:T(8,128)(2,1)S(1)}, u32[]{:S(2)}, u32[]{:S(2)}) collective-permute-start(bf16[16,1024]{1,0:T(8,128)(2,1)S(1)} %get-tuple-element.69), channel_id=1, source_target_pairs={{0,2},{1,3},{2,0},{3,1},{4,6},{5,7},{6,4},{7,5},{8,10},{9,11},{10,... | collective-permute-start | bytes 98312 | tf_op jit(solution)/shard_map/ppermute | solution.py:61
  47.9 1.3 %collective-permute-done.12 = bf16[16,1024]{1,0:T(8,128)(2,1)S(1)} collective-permute-done((bf16[16,1024]{1,0:T(8,128)(2,1)S(1)}, bf16[16,1024]{1,0:T(8,128)(2,1)S(1)}, u32[]{:S(2)}, u32[]{:S(2)}) %collective-permute-start.12) | collective-permute-done | bytes 32800 | tf_op jit(solution)/shard_map/ppermute | solution.py:61
  49.2 0.9 collective-permute-done.13
  50.2 2.2 %collective-permute-start.15 = (bf16[16,1024]{1,0:T(8,128)(2,1)S(1)}, bf16[16,1024]{1,0:T(8,128)(2,1)S(1)}, u32[]{:S(2)}, u32[]{:S(2)}) collective-permute-start(bf16[16,1024]{1,0:T(8,128)(2,1)S(1)} %fusion.32), channel_id=1, source_target_pairs={{0,6},{1,7},{2,4},{3,5},{4,2},{5,3},{6,0},{7,1},{8,14},{9,15},{10,... | collective-permute-start | bytes 98312 | tf_op jit(solution)/shard_map/ppermute | solution.py:61
  52.4 1.0 collective-permute-start.16
  53.4 1.3 %collective-permute-start.17 = (bf16[16,1024]{1,0:T(8,128)(2,1)S(1)}, bf16[16,1024]{1,0:T(8,128)(2,1)S(1)}, u32[]{:S(2)}, u32[]{:S(2)}) collective-permute-start(bf16[16,1024]{1,0:T(8,128)(2,1)S(1)} %fusion.32), channel_id=1, source_target_pairs={{0,2},{1,3},{2,0},{3,1},{4,6},{5,7},{6,4},{7,5},{8,10},{9,11},{10,... | collective-permute-start | bytes 98312 | tf_op jit(solution)/shard_map/ppermute | solution.py:61
  54.6 1.6 %pad_maximum_fusion = bf16[1280,1024]{1,0:T(8,128)(2,1)S(1)} fusion(bf16[640,1024]{1,0:T(8,128)(2,1)} %collective-permute-done.18, bf16[640,1024]{1,0:T(8,128)(2,1)S(1)} %get-tuple-element.41), kind=kLoop, calls=%fused_computation | loop fusion | flops 5242880 | bytes 5242880 | tf_op jit(solution)/shard_map/concatenate | solution.py:333
  56.2 1.0 collective-permute-done.16
  57.2 0.3 collective-permute-done.17
  57.5 0.9 fusion.47
  58.4 1.5 %collective-permute-start.19 = (bf16[64,1280]{1,0:T(8,128)(2,1)S(1)}, bf16[64,1280]{1,0:T(8,128)(2,1)S(1)}, u32[]{:S(2)}, u32[]{:S(2)}) collective-permute-start(bf16[64,1280]{1,0:T(8,128)(2,1)S(1)} %get-tuple-element.73), channel_id=1, source_target_pairs={{0,24},{8,16},{16,8},{24,0},{1,25},{9,17},{17,9},{25,1},{2,26},{10... | collective-permute-start | bytes 491528 | tf_op jit(solution)/shard_map/ppermute | solution.py:70
  59.9 0.6 collective-permute-start.20
  60.6 1.4 %collective-permute-start.21 = (bf16[64,1280]{1,0:T(8,128)(2,1)S(1)}, bf16[64,1280]{1,0:T(8,128)(2,1)S(1)}, u32[]{:S(2)}, u32[]{:S(2)}) collective-permute-start(bf16[64,1280]{1,0:T(8,128)(2,1)S(1)} %get-tuple-element.73), channel_id=1, source_target_pairs={{0,8},{8,0},{16,24},{24,16},{1,9},{9,1},{17,25},{25,17},{2,10},{10... | collective-permute-start | bytes 491528 | tf_op jit(solution)/shard_map/ppermute | solution.py:70
  62.0 3.3 %collective-permute-done.19 = bf16[64,1280]{1,0:T(8,128)(2,1)S(1)} collective-permute-done((bf16[64,1280]{1,0:T(8,128)(2,1)S(1)}, bf16[64,1280]{1,0:T(8,128)(2,1)S(1)}, u32[]{:S(2)}, u32[]{:S(2)}) %collective-permute-start.19) | collective-permute-done | bytes 163872 | tf_op jit(solution)/shard_map/ppermute | solution.py:70
  65.3 1.5 %collective-permute-done.20 = bf16[64,1280]{1,0:T(8,128)(2,1)S(1)} collective-permute-done((bf16[64,1280]{1,0:T(8,128)(2,1)S(1)}, bf16[64,1280]{1,0:T(8,128)(2,1)S(1)}, u32[]{:S(2)}, u32[]{:S(2)}) %collective-permute-start.20) | collective-permute-done | bytes 163872 | tf_op jit(solution)/shard_map/ppermute | solution.py:70
  66.9 0.6 fusion.48
  67.5 1.9 %collective-permute-start.23 = (bf16[16,1024]{1,0:T(8,128)(2,1)S(1)}, bf16[16,1024]{1,0:T(8,128)(2,1)S(1)}, u32[]{:S(2)}, u32[]{:S(2)}) collective-permute-start(bf16[16,1024]{1,0:T(8,128)(2,1)S(1)} %get-tuple-element.65), channel_id=1, source_target_pairs={{0,6},{1,7},{2,4},{3,5},{4,2},{5,3},{6,0},{7,1},{8,14},{9,15},{10,... | collective-permute-start | bytes 98312 | tf_op jit(solution)/shard_map/ppermute | solution.py:61
  69.3 0.7 collective-permute-start.24
  70.0 1.9 %collective-permute-start.25 = (bf16[16,1024]{1,0:T(8,128)(2,1)S(1)}, bf16[16,1024]{1,0:T(8,128)(2,1)S(1)}, u32[]{:S(2)}, u32[]{:S(2)}) collective-permute-start(bf16[16,1024]{1,0:T(8,128)(2,1)S(1)} %get-tuple-element.66), channel_id=1, source_target_pairs={{0,2},{1,3},{2,0},{3,1},{4,6},{5,7},{6,4},{7,5},{8,10},{9,11},{10,... | collective-permute-start | bytes 98312 | tf_op jit(solution)/shard_map/ppermute | solution.py:61
  71.9 1.4 %collective-permute-done.23 = bf16[16,1024]{1,0:T(8,128)(2,1)S(1)} collective-permute-done((bf16[16,1024]{1,0:T(8,128)(2,1)S(1)}, bf16[16,1024]{1,0:T(8,128)(2,1)S(1)}, u32[]{:S(2)}, u32[]{:S(2)}) %collective-permute-start.23) | collective-permute-done | bytes 32800 | tf_op jit(solution)/shard_map/ppermute | solution.py:61
  73.3 1.4 %collective-permute-done.24 = bf16[16,1024]{1,0:T(8,128)(2,1)S(1)} collective-permute-done((bf16[16,1024]{1,0:T(8,128)(2,1)S(1)}, bf16[16,1024]{1,0:T(8,128)(2,1)S(1)}, u32[]{:S(2)}, u32[]{:S(2)}) %collective-permute-start.24) | collective-permute-done | bytes 32800 | tf_op jit(solution)/shard_map/ppermute | solution.py:61
  74.7 2.3 %collective-permute-start.26 = (bf16[16,1024]{1,0:T(8,128)(2,1)S(1)}, bf16[16,1024]{1,0:T(8,128)(2,1)S(1)}, u32[]{:S(2)}, u32[]{:S(2)}) collective-permute-start(bf16[16,1024]{1,0:T(8,128)(2,1)S(1)} %fusion.33), channel_id=1, source_target_pairs={{0,6},{1,7},{2,4},{3,5},{4,2},{5,3},{6,0},{7,1},{8,14},{9,15},{10,... | collective-permute-start | bytes 98312 | tf_op jit(solution)/shard_map/ppermute | solution.py:61
  77.1 0.3 collective-permute-start.27
  77.4 1.8 %collective-permute-start.28 = (bf16[16,1024]{1,0:T(8,128)(2,1)S(1)}, bf16[16,1024]{1,0:T(8,128)(2,1)S(1)}, u32[]{:S(2)}, u32[]{:S(2)}) collective-permute-start(bf16[16,1024]{1,0:T(8,128)(2,1)S(1)} %fusion.33), channel_id=1, source_target_pairs={{0,2},{1,3},{2,0},{3,1},{4,6},{5,7},{6,4},{7,5},{8,10},{9,11},{10,... | collective-permute-start | bytes 98312 | tf_op jit(solution)/shard_map/ppermute | solution.py:61
  79.2 1.3 %collective-permute-done.26 = bf16[16,1024]{1,0:T(8,128)(2,1)S(1)} collective-permute-done((bf16[16,1024]{1,0:T(8,128)(2,1)S(1)}, bf16[16,1024]{1,0:T(8,128)(2,1)S(1)}, u32[]{:S(2)}, u32[]{:S(2)}) %collective-permute-start.26) | collective-permute-done | bytes 32800 | tf_op jit(solution)/shard_map/ppermute | solution.py:61
  80.5 1.4 %collective-permute-done.27 = bf16[16,1024]{1,0:T(8,128)(2,1)S(1)} collective-permute-done((bf16[16,1024]{1,0:T(8,128)(2,1)S(1)}, bf16[16,1024]{1,0:T(8,128)(2,1)S(1)}, u32[]{:S(2)}, u32[]{:S(2)}) %collective-permute-start.27) | collective-permute-done | bytes 32800 | tf_op jit(solution)/shard_map/ppermute | solution.py:61
  81.9 0.9 fusion.49
  82.8 1.5 %collective-permute-start.29 = (bf16[64,1280]{1,0:T(8,128)(2,1)S(1)}, bf16[64,1280]{1,0:T(8,128)(2,1)S(1)}, u32[]{:S(2)}, u32[]{:S(2)}) collective-permute-start(bf16[64,1280]{1,0:T(8,128)(2,1)S(1)} %get-tuple-element.77), channel_id=1, source_target_pairs={{0,24},{8,16},{16,8},{24,0},{1,25},{9,17},{17,9},{25,1},{2,26},{10... | collective-permute-start | bytes 491528 | tf_op jit(solution)/shard_map/ppermute | solution.py:70
  84.4 0.9 collective-permute-start.30
  85.3 1.1 %collective-permute-start.31 = (bf16[64,1280]{1,0:T(8,128)(2,1)S(1)}, bf16[64,1280]{1,0:T(8,128)(2,1)S(1)}, u32[]{:S(2)}, u32[]{:S(2)}) collective-permute-start(bf16[64,1280]{1,0:T(8,128)(2,1)S(1)} %get-tuple-element.77), channel_id=1, source_target_pairs={{0,8},{8,0},{16,24},{24,16},{1,9},{9,1},{17,25},{25,17},{2,10},{10... | collective-permute-start | bytes 491528 | tf_op jit(solution)/shard_map/ppermute | solution.py:70
  86.4 2.8 %collective-permute-done.29 = bf16[64,1280]{1,0:T(8,128)(2,1)S(1)} collective-permute-done((bf16[64,1280]{1,0:T(8,128)(2,1)S(1)}, bf16[64,1280]{1,0:T(8,128)(2,1)S(1)}, u32[]{:S(2)}, u32[]{:S(2)}) %collective-permute-start.29) | collective-permute-done | bytes 163872 | tf_op jit(solution)/shard_map/ppermute | solution.py:70
  89.2 1.7 %collective-permute-done.30 = bf16[64,1280]{1,0:T(8,128)(2,1)S(1)} collective-permute-done((bf16[64,1280]{1,0:T(8,128)(2,1)S(1)}, bf16[64,1280]{1,0:T(8,128)(2,1)S(1)}, u32[]{:S(2)}, u32[]{:S(2)}) %collective-permute-start.30) | collective-permute-done | bytes 163872 | tf_op jit(solution)/shard_map/ppermute | solution.py:70
  91.0 2.3 %fusion.50 = (bf16[64,1024]{1,0:T(8,128)(2,1)S(1)}, f32[64,1024]{1,0:T(8,128)S(1)}) fusion(bf16[64,1280]{1,0:T(8,128)(2,1)S(1)} %get-tuple-element.44, bf16[1280,1024]{1,0:T(8,128)(2,1)} %copy-done.1), kind=kOutput, calls=%fused_computation.93 | convolution fusion | flops 167837696 | bytes 3178496 | tf_op jit(solution)/shard_map/dot_general | solution.py:51
  93.5 1.9 %collective-permute-start.33 = (bf16[16,1024]{1,0:T(8,128)(2,1)S(1)}, bf16[16,1024]{1,0:T(8,128)(2,1)S(1)}, u32[]{:S(2)}, u32[]{:S(2)}) collective-permute-start(bf16[16,1024]{1,0:T(8,128)(2,1)S(1)} %get-tuple-element.62), channel_id=1, source_target_pairs={{0,6},{1,7},{2,4},{3,5},{4,2},{5,3},{6,0},{7,1},{8,14},{9,15},{10,... | collective-permute-start | bytes 98312 | tf_op jit(solution)/shard_map/ppermute | solution.py:61
  95.4 0.9 collective-permute-start.34
  96.3 1.7 %collective-permute-start.35 = (bf16[16,1024]{1,0:T(8,128)(2,1)S(1)}, bf16[16,1024]{1,0:T(8,128)(2,1)S(1)}, u32[]{:S(2)}, u32[]{:S(2)}) collective-permute-start(bf16[16,1024]{1,0:T(8,128)(2,1)S(1)} %get-tuple-element.63), channel_id=1, source_target_pairs={{0,2},{1,3},{2,0},{3,1},{4,6},{5,7},{6,4},{7,5},{8,10},{9,11},{10,... | collective-permute-start | bytes 98312 | tf_op jit(solution)/shard_map/ppermute | solution.py:61
  98.0 0.6 fusion.17
  98.7 0.7 collective-permute-done.33
  99.4 1.3 %collective-permute-done.34 = bf16[16,1024]{1,0:T(8,128)(2,1)S(1)} collective-permute-done((bf16[16,1024]{1,0:T(8,128)(2,1)S(1)}, bf16[16,1024]{1,0:T(8,128)(2,1)S(1)}, u32[]{:S(2)}, u32[]{:S(2)}) %collective-permute-start.34) | collective-permute-done | bytes 32800 | tf_op jit(solution)/shard_map/ppermute | solution.py:61
  100.7 0.6 add_bitcast_fusion
  (60 shorter events, 1.9 us)
Async XLA Ops:
  0.6 42.0 %copy-start = (s32[1024,128]{1,0:T(8,128)S(1)}, s32[1024,128]{1,0:T(8,128)}, u32[]{:S(2)}) copy-start(s32[1024,128]{1,0:T(8,128)} %param.9) | copy-start | bytes 1572868
  0.6 22.5 %copy-start.3 = (f32[640]{0:T(1024)S(1)}, f32[640]{0:T(1024)}, u32[]{:S(2)}) copy-start(f32[640]{0:T(1024)} %param.7) | copy-start | bytes 7684
  1.9 10.4 %collective-permute-start.1 = (s16[144,1024]{1,0:T(8,128)(2,1)S(1)}, s16[144,1024]{1,0:T(8,128)(2,1)S(1)}, u32[]{:S(2)}, u32[]{:S(2)}) collective-permute-start(s16[144,1024]{1,0:T(8,128)(2,1)S(1)} %fusion.refs_0_), channel_id=1, source_target_pairs={{0,4},{1,5},{4,6},{5,7},{6,2},{7,3},{2,0},{3,1},{8,12},{9,13},{12,... | collective-permute-start | bytes 884744 | tf_op jit(solution)/shard_map/ppermute | solution.py:65
  8.1 11.0 %collective-permute-start.2 = (s16[320,640]{1,0:T(8,128)(2,1)S(1)}, s16[320,640]{1,0:T(8,128)(2,1)S(1)}, u32[]{:S(2)}, u32[]{:S(2)}) collective-permute-start(s16[320,640]{1,0:T(8,128)(2,1)S(1)} %pad_add_fusion.refs_6_), channel_id=1, source_target_pairs={{0,8},{8,0},{16,24},{24,16},{1,9},{9,1},{17,25},{25,17},{2,10},{10... | collective-permute-start | bytes 1228808 | tf_op jit(solution)/shard_map/ppermute | solution.py:70
  9.6 10.6 %collective-permute-start.3 = (s16[320,640]{1,0:T(8,128)(2,1)S(1)}, s16[320,640]{1,0:T(8,128)(2,1)S(1)}, u32[]{:S(2)}, u32[]{:S(2)}) collective-permute-start(s16[320,640]{1,0:T(8,128)(2,1)S(1)} %pad_add_fusion.refs_6_), channel_id=1, source_target_pairs={{0,16},{8,24},{16,0},{24,8},{1,17},{9,25},{17,1},{25,9},{2,18},{10... | collective-permute-start | bytes 1228808 | tf_op jit(solution)/shard_map/ppermute | solution.py:70
  12.2 8.0 %collective-permute-start.4 = (s16[144,1024]{1,0:T(8,128)(2,1)S(1)}, s16[144,1024]{1,0:T(8,128)(2,1)S(1)}, u32[]{:S(2)}, u32[]{:S(2)}) collective-permute-start(s16[144,1024]{1,0:T(8,128)(2,1)S(1)} %collective-permute-done.1.refs_2_), channel_id=1, source_target_pairs={{0,1},{1,0},{2,3},{3,2},{4,5},{5,4},{6,7},{7,6},{8,9},{9,8},{10,11... | collective-permute-start | bytes 884744 | tf_op jit(solution)/shard_map/ppermute | solution.py:56
  12.2 16.4 %collective-permute-start = (s16[144,1024]{1,0:T(8,128)(2,1)S(1)}, s16[144,1024]{1,0:T(8,128)(2,1)}, u32[]{:S(2)}, u32[]{:S(2)}) collective-permute-start(s16[144,1024]{1,0:T(8,128)(2,1)S(1)} %fusion.refs_0_), channel_id=1, source_target_pairs={{0,1},{1,0},{2,3},{3,2},{4,5},{5,4},{6,7},{7,6},{8,9},{9,8},{10,11... | collective-permute-start | bytes 884744 | tf_op jit(solution)/shard_map/ppermute | solution.py:56
  12.7 10.6 %collective-permute-start.7 = (s16[144,1024]{1,0:T(8,128)(2,1)S(1)}, s16[144,1024]{1,0:T(8,128)(2,1)S(1)}, u32[]{:S(2)}, u32[]{:S(2)}) collective-permute-start(s16[144,1024]{1,0:T(8,128)(2,1)S(1)} %collective-permute-done.1.refs_2_), channel_id=1, source_target_pairs={{0,4},{1,5},{4,6},{5,7},{6,2},{7,3},{2,0},{3,1},{8,12},{9,13},{12,... | collective-permute-start | bytes 884744 | tf_op jit(solution)/shard_map/ppermute | solution.py:65
  20.3 5.8 %collective-permute-start.5 = (s16[160,640]{1,0:T(8,128)(2,1)S(1)}, s16[160,640]{1,0:T(8,128)(2,1)S(1)}, u32[]{:S(2)}, u32[]{:S(2)}) collective-permute-start(s16[160,640]{1,0:T(8,128)(2,1)S(1)} %slice.100), channel_id=1, source_target_pairs={{0,16},{8,24},{16,0},{24,8},{1,17},{9,25},{17,1},{25,9},{2,18},{10... | collective-permute-start | bytes 614408 | tf_op jit(solution)/shard_map/ppermute | solution.py:70
  22.6 6.0 %collective-permute-start.6 = (s16[160,640]{1,0:T(8,128)(2,1)}, s16[160,640]{1,0:T(8,128)(2,1)S(1)}, u32[]{:S(2)}, u32[]{:S(2)}) collective-permute-start(s16[160,640]{1,0:T(8,128)(2,1)} %slice.101), channel_id=1, source_target_pairs={{0,8},{8,0},{16,24},{24,16},{1,9},{9,1},{17,25},{25,17},{2,10},{10... | collective-permute-start | bytes 614408 | tf_op jit(solution)/shard_map/ppermute | solution.py:70
  23.3 5.3 %collective-permute-start.8 = (s16[144,1024]{1,0:T(8,128)(2,1)S(1)}, s16[144,1024]{1,0:T(8,128)(2,1)S(1)}, u32[]{:S(2)}, u32[]{:S(2)}) collective-permute-start(s16[144,1024]{1,0:T(8,128)(2,1)S(1)} %collective-permute-done.7.refs_4_), channel_id=1, source_target_pairs={{0,1},{1,0},{2,3},{3,2},{4,5},{5,4},{6,7},{7,6},{8,9},{9,8},{10,11... | collective-permute-start | bytes 884744 | tf_op jit(solution)/shard_map/ppermute | solution.py:56
  23.4 11.5 %collective-permute-start.9 = (s16[144,1024]{1,0:T(8,128)(2,1)S(1)}, s16[144,1024]{1,0:T(8,128)(2,1)S(1)}, u32[]{:S(2)}, u32[]{:S(2)}) collective-permute-start(s16[144,1024]{1,0:T(8,128)(2,1)S(1)} %collective-permute-done.7.refs_4_), channel_id=1, source_target_pairs={{0,4},{1,5},{4,6},{5,7},{6,2},{7,3},{2,0},{3,1},{8,12},{9,13},{12,... | collective-permute-start | bytes 884744 | tf_op jit(solution)/shard_map/ppermute | solution.py:65
  34.9 1.6 %collective-permute-start.10 = (s16[144,1024]{1,0:T(8,128)(2,1)S(1)}, s16[144,1024]{1,0:T(8,128)(2,1)S(1)}, u32[]{:S(2)}, u32[]{:S(2)}) collective-permute-start(s16[144,1024]{1,0:T(8,128)(2,1)S(1)} %collective-permute-done.9.own_ref), channel_id=1, source_target_pairs={{0,1},{1,0},{2,3},{3,2},{4,5},{5,4},{6,7},{7,6},{8,9},{9,8},{10,11... | collective-permute-start | bytes 884744 | tf_op jit(solution)/shard_map/ppermute | solution.py:56
  41.0 1.4 %collective-permute-start.11 = (bf16[64,1024]{1,0:T(8,128)(2,1)S(1)}, bf16[64,1024]{1,0:T(8,128)(2,1)S(1)}, u32[]{:S(2)}, u32[]{:S(2)}) collective-permute-start(bf16[64,1024]{1,0:T(8,128)(2,1)S(1)} %get-tuple-element.39), channel_id=1, source_target_pairs={{0,1},{1,0},{2,3},{3,2},{4,5},{5,4},{6,7},{7,6},{8,9},{9,8},{10,11... | collective-permute-start | bytes 393224 | tf_op jit(solution)/shard_map/ppermute | solution.py:56
  42.4 12.2 %collective-permute-start.18 = (bf16[640,1024]{1,0:T(8,128)(2,1)S(1)}, bf16[640,1024]{1,0:T(8,128)(2,1)}, u32[]{:S(2)}, u32[]{:S(2)}) collective-permute-start(bf16[640,1024]{1,0:T(8,128)(2,1)S(1)} %get-tuple-element.41), channel_id=1, source_target_pairs={{0,1},{1,0},{2,3},{3,2},{4,5},{5,4},{6,7},{7,6},{8,9},{9,8},{10,11... | collective-permute-start | bytes 3932168 | tf_op jit(solution)/shard_map/ppermute | solution.py:56
  43.0 19.0 %collective-permute-start.22 = (s16[64,640]{1,0:T(8,128)(2,1)S(1)}, s16[64,640]{1,0:T(8,128)(2,1)S(1)}, u32[]{:S(2)}, u32[]{:S(2)}) collective-permute-start(s16[64,640]{1,0:T(8,128)(2,1)S(1)} %get-tuple-element.37), channel_id=1, source_target_pairs={{0,1},{1,0},{2,3},{3,2},{4,5},{5,4},{6,7},{7,6},{8,9},{9,8},{10,11... | collective-permute-start | bytes 245768 | tf_op jit(solution)/shard_map/ppermute | solution.py:56
  43.4 5.8 %collective-permute-start.12 = (bf16[16,1024]{1,0:T(8,128)(2,1)S(1)}, bf16[16,1024]{1,0:T(8,128)(2,1)S(1)}, u32[]{:S(2)}, u32[]{:S(2)}) collective-permute-start(bf16[16,1024]{1,0:T(8,128)(2,1)S(1)} %get-tuple-element.68), channel_id=1, source_target_pairs={{0,6},{1,7},{2,4},{3,5},{4,2},{5,3},{6,0},{7,1},{8,14},{9,15},{10,... | collective-permute-start | bytes 98312 | tf_op jit(solution)/shard_map/ppermute | solution.py:61
  44.8 5.3 %collective-permute-start.13 = (bf16[16,1024]{1,0:T(8,128)(2,1)S(1)}, bf16[16,1024]{1,0:T(8,128)(2,1)S(1)}, u32[]{:S(2)}, u32[]{:S(2)}) collective-permute-start(bf16[16,1024]{1,0:T(8,128)(2,1)S(1)} %get-tuple-element.70), channel_id=1, source_target_pairs={{0,4},{1,5},{2,6},{3,7},{4,0},{5,1},{6,2},{7,3},{8,12},{9,13},{10,... | collective-permute-start | bytes 98312 | tf_op jit(solution)/shard_map/ppermute | solution.py:61
  45.2 4.9 %collective-permute-start.14 = (bf16[16,1024]{1,0:T(8,128)(2,1)S(1)}, bf16[16,1024]{1,0:T(8,128)(2,1)S(1)}, u32[]{:S(2)}, u32[]{:S(2)}) collective-permute-start(bf16[16,1024]{1,0:T(8,128)(2,1)S(1)} %get-tuple-element.69), channel_id=1, source_target_pairs={{0,2},{1,3},{2,0},{3,1},{4,6},{5,7},{6,4},{7,5},{8,10},{9,11},{10,... | collective-permute-start | bytes 98312 | tf_op jit(solution)/shard_map/ppermute | solution.py:61
  50.2 6.0 %collective-permute-start.15 = (bf16[16,1024]{1,0:T(8,128)(2,1)S(1)}, bf16[16,1024]{1,0:T(8,128)(2,1)S(1)}, u32[]{:S(2)}, u32[]{:S(2)}) collective-permute-start(bf16[16,1024]{1,0:T(8,128)(2,1)S(1)} %fusion.32), channel_id=1, source_target_pairs={{0,6},{1,7},{2,4},{3,5},{4,2},{5,3},{6,0},{7,1},{8,14},{9,15},{10,... | collective-permute-start | bytes 98312 | tf_op jit(solution)/shard_map/ppermute | solution.py:61
  52.4 4.8 %collective-permute-start.16 = (bf16[16,1024]{1,0:T(8,128)(2,1)S(1)}, bf16[16,1024]{1,0:T(8,128)(2,1)S(1)}, u32[]{:S(2)}, u32[]{:S(2)}) collective-permute-start(bf16[16,1024]{1,0:T(8,128)(2,1)S(1)} %fusion.32), channel_id=1, source_target_pairs={{0,4},{1,5},{2,6},{3,7},{4,0},{5,1},{6,2},{7,3},{8,12},{9,13},{10,... | collective-permute-start | bytes 98312 | tf_op jit(solution)/shard_map/ppermute | solution.py:61
  53.4 4.2 %collective-permute-start.17 = (bf16[16,1024]{1,0:T(8,128)(2,1)S(1)}, bf16[16,1024]{1,0:T(8,128)(2,1)S(1)}, u32[]{:S(2)}, u32[]{:S(2)}) collective-permute-start(bf16[16,1024]{1,0:T(8,128)(2,1)S(1)} %fusion.32), channel_id=1, source_target_pairs={{0,2},{1,3},{2,0},{3,1},{4,6},{5,7},{6,4},{7,5},{8,10},{9,11},{10,... | collective-permute-start | bytes 98312 | tf_op jit(solution)/shard_map/ppermute | solution.py:61
  56.2 25.7 %copy-start.1 = (bf16[1280,1024]{1,0:T(8,128)(2,1)}, bf16[1280,1024]{1,0:T(8,128)(2,1)S(1)}, u32[]{:S(2)}) copy-start(bf16[1280,1024]{1,0:T(8,128)(2,1)S(1)} %pad_maximum_fusion) | copy-start | bytes 7864324
  58.4 6.9 %collective-permute-start.19 = (bf16[64,1280]{1,0:T(8,128)(2,1)S(1)}, bf16[64,1280]{1,0:T(8,128)(2,1)S(1)}, u32[]{:S(2)}, u32[]{:S(2)}) collective-permute-start(bf16[64,1280]{1,0:T(8,128)(2,1)S(1)} %get-tuple-element.73), channel_id=1, source_target_pairs={{0,24},{8,16},{16,8},{24,0},{1,25},{9,17},{17,9},{25,1},{2,26},{10... | collective-permute-start | bytes 491528 | tf_op jit(solution)/shard_map/ppermute | solution.py:70
  59.9 6.8 %collective-permute-start.20 = (bf16[64,1280]{1,0:T(8,128)(2,1)S(1)}, bf16[64,1280]{1,0:T(8,128)(2,1)S(1)}, u32[]{:S(2)}, u32[]{:S(2)}) collective-permute-start(bf16[64,1280]{1,0:T(8,128)(2,1)S(1)} %get-tuple-element.73), channel_id=1, source_target_pairs={{0,16},{8,24},{16,0},{24,8},{1,17},{9,25},{17,1},{25,9},{2,18},{10... | collective-permute-start | bytes 491528 | tf_op jit(solution)/shard_map/ppermute | solution.py:70
  60.6 6.2 %collective-permute-start.21 = (bf16[64,1280]{1,0:T(8,128)(2,1)S(1)}, bf16[64,1280]{1,0:T(8,128)(2,1)S(1)}, u32[]{:S(2)}, u32[]{:S(2)}) collective-permute-start(bf16[64,1280]{1,0:T(8,128)(2,1)S(1)} %get-tuple-element.73), channel_id=1, source_target_pairs={{0,8},{8,0},{16,24},{24,16},{1,9},{9,1},{17,25},{25,17},{2,10},{10... | collective-permute-start | bytes 491528 | tf_op jit(solution)/shard_map/ppermute | solution.py:70
  67.5 5.8 %collective-permute-start.23 = (bf16[16,1024]{1,0:T(8,128)(2,1)S(1)}, bf16[16,1024]{1,0:T(8,128)(2,1)S(1)}, u32[]{:S(2)}, u32[]{:S(2)}) collective-permute-start(bf16[16,1024]{1,0:T(8,128)(2,1)S(1)} %get-tuple-element.65), channel_id=1, source_target_pairs={{0,6},{1,7},{2,4},{3,5},{4,2},{5,3},{6,0},{7,1},{8,14},{9,15},{10,... | collective-permute-start | bytes 98312 | tf_op jit(solution)/shard_map/ppermute | solution.py:61
  69.3 5.3 %collective-permute-start.24 = (bf16[16,1024]{1,0:T(8,128)(2,1)S(1)}, bf16[16,1024]{1,0:T(8,128)(2,1)S(1)}, u32[]{:S(2)}, u32[]{:S(2)}) collective-permute-start(bf16[16,1024]{1,0:T(8,128)(2,1)S(1)} %get-tuple-element.67), channel_id=1, source_target_pairs={{0,4},{1,5},{2,6},{3,7},{4,0},{5,1},{6,2},{7,3},{8,12},{9,13},{10,... | collective-permute-start | bytes 98312 | tf_op jit(solution)/shard_map/ppermute | solution.py:61
  70.0 4.7 %collective-permute-start.25 = (bf16[16,1024]{1,0:T(8,128)(2,1)S(1)}, bf16[16,1024]{1,0:T(8,128)(2,1)S(1)}, u32[]{:S(2)}, u32[]{:S(2)}) collective-permute-start(bf16[16,1024]{1,0:T(8,128)(2,1)S(1)} %get-tuple-element.66), channel_id=1, source_target_pairs={{0,2},{1,3},{2,0},{3,1},{4,6},{5,7},{6,4},{7,5},{8,10},{9,11},{10,... | collective-permute-start | bytes 98312 | tf_op jit(solution)/shard_map/ppermute | solution.py:61
  74.7 5.8 %collective-permute-start.26 = (bf16[16,1024]{1,0:T(8,128)(2,1)S(1)}, bf16[16,1024]{1,0:T(8,128)(2,1)S(1)}, u32[]{:S(2)}, u32[]{:S(2)}) collective-permute-start(bf16[16,1024]{1,0:T(8,128)(2,1)S(1)} %fusion.33), channel_id=1, source_target_pairs={{0,6},{1,7},{2,4},{3,5},{4,2},{5,3},{6,0},{7,1},{8,14},{9,15},{10,... | collective-permute-start | bytes 98312 | tf_op jit(solution)/shard_map/ppermute | solution.py:61
  77.1 4.8 %collective-permute-start.27 = (bf16[16,1024]{1,0:T(8,128)(2,1)S(1)}, bf16[16,1024]{1,0:T(8,128)(2,1)S(1)}, u32[]{:S(2)}, u32[]{:S(2)}) collective-permute-start(bf16[16,1024]{1,0:T(8,128)(2,1)S(1)} %fusion.33), channel_id=1, source_target_pairs={{0,4},{1,5},{2,6},{3,7},{4,0},{5,1},{6,2},{7,3},{8,12},{9,13},{10,... | collective-permute-start | bytes 98312 | tf_op jit(solution)/shard_map/ppermute | solution.py:61
  77.4 4.5 %collective-permute-start.28 = (bf16[16,1024]{1,0:T(8,128)(2,1)S(1)}, bf16[16,1024]{1,0:T(8,128)(2,1)S(1)}, u32[]{:S(2)}, u32[]{:S(2)}) collective-permute-start(bf16[16,1024]{1,0:T(8,128)(2,1)S(1)} %fusion.33), channel_id=1, source_target_pairs={{0,2},{1,3},{2,0},{3,1},{4,6},{5,7},{6,4},{7,5},{8,10},{9,11},{10,... | collective-permute-start | bytes 98312 | tf_op jit(solution)/shard_map/ppermute | solution.py:61
  82.8 6.4 %collective-permute-start.29 = (bf16[64,1280]{1,0:T(8,128)(2,1)S(1)}, bf16[64,1280]{1,0:T(8,128)(2,1)S(1)}, u32[]{:S(2)}, u32[]{:S(2)}) collective-permute-start(bf16[64,1280]{1,0:T(8,128)(2,1)S(1)} %get-tuple-element.77), channel_id=1, source_target_pairs={{0,24},{8,16},{16,8},{24,0},{1,25},{9,17},{17,9},{25,1},{2,26},{10... | collective-permute-start | bytes 491528 | tf_op jit(solution)/shard_map/ppermute | solution.py:70
  84.4 6.5 %collective-permute-start.30 = (bf16[64,1280]{1,0:T(8,128)(2,1)S(1)}, bf16[64,1280]{1,0:T(8,128)(2,1)S(1)}, u32[]{:S(2)}, u32[]{:S(2)}) collective-permute-start(bf16[64,1280]{1,0:T(8,128)(2,1)S(1)} %get-tuple-element.77), channel_id=1, source_target_pairs={{0,16},{8,24},{16,0},{24,8},{1,17},{9,25},{17,1},{25,9},{2,18},{10... | collective-permute-start | bytes 491528 | tf_op jit(solution)/shard_map/ppermute | solution.py:70
  85.3 5.6 %collective-permute-start.31 = (bf16[64,1280]{1,0:T(8,128)(2,1)S(1)}, bf16[64,1280]{1,0:T(8,128)(2,1)S(1)}, u32[]{:S(2)}, u32[]{:S(2)}) collective-permute-start(bf16[64,1280]{1,0:T(8,128)(2,1)S(1)} %get-tuple-element.77), channel_id=1, source_target_pairs={{0,8},{8,0},{16,24},{24,16},{1,9},{9,1},{17,25},{25,17},{2,10},{10... | collective-permute-start | bytes 491528 | tf_op jit(solution)/shard_map/ppermute | solution.py:70
  91.0 7.0 %copy-start.2 = (f32[640,32]{0,1:T(8,128)S(1)}, f32[640,32]{0,1:T(8,128)}, u32[]{:S(2)}) copy-start(f32[640,32]{0,1:T(8,128)} %param.8) | copy-start | bytes 245764
  93.4 4.6 %collective-permute-start.32 = (f32[64,640]{1,0:T(8,128)S(1)}, f32[64,640]{1,0:T(8,128)S(1)}, u32[]{:S(2)}, u32[]{:S(2)}) collective-permute-start(f32[64,640]{1,0:T(8,128)S(1)} %get-tuple-element.53), channel_id=1, source_target_pairs={{0,1},{1,0},{2,3},{3,2},{4,5},{5,4},{6,7},{7,6},{8,9},{9,8},{10,11... | collective-permute-start | bytes 491528 | tf_op jit(solution)/shard_map/ppermute | solution.py:56
  93.5 5.8 %collective-permute-start.33 = (bf16[16,1024]{1,0:T(8,128)(2,1)S(1)}, bf16[16,1024]{1,0:T(8,128)(2,1)S(1)}, u32[]{:S(2)}, u32[]{:S(2)}) collective-permute-start(bf16[16,1024]{1,0:T(8,128)(2,1)S(1)} %get-tuple-element.62), channel_id=1, source_target_pairs={{0,6},{1,7},{2,4},{3,5},{4,2},{5,3},{6,0},{7,1},{8,14},{9,15},{10,... | collective-permute-start | bytes 98312 | tf_op jit(solution)/shard_map/ppermute | solution.py:61
  95.4 5.3 %collective-permute-start.34 = (bf16[16,1024]{1,0:T(8,128)(2,1)S(1)}, bf16[16,1024]{1,0:T(8,128)(2,1)S(1)}, u32[]{:S(2)}, u32[]{:S(2)}) collective-permute-start(bf16[16,1024]{1,0:T(8,128)(2,1)S(1)} %get-tuple-element.64), channel_id=1, source_target_pairs={{0,4},{1,5},{2,6},{3,7},{4,0},{5,1},{6,2},{7,3},{8,12},{9,13},{10,... | collective-permute-start | bytes 98312 | tf_op jit(solution)/shard_map/ppermute | solution.py:61
  96.3 4.4 %collective-permute-start.35 = (bf16[16,1024]{1,0:T(8,128)(2,1)S(1)}, bf16[16,1024]{1,0:T(8,128)(2,1)S(1)}, u32[]{:S(2)}, u32[]{:S(2)}) collective-permute-start(bf16[16,1024]{1,0:T(8,128)(2,1)S(1)} %get-tuple-element.63), channel_id=1, source_target_pairs={{0,2},{1,3},{2,0},{3,1},{4,6},{5,7},{6,4},{7,5},{8,10},{9,11},{10,... | collective-permute-start | bytes 98312 | tf_op jit(solution)/shard_map/ppermute | solution.py:61

commit v8 on v7

--- a/solution.py
+++ b/solution.py
@@ -158,7 +158,7 @@
     freqs = [freq_code, freq_x, freq_y, clip_swap(x_again[:rows], 2), clip_swap(y_again[rows:], 1)]
     other.append(core_swap(own[2]))
     *freqs, own[2] = tie((*freqs, own[2]))
-    betas, cast = prepare(freqs)
+    betas, cast, targets = prepare(freqs)
     early = [x for pair in zip(own[:3], other) for x in pair]
     used = len(early) * columns
     depth = -(-used // LANES) * LANES
@@ -193,6 +193,7 @@
         name="early_angles",
     )(jnp.stack([line, clip, core]).astype(jnp.int32), *early, *freqs)
     last, freq_last = tie((own[3], freq_last))
+    cast, betas = tie((cast, betas))
     outputs = cast.shape[0]
     phi, keep, send = pl.pallas_call(
         functools.partial(late_kernel, scale=scale),
@@ -221,7 +222,7 @@
         ),
         name="late_angles",
     )(summed, last, core_swap(last), freq_last, column, cast)
-    return phi, keep, send, betas
+    return phi, keep, send, betas, targets
 
 
 def phi_by_ring(embed_code, freq_code, column, scale, line, core, clip, prepare):
@@ -253,10 +254,10 @@
     freq_high, freq_low = split(freq_all)
     total = dot0(freq_high, embed_high) + (dot0(freq_high, embed_low) + dot0(freq_low, embed_high))
     phi = scaled_cos(total * PER_TURN + column, scale)
-    betas, cast = prepare(freqs)
+    betas, cast, targets = prepare(freqs)
     logits = mix(cast, phi)
     half = logits.shape[0] // 2
-    return phi, logits[:half], logits[half:].astype(jnp.bfloat16), betas
+    return phi, logits[:half], logits[half:].astype(jnp.bfloat16), betas, targets
 
 
 def per_device(embeds, frequencies, phases, weights, labels):
@@ -304,7 +305,8 @@
 
         own, sent = lax.optimization_barrier((ordered(core), ordered(1 - core)))
         cast = lax.optimization_barrier(decode(jnp.concatenate([own, sent])).astype(jnp.bfloat16))
-        return (decode(own), decode(core_swap(sent))), cast
+        targets = lax.dynamic_slice_in_dim(labels.T, feat * block, block, 0).astype(jnp.float32)
+        return (decode(own), decode(core_swap(sent))), cast, targets
 
     def share_of(parts):
         parts = parts.reshape(places, block, -1)
@@ -323,10 +325,9 @@
 
     by_kernels = places == 4 and n_clip == 4 and columns % 16 == 0 and slab == 2 * columns
     phi_of = phi_by_kernels if by_kernels else phi_by_ring
-    phi, keep, send, (beta_own, beta_other) = phi_of(
+    phi, keep, send, (beta_own, beta_other), targets = phi_of(
         embed_code, freq_code, column, scale, line, core, clip, prepare
     )
-    targets = lax.dynamic_slice_in_dim(labels.T, feat * block, block, 0).astype(jnp.float32)
     there = core_swap(send)
     parts = keep + there.astype(jnp.float32)
     phi_other = core_swap(lax.optimization_barrier((phi, there))[0])

time: 102 us -> 101 us (level)
  waiting for transfers between devices: 30.8 us -> 29.6 us
  transfers between devices with their start and end apart: 36 -> 36, of which waited for: 21 -> 22; matrix products, arithmetic and copies ran while one was open for 7% -> 6% of each run, Pallas kernels for 6% -> 6%
where the time goes in v8:
time: 101 us
  starting transfers between devices  46.6 us (46%)
  waiting for transfers between devices  29.6 us (29%)
  Pallas kernels  10.7 us (11%)
  other arithmetic  6.78 us (7%)
  matrix products  4.75 us (5%)
  local copies, waits for them, and re-layouts  1.44 us (1%)
    ppermute x15, starting transfers between devices, line_swap(): return lax.ppermute(x, 'feat', [(i, i ^ 2 * k) for i in range(n)])  22.3 us
    ppermute x10, waiting for transfers between devices, clip_swap(): return lax.ppermute(x, 'clip', [(i, i ^ k) for i in range(n)])  16.1 us
    ppermute x10, starting transfers between devices, clip_swap(): return lax.ppermute(x, 'clip', [(i, i ^ k) for i in range(n)])  12.3 us
    ppermute x15, waiting for transfers between devices, line_swap(): return lax.ppermute(x, 'feat', [(i, i ^ 2 * k) for i in range(n)])  10.3 us
    ppermute x3, starting transfers between devices, line_move(): lax.ppermute(x, 'feat', [(2 * a + c, 2 * b + c) for a, b in pairs for c i...  10 us
    pallas_call x1, Pallas kernels, phi_by_kernels(): pl.pallas_call(functools.partial(early_kernel, n_embeds=len(early), n_fre...  6.26 us
    pallas_call x1, Pallas kernels, phi_by_kernels(): pl.pallas_call(functools.partial(late_kernel, scale=scale), grid=(clips /...  4.43 us
    convert_element_type x3, other arithmetic, encode(): return jnp.round(x * (CODE_MAX / bound)).astype(jnp.int16)  3.26 us
  transfers between devices with their start and end apart: 36, of which 22 were waited for; matrix products, arithmetic and copies ran while one was open for 6% of the time, Pallas kernels for 6%

profile of v8, /device:TPU:0, one launch (start us, length us, event | category | flops | bytes accessed | tf_op | source)
XLA Modules:
  0.0 100.9 jit_solution(9167900681410180678)
XLA Ops:
  0.7 1.2 %fusion.refs_0_ = s16[144,1024]{1,0:T(8,128)(2,1)S(1)} fusion(f32[1024,144]{0,1:T(8,128)} %param.5), kind=kLoop, calls=%fused_computation.10 | loop fusion | flops 442368 | bytes 884736 | tf_op jit(solution)/shard_map/convert_element_type | solution.py:32
  1.9 4.1 %collective-permute-start.1 = (s16[144,1024]{1,0:T(8,128)(2,1)S(1)}, s16[144,1024]{1,0:T(8,128)(2,1)S(1)}, u32[]{:S(2)}, u32[]{:S(2)}) collective-permute-start(s16[144,1024]{1,0:T(8,128)(2,1)S(1)} %fusion.refs_0_), channel_id=1, source_target_pairs={{0,4},{1,5},{4,6},{5,7},{6,2},{7,3},{2,0},{3,1},{8,12},{9,13},{12,... | collective-permute-start | bytes 884744 | tf_op jit(solution)/shard_map/ppermute | solution.py:65
  6.0 1.2 %round-nearest-even_convert_fusion.2 = (s16[144,640]{1,0:T(8,128)(2,1)S(1)}, s16[144,640]{1,0:T(8,128)(2,1)S(1)}) fusion(f32[288,640]{1,0:T(8,128)} %param.6), kind=kLoop, calls=%fused_computation.4 | loop fusion | flops 552960 | bytes 1105920 | tf_op jit(solution)/shard_map/convert_element_type | solution.py:32
  7.2 0.8 fusion.38
  8.1 1.6 %collective-permute-start.2 = (s16[320,640]{1,0:T(8,128)(2,1)S(1)}, s16[320,640]{1,0:T(8,128)(2,1)S(1)}, u32[]{:S(2)}, u32[]{:S(2)}) collective-permute-start(s16[320,640]{1,0:T(8,128)(2,1)S(1)} %pad_add_fusion.refs_6_), channel_id=1, source_target_pairs={{0,8},{8,0},{16,24},{24,16},{1,9},{9,1},{17,25},{25,17},{2,10},{10... | collective-permute-start | bytes 1228808 | tf_op jit(solution)/shard_map/ppermute | solution.py:70
  9.6 1.5 %collective-permute-start.3 = (s16[320,640]{1,0:T(8,128)(2,1)S(1)}, s16[320,640]{1,0:T(8,128)(2,1)S(1)}, u32[]{:S(2)}, u32[]{:S(2)}) collective-permute-start(s16[320,640]{1,0:T(8,128)(2,1)S(1)} %pad_add_fusion.refs_6_), channel_id=1, source_target_pairs={{0,16},{8,24},{16,0},{24,8},{1,17},{9,25},{17,1},{25,9},{2,18},{10... | collective-permute-start | bytes 1228808 | tf_op jit(solution)/shard_map/ppermute | solution.py:70
  11.1 1.1 %collective-permute-done.1.refs_2_ = s16[144,1024]{1,0:T(8,128)(2,1)S(1)} collective-permute-done((s16[144,1024]{1,0:T(8,128)(2,1)S(1)}, s16[144,1024]{1,0:T(8,128)(2,1)S(1)}, u32[]{:S(2)}, u32[]{:S(2)}) %collective-permute-start.1) | collective-permute-done | bytes 294944 | tf_op jit(solution)/shard_map/ppermute | solution.py:65
  12.2 0.5 collective-permute-start
  12.7 3.4 %collective-permute-start.7 = (s16[144,1024]{1,0:T(8,128)(2,1)S(1)}, s16[144,1024]{1,0:T(8,128)(2,1)S(1)}, u32[]{:S(2)}, u32[]{:S(2)}) collective-permute-start(s16[144,1024]{1,0:T(8,128)(2,1)S(1)} %collective-permute-done.1.refs_2_), channel_id=1, source_target_pairs={{0,4},{1,5},{4,6},{5,7},{6,2},{7,3},{2,0},{3,1},{8,12},{9,13},{12,... | collective-permute-start | bytes 884744 | tf_op jit(solution)/shard_map/ppermute | solution.py:65
  16.1 2.9 %collective-permute-done.2.refs_7_ = s16[320,640]{1,0:T(8,128)(2,1)S(1)} collective-permute-done((s16[320,640]{1,0:T(8,128)(2,1)S(1)}, s16[320,640]{1,0:T(8,128)(2,1)S(1)}, u32[]{:S(2)}, u32[]{:S(2)}) %collective-permute-start.2) | collective-permute-done | bytes 409632 | tf_op jit(solution)/shard_map/ppermute | solution.py:70
  19.0 1.2 %collective-permute-done.3.refs_8_ = s16[320,640]{1,0:T(8,128)(2,1)S(1)} collective-permute-done((s16[320,640]{1,0:T(8,128)(2,1)S(1)}, s16[320,640]{1,0:T(8,128)(2,1)S(1)}, u32[]{:S(2)}, u32[]{:S(2)}) %collective-permute-start.3) | collective-permute-done | bytes 409632 | tf_op jit(solution)/shard_map/ppermute | solution.py:70
  20.3 1.6 %collective-permute-start.5 = (s16[160,640]{1,0:T(8,128)(2,1)S(1)}, s16[160,640]{1,0:T(8,128)(2,1)S(1)}, u32[]{:S(2)}, u32[]{:S(2)}) collective-permute-start(s16[160,640]{1,0:T(8,128)(2,1)S(1)} %slice.100), channel_id=1, source_target_pairs={{0,16},{8,24},{16,0},{24,8},{1,17},{9,25},{17,1},{25,9},{2,18},{10... | collective-permute-start | bytes 614408 | tf_op jit(solution)/shard_map/ppermute | solution.py:70
  21.9 0.7 slice.101
  22.6 0.5 collective-permute-start.6
  23.4 2.6 %collective-permute-start.9 = (s16[144,1024]{1,0:T(8,128)(2,1)S(1)}, s16[144,1024]{1,0:T(8,128)(2,1)S(1)}, u32[]{:S(2)}, u32[]{:S(2)}) collective-permute-start(s16[144,1024]{1,0:T(8,128)(2,1)S(1)} %collective-permute-done.7.refs_4_), channel_id=1, source_target_pairs={{0,4},{1,5},{4,6},{5,7},{6,2},{7,3},{2,0},{3,1},{8,12},{9,13},{12,... | collective-permute-start | bytes 884744 | tf_op jit(solution)/shard_map/ppermute | solution.py:65
  26.1 2.4 %collective-permute-done.6.refs_10_ = s16[160,640]{1,0:T(8,128)(2,1)S(1)} collective-permute-done((s16[160,640]{1,0:T(8,128)(2,1)}, s16[160,640]{1,0:T(8,128)(2,1)S(1)}, u32[]{:S(2)}, u32[]{:S(2)}) %collective-permute-start.6) | collective-permute-done | bytes 204832 | tf_op jit(solution)/shard_map/ppermute | solution.py:70
  28.8 6.3 %early_angles.1 = (f32[640,1024]{1,0:T(8,128)S(1)}, s16[640,288]{1,0:T(8,128)(2,1)S(1)}) custom-call(s32[3]{0:T(128)S(1)} %pad_add_fusion.3.at_ref, s16[144,1024]{1,0:T(8,128)(2,1)S(1)} %fusion.refs_0_, s16[144,1024]{1,0:T(8,128)(2,1)} %collective-permute-done.refs_1_, s16[144,1024]{1,0:T(8,128)(2,1)S(1)} %collective-permute-done.1.refs_2_, ...), custom_call_target="tpu_custom_call" | custom-call | flops 3523215360 | bytes 5242880 | tf_op jit(solution)/shard_map/early_angles/pallas_call | solution.py:173
  35.1 0.6 collective-permute-start.10
  35.8 1.1 %collective-permute-done.10.other_ref = s16[144,1024]{1,0:T(8,128)(2,1)S(1)} collective-permute-done((s16[144,1024]{1,0:T(8,128)(2,1)S(1)}, s16[144,1024]{1,0:T(8,128)(2,1)S(1)}, u32[]{:S(2)}, u32[]{:S(2)}) %collective-permute-start.10) | collective-permute-done | bytes 294944 | tf_op jit(solution)/shard_map/ppermute | solution.py:56
  36.9 4.4 %late_angles.1 = (bf16[640,1024]{1,0:T(8,128)(2,1)S(1)}, f32[64,1024]{1,0:T(8,128)S(1)}, bf16[64,1024]{1,0:T(8,128)(2,1)S(1)}) custom-call(f32[640,1024]{1,0:T(8,128)S(1)} %get-tuple-element.35.sum_ref, s16[144,1024]{1,0:T(8,128)(2,1)S(1)} %collective-permute-done.9.own_ref, s16[144,1024]{1,0:T(8,128)(2,1)S(1)} %collective-permute-done.10.other_ref, ...), custom_call_target="tpu_custom_call" | custom-call | flops 1132462080 | bytes 3932160 | tf_op jit(solution)/shard_map/late_angles/pallas_call | solution.py:198
  41.3 0.4 collective-permute-start.12
  41.8 1.0 collective-permute-done.12
  42.7 0.4 collective-permute-start.19
  43.2 1.4 %collective-permute-start.13 = (bf16[16,1024]{1,0:T(8,128)(2,1)S(1)}, bf16[16,1024]{1,0:T(8,128)(2,1)S(1)}, u32[]{:S(2)}, u32[]{:S(2)}) collective-permute-start(bf16[16,1024]{1,0:T(8,128)(2,1)S(1)} %get-tuple-element.74), channel_id=1, source_target_pairs={{0,6},{1,7},{2,4},{3,5},{4,2},{5,3},{6,0},{7,1},{8,14},{9,15},{10,... | collective-permute-start | bytes 98312 | tf_op jit(solution)/shard_map/ppermute | solution.py:61
  44.9 2.7 %collective-permute-start.15 = (bf16[16,1024]{1,0:T(8,128)(2,1)S(1)}, bf16[16,1024]{1,0:T(8,128)(2,1)S(1)}, u32[]{:S(2)}, u32[]{:S(2)}) collective-permute-start(bf16[16,1024]{1,0:T(8,128)(2,1)S(1)} %get-tuple-element.75), channel_id=1, source_target_pairs={{0,2},{1,3},{2,0},{3,1},{4,6},{5,7},{6,4},{7,5},{8,10},{9,11},{10,... | collective-permute-start | bytes 98312 | tf_op jit(solution)/shard_map/ppermute | solution.py:61
  48.0 1.0 collective-permute-done.13
  48.9 0.9 collective-permute-done.14
  49.9 2.2 %collective-permute-start.16 = (bf16[16,1024]{1,0:T(8,128)(2,1)S(1)}, bf16[16,1024]{1,0:T(8,128)(2,1)S(1)}, u32[]{:S(2)}, u32[]{:S(2)}) collective-permute-start(bf16[16,1024]{1,0:T(8,128)(2,1)S(1)} %fusion.32), channel_id=1, source_target_pairs={{0,6},{1,7},{2,4},{3,5},{4,2},{5,3},{6,0},{7,1},{8,14},{9,15},{10,... | collective-permute-start | bytes 98312 | tf_op jit(solution)/shard_map/ppermute | solution.py:61
  52.1 1.0 collective-permute-start.17
  53.1 1.3 %collective-permute-start.18 = (bf16[16,1024]{1,0:T(8,128)(2,1)S(1)}, bf16[16,1024]{1,0:T(8,128)(2,1)S(1)}, u32[]{:S(2)}, u32[]{:S(2)}) collective-permute-start(bf16[16,1024]{1,0:T(8,128)(2,1)S(1)} %fusion.32), channel_id=1, source_target_pairs={{0,2},{1,3},{2,0},{3,1},{4,6},{5,7},{6,4},{7,5},{8,10},{9,11},{10,... | collective-permute-start | bytes 98312 | tf_op jit(solution)/shard_map/ppermute | solution.py:61
  54.4 1.6 %pad_maximum_fusion = bf16[1280,1024]{1,0:T(8,128)(2,1)S(1)} fusion(bf16[640,1024]{1,0:T(8,128)(2,1)} %collective-permute-done.19, bf16[640,1024]{1,0:T(8,128)(2,1)S(1)} %get-tuple-element.45), kind=kLoop, calls=%fused_computation | loop fusion | flops 5242880 | bytes 5242880 | tf_op jit(solution)/shard_map/concatenate | solution.py:334
  56.0 1.0 collective-permute-done.17
  56.9 0.3 collective-permute-done.18
  57.3 0.9 fusion.47
  58.2 1.0 collective-permute-start.20
  59.2 1.2 %collective-permute-start.21 = (bf16[64,1280]{1,0:T(8,128)(2,1)S(1)}, bf16[64,1280]{1,0:T(8,128)(2,1)S(1)}, u32[]{:S(2)}, u32[]{:S(2)}) collective-permute-start(bf16[64,1280]{1,0:T(8,128)(2,1)S(1)} %get-tuple-element.79), channel_id=1, source_target_pairs={{0,16},{8,24},{16,0},{24,8},{1,17},{9,25},{17,1},{25,9},{2,18},{10... | collective-permute-start | bytes 491528 | tf_op jit(solution)/shard_map/ppermute | solution.py:70
  60.3 1.4 %collective-permute-start.22 = (bf16[64,1280]{1,0:T(8,128)(2,1)S(1)}, bf16[64,1280]{1,0:T(8,128)(2,1)S(1)}, u32[]{:S(2)}, u32[]{:S(2)}) collective-permute-start(bf16[64,1280]{1,0:T(8,128)(2,1)S(1)} %get-tuple-element.79), channel_id=1, source_target_pairs={{0,8},{8,0},{16,24},{24,16},{1,9},{9,1},{17,25},{25,17},{2,10},{10... | collective-permute-start | bytes 491528 | tf_op jit(solution)/shard_map/ppermute | solution.py:70
  61.8 3.3 %collective-permute-done.20 = bf16[64,1280]{1,0:T(8,128)(2,1)S(1)} collective-permute-done((bf16[64,1280]{1,0:T(8,128)(2,1)S(1)}, bf16[64,1280]{1,0:T(8,128)(2,1)S(1)}, u32[]{:S(2)}, u32[]{:S(2)}) %collective-permute-start.20) | collective-permute-done | bytes 163872 | tf_op jit(solution)/shard_map/ppermute | solution.py:70
  65.0 1.6 %collective-permute-done.21 = bf16[64,1280]{1,0:T(8,128)(2,1)S(1)} collective-permute-done((bf16[64,1280]{1,0:T(8,128)(2,1)S(1)}, bf16[64,1280]{1,0:T(8,128)(2,1)S(1)}, u32[]{:S(2)}, u32[]{:S(2)}) %collective-permute-start.21) | collective-permute-done | bytes 163872 | tf_op jit(solution)/shard_map/ppermute | solution.py:70
  66.8 0.6 fusion.48
  67.3 1.7 %collective-permute-start.23 = (bf16[16,1024]{1,0:T(8,128)(2,1)S(1)}, bf16[16,1024]{1,0:T(8,128)(2,1)S(1)}, u32[]{:S(2)}, u32[]{:S(2)}) collective-permute-start(bf16[16,1024]{1,0:T(8,128)(2,1)S(1)} %get-tuple-element.71), channel_id=1, source_target_pairs={{0,6},{1,7},{2,4},{3,5},{4,2},{5,3},{6,0},{7,1},{8,14},{9,15},{10,... | collective-permute-start | bytes 98312 | tf_op jit(solution)/shard_map/ppermute | solution.py:61
  69.1 0.5 collective-permute-start.24
  69.6 2.2 %collective-permute-start.25 = (bf16[16,1024]{1,0:T(8,128)(2,1)S(1)}, bf16[16,1024]{1,0:T(8,128)(2,1)S(1)}, u32[]{:S(2)}, u32[]{:S(2)}) collective-permute-start(bf16[16,1024]{1,0:T(8,128)(2,1)S(1)} %get-tuple-element.72), channel_id=1, source_target_pairs={{0,2},{1,3},{2,0},{3,1},{4,6},{5,7},{6,4},{7,5},{8,10},{9,11},{10,... | collective-permute-start | bytes 98312 | tf_op jit(solution)/shard_map/ppermute | solution.py:61
  71.8 1.3 %collective-permute-done.23 = bf16[16,1024]{1,0:T(8,128)(2,1)S(1)} collective-permute-done((bf16[16,1024]{1,0:T(8,128)(2,1)S(1)}, bf16[16,1024]{1,0:T(8,128)(2,1)S(1)}, u32[]{:S(2)}, u32[]{:S(2)}) %collective-permute-start.23) | collective-permute-done | bytes 32800 | tf_op jit(solution)/shard_map/ppermute | solution.py:61
  73.1 0.9 collective-permute-done.24
  74.1 2.1 %collective-permute-start.26 = (bf16[16,1024]{1,0:T(8,128)(2,1)S(1)}, bf16[16,1024]{1,0:T(8,128)(2,1)S(1)}, u32[]{:S(2)}, u32[]{:S(2)}) collective-permute-start(bf16[16,1024]{1,0:T(8,128)(2,1)S(1)} %fusion.33), channel_id=1, source_target_pairs={{0,6},{1,7},{2,4},{3,5},{4,2},{5,3},{6,0},{7,1},{8,14},{9,15},{10,... | collective-permute-start | bytes 98312 | tf_op jit(solution)/shard_map/ppermute | solution.py:61
  76.2 1.1 %collective-permute-start.27 = (bf16[16,1024]{1,0:T(8,128)(2,1)S(1)}, bf16[16,1024]{1,0:T(8,128)(2,1)S(1)}, u32[]{:S(2)}, u32[]{:S(2)}) collective-permute-start(bf16[16,1024]{1,0:T(8,128)(2,1)S(1)} %fusion.33), channel_id=1, source_target_pairs={{0,4},{1,5},{2,6},{3,7},{4,0},{5,1},{6,2},{7,3},{8,12},{9,13},{10,... | collective-permute-start | bytes 98312 | tf_op jit(solution)/shard_map/ppermute | solution.py:61
  77.3 1.3 %collective-permute-start.28 = (bf16[16,1024]{1,0:T(8,128)(2,1)S(1)}, bf16[16,1024]{1,0:T(8,128)(2,1)S(1)}, u32[]{:S(2)}, u32[]{:S(2)}) collective-permute-start(bf16[16,1024]{1,0:T(8,128)(2,1)S(1)} %fusion.33), channel_id=1, source_target_pairs={{0,2},{1,3},{2,0},{3,1},{4,6},{5,7},{6,4},{7,5},{8,10},{9,11},{10,... | collective-permute-start | bytes 98312 | tf_op jit(solution)/shard_map/ppermute | solution.py:61
  78.5 1.3 %collective-permute-done.26 = bf16[16,1024]{1,0:T(8,128)(2,1)S(1)} collective-permute-done((bf16[16,1024]{1,0:T(8,128)(2,1)S(1)}, bf16[16,1024]{1,0:T(8,128)(2,1)S(1)}, u32[]{:S(2)}, u32[]{:S(2)}) %collective-permute-start.26) | collective-permute-done | bytes 32800 | tf_op jit(solution)/shard_map/ppermute | solution.py:61
  79.9 1.4 %collective-permute-done.27 = bf16[16,1024]{1,0:T(8,128)(2,1)S(1)} collective-permute-done((bf16[16,1024]{1,0:T(8,128)(2,1)S(1)}, bf16[16,1024]{1,0:T(8,128)(2,1)S(1)}, u32[]{:S(2)}, u32[]{:S(2)}) %collective-permute-start.27) | collective-permute-done | bytes 32800 | tf_op jit(solution)/shard_map/ppermute | solution.py:61
  81.5 0.9 fusion.49
  82.5 1.6 %collective-permute-start.29 = (bf16[64,1280]{1,0:T(8,128)(2,1)S(1)}, bf16[64,1280]{1,0:T(8,128)(2,1)S(1)}, u32[]{:S(2)}, u32[]{:S(2)}) collective-permute-start(bf16[64,1280]{1,0:T(8,128)(2,1)S(1)} %get-tuple-element.83), channel_id=1, source_target_pairs={{0,24},{8,16},{16,8},{24,0},{1,25},{9,17},{17,9},{25,1},{2,26},{10... | collective-permute-start | bytes 491528 | tf_op jit(solution)/shard_map/ppermute | solution.py:70
  84.1 0.8 collective-permute-start.30
  84.8 1.2 %collective-permute-start.31 = (bf16[64,1280]{1,0:T(8,128)(2,1)S(1)}, bf16[64,1280]{1,0:T(8,128)(2,1)S(1)}, u32[]{:S(2)}, u32[]{:S(2)}) collective-permute-start(bf16[64,1280]{1,0:T(8,128)(2,1)S(1)} %get-tuple-element.83), channel_id=1, source_target_pairs={{0,8},{8,0},{16,24},{24,16},{1,9},{9,1},{17,25},{25,17},{2,10},{10... | collective-permute-start | bytes 491528 | tf_op jit(solution)/shard_map/ppermute | solution.py:70
  86.0 2.8 %collective-permute-done.29 = bf16[64,1280]{1,0:T(8,128)(2,1)S(1)} collective-permute-done((bf16[64,1280]{1,0:T(8,128)(2,1)S(1)}, bf16[64,1280]{1,0:T(8,128)(2,1)S(1)}, u32[]{:S(2)}, u32[]{:S(2)}) %collective-permute-start.29) | collective-permute-done | bytes 163872 | tf_op jit(solution)/shard_map/ppermute | solution.py:70
  88.8 1.7 %collective-permute-done.30 = bf16[64,1280]{1,0:T(8,128)(2,1)S(1)} collective-permute-done((bf16[64,1280]{1,0:T(8,128)(2,1)S(1)}, bf16[64,1280]{1,0:T(8,128)(2,1)S(1)}, u32[]{:S(2)}, u32[]{:S(2)}) %collective-permute-start.30) | collective-permute-done | bytes 163872 | tf_op jit(solution)/shard_map/ppermute | solution.py:70
  90.7 2.3 %fusion.50 = (bf16[64,1024]{1,0:T(8,128)(2,1)S(1)}, f32[64,1024]{1,0:T(8,128)S(1)}) fusion(bf16[64,1280]{1,0:T(8,128)(2,1)S(1)} %get-tuple-element.50, bf16[1280,1024]{1,0:T(8,128)(2,1)} %copy-done.1), kind=kOutput, calls=%fused_computation.94 | convolution fusion | flops 167837696 | bytes 3178496 | tf_op jit(solution)/shard_map/dot_general | solution.py:51
  93.2 1.7 %collective-permute-start.33 = (bf16[16,1024]{1,0:T(8,128)(2,1)S(1)}, bf16[16,1024]{1,0:T(8,128)(2,1)S(1)}, u32[]{:S(2)}, u32[]{:S(2)}) collective-permute-start(bf16[16,1024]{1,0:T(8,128)(2,1)S(1)} %get-tuple-element.68), channel_id=1, source_target_pairs={{0,6},{1,7},{2,4},{3,5},{4,2},{5,3},{6,0},{7,1},{8,14},{9,15},{10,... | collective-permute-start | bytes 98312 | tf_op jit(solution)/shard_map/ppermute | solution.py:61
  94.8 0.8 collective-permute-start.34
  95.6 2.0 %collective-permute-start.35 = (bf16[16,1024]{1,0:T(8,128)(2,1)S(1)}, bf16[16,1024]{1,0:T(8,128)(2,1)S(1)}, u32[]{:S(2)}, u32[]{:S(2)}) collective-permute-start(bf16[16,1024]{1,0:T(8,128)(2,1)S(1)} %get-tuple-element.69), channel_id=1, source_target_pairs={{0,2},{1,3},{2,0},{3,1},{4,6},{5,7},{6,4},{7,5},{8,10},{9,11},{10,... | collective-permute-start | bytes 98312 | tf_op jit(solution)/shard_map/ppermute | solution.py:61
  97.7 0.6 fusion.17
  98.3 0.9 collective-permute-done.33
  99.2 1.0 collective-permute-done.34
  100.2 0.7 add_bitcast_fusion
  (62 shorter events, 2.3 us)
Async XLA Ops:
  0.6 47.0 %copy-start = (s32[1024,128]{1,0:T(8,128)S(1)}, s32[1024,128]{1,0:T(8,128)}, u32[]{:S(2)}) copy-start(s32[1024,128]{1,0:T(8,128)} %param.9) | copy-start | bytes 1572868
  0.6 22.5 %copy-start.3 = (f32[640]{0:T(1024)S(1)}, f32[640]{0:T(1024)}, u32[]{:S(2)}) copy-start(f32[640]{0:T(1024)} %param.7) | copy-start | bytes 7684
  1.9 10.4 %collective-permute-start.1 = (s16[144,1024]{1,0:T(8,128)(2,1)S(1)}, s16[144,1024]{1,0:T(8,128)(2,1)S(1)}, u32[]{:S(2)}, u32[]{:S(2)}) collective-permute-start(s16[144,1024]{1,0:T(8,128)(2,1)S(1)} %fusion.refs_0_), channel_id=1, source_target_pairs={{0,4},{1,5},{4,6},{5,7},{6,2},{7,3},{2,0},{3,1},{8,12},{9,13},{12,... | collective-permute-start | bytes 884744 | tf_op jit(solution)/shard_map/ppermute | solution.py:65
  8.1 11.0 %collective-permute-start.2 = (s16[320,640]{1,0:T(8,128)(2,1)S(1)}, s16[320,640]{1,0:T(8,128)(2,1)S(1)}, u32[]{:S(2)}, u32[]{:S(2)}) collective-permute-start(s16[320,640]{1,0:T(8,128)(2,1)S(1)} %pad_add_fusion.refs_6_), channel_id=1, source_target_pairs={{0,8},{8,0},{16,24},{24,16},{1,9},{9,1},{17,25},{25,17},{2,10},{10... | collective-permute-start | bytes 1228808 | tf_op jit(solution)/shard_map/ppermute | solution.py:70
  9.6 10.6 %collective-permute-start.3 = (s16[320,640]{1,0:T(8,128)(2,1)S(1)}, s16[320,640]{1,0:T(8,128)(2,1)S(1)}, u32[]{:S(2)}, u32[]{:S(2)}) collective-permute-start(s16[320,640]{1,0:T(8,128)(2,1)S(1)} %pad_add_fusion.refs_6_), channel_id=1, source_target_pairs={{0,16},{8,24},{16,0},{24,8},{1,17},{9,25},{17,1},{25,9},{2,18},{10... | collective-permute-start | bytes 1228808 | tf_op jit(solution)/shard_map/ppermute | solution.py:70
  12.2 8.0 %collective-permute-start.4 = (s16[144,1024]{1,0:T(8,128)(2,1)S(1)}, s16[144,1024]{1,0:T(8,128)(2,1)S(1)}, u32[]{:S(2)}, u32[]{:S(2)}) collective-permute-start(s16[144,1024]{1,0:T(8,128)(2,1)S(1)} %collective-permute-done.1.refs_2_), channel_id=1, source_target_pairs={{0,1},{1,0},{2,3},{3,2},{4,5},{5,4},{6,7},{7,6},{8,9},{9,8},{10,11... | collective-permute-start | bytes 884744 | tf_op jit(solution)/shard_map/ppermute | solution.py:56
  12.2 16.6 %collective-permute-start = (s16[144,1024]{1,0:T(8,128)(2,1)S(1)}, s16[144,1024]{1,0:T(8,128)(2,1)}, u32[]{:S(2)}, u32[]{:S(2)}) collective-permute-start(s16[144,1024]{1,0:T(8,128)(2,1)S(1)} %fusion.refs_0_), channel_id=1, source_target_pairs={{0,1},{1,0},{2,3},{3,2},{4,5},{5,4},{6,7},{7,6},{8,9},{9,8},{10,11... | collective-permute-start | bytes 884744 | tf_op jit(solution)/shard_map/ppermute | solution.py:56
  12.7 10.6 %collective-permute-start.7 = (s16[144,1024]{1,0:T(8,128)(2,1)S(1)}, s16[144,1024]{1,0:T(8,128)(2,1)S(1)}, u32[]{:S(2)}, u32[]{:S(2)}) collective-permute-start(s16[144,1024]{1,0:T(8,128)(2,1)S(1)} %collective-permute-done.1.refs_2_), channel_id=1, source_target_pairs={{0,4},{1,5},{4,6},{5,7},{6,2},{7,3},{2,0},{3,1},{8,12},{9,13},{12,... | collective-permute-start | bytes 884744 | tf_op jit(solution)/shard_map/ppermute | solution.py:65
  20.3 5.8 %collective-permute-start.5 = (s16[160,640]{1,0:T(8,128)(2,1)S(1)}, s16[160,640]{1,0:T(8,128)(2,1)S(1)}, u32[]{:S(2)}, u32[]{:S(2)}) collective-permute-start(s16[160,640]{1,0:T(8,128)(2,1)S(1)} %slice.100), channel_id=1, source_target_pairs={{0,16},{8,24},{16,0},{24,8},{1,17},{9,25},{17,1},{25,9},{2,18},{10... | collective-permute-start | bytes 614408 | tf_op jit(solution)/shard_map/ppermute | solution.py:70
  22.6 6.0 %collective-permute-start.6 = (s16[160,640]{1,0:T(8,128)(2,1)}, s16[160,640]{1,0:T(8,128)(2,1)S(1)}, u32[]{:S(2)}, u32[]{:S(2)}) collective-permute-start(s16[160,640]{1,0:T(8,128)(2,1)} %slice.101), channel_id=1, source_target_pairs={{0,8},{8,0},{16,24},{24,16},{1,9},{9,1},{17,25},{25,17},{2,10},{10... | collective-permute-start | bytes 614408 | tf_op jit(solution)/shard_map/ppermute | solution.py:70
  23.3 5.5 %collective-permute-start.8 = (s16[144,1024]{1,0:T(8,128)(2,1)S(1)}, s16[144,1024]{1,0:T(8,128)(2,1)S(1)}, u32[]{:S(2)}, u32[]{:S(2)}) collective-permute-start(s16[144,1024]{1,0:T(8,128)(2,1)S(1)} %collective-permute-done.7.refs_4_), channel_id=1, source_target_pairs={{0,1},{1,0},{2,3},{3,2},{4,5},{5,4},{6,7},{7,6},{8,9},{9,8},{10,11... | collective-permute-start | bytes 884744 | tf_op jit(solution)/shard_map/ppermute | solution.py:56
  23.4 11.7 %collective-permute-start.9 = (s16[144,1024]{1,0:T(8,128)(2,1)S(1)}, s16[144,1024]{1,0:T(8,128)(2,1)S(1)}, u32[]{:S(2)}, u32[]{:S(2)}) collective-permute-start(s16[144,1024]{1,0:T(8,128)(2,1)S(1)} %collective-permute-done.7.refs_4_), channel_id=1, source_target_pairs={{0,4},{1,5},{4,6},{5,7},{6,2},{7,3},{2,0},{3,1},{8,12},{9,13},{12,... | collective-permute-start | bytes 884744 | tf_op jit(solution)/shard_map/ppermute | solution.py:65
  28.7 7.0 %collective-permute-start.11 = (s16[64,640]{1,0:T(8,128)(2,1)S(1)}, s16[64,640]{1,0:T(8,128)(2,1)S(1)}, u32[]{:S(2)}, u32[]{:S(2)}) collective-permute-start(s16[64,640]{1,0:T(8,128)(2,1)S(1)} %get-tuple-element.40), channel_id=1, source_target_pairs={{0,1},{1,0},{2,3},{3,2},{4,5},{5,4},{6,7},{7,6},{8,9},{9,8},{10,11... | collective-permute-start | bytes 245768 | tf_op jit(solution)/shard_map/ppermute | solution.py:56
  35.1 1.8 %collective-permute-start.10 = (s16[144,1024]{1,0:T(8,128)(2,1)S(1)}, s16[144,1024]{1,0:T(8,128)(2,1)S(1)}, u32[]{:S(2)}, u32[]{:S(2)}) collective-permute-start(s16[144,1024]{1,0:T(8,128)(2,1)S(1)} %collective-permute-done.9.own_ref), channel_id=1, source_target_pairs={{0,1},{1,0},{2,3},{3,2},{4,5},{5,4},{6,7},{7,6},{8,9},{9,8},{10,11... | collective-permute-start | bytes 884744 | tf_op jit(solution)/shard_map/ppermute | solution.py:56
  41.3 1.4 %collective-permute-start.12 = (bf16[64,1024]{1,0:T(8,128)(2,1)S(1)}, bf16[64,1024]{1,0:T(8,128)(2,1)S(1)}, u32[]{:S(2)}, u32[]{:S(2)}) collective-permute-start(bf16[64,1024]{1,0:T(8,128)(2,1)S(1)} %get-tuple-element.43), channel_id=1, source_target_pairs={{0,1},{1,0},{2,3},{3,2},{4,5},{5,4},{6,7},{7,6},{8,9},{9,8},{10,11... | collective-permute-start | bytes 393224 | tf_op jit(solution)/shard_map/ppermute | solution.py:56
  42.7 11.6 %collective-permute-start.19 = (bf16[640,1024]{1,0:T(8,128)(2,1)S(1)}, bf16[640,1024]{1,0:T(8,128)(2,1)}, u32[]{:S(2)}, u32[]{:S(2)}) collective-permute-start(bf16[640,1024]{1,0:T(8,128)(2,1)S(1)} %get-tuple-element.45), channel_id=1, source_target_pairs={{0,1},{1,0},{2,3},{3,2},{4,5},{5,4},{6,7},{7,6},{8,9},{9,8},{10,11... | collective-permute-start | bytes 3932168 | tf_op jit(solution)/shard_map/ppermute | solution.py:56
  43.2 5.8 %collective-permute-start.13 = (bf16[16,1024]{1,0:T(8,128)(2,1)S(1)}, bf16[16,1024]{1,0:T(8,128)(2,1)S(1)}, u32[]{:S(2)}, u32[]{:S(2)}) collective-permute-start(bf16[16,1024]{1,0:T(8,128)(2,1)S(1)} %get-tuple-element.74), channel_id=1, source_target_pairs={{0,6},{1,7},{2,4},{3,5},{4,2},{5,3},{6,0},{7,1},{8,14},{9,15},{10,... | collective-permute-start | bytes 98312 | tf_op jit(solution)/shard_map/ppermute | solution.py:61
  44.6 5.3 %collective-permute-start.14 = (bf16[16,1024]{1,0:T(8,128)(2,1)S(1)}, bf16[16,1024]{1,0:T(8,128)(2,1)S(1)}, u32[]{:S(2)}, u32[]{:S(2)}) collective-permute-start(bf16[16,1024]{1,0:T(8,128)(2,1)S(1)} %get-tuple-element.76), channel_id=1, source_target_pairs={{0,4},{1,5},{2,6},{3,7},{4,0},{5,1},{6,2},{7,3},{8,12},{9,13},{10,... | collective-permute-start | bytes 98312 | tf_op jit(solution)/shard_map/ppermute | solution.py:61
  44.9 5.0 %collective-permute-start.15 = (bf16[16,1024]{1,0:T(8,128)(2,1)S(1)}, bf16[16,1024]{1,0:T(8,128)(2,1)S(1)}, u32[]{:S(2)}, u32[]{:S(2)}) collective-permute-start(bf16[16,1024]{1,0:T(8,128)(2,1)S(1)} %get-tuple-element.75), channel_id=1, source_target_pairs={{0,2},{1,3},{2,0},{3,1},{4,6},{5,7},{6,4},{7,5},{8,10},{9,11},{10,... | collective-permute-start | bytes 98312 | tf_op jit(solution)/shard_map/ppermute | solution.py:61
  49.9 6.0 %collective-permute-start.16 = (bf16[16,1024]{1,0:T(8,128)(2,1)S(1)}, bf16[16,1024]{1,0:T(8,128)(2,1)S(1)}, u32[]{:S(2)}, u32[]{:S(2)}) collective-permute-start(bf16[16,1024]{1,0:T(8,128)(2,1)S(1)} %fusion.32), channel_id=1, source_target_pairs={{0,6},{1,7},{2,4},{3,5},{4,2},{5,3},{6,0},{7,1},{8,14},{9,15},{10,... | collective-permute-start | bytes 98312 | tf_op jit(solution)/shard_map/ppermute | solution.py:61
  52.1 4.8 %collective-permute-start.17 = (bf16[16,1024]{1,0:T(8,128)(2,1)S(1)}, bf16[16,1024]{1,0:T(8,128)(2,1)S(1)}, u32[]{:S(2)}, u32[]{:S(2)}) collective-permute-start(bf16[16,1024]{1,0:T(8,128)(2,1)S(1)} %fusion.32), channel_id=1, source_target_pairs={{0,4},{1,5},{2,6},{3,7},{4,0},{5,1},{6,2},{7,3},{8,12},{9,13},{10,... | collective-permute-start | bytes 98312 | tf_op jit(solution)/shard_map/ppermute | solution.py:61
  53.1 4.2 %collective-permute-start.18 = (bf16[16,1024]{1,0:T(8,128)(2,1)S(1)}, bf16[16,1024]{1,0:T(8,128)(2,1)S(1)}, u32[]{:S(2)}, u32[]{:S(2)}) collective-permute-start(bf16[16,1024]{1,0:T(8,128)(2,1)S(1)} %fusion.32), channel_id=1, source_target_pairs={{0,2},{1,3},{2,0},{3,1},{4,6},{5,7},{6,4},{7,5},{8,10},{9,11},{10,... | collective-permute-start | bytes 98312 | tf_op jit(solution)/shard_map/ppermute | solution.py:61
  55.9 25.6 %copy-start.1 = (bf16[1280,1024]{1,0:T(8,128)(2,1)}, bf16[1280,1024]{1,0:T(8,128)(2,1)S(1)}, u32[]{:S(2)}) copy-start(bf16[1280,1024]{1,0:T(8,128)(2,1)S(1)} %pad_maximum_fusion) | copy-start | bytes 7864324
  58.2 6.9 %collective-permute-start.20 = (bf16[64,1280]{1,0:T(8,128)(2,1)S(1)}, bf16[64,1280]{1,0:T(8,128)(2,1)S(1)}, u32[]{:S(2)}, u32[]{:S(2)}) collective-permute-start(bf16[64,1280]{1,0:T(8,128)(2,1)S(1)} %get-tuple-element.79), channel_id=1, source_target_pairs={{0,24},{8,16},{16,8},{24,0},{1,25},{9,17},{17,9},{25,1},{2,26},{10... | collective-permute-start | bytes 491528 | tf_op jit(solution)/shard_map/ppermute | solution.py:70
  59.2 7.5 %collective-permute-start.21 = (bf16[64,1280]{1,0:T(8,128)(2,1)S(1)}, bf16[64,1280]{1,0:T(8,128)(2,1)S(1)}, u32[]{:S(2)}, u32[]{:S(2)}) collective-permute-start(bf16[64,1280]{1,0:T(8,128)(2,1)S(1)} %get-tuple-element.79), channel_id=1, source_target_pairs={{0,16},{8,24},{16,0},{24,8},{1,17},{9,25},{17,1},{25,9},{2,18},{10... | collective-permute-start | bytes 491528 | tf_op jit(solution)/shard_map/ppermute | solution.py:70
  60.3 6.3 %collective-permute-start.22 = (bf16[64,1280]{1,0:T(8,128)(2,1)S(1)}, bf16[64,1280]{1,0:T(8,128)(2,1)S(1)}, u32[]{:S(2)}, u32[]{:S(2)}) collective-permute-start(bf16[64,1280]{1,0:T(8,128)(2,1)S(1)} %get-tuple-element.79), channel_id=1, source_target_pairs={{0,8},{8,0},{16,24},{24,16},{1,9},{9,1},{17,25},{25,17},{2,10},{10... | collective-permute-start | bytes 491528 | tf_op jit(solution)/shard_map/ppermute | solution.py:70
  67.3 5.8 %collective-permute-start.23 = (bf16[16,1024]{1,0:T(8,128)(2,1)S(1)}, bf16[16,1024]{1,0:T(8,128)(2,1)S(1)}, u32[]{:S(2)}, u32[]{:S(2)}) collective-permute-start(bf16[16,1024]{1,0:T(8,128)(2,1)S(1)} %get-tuple-element.71), channel_id=1, source_target_pairs={{0,6},{1,7},{2,4},{3,5},{4,2},{5,3},{6,0},{7,1},{8,14},{9,15},{10,... | collective-permute-start | bytes 98312 | tf_op jit(solution)/shard_map/ppermute | solution.py:61
  69.1 4.9 %collective-permute-start.24 = (bf16[16,1024]{1,0:T(8,128)(2,1)S(1)}, bf16[16,1024]{1,0:T(8,128)(2,1)S(1)}, u32[]{:S(2)}, u32[]{:S(2)}) collective-permute-start(bf16[16,1024]{1,0:T(8,128)(2,1)S(1)} %get-tuple-element.73), channel_id=1, source_target_pairs={{0,4},{1,5},{2,6},{3,7},{4,0},{5,1},{6,2},{7,3},{8,12},{9,13},{10,... | collective-permute-start | bytes 98312 | tf_op jit(solution)/shard_map/ppermute | solution.py:61
  69.6 4.5 %collective-permute-start.25 = (bf16[16,1024]{1,0:T(8,128)(2,1)S(1)}, bf16[16,1024]{1,0:T(8,128)(2,1)S(1)}, u32[]{:S(2)}, u32[]{:S(2)}) collective-permute-start(bf16[16,1024]{1,0:T(8,128)(2,1)S(1)} %get-tuple-element.72), channel_id=1, source_target_pairs={{0,2},{1,3},{2,0},{3,1},{4,6},{5,7},{6,4},{7,5},{8,10},{9,11},{10,... | collective-permute-start | bytes 98312 | tf_op jit(solution)/shard_map/ppermute | solution.py:61
  74.1 5.8 %collective-permute-start.26 = (bf16[16,1024]{1,0:T(8,128)(2,1)S(1)}, bf16[16,1024]{1,0:T(8,128)(2,1)S(1)}, u32[]{:S(2)}, u32[]{:S(2)}) collective-permute-start(bf16[16,1024]{1,0:T(8,128)(2,1)S(1)} %fusion.33), channel_id=1, source_target_pairs={{0,6},{1,7},{2,4},{3,5},{4,2},{5,3},{6,0},{7,1},{8,14},{9,15},{10,... | collective-permute-start | bytes 98312 | tf_op jit(solution)/shard_map/ppermute | solution.py:61
  76.2 5.1 %collective-permute-start.27 = (bf16[16,1024]{1,0:T(8,128)(2,1)S(1)}, bf16[16,1024]{1,0:T(8,128)(2,1)S(1)}, u32[]{:S(2)}, u32[]{:S(2)}) collective-permute-start(bf16[16,1024]{1,0:T(8,128)(2,1)S(1)} %fusion.33), channel_id=1, source_target_pairs={{0,4},{1,5},{2,6},{3,7},{4,0},{5,1},{6,2},{7,3},{8,12},{9,13},{10,... | collective-permute-start | bytes 98312 | tf_op jit(solution)/shard_map/ppermute | solution.py:61
  77.3 4.2 %collective-permute-start.28 = (bf16[16,1024]{1,0:T(8,128)(2,1)S(1)}, bf16[16,1024]{1,0:T(8,128)(2,1)S(1)}, u32[]{:S(2)}, u32[]{:S(2)}) collective-permute-start(bf16[16,1024]{1,0:T(8,128)(2,1)S(1)} %fusion.33), channel_id=1, source_target_pairs={{0,2},{1,3},{2,0},{3,1},{4,6},{5,7},{6,4},{7,5},{8,10},{9,11},{10,... | collective-permute-start | bytes 98312 | tf_op jit(solution)/shard_map/ppermute | solution.py:61
  82.5 6.4 %collective-permute-start.29 = (bf16[64,1280]{1,0:T(8,128)(2,1)S(1)}, bf16[64,1280]{1,0:T(8,128)(2,1)S(1)}, u32[]{:S(2)}, u32[]{:S(2)}) collective-permute-start(bf16[64,1280]{1,0:T(8,128)(2,1)S(1)} %get-tuple-element.83), channel_id=1, source_target_pairs={{0,24},{8,16},{16,8},{24,0},{1,25},{9,17},{17,9},{25,1},{2,26},{10... | collective-permute-start | bytes 491528 | tf_op jit(solution)/shard_map/ppermute | solution.py:70
  84.1 6.4 %collective-permute-start.30 = (bf16[64,1280]{1,0:T(8,128)(2,1)S(1)}, bf16[64,1280]{1,0:T(8,128)(2,1)S(1)}, u32[]{:S(2)}, u32[]{:S(2)}) collective-permute-start(bf16[64,1280]{1,0:T(8,128)(2,1)S(1)} %get-tuple-element.83), channel_id=1, source_target_pairs={{0,16},{8,24},{16,0},{24,8},{1,17},{9,25},{17,1},{25,9},{2,18},{10... | collective-permute-start | bytes 491528 | tf_op jit(solution)/shard_map/ppermute | solution.py:70
  84.8 5.7 %collective-permute-start.31 = (bf16[64,1280]{1,0:T(8,128)(2,1)S(1)}, bf16[64,1280]{1,0:T(8,128)(2,1)S(1)}, u32[]{:S(2)}, u32[]{:S(2)}) collective-permute-start(bf16[64,1280]{1,0:T(8,128)(2,1)S(1)} %get-tuple-element.83), channel_id=1, source_target_pairs={{0,8},{8,0},{16,24},{24,16},{1,9},{9,1},{17,25},{25,17},{2,10},{10... | collective-permute-start | bytes 491528 | tf_op jit(solution)/shard_map/ppermute | solution.py:70
  90.7 7.0 %copy-start.2 = (f32[640,32]{0,1:T(8,128)S(1)}, f32[640,32]{0,1:T(8,128)}, u32[]{:S(2)}) copy-start(f32[640,32]{0,1:T(8,128)} %param.8) | copy-start | bytes 245764
  93.1 4.6 %collective-permute-start.32 = (f32[64,640]{1,0:T(8,128)S(1)}, f32[64,640]{1,0:T(8,128)S(1)}, u32[]{:S(2)}, u32[]{:S(2)}) collective-permute-start(f32[64,640]{1,0:T(8,128)S(1)} %get-tuple-element.59), channel_id=1, source_target_pairs={{0,1},{1,0},{2,3},{3,2},{4,5},{5,4},{6,7},{7,6},{8,9},{9,8},{10,11... | collective-permute-start | bytes 491528 | tf_op jit(solution)/shard_map/ppermute | solution.py:56
  93.2 6.1 %collective-permute-start.33 = (bf16[16,1024]{1,0:T(8,128)(2,1)S(1)}, bf16[16,1024]{1,0:T(8,128)(2,1)S(1)}, u32[]{:S(2)}, u32[]{:S(2)}) collective-permute-start(bf16[16,1024]{1,0:T(8,128)(2,1)S(1)} %get-tuple-element.68), channel_id=1, source_target_pairs={{0,6},{1,7},{2,4},{3,5},{4,2},{5,3},{6,0},{7,1},{8,14},{9,15},{10,... | collective-permute-start | bytes 98312 | tf_op jit(solution)/shard_map/ppermute | solution.py:61
  94.8 5.4 %collective-permute-start.34 = (bf16[16,1024]{1,0:T(8,128)(2,1)S(1)}, bf16[16,1024]{1,0:T(8,128)(2,1)S(1)}, u32[]{:S(2)}, u32[]{:S(2)}) collective-permute-start(bf16[16,1024]{1,0:T(8,128)(2,1)S(1)} %get-tuple-element.70), channel_id=1, source_target_pairs={{0,4},{1,5},{2,6},{3,7},{4,0},{5,1},{6,2},{7,3},{8,12},{9,13},{10,... | collective-permute-start | bytes 98312 | tf_op jit(solution)/shard_map/ppermute | solution.py:61
  95.6 4.6 %collective-permute-start.35 = (bf16[16,1024]{1,0:T(8,128)(2,1)S(1)}, bf16[16,1024]{1,0:T(8,128)(2,1)S(1)}, u32[]{:S(2)}, u32[]{:S(2)}) collective-permute-start(bf16[16,1024]{1,0:T(8,128)(2,1)S(1)} %get-tuple-element.69), channel_id=1, source_target_pairs={{0,2},{1,3},{2,0},{3,1},{4,6},{5,7},{6,4},{7,5},{8,10},{9,11},{10,... | collective-permute-start | bytes 98312 | tf_op jit(solution)/shard_map/ppermute | solution.py:61

commit v9 on v8

--- a/solution.py
+++ b/solution.py
@@ -154,15 +154,17 @@
     for _ in range(slabs - 1):
         own.append(line_move(own[-1], ring))
     other = [core_swap(own[0]), core_swap(own[1])]
-    x_again, y_again, other[1] = tie((freq_x, freq_y, other[1]))
-    freqs = [freq_code, freq_x, freq_y, clip_swap(x_again[:rows], 2), clip_swap(y_again[rows:], 1)]
+    x_again, other[1] = tie((freq_x, other[1]))
+    half_x = clip_swap(x_again[:rows], 2)
+    y_again, half_x_first = tie((freq_y, x_again[:rows]))
+    freqs = [freq_code, freq_x, freq_y, half_x, clip_swap(y_again[rows:], 1)]
     other.append(core_swap(own[2]))
     *freqs, own[2] = tie((*freqs, own[2]))
     betas, cast, targets = prepare(freqs)
     early = [x for pair in zip(own[:3], other) for x in pair]
     used = len(early) * columns
     depth = -(-used // LANES) * LANES
-    tile = 512 if clips % 512 == 0 else clips
+    tile = clips
 
     def whole(*shape):
         return pl.BlockSpec(shape, lambda i: (0,) * len(shape))

time: 101 us -> 99.2 us (0.982)
  Pallas kernels: 10.7 us -> 8.62 us
  starting transfers between devices: 46.6 us -> 47.8 us
  waiting for transfers between devices: 29.6 us -> 28.5 us
    ppermute x10, waiting for transfers between devices: 16.1 us -> 14.2 us  [clip_swap(): return lax.ppermute(x, 'clip', [(i, i ^ k) for i in range(n)])]
    pallas_call x1, Pallas kernels: 4.43 us -> 3 us  [phi_by_kernels(): pl.pallas_call(functools.partial(late_kernel, scale=scale), grid=(clips /...]
where the time goes in v9:
time: 99.2 us; the launch traced here: 98.9 us
  starting transfers between devices  47.8 us (48%)
  waiting for transfers between devices  28.5 us (29%)
  Pallas kernels  8.62 us (9%)
  other arithmetic  6.78 us (7%)
  matrix products  4.75 us (5%)
  local copies, waits for them, and re-layouts  1.44 us (1%)
    ppermute x15, starting transfers between devices, line_swap(): return lax.ppermute(x, 'feat', [(i, i ^ 2 * k) for i in range(n)])  22.3 us
    ppermute x10, waiting for transfers between devices, clip_swap(): return lax.ppermute(x, 'clip', [(i, i ^ k) for i in range(n)])  14.2 us
    ppermute x10, starting transfers between devices, clip_swap(): return lax.ppermute(x, 'clip', [(i, i ^ k) for i in range(n)])  13.3 us
    ppermute x15, waiting for transfers between devices, line_swap(): return lax.ppermute(x, 'feat', [(i, i ^ 2 * k) for i in range(n)])  11.1 us
    ppermute x3, starting transfers between devices, line_move(): lax.ppermute(x, 'feat', [(2 * a + c, 2 * b + c) for a, b in pairs for c i...  10.3 us
    pallas_call x1, Pallas kernels, phi_by_kernels(): pl.pallas_call(functools.partial(early_kernel, n_embeds=len(early), n_fre...  5.63 us
    convert_element_type x3, other arithmetic, encode(): return jnp.round(x * (CODE_MAX / bound)).astype(jnp.int16)  3.26 us
    pallas_call x1, Pallas kernels, phi_by_kernels(): pl.pallas_call(functools.partial(late_kernel, scale=scale), grid=(clips /...  3 us
  transfers between devices with their start and end apart: 36, of which 22 were waited for; matrix products, arithmetic and copies ran while one was open for 6% of the time, Pallas kernels for 6%

profile of v9, /device:TPU:0, one launch (start us, length us, event | category | flops | bytes accessed | tf_op | source)
XLA Modules:
  0.0 98.9 jit_solution(2251570797060978584)
XLA Ops:
  0.7 1.2 %fusion.refs_0_ = s16[144,1024]{1,0:T(8,128)(2,1)S(1)} fusion(f32[1024,144]{0,1:T(8,128)} %param.5), kind=kLoop, calls=%fused_computation.10 | loop fusion | flops 442368 | bytes 884736 | tf_op jit(solution)/shard_map/convert_element_type | solution.py:32
  1.9 4.1 %collective-permute-start.1 = (s16[144,1024]{1,0:T(8,128)(2,1)S(1)}, s16[144,1024]{1,0:T(8,128)(2,1)S(1)}, u32[]{:S(2)}, u32[]{:S(2)}) collective-permute-start(s16[144,1024]{1,0:T(8,128)(2,1)S(1)} %fusion.refs_0_), channel_id=1, source_target_pairs={{0,4},{1,5},{4,6},{5,7},{6,2},{7,3},{2,0},{3,1},{8,12},{9,13},{12,... | collective-permute-start | bytes 884744 | tf_op jit(solution)/shard_map/ppermute | solution.py:65
  6.0 1.2 %round-nearest-even_convert_fusion.2 = (s16[144,640]{1,0:T(8,128)(2,1)S(1)}, s16[144,640]{1,0:T(8,128)(2,1)S(1)}) fusion(f32[288,640]{1,0:T(8,128)} %param.6), kind=kLoop, calls=%fused_computation.4 | loop fusion | flops 552960 | bytes 1105920 | tf_op jit(solution)/shard_map/convert_element_type | solution.py:32
  7.2 0.8 fusion.38
  8.1 1.6 %collective-permute-start.2 = (s16[320,640]{1,0:T(8,128)(2,1)S(1)}, s16[320,640]{1,0:T(8,128)(2,1)S(1)}, u32[]{:S(2)}, u32[]{:S(2)}) collective-permute-start(s16[320,640]{1,0:T(8,128)(2,1)S(1)} %pad_add_fusion.refs_6_), channel_id=1, source_target_pairs={{0,8},{8,0},{16,24},{24,16},{1,9},{9,1},{17,25},{25,17},{2,10},{10... | collective-permute-start | bytes 1228808 | tf_op jit(solution)/shard_map/ppermute | solution.py:70
  9.6 1.5 %collective-permute-start.4 = (s16[320,640]{1,0:T(8,128)(2,1)S(1)}, s16[320,640]{1,0:T(8,128)(2,1)S(1)}, u32[]{:S(2)}, u32[]{:S(2)}) collective-permute-start(s16[320,640]{1,0:T(8,128)(2,1)S(1)} %pad_add_fusion.refs_6_), channel_id=1, source_target_pairs={{0,16},{8,24},{16,0},{24,8},{1,17},{9,25},{17,1},{25,9},{2,18},{10... | collective-permute-start | bytes 1228808 | tf_op jit(solution)/shard_map/ppermute | solution.py:70
  11.1 1.1 %collective-permute-done.1.refs_2_ = s16[144,1024]{1,0:T(8,128)(2,1)S(1)} collective-permute-done((s16[144,1024]{1,0:T(8,128)(2,1)S(1)}, s16[144,1024]{1,0:T(8,128)(2,1)S(1)}, u32[]{:S(2)}, u32[]{:S(2)}) %collective-permute-start.1) | collective-permute-done | bytes 294944 | tf_op jit(solution)/shard_map/ppermute | solution.py:65
  12.2 0.5 collective-permute-start
  12.7 3.4 %collective-permute-start.7 = (s16[144,1024]{1,0:T(8,128)(2,1)S(1)}, s16[144,1024]{1,0:T(8,128)(2,1)S(1)}, u32[]{:S(2)}, u32[]{:S(2)}) collective-permute-start(s16[144,1024]{1,0:T(8,128)(2,1)S(1)} %collective-permute-done.1.refs_2_), channel_id=1, source_target_pairs={{0,4},{1,5},{4,6},{5,7},{6,2},{7,3},{2,0},{3,1},{8,12},{9,13},{12,... | collective-permute-start | bytes 884744 | tf_op jit(solution)/shard_map/ppermute | solution.py:65
  16.1 2.9 %collective-permute-done.2.refs_7_ = s16[320,640]{1,0:T(8,128)(2,1)S(1)} collective-permute-done((s16[320,640]{1,0:T(8,128)(2,1)S(1)}, s16[320,640]{1,0:T(8,128)(2,1)S(1)}, u32[]{:S(2)}, u32[]{:S(2)}) %collective-permute-start.2) | collective-permute-done | bytes 409632 | tf_op jit(solution)/shard_map/ppermute | solution.py:70
  19.1 1.6 %collective-permute-start.5 = (s16[160,640]{1,0:T(8,128)(2,1)S(1)}, s16[160,640]{1,0:T(8,128)(2,1)S(1)}, u32[]{:S(2)}, u32[]{:S(2)}) collective-permute-start(s16[160,640]{1,0:T(8,128)(2,1)S(1)} %slice.101), channel_id=1, source_target_pairs={{0,16},{8,24},{16,0},{24,8},{1,17},{9,25},{17,1},{25,9},{2,18},{10... | collective-permute-start | bytes 614408 | tf_op jit(solution)/shard_map/ppermute | solution.py:70
  20.7 0.7 slice.102
  21.4 1.5 %collective-permute-start.6 = (s16[160,640]{1,0:T(8,128)(2,1)}, s16[160,640]{1,0:T(8,128)(2,1)S(1)}, u32[]{:S(2)}, u32[]{:S(2)}) collective-permute-start(s16[160,640]{1,0:T(8,128)(2,1)} %slice.102), channel_id=1, source_target_pairs={{0,8},{8,0},{16,24},{24,16},{1,9},{9,1},{17,25},{25,17},{2,10},{10... | collective-permute-start | bytes 614408 | tf_op jit(solution)/shard_map/ppermute | solution.py:70
  23.1 2.8 %collective-permute-start.9 = (s16[144,1024]{1,0:T(8,128)(2,1)S(1)}, s16[144,1024]{1,0:T(8,128)(2,1)S(1)}, u32[]{:S(2)}, u32[]{:S(2)}) collective-permute-start(s16[144,1024]{1,0:T(8,128)(2,1)S(1)} %collective-permute-done.7.refs_4_), channel_id=1, source_target_pairs={{0,4},{1,5},{4,6},{5,7},{6,2},{7,3},{2,0},{3,1},{8,12},{9,13},{12,... | collective-permute-start | bytes 884744 | tf_op jit(solution)/shard_map/ppermute | solution.py:65
  25.9 1.4 %collective-permute-done.6.refs_10_ = s16[160,640]{1,0:T(8,128)(2,1)S(1)} collective-permute-done((s16[160,640]{1,0:T(8,128)(2,1)}, s16[160,640]{1,0:T(8,128)(2,1)S(1)}, u32[]{:S(2)}, u32[]{:S(2)}) %collective-permute-start.6) | collective-permute-done | bytes 204832 | tf_op jit(solution)/shard_map/ppermute | solution.py:70
  27.6 5.6 %early_angles.1 = (f32[640,1024]{1,0:T(8,128)S(1)}, s16[640,288]{1,0:T(8,128)(2,1)S(1)}) custom-call(s32[3]{0:T(128)S(1)} %pad_add_fusion.3.at_ref, s16[144,1024]{1,0:T(8,128)(2,1)S(1)} %fusion.refs_0_, s16[144,1024]{1,0:T(8,128)(2,1)} %collective-permute-done.refs_1_, s16[144,1024]{1,0:T(8,128)(2,1)S(1)} %collective-permute-done.1.refs_2_, ...), custom_call_target="tpu_custom_call" | custom-call | flops 3523215360 | bytes 5242880 | tf_op jit(solution)/shard_map/early_angles/pallas_call | solution.py:175
  33.3 0.6 collective-permute-start.10
  33.9 1.1 %collective-permute-done.10.other_ref = s16[144,1024]{1,0:T(8,128)(2,1)S(1)} collective-permute-done((s16[144,1024]{1,0:T(8,128)(2,1)S(1)}, s16[144,1024]{1,0:T(8,128)(2,1)S(1)}, u32[]{:S(2)}, u32[]{:S(2)}) %collective-permute-start.10) | collective-permute-done | bytes 294944 | tf_op jit(solution)/shard_map/ppermute | solution.py:56
  35.0 3.0 %late_angles.1 = (bf16[640,1024]{1,0:T(8,128)(2,1)S(1)}, f32[64,1024]{1,0:T(8,128)S(1)}, bf16[64,1024]{1,0:T(8,128)(2,1)S(1)}) custom-call(f32[640,1024]{1,0:T(8,128)S(1)} %get-tuple-element.35.sum_ref, s16[144,1024]{1,0:T(8,128)(2,1)S(1)} %collective-permute-done.9.own_ref, s16[144,1024]{1,0:T(8,128)(2,1)S(1)} %collective-permute-done.10.other_ref, ...), custom_call_target="tpu_custom_call" | custom-call | flops 1132462080 | bytes 3932160 | tf_op jit(solution)/shard_map/late_angles/pallas_call | solution.py:200
  38.0 0.4 collective-permute-start.12
  38.5 1.0 collective-permute-done.12
  39.5 0.4 collective-permute-start.19
  39.9 1.5 %collective-permute-start.13 = (bf16[16,1024]{1,0:T(8,128)(2,1)S(1)}, bf16[16,1024]{1,0:T(8,128)(2,1)S(1)}, u32[]{:S(2)}, u32[]{:S(2)}) collective-permute-start(bf16[16,1024]{1,0:T(8,128)(2,1)S(1)} %get-tuple-element.74), channel_id=1, source_target_pairs={{0,6},{1,7},{2,4},{3,5},{4,2},{5,3},{6,0},{7,1},{8,14},{9,15},{10,... | collective-permute-start | bytes 98312 | tf_op jit(solution)/shard_map/ppermute | solution.py:61
  41.4 1.6 %collective-permute-start.14 = (bf16[16,1024]{1,0:T(8,128)(2,1)S(1)}, bf16[16,1024]{1,0:T(8,128)(2,1)S(1)}, u32[]{:S(2)}, u32[]{:S(2)}) collective-permute-start(bf16[16,1024]{1,0:T(8,128)(2,1)S(1)} %get-tuple-element.76), channel_id=1, source_target_pairs={{0,4},{1,5},{2,6},{3,7},{4,0},{5,1},{6,2},{7,3},{8,12},{9,13},{10,... | collective-permute-start | bytes 98312 | tf_op jit(solution)/shard_map/ppermute | solution.py:61
  43.0 1.3 %collective-permute-start.15 = (bf16[16,1024]{1,0:T(8,128)(2,1)S(1)}, bf16[16,1024]{1,0:T(8,128)(2,1)S(1)}, u32[]{:S(2)}, u32[]{:S(2)}) collective-permute-start(bf16[16,1024]{1,0:T(8,128)(2,1)S(1)} %get-tuple-element.75), channel_id=1, source_target_pairs={{0,2},{1,3},{2,0},{3,1},{4,6},{5,7},{6,4},{7,5},{8,10},{9,11},{10,... | collective-permute-start | bytes 98312 | tf_op jit(solution)/shard_map/ppermute | solution.py:61
  44.7 1.0 collective-permute-done.13
  45.7 0.9 collective-permute-done.14
  46.6 0.4 collective-permute-done.15
  47.0 2.5 %collective-permute-start.16 = (bf16[16,1024]{1,0:T(8,128)(2,1)S(1)}, bf16[16,1024]{1,0:T(8,128)(2,1)S(1)}, u32[]{:S(2)}, u32[]{:S(2)}) collective-permute-start(bf16[16,1024]{1,0:T(8,128)(2,1)S(1)} %fusion.32), channel_id=1, source_target_pairs={{0,6},{1,7},{2,4},{3,5},{4,2},{5,3},{6,0},{7,1},{8,14},{9,15},{10,... | collective-permute-start | bytes 98312 | tf_op jit(solution)/shard_map/ppermute | solution.py:61
  49.5 0.3 collective-permute-start.17
  49.8 1.6 %collective-permute-start.18 = (bf16[16,1024]{1,0:T(8,128)(2,1)S(1)}, bf16[16,1024]{1,0:T(8,128)(2,1)S(1)}, u32[]{:S(2)}, u32[]{:S(2)}) collective-permute-start(bf16[16,1024]{1,0:T(8,128)(2,1)S(1)} %fusion.32), channel_id=1, source_target_pairs={{0,2},{1,3},{2,0},{3,1},{4,6},{5,7},{6,4},{7,5},{8,10},{9,11},{10,... | collective-permute-start | bytes 98312 | tf_op jit(solution)/shard_map/ppermute | solution.py:61
  51.4 1.6 %pad_maximum_fusion = bf16[1280,1024]{1,0:T(8,128)(2,1)S(1)} fusion(bf16[640,1024]{1,0:T(8,128)(2,1)} %collective-permute-done.19, bf16[640,1024]{1,0:T(8,128)(2,1)S(1)} %get-tuple-element.45), kind=kLoop, calls=%fused_computation | loop fusion | flops 5242880 | bytes 5242880 | tf_op jit(solution)/shard_map/concatenate | solution.py:336
  53.0 1.3 %collective-permute-done.17 = bf16[16,1024]{1,0:T(8,128)(2,1)S(1)} collective-permute-done((bf16[16,1024]{1,0:T(8,128)(2,1)S(1)}, bf16[16,1024]{1,0:T(8,128)(2,1)S(1)}, u32[]{:S(2)}, u32[]{:S(2)}) %collective-permute-start.17) | collective-permute-done | bytes 32800 | tf_op jit(solution)/shard_map/ppermute | solution.py:61
  54.3 0.9 fusion.47
  55.2 2.5 %collective-permute-start.20 = (bf16[64,1280]{1,0:T(8,128)(2,1)S(1)}, bf16[64,1280]{1,0:T(8,128)(2,1)S(1)}, u32[]{:S(2)}, u32[]{:S(2)}) collective-permute-start(bf16[64,1280]{1,0:T(8,128)(2,1)S(1)} %get-tuple-element.79), channel_id=1, source_target_pairs={{0,24},{8,16},{16,8},{24,0},{1,25},{9,17},{17,9},{25,1},{2,26},{10... | collective-permute-start | bytes 491528 | tf_op jit(solution)/shard_map/ppermute | solution.py:70
  57.7 0.5 collective-permute-start.21
  58.2 0.5 collective-permute-start.22
  58.8 4.3 %collective-permute-done.20 = bf16[64,1280]{1,0:T(8,128)(2,1)S(1)} collective-permute-done((bf16[64,1280]{1,0:T(8,128)(2,1)S(1)}, bf16[64,1280]{1,0:T(8,128)(2,1)S(1)}, u32[]{:S(2)}, u32[]{:S(2)}) %collective-permute-start.20) | collective-permute-done | bytes 163872 | tf_op jit(solution)/shard_map/ppermute | solution.py:70
  63.1 1.0 %collective-permute-done.21 = bf16[64,1280]{1,0:T(8,128)(2,1)S(1)} collective-permute-done((bf16[64,1280]{1,0:T(8,128)(2,1)S(1)}, bf16[64,1280]{1,0:T(8,128)(2,1)S(1)}, u32[]{:S(2)}, u32[]{:S(2)}) %collective-permute-start.21) | collective-permute-done | bytes 163872 | tf_op jit(solution)/shard_map/ppermute | solution.py:70
  64.3 0.6 fusion.48
  64.9 1.7 %collective-permute-start.23 = (bf16[16,1024]{1,0:T(8,128)(2,1)S(1)}, bf16[16,1024]{1,0:T(8,128)(2,1)S(1)}, u32[]{:S(2)}, u32[]{:S(2)}) collective-permute-start(bf16[16,1024]{1,0:T(8,128)(2,1)S(1)} %get-tuple-element.71), channel_id=1, source_target_pairs={{0,6},{1,7},{2,4},{3,5},{4,2},{5,3},{6,0},{7,1},{8,14},{9,15},{10,... | collective-permute-start | bytes 98312 | tf_op jit(solution)/shard_map/ppermute | solution.py:61
  66.6 0.9 collective-permute-start.24
  67.5 1.8 %collective-permute-start.25 = (bf16[16,1024]{1,0:T(8,128)(2,1)S(1)}, bf16[16,1024]{1,0:T(8,128)(2,1)S(1)}, u32[]{:S(2)}, u32[]{:S(2)}) collective-permute-start(bf16[16,1024]{1,0:T(8,128)(2,1)S(1)} %get-tuple-element.72), channel_id=1, source_target_pairs={{0,2},{1,3},{2,0},{3,1},{4,6},{5,7},{6,4},{7,5},{8,10},{9,11},{10,... | collective-permute-start | bytes 98312 | tf_op jit(solution)/shard_map/ppermute | solution.py:61
  69.3 1.3 %collective-permute-done.23 = bf16[16,1024]{1,0:T(8,128)(2,1)S(1)} collective-permute-done((bf16[16,1024]{1,0:T(8,128)(2,1)S(1)}, bf16[16,1024]{1,0:T(8,128)(2,1)S(1)}, u32[]{:S(2)}, u32[]{:S(2)}) %collective-permute-start.23) | collective-permute-done | bytes 32800 | tf_op jit(solution)/shard_map/ppermute | solution.py:61
  70.7 1.5 %collective-permute-done.24 = bf16[16,1024]{1,0:T(8,128)(2,1)S(1)} collective-permute-done((bf16[16,1024]{1,0:T(8,128)(2,1)S(1)}, bf16[16,1024]{1,0:T(8,128)(2,1)S(1)}, u32[]{:S(2)}, u32[]{:S(2)}) %collective-permute-start.24) | collective-permute-done | bytes 32800 | tf_op jit(solution)/shard_map/ppermute | solution.py:61
  72.1 2.0 %collective-permute-start.26 = (bf16[16,1024]{1,0:T(8,128)(2,1)S(1)}, bf16[16,1024]{1,0:T(8,128)(2,1)S(1)}, u32[]{:S(2)}, u32[]{:S(2)}) collective-permute-start(bf16[16,1024]{1,0:T(8,128)(2,1)S(1)} %fusion.33), channel_id=1, source_target_pairs={{0,6},{1,7},{2,4},{3,5},{4,2},{5,3},{6,0},{7,1},{8,14},{9,15},{10,... | collective-permute-start | bytes 98312 | tf_op jit(solution)/shard_map/ppermute | solution.py:61
  74.1 0.9 collective-permute-start.27
  75.1 1.5 %collective-permute-start.28 = (bf16[16,1024]{1,0:T(8,128)(2,1)S(1)}, bf16[16,1024]{1,0:T(8,128)(2,1)S(1)}, u32[]{:S(2)}, u32[]{:S(2)}) collective-permute-start(bf16[16,1024]{1,0:T(8,128)(2,1)S(1)} %fusion.33), channel_id=1, source_target_pairs={{0,2},{1,3},{2,0},{3,1},{4,6},{5,7},{6,4},{7,5},{8,10},{9,11},{10,... | collective-permute-start | bytes 98312 | tf_op jit(solution)/shard_map/ppermute | solution.py:61
  76.6 1.3 %collective-permute-done.26 = bf16[16,1024]{1,0:T(8,128)(2,1)S(1)} collective-permute-done((bf16[16,1024]{1,0:T(8,128)(2,1)S(1)}, bf16[16,1024]{1,0:T(8,128)(2,1)S(1)}, u32[]{:S(2)}, u32[]{:S(2)}) %collective-permute-start.26) | collective-permute-done | bytes 32800 | tf_op jit(solution)/shard_map/ppermute | solution.py:61
  77.9 1.2 %collective-permute-done.27 = bf16[16,1024]{1,0:T(8,128)(2,1)S(1)} collective-permute-done((bf16[16,1024]{1,0:T(8,128)(2,1)S(1)}, bf16[16,1024]{1,0:T(8,128)(2,1)S(1)}, u32[]{:S(2)}, u32[]{:S(2)}) %collective-permute-start.27) | collective-permute-done | bytes 32800 | tf_op jit(solution)/shard_map/ppermute | solution.py:61
  79.3 0.9 fusion.49
  80.3 1.5 %collective-permute-start.29 = (bf16[64,1280]{1,0:T(8,128)(2,1)S(1)}, bf16[64,1280]{1,0:T(8,128)(2,1)S(1)}, u32[]{:S(2)}, u32[]{:S(2)}) collective-permute-start(bf16[64,1280]{1,0:T(8,128)(2,1)S(1)} %get-tuple-element.83), channel_id=1, source_target_pairs={{0,24},{8,16},{16,8},{24,0},{1,25},{9,17},{17,9},{25,1},{2,26},{10... | collective-permute-start | bytes 491528 | tf_op jit(solution)/shard_map/ppermute | solution.py:70
  81.7 1.2 %collective-permute-start.30 = (bf16[64,1280]{1,0:T(8,128)(2,1)S(1)}, bf16[64,1280]{1,0:T(8,128)(2,1)S(1)}, u32[]{:S(2)}, u32[]{:S(2)}) collective-permute-start(bf16[64,1280]{1,0:T(8,128)(2,1)S(1)} %get-tuple-element.83), channel_id=1, source_target_pairs={{0,16},{8,24},{16,0},{24,8},{1,17},{9,25},{17,1},{25,9},{2,18},{10... | collective-permute-start | bytes 491528 | tf_op jit(solution)/shard_map/ppermute | solution.py:70
  83.0 0.8 collective-permute-start.31
  83.8 2.8 %collective-permute-done.29 = bf16[64,1280]{1,0:T(8,128)(2,1)S(1)} collective-permute-done((bf16[64,1280]{1,0:T(8,128)(2,1)S(1)}, bf16[64,1280]{1,0:T(8,128)(2,1)S(1)}, u32[]{:S(2)}, u32[]{:S(2)}) %collective-permute-start.29) | collective-permute-done | bytes 163872 | tf_op jit(solution)/shard_map/ppermute | solution.py:70
  86.6 1.7 %collective-permute-done.30 = bf16[64,1280]{1,0:T(8,128)(2,1)S(1)} collective-permute-done((bf16[64,1280]{1,0:T(8,128)(2,1)S(1)}, bf16[64,1280]{1,0:T(8,128)(2,1)S(1)}, u32[]{:S(2)}, u32[]{:S(2)}) %collective-permute-start.30) | collective-permute-done | bytes 163872 | tf_op jit(solution)/shard_map/ppermute | solution.py:70
  88.5 2.3 %fusion.50 = (bf16[64,1024]{1,0:T(8,128)(2,1)S(1)}, f32[64,1024]{1,0:T(8,128)S(1)}) fusion(bf16[64,1280]{1,0:T(8,128)(2,1)S(1)} %get-tuple-element.50, bf16[1280,1024]{1,0:T(8,128)(2,1)} %copy-done.1), kind=kOutput, calls=%fused_computation.94 | convolution fusion | flops 167837696 | bytes 3178496 | tf_op jit(solution)/shard_map/dot_general | solution.py:51
  91.0 1.9 %collective-permute-start.33 = (bf16[16,1024]{1,0:T(8,128)(2,1)S(1)}, bf16[16,1024]{1,0:T(8,128)(2,1)S(1)}, u32[]{:S(2)}, u32[]{:S(2)}) collective-permute-start(bf16[16,1024]{1,0:T(8,128)(2,1)S(1)} %get-tuple-element.68), channel_id=1, source_target_pairs={{0,6},{1,7},{2,4},{3,5},{4,2},{5,3},{6,0},{7,1},{8,14},{9,15},{10,... | collective-permute-start | bytes 98312 | tf_op jit(solution)/shard_map/ppermute | solution.py:61
  92.8 0.8 collective-permute-start.34
  93.7 1.7 %collective-permute-start.35 = (bf16[16,1024]{1,0:T(8,128)(2,1)S(1)}, bf16[16,1024]{1,0:T(8,128)(2,1)S(1)}, u32[]{:S(2)}, u32[]{:S(2)}) collective-permute-start(bf16[16,1024]{1,0:T(8,128)(2,1)S(1)} %get-tuple-element.69), channel_id=1, source_target_pairs={{0,2},{1,3},{2,0},{3,1},{4,6},{5,7},{6,4},{7,5},{8,10},{9,11},{10,... | collective-permute-start | bytes 98312 | tf_op jit(solution)/shard_map/ppermute | solution.py:61
  95.5 0.6 fusion.17
  96.1 1.0 %collective-permute-done.33 = bf16[16,1024]{1,0:T(8,128)(2,1)S(1)} collective-permute-done((bf16[16,1024]{1,0:T(8,128)(2,1)S(1)}, bf16[16,1024]{1,0:T(8,128)(2,1)S(1)}, u32[]{:S(2)}, u32[]{:S(2)}) %collective-permute-start.33) | collective-permute-done | bytes 32800 | tf_op jit(solution)/shard_map/ppermute | solution.py:61
  97.1 1.1 %collective-permute-done.34 = bf16[16,1024]{1,0:T(8,128)(2,1)S(1)} collective-permute-done((bf16[16,1024]{1,0:T(8,128)(2,1)S(1)}, bf16[16,1024]{1,0:T(8,128)(2,1)S(1)}, u32[]{:S(2)}, u32[]{:S(2)}) %collective-permute-start.34) | collective-permute-done | bytes 32800 | tf_op jit(solution)/shard_map/ppermute | solution.py:61
  98.2 0.6 add_bitcast_fusion
  (62 shorter events, 1.9 us)
Async XLA Ops:
  0.6 43.7 %copy-start = (s32[1024,128]{1,0:T(8,128)S(1)}, s32[1024,128]{1,0:T(8,128)}, u32[]{:S(2)}) copy-start(s32[1024,128]{1,0:T(8,128)} %param.9) | copy-start | bytes 1572868
  0.6 22.2 %copy-start.3 = (f32[640]{0:T(1024)S(1)}, f32[640]{0:T(1024)}, u32[]{:S(2)}) copy-start(f32[640]{0:T(1024)} %param.7) | copy-start | bytes 7684
  1.9 10.4 %collective-permute-start.1 = (s16[144,1024]{1,0:T(8,128)(2,1)S(1)}, s16[144,1024]{1,0:T(8,128)(2,1)S(1)}, u32[]{:S(2)}, u32[]{:S(2)}) collective-permute-start(s16[144,1024]{1,0:T(8,128)(2,1)S(1)} %fusion.refs_0_), channel_id=1, source_target_pairs={{0,4},{1,5},{4,6},{5,7},{6,2},{7,3},{2,0},{3,1},{8,12},{9,13},{12,... | collective-permute-start | bytes 884744 | tf_op jit(solution)/shard_map/ppermute | solution.py:65
  8.1 11.0 %collective-permute-start.2 = (s16[320,640]{1,0:T(8,128)(2,1)S(1)}, s16[320,640]{1,0:T(8,128)(2,1)S(1)}, u32[]{:S(2)}, u32[]{:S(2)}) collective-permute-start(s16[320,640]{1,0:T(8,128)(2,1)S(1)} %pad_add_fusion.refs_6_), channel_id=1, source_target_pairs={{0,8},{8,0},{16,24},{24,16},{1,9},{9,1},{17,25},{25,17},{2,10},{10... | collective-permute-start | bytes 1228808 | tf_op jit(solution)/shard_map/ppermute | solution.py:70
  9.6 11.0 %collective-permute-start.4 = (s16[320,640]{1,0:T(8,128)(2,1)S(1)}, s16[320,640]{1,0:T(8,128)(2,1)S(1)}, u32[]{:S(2)}, u32[]{:S(2)}) collective-permute-start(s16[320,640]{1,0:T(8,128)(2,1)S(1)} %pad_add_fusion.refs_6_), channel_id=1, source_target_pairs={{0,16},{8,24},{16,0},{24,8},{1,17},{9,25},{17,1},{25,9},{2,18},{10... | collective-permute-start | bytes 1228808 | tf_op jit(solution)/shard_map/ppermute | solution.py:70
  12.2 6.8 %collective-permute-start.3 = (s16[144,1024]{1,0:T(8,128)(2,1)S(1)}, s16[144,1024]{1,0:T(8,128)(2,1)S(1)}, u32[]{:S(2)}, u32[]{:S(2)}) collective-permute-start(s16[144,1024]{1,0:T(8,128)(2,1)S(1)} %collective-permute-done.1.refs_2_), channel_id=1, source_target_pairs={{0,1},{1,0},{2,3},{3,2},{4,5},{5,4},{6,7},{7,6},{8,9},{9,8},{10,11... | collective-permute-start | bytes 884744 | tf_op jit(solution)/shard_map/ppermute | solution.py:56
  12.2 15.4 %collective-permute-start = (s16[144,1024]{1,0:T(8,128)(2,1)S(1)}, s16[144,1024]{1,0:T(8,128)(2,1)}, u32[]{:S(2)}, u32[]{:S(2)}) collective-permute-start(s16[144,1024]{1,0:T(8,128)(2,1)S(1)} %fusion.refs_0_), channel_id=1, source_target_pairs={{0,1},{1,0},{2,3},{3,2},{4,5},{5,4},{6,7},{7,6},{8,9},{9,8},{10,11... | collective-permute-start | bytes 884744 | tf_op jit(solution)/shard_map/ppermute | solution.py:56
  12.7 10.4 %collective-permute-start.7 = (s16[144,1024]{1,0:T(8,128)(2,1)S(1)}, s16[144,1024]{1,0:T(8,128)(2,1)S(1)}, u32[]{:S(2)}, u32[]{:S(2)}) collective-permute-start(s16[144,1024]{1,0:T(8,128)(2,1)S(1)} %collective-permute-done.1.refs_2_), channel_id=1, source_target_pairs={{0,4},{1,5},{4,6},{5,7},{6,2},{7,3},{2,0},{3,1},{8,12},{9,13},{12,... | collective-permute-start | bytes 884744 | tf_op jit(solution)/shard_map/ppermute | solution.py:65
  19.1 8.3 %collective-permute-start.5 = (s16[160,640]{1,0:T(8,128)(2,1)S(1)}, s16[160,640]{1,0:T(8,128)(2,1)S(1)}, u32[]{:S(2)}, u32[]{:S(2)}) collective-permute-start(s16[160,640]{1,0:T(8,128)(2,1)S(1)} %slice.101), channel_id=1, source_target_pairs={{0,16},{8,24},{16,0},{24,8},{1,17},{9,25},{17,1},{25,9},{2,18},{10... | collective-permute-start | bytes 614408 | tf_op jit(solution)/shard_map/ppermute | solution.py:70
  21.4 6.0 %collective-permute-start.6 = (s16[160,640]{1,0:T(8,128)(2,1)}, s16[160,640]{1,0:T(8,128)(2,1)S(1)}, u32[]{:S(2)}, u32[]{:S(2)}) collective-permute-start(s16[160,640]{1,0:T(8,128)(2,1)} %slice.102), channel_id=1, source_target_pairs={{0,8},{8,0},{16,24},{24,16},{1,9},{9,1},{17,25},{25,17},{2,10},{10... | collective-permute-start | bytes 614408 | tf_op jit(solution)/shard_map/ppermute | solution.py:70
  23.1 4.5 %collective-permute-start.8 = (s16[144,1024]{1,0:T(8,128)(2,1)S(1)}, s16[144,1024]{1,0:T(8,128)(2,1)S(1)}, u32[]{:S(2)}, u32[]{:S(2)}) collective-permute-start(s16[144,1024]{1,0:T(8,128)(2,1)S(1)} %collective-permute-done.7.refs_4_), channel_id=1, source_target_pairs={{0,1},{1,0},{2,3},{3,2},{4,5},{5,4},{6,7},{7,6},{8,9},{9,8},{10,11... | collective-permute-start | bytes 884744 | tf_op jit(solution)/shard_map/ppermute | solution.py:56
  23.1 10.1 %collective-permute-start.9 = (s16[144,1024]{1,0:T(8,128)(2,1)S(1)}, s16[144,1024]{1,0:T(8,128)(2,1)S(1)}, u32[]{:S(2)}, u32[]{:S(2)}) collective-permute-start(s16[144,1024]{1,0:T(8,128)(2,1)S(1)} %collective-permute-done.7.refs_4_), channel_id=1, source_target_pairs={{0,4},{1,5},{4,6},{5,7},{6,2},{7,3},{2,0},{3,1},{8,12},{9,13},{12,... | collective-permute-start | bytes 884744 | tf_op jit(solution)/shard_map/ppermute | solution.py:65
  27.5 6.4 %collective-permute-start.11 = (s16[64,640]{1,0:T(8,128)(2,1)S(1)}, s16[64,640]{1,0:T(8,128)(2,1)S(1)}, u32[]{:S(2)}, u32[]{:S(2)}) collective-permute-start(s16[64,640]{1,0:T(8,128)(2,1)S(1)} %get-tuple-element.40), channel_id=1, source_target_pairs={{0,1},{1,0},{2,3},{3,2},{4,5},{5,4},{6,7},{7,6},{8,9},{9,8},{10,11... | collective-permute-start | bytes 245768 | tf_op jit(solution)/shard_map/ppermute | solution.py:56
  33.3 1.8 %collective-permute-start.10 = (s16[144,1024]{1,0:T(8,128)(2,1)S(1)}, s16[144,1024]{1,0:T(8,128)(2,1)S(1)}, u32[]{:S(2)}, u32[]{:S(2)}) collective-permute-start(s16[144,1024]{1,0:T(8,128)(2,1)S(1)} %collective-permute-done.9.own_ref), channel_id=1, source_target_pairs={{0,1},{1,0},{2,3},{3,2},{4,5},{5,4},{6,7},{7,6},{8,9},{9,8},{10,11... | collective-permute-start | bytes 884744 | tf_op jit(solution)/shard_map/ppermute | solution.py:56
  38.0 1.4 %collective-permute-start.12 = (bf16[64,1024]{1,0:T(8,128)(2,1)S(1)}, bf16[64,1024]{1,0:T(8,128)(2,1)S(1)}, u32[]{:S(2)}, u32[]{:S(2)}) collective-permute-start(bf16[64,1024]{1,0:T(8,128)(2,1)S(1)} %get-tuple-element.43), channel_id=1, source_target_pairs={{0,1},{1,0},{2,3},{3,2},{4,5},{5,4},{6,7},{7,6},{8,9},{9,8},{10,11... | collective-permute-start | bytes 393224 | tf_op jit(solution)/shard_map/ppermute | solution.py:56
  39.5 12.0 %collective-permute-start.19 = (bf16[640,1024]{1,0:T(8,128)(2,1)S(1)}, bf16[640,1024]{1,0:T(8,128)(2,1)}, u32[]{:S(2)}, u32[]{:S(2)}) collective-permute-start(bf16[640,1024]{1,0:T(8,128)(2,1)S(1)} %get-tuple-element.45), channel_id=1, source_target_pairs={{0,1},{1,0},{2,3},{3,2},{4,5},{5,4},{6,7},{7,6},{8,9},{9,8},{10,11... | collective-permute-start | bytes 3932168 | tf_op jit(solution)/shard_map/ppermute | solution.py:56
  39.9 5.8 %collective-permute-start.13 = (bf16[16,1024]{1,0:T(8,128)(2,1)S(1)}, bf16[16,1024]{1,0:T(8,128)(2,1)S(1)}, u32[]{:S(2)}, u32[]{:S(2)}) collective-permute-start(bf16[16,1024]{1,0:T(8,128)(2,1)S(1)} %get-tuple-element.74), channel_id=1, source_target_pairs={{0,6},{1,7},{2,4},{3,5},{4,2},{5,3},{6,0},{7,1},{8,14},{9,15},{10,... | collective-permute-start | bytes 98312 | tf_op jit(solution)/shard_map/ppermute | solution.py:61
  41.4 5.2 %collective-permute-start.14 = (bf16[16,1024]{1,0:T(8,128)(2,1)S(1)}, bf16[16,1024]{1,0:T(8,128)(2,1)S(1)}, u32[]{:S(2)}, u32[]{:S(2)}) collective-permute-start(bf16[16,1024]{1,0:T(8,128)(2,1)S(1)} %get-tuple-element.76), channel_id=1, source_target_pairs={{0,4},{1,5},{2,6},{3,7},{4,0},{5,1},{6,2},{7,3},{8,12},{9,13},{10,... | collective-permute-start | bytes 98312 | tf_op jit(solution)/shard_map/ppermute | solution.py:61
  43.0 3.9 %collective-permute-start.15 = (bf16[16,1024]{1,0:T(8,128)(2,1)S(1)}, bf16[16,1024]{1,0:T(8,128)(2,1)S(1)}, u32[]{:S(2)}, u32[]{:S(2)}) collective-permute-start(bf16[16,1024]{1,0:T(8,128)(2,1)S(1)} %get-tuple-element.75), channel_id=1, source_target_pairs={{0,2},{1,3},{2,0},{3,1},{4,6},{5,7},{6,4},{7,5},{8,10},{9,11},{10,... | collective-permute-start | bytes 98312 | tf_op jit(solution)/shard_map/ppermute | solution.py:61
  47.0 6.0 %collective-permute-start.16 = (bf16[16,1024]{1,0:T(8,128)(2,1)S(1)}, bf16[16,1024]{1,0:T(8,128)(2,1)S(1)}, u32[]{:S(2)}, u32[]{:S(2)}) collective-permute-start(bf16[16,1024]{1,0:T(8,128)(2,1)S(1)} %fusion.32), channel_id=1, source_target_pairs={{0,6},{1,7},{2,4},{3,5},{4,2},{5,3},{6,0},{7,1},{8,14},{9,15},{10,... | collective-permute-start | bytes 98312 | tf_op jit(solution)/shard_map/ppermute | solution.py:61
  49.5 4.8 %collective-permute-start.17 = (bf16[16,1024]{1,0:T(8,128)(2,1)S(1)}, bf16[16,1024]{1,0:T(8,128)(2,1)S(1)}, u32[]{:S(2)}, u32[]{:S(2)}) collective-permute-start(bf16[16,1024]{1,0:T(8,128)(2,1)S(1)} %fusion.32), channel_id=1, source_target_pairs={{0,4},{1,5},{2,6},{3,7},{4,0},{5,1},{6,2},{7,3},{8,12},{9,13},{10,... | collective-permute-start | bytes 98312 | tf_op jit(solution)/shard_map/ppermute | solution.py:61
  49.8 4.5 %collective-permute-start.18 = (bf16[16,1024]{1,0:T(8,128)(2,1)S(1)}, bf16[16,1024]{1,0:T(8,128)(2,1)S(1)}, u32[]{:S(2)}, u32[]{:S(2)}) collective-permute-start(bf16[16,1024]{1,0:T(8,128)(2,1)S(1)} %fusion.32), channel_id=1, source_target_pairs={{0,2},{1,3},{2,0},{3,1},{4,6},{5,7},{6,4},{7,5},{8,10},{9,11},{10,... | collective-permute-start | bytes 98312 | tf_op jit(solution)/shard_map/ppermute | solution.py:61
  53.0 26.3 %copy-start.1 = (bf16[1280,1024]{1,0:T(8,128)(2,1)}, bf16[1280,1024]{1,0:T(8,128)(2,1)S(1)}, u32[]{:S(2)}) copy-start(bf16[1280,1024]{1,0:T(8,128)(2,1)S(1)} %pad_maximum_fusion) | copy-start | bytes 7864324
  55.2 7.9 %collective-permute-start.20 = (bf16[64,1280]{1,0:T(8,128)(2,1)S(1)}, bf16[64,1280]{1,0:T(8,128)(2,1)S(1)}, u32[]{:S(2)}, u32[]{:S(2)}) collective-permute-start(bf16[64,1280]{1,0:T(8,128)(2,1)S(1)} %get-tuple-element.79), channel_id=1, source_target_pairs={{0,24},{8,16},{16,8},{24,0},{1,25},{9,17},{17,9},{25,1},{2,26},{10... | collective-permute-start | bytes 491528 | tf_op jit(solution)/shard_map/ppermute | solution.py:70
  57.7 6.4 %collective-permute-start.21 = (bf16[64,1280]{1,0:T(8,128)(2,1)S(1)}, bf16[64,1280]{1,0:T(8,128)(2,1)S(1)}, u32[]{:S(2)}, u32[]{:S(2)}) collective-permute-start(bf16[64,1280]{1,0:T(8,128)(2,1)S(1)} %get-tuple-element.79), channel_id=1, source_target_pairs={{0,16},{8,24},{16,0},{24,8},{1,17},{9,25},{17,1},{25,9},{2,18},{10... | collective-permute-start | bytes 491528 | tf_op jit(solution)/shard_map/ppermute | solution.py:70
  58.2 5.9 %collective-permute-start.22 = (bf16[64,1280]{1,0:T(8,128)(2,1)S(1)}, bf16[64,1280]{1,0:T(8,128)(2,1)S(1)}, u32[]{:S(2)}, u32[]{:S(2)}) collective-permute-start(bf16[64,1280]{1,0:T(8,128)(2,1)S(1)} %get-tuple-element.79), channel_id=1, source_target_pairs={{0,8},{8,0},{16,24},{24,16},{1,9},{9,1},{17,25},{25,17},{2,10},{10... | collective-permute-start | bytes 491528 | tf_op jit(solution)/shard_map/ppermute | solution.py:70
  64.9 5.8 %collective-permute-start.23 = (bf16[16,1024]{1,0:T(8,128)(2,1)S(1)}, bf16[16,1024]{1,0:T(8,128)(2,1)S(1)}, u32[]{:S(2)}, u32[]{:S(2)}) collective-permute-start(bf16[16,1024]{1,0:T(8,128)(2,1)S(1)} %get-tuple-element.71), channel_id=1, source_target_pairs={{0,6},{1,7},{2,4},{3,5},{4,2},{5,3},{6,0},{7,1},{8,14},{9,15},{10,... | collective-permute-start | bytes 98312 | tf_op jit(solution)/shard_map/ppermute | solution.py:61
  66.6 5.5 %collective-permute-start.24 = (bf16[16,1024]{1,0:T(8,128)(2,1)S(1)}, bf16[16,1024]{1,0:T(8,128)(2,1)S(1)}, u32[]{:S(2)}, u32[]{:S(2)}) collective-permute-start(bf16[16,1024]{1,0:T(8,128)(2,1)S(1)} %get-tuple-element.73), channel_id=1, source_target_pairs={{0,4},{1,5},{2,6},{3,7},{4,0},{5,1},{6,2},{7,3},{8,12},{9,13},{10,... | collective-permute-start | bytes 98312 | tf_op jit(solution)/shard_map/ppermute | solution.py:61
  67.5 4.6 %collective-permute-start.25 = (bf16[16,1024]{1,0:T(8,128)(2,1)S(1)}, bf16[16,1024]{1,0:T(8,128)(2,1)S(1)}, u32[]{:S(2)}, u32[]{:S(2)}) collective-permute-start(bf16[16,1024]{1,0:T(8,128)(2,1)S(1)} %get-tuple-element.72), channel_id=1, source_target_pairs={{0,2},{1,3},{2,0},{3,1},{4,6},{5,7},{6,4},{7,5},{8,10},{9,11},{10,... | collective-permute-start | bytes 98312 | tf_op jit(solution)/shard_map/ppermute | solution.py:61
  72.1 5.8 %collective-permute-start.26 = (bf16[16,1024]{1,0:T(8,128)(2,1)S(1)}, bf16[16,1024]{1,0:T(8,128)(2,1)S(1)}, u32[]{:S(2)}, u32[]{:S(2)}) collective-permute-start(bf16[16,1024]{1,0:T(8,128)(2,1)S(1)} %fusion.33), channel_id=1, source_target_pairs={{0,6},{1,7},{2,4},{3,5},{4,2},{5,3},{6,0},{7,1},{8,14},{9,15},{10,... | collective-permute-start | bytes 98312 | tf_op jit(solution)/shard_map/ppermute | solution.py:61
  74.1 5.0 %collective-permute-start.27 = (bf16[16,1024]{1,0:T(8,128)(2,1)S(1)}, bf16[16,1024]{1,0:T(8,128)(2,1)S(1)}, u32[]{:S(2)}, u32[]{:S(2)}) collective-permute-start(bf16[16,1024]{1,0:T(8,128)(2,1)S(1)} %fusion.33), channel_id=1, source_target_pairs={{0,4},{1,5},{2,6},{3,7},{4,0},{5,1},{6,2},{7,3},{8,12},{9,13},{10,... | collective-permute-start | bytes 98312 | tf_op jit(solution)/shard_map/ppermute | solution.py:61
  75.1 4.3 %collective-permute-start.28 = (bf16[16,1024]{1,0:T(8,128)(2,1)S(1)}, bf16[16,1024]{1,0:T(8,128)(2,1)S(1)}, u32[]{:S(2)}, u32[]{:S(2)}) collective-permute-start(bf16[16,1024]{1,0:T(8,128)(2,1)S(1)} %fusion.33), channel_id=1, source_target_pairs={{0,2},{1,3},{2,0},{3,1},{4,6},{5,7},{6,4},{7,5},{8,10},{9,11},{10,... | collective-permute-start | bytes 98312 | tf_op jit(solution)/shard_map/ppermute | solution.py:61
  80.3 6.4 %collective-permute-start.29 = (bf16[64,1280]{1,0:T(8,128)(2,1)S(1)}, bf16[64,1280]{1,0:T(8,128)(2,1)S(1)}, u32[]{:S(2)}, u32[]{:S(2)}) collective-permute-start(bf16[64,1280]{1,0:T(8,128)(2,1)S(1)} %get-tuple-element.83), channel_id=1, source_target_pairs={{0,24},{8,16},{16,8},{24,0},{1,25},{9,17},{17,9},{25,1},{2,26},{10... | collective-permute-start | bytes 491528 | tf_op jit(solution)/shard_map/ppermute | solution.py:70
  81.7 6.5 %collective-permute-start.30 = (bf16[64,1280]{1,0:T(8,128)(2,1)S(1)}, bf16[64,1280]{1,0:T(8,128)(2,1)S(1)}, u32[]{:S(2)}, u32[]{:S(2)}) collective-permute-start(bf16[64,1280]{1,0:T(8,128)(2,1)S(1)} %get-tuple-element.83), channel_id=1, source_target_pairs={{0,16},{8,24},{16,0},{24,8},{1,17},{9,25},{17,1},{25,9},{2,18},{10... | collective-permute-start | bytes 491528 | tf_op jit(solution)/shard_map/ppermute | solution.py:70
  83.0 5.3 %collective-permute-start.31 = (bf16[64,1280]{1,0:T(8,128)(2,1)S(1)}, bf16[64,1280]{1,0:T(8,128)(2,1)S(1)}, u32[]{:S(2)}, u32[]{:S(2)}) collective-permute-start(bf16[64,1280]{1,0:T(8,128)(2,1)S(1)} %get-tuple-element.83), channel_id=1, source_target_pairs={{0,8},{8,0},{16,24},{24,16},{1,9},{9,1},{17,25},{25,17},{2,10},{10... | collective-permute-start | bytes 491528 | tf_op jit(solution)/shard_map/ppermute | solution.py:70
  88.5 7.0 %copy-start.2 = (f32[640,32]{0,1:T(8,128)S(1)}, f32[640,32]{0,1:T(8,128)}, u32[]{:S(2)}) copy-start(f32[640,32]{0,1:T(8,128)} %param.8) | copy-start | bytes 245764
  90.9 4.6 %collective-permute-start.32 = (f32[64,640]{1,0:T(8,128)S(1)}, f32[64,640]{1,0:T(8,128)S(1)}, u32[]{:S(2)}, u32[]{:S(2)}) collective-permute-start(f32[64,640]{1,0:T(8,128)S(1)} %get-tuple-element.59), channel_id=1, source_target_pairs={{0,1},{1,0},{2,3},{3,2},{4,5},{5,4},{6,7},{7,6},{8,9},{9,8},{10,11... | collective-permute-start | bytes 491528 | tf_op jit(solution)/shard_map/ppermute | solution.py:56
  91.0 6.1 %collective-permute-start.33 = (bf16[16,1024]{1,0:T(8,128)(2,1)S(1)}, bf16[16,1024]{1,0:T(8,128)(2,1)S(1)}, u32[]{:S(2)}, u32[]{:S(2)}) collective-permute-start(bf16[16,1024]{1,0:T(8,128)(2,1)S(1)} %get-tuple-element.68), channel_id=1, source_target_pairs={{0,6},{1,7},{2,4},{3,5},{4,2},{5,3},{6,0},{7,1},{8,14},{9,15},{10,... | collective-permute-start | bytes 98312 | tf_op jit(solution)/shard_map/ppermute | solution.py:61
  92.8 5.3 %collective-permute-start.34 = (bf16[16,1024]{1,0:T(8,128)(2,1)S(1)}, bf16[16,1024]{1,0:T(8,128)(2,1)S(1)}, u32[]{:S(2)}, u32[]{:S(2)}) collective-permute-start(bf16[16,1024]{1,0:T(8,128)(2,1)S(1)} %get-tuple-element.70), channel_id=1, source_target_pairs={{0,4},{1,5},{2,6},{3,7},{4,0},{5,1},{6,2},{7,3},{8,12},{9,13},{10,... | collective-permute-start | bytes 98312 | tf_op jit(solution)/shard_map/ppermute | solution.py:61
  93.7 4.5 %collective-permute-start.35 = (bf16[16,1024]{1,0:T(8,128)(2,1)S(1)}, bf16[16,1024]{1,0:T(8,128)(2,1)S(1)}, u32[]{:S(2)}, u32[]{:S(2)}) collective-permute-start(bf16[16,1024]{1,0:T(8,128)(2,1)S(1)} %get-tuple-element.69), channel_id=1, source_target_pairs={{0,2},{1,3},{2,0},{3,1},{4,6},{5,7},{6,4},{7,5},{8,10},{9,11},{10,... | collective-permute-start | bytes 98312 | tf_op jit(solution)/shard_map/ppermute | solution.py:61

commit v10 on v9

--- a/solution.py
+++ b/solution.py
@@ -14,16 +14,15 @@
 CODE_MAX = 32766.0
 LANES = 128
 VMEM_BYTES = 16 * 1024 * 1024
-EARLY_VMEM_BYTES = 36 * 1024 * 1024
+EARLY_VMEM_BYTES = 28 * 1024 * 1024
 WEIGHT_BOUND = 6.0
 COS_TURNS = (
-    0.9999999890590243,
-    -19.739204499454,
-    64.93911745989858,
-    -85.45013953092679,
-    60.16763095123224,
-    -25.967599249288032,
-    6.528658162158786,
+    0.9999992107823231,
+    -19.738980355764067,
+    64.9286574210343,
+    -85.27162153430471,
+    58.790492120138815,
+    -21.07110562713763,
 )
 PER_TURN = EMBED_BOUND * FREQ_BOUND / (CODE_MAX * CODE_MAX * 2.0 * math.pi)
 

time: 99.2 us -> 98.9 us (level)
  no operation moved by 1% of the time
where the time goes in v10:
time: 98.9 us; the launch traced here: 98.6 us
  starting transfers between devices  47.8 us (48%)
  waiting for transfers between devices  28.5 us (29%)
  Pallas kernels  8.33 us (8%)
  other arithmetic  6.78 us (7%)
  matrix products  4.75 us (5%)
  local copies, waits for them, and re-layouts  1.44 us (1%)
    ppermute x15, starting transfers between devices, line_swap(): return lax.ppermute(x, 'feat', [(i, i ^ 2 * k) for i in range(n)])  22.3 us
    ppermute x10, waiting for transfers between devices, clip_swap(): return lax.ppermute(x, 'clip', [(i, i ^ k) for i in range(n)])  14.3 us
    ppermute x10, starting transfers between devices, clip_swap(): return lax.ppermute(x, 'clip', [(i, i ^ k) for i in range(n)])  13.3 us
    ppermute x15, waiting for transfers between devices, line_swap(): return lax.ppermute(x, 'feat', [(i, i ^ 2 * k) for i in range(n)])  10.9 us
    ppermute x3, starting transfers between devices, line_move(): lax.ppermute(x, 'feat', [(2 * a + c, 2 * b + c) for a, b in pairs for c i...  10.3 us
    pallas_call x1, Pallas kernels, phi_by_kernels(): pl.pallas_call(functools.partial(early_kernel, n_embeds=len(early), n_fre...  5.63 us
    convert_element_type x3, other arithmetic, encode(): return jnp.round(x * (CODE_MAX / bound)).astype(jnp.int16)  3.26 us
    dot_general x2, matrix products, mix(): return jnp.dot(a, b, preferred_element_type=jnp.float32)  2.91 us
  transfers between devices with their start and end apart: 36, of which 22 were waited for; matrix products, arithmetic and copies ran while one was open for 6% of the time, Pallas kernels for 6%

profile of v10, /device:TPU:0, one launch (start us, length us, event | category | flops | bytes accessed | tf_op | source)
XLA Modules:
  0.0 98.6 jit_solution(17317086139288437985)
XLA Ops:
  0.7 1.2 %fusion.refs_0_ = s16[144,1024]{1,0:T(8,128)(2,1)S(1)} fusion(f32[1024,144]{0,1:T(8,128)} %param.5), kind=kLoop, calls=%fused_computation.10 | loop fusion | flops 442368 | bytes 884736 | tf_op jit(solution)/shard_map/convert_element_type | solution.py:31
  1.9 4.1 %collective-permute-start.1 = (s16[144,1024]{1,0:T(8,128)(2,1)S(1)}, s16[144,1024]{1,0:T(8,128)(2,1)S(1)}, u32[]{:S(2)}, u32[]{:S(2)}) collective-permute-start(s16[144,1024]{1,0:T(8,128)(2,1)S(1)} %fusion.refs_0_), channel_id=1, source_target_pairs={{0,4},{1,5},{4,6},{5,7},{6,2},{7,3},{2,0},{3,1},{8,12},{9,13},{12,... | collective-permute-start | bytes 884744 | tf_op jit(solution)/shard_map/ppermute | solution.py:64
  6.0 1.2 %round-nearest-even_convert_fusion.2 = (s16[144,640]{1,0:T(8,128)(2,1)S(1)}, s16[144,640]{1,0:T(8,128)(2,1)S(1)}) fusion(f32[288,640]{1,0:T(8,128)} %param.6), kind=kLoop, calls=%fused_computation.4 | loop fusion | flops 552960 | bytes 1105920 | tf_op jit(solution)/shard_map/convert_element_type | solution.py:31
  7.2 0.8 fusion.38
  8.1 1.6 %collective-permute-start.2 = (s16[320,640]{1,0:T(8,128)(2,1)S(1)}, s16[320,640]{1,0:T(8,128)(2,1)S(1)}, u32[]{:S(2)}, u32[]{:S(2)}) collective-permute-start(s16[320,640]{1,0:T(8,128)(2,1)S(1)} %pad_add_fusion.refs_6_), channel_id=1, source_target_pairs={{0,8},{8,0},{16,24},{24,16},{1,9},{9,1},{17,25},{25,17},{2,10},{10... | collective-permute-start | bytes 1228808 | tf_op jit(solution)/shard_map/ppermute | solution.py:69
  9.6 1.5 %collective-permute-start.4 = (s16[320,640]{1,0:T(8,128)(2,1)S(1)}, s16[320,640]{1,0:T(8,128)(2,1)S(1)}, u32[]{:S(2)}, u32[]{:S(2)}) collective-permute-start(s16[320,640]{1,0:T(8,128)(2,1)S(1)} %pad_add_fusion.refs_6_), channel_id=1, source_target_pairs={{0,16},{8,24},{16,0},{24,8},{1,17},{9,25},{17,1},{25,9},{2,18},{10... | collective-permute-start | bytes 1228808 | tf_op jit(solution)/shard_map/ppermute | solution.py:69
  11.1 1.1 %collective-permute-done.1.refs_2_ = s16[144,1024]{1,0:T(8,128)(2,1)S(1)} collective-permute-done((s16[144,1024]{1,0:T(8,128)(2,1)S(1)}, s16[144,1024]{1,0:T(8,128)(2,1)S(1)}, u32[]{:S(2)}, u32[]{:S(2)}) %collective-permute-start.1) | collective-permute-done | bytes 294944 | tf_op jit(solution)/shard_map/ppermute | solution.py:64
  12.2 0.5 collective-permute-start
  12.7 3.4 %collective-permute-start.7 = (s16[144,1024]{1,0:T(8,128)(2,1)S(1)}, s16[144,1024]{1,0:T(8,128)(2,1)S(1)}, u32[]{:S(2)}, u32[]{:S(2)}) collective-permute-start(s16[144,1024]{1,0:T(8,128)(2,1)S(1)} %collective-permute-done.1.refs_2_), channel_id=1, source_target_pairs={{0,4},{1,5},{4,6},{5,7},{6,2},{7,3},{2,0},{3,1},{8,12},{9,13},{12,... | collective-permute-start | bytes 884744 | tf_op jit(solution)/shard_map/ppermute | solution.py:64
  16.1 2.9 %collective-permute-done.2.refs_7_ = s16[320,640]{1,0:T(8,128)(2,1)S(1)} collective-permute-done((s16[320,640]{1,0:T(8,128)(2,1)S(1)}, s16[320,640]{1,0:T(8,128)(2,1)S(1)}, u32[]{:S(2)}, u32[]{:S(2)}) %collective-permute-start.2) | collective-permute-done | bytes 409632 | tf_op jit(solution)/shard_map/ppermute | solution.py:69
  19.1 1.6 %collective-permute-start.5 = (s16[160,640]{1,0:T(8,128)(2,1)S(1)}, s16[160,640]{1,0:T(8,128)(2,1)S(1)}, u32[]{:S(2)}, u32[]{:S(2)}) collective-permute-start(s16[160,640]{1,0:T(8,128)(2,1)S(1)} %slice.101), channel_id=1, source_target_pairs={{0,16},{8,24},{16,0},{24,8},{1,17},{9,25},{17,1},{25,9},{2,18},{10... | collective-permute-start | bytes 614408 | tf_op jit(solution)/shard_map/ppermute | solution.py:69
  20.7 0.7 slice.102
  21.4 1.5 %collective-permute-start.6 = (s16[160,640]{1,0:T(8,128)(2,1)}, s16[160,640]{1,0:T(8,128)(2,1)S(1)}, u32[]{:S(2)}, u32[]{:S(2)}) collective-permute-start(s16[160,640]{1,0:T(8,128)(2,1)} %slice.102), channel_id=1, source_target_pairs={{0,8},{8,0},{16,24},{24,16},{1,9},{9,1},{17,25},{25,17},{2,10},{10... | collective-permute-start | bytes 614408 | tf_op jit(solution)/shard_map/ppermute | solution.py:69
  23.1 2.8 %collective-permute-start.9 = (s16[144,1024]{1,0:T(8,128)(2,1)S(1)}, s16[144,1024]{1,0:T(8,128)(2,1)S(1)}, u32[]{:S(2)}, u32[]{:S(2)}) collective-permute-start(s16[144,1024]{1,0:T(8,128)(2,1)S(1)} %collective-permute-done.7.refs_4_), channel_id=1, source_target_pairs={{0,4},{1,5},{4,6},{5,7},{6,2},{7,3},{2,0},{3,1},{8,12},{9,13},{12,... | collective-permute-start | bytes 884744 | tf_op jit(solution)/shard_map/ppermute | solution.py:64
  25.9 1.4 %collective-permute-done.6.refs_10_ = s16[160,640]{1,0:T(8,128)(2,1)S(1)} collective-permute-done((s16[160,640]{1,0:T(8,128)(2,1)}, s16[160,640]{1,0:T(8,128)(2,1)S(1)}, u32[]{:S(2)}, u32[]{:S(2)}) %collective-permute-start.6) | collective-permute-done | bytes 204832 | tf_op jit(solution)/shard_map/ppermute | solution.py:69
  27.6 5.6 %early_angles.1 = (f32[640,1024]{1,0:T(8,128)S(1)}, s16[640,288]{1,0:T(8,128)(2,1)S(1)}) custom-call(s32[3]{0:T(128)S(1)} %pad_add_fusion.3.at_ref, s16[144,1024]{1,0:T(8,128)(2,1)S(1)} %fusion.refs_0_, s16[144,1024]{1,0:T(8,128)(2,1)} %collective-permute-done.refs_1_, s16[144,1024]{1,0:T(8,128)(2,1)S(1)} %collective-permute-done.1.refs_2_, ...), custom_call_target="tpu_custom_call" | custom-call | flops 3523215360 | bytes 5242880 | tf_op jit(solution)/shard_map/early_angles/pallas_call | solution.py:174
  33.3 0.6 collective-permute-start.10
  33.9 1.1 %collective-permute-done.10.other_ref = s16[144,1024]{1,0:T(8,128)(2,1)S(1)} collective-permute-done((s16[144,1024]{1,0:T(8,128)(2,1)S(1)}, s16[144,1024]{1,0:T(8,128)(2,1)S(1)}, u32[]{:S(2)}, u32[]{:S(2)}) %collective-permute-start.10) | collective-permute-done | bytes 294944 | tf_op jit(solution)/shard_map/ppermute | solution.py:55
  35.0 2.7 %late_angles.1 = (bf16[640,1024]{1,0:T(8,128)(2,1)S(1)}, f32[64,1024]{1,0:T(8,128)S(1)}, bf16[64,1024]{1,0:T(8,128)(2,1)S(1)}) custom-call(f32[640,1024]{1,0:T(8,128)S(1)} %get-tuple-element.35.sum_ref, s16[144,1024]{1,0:T(8,128)(2,1)S(1)} %collective-permute-done.9.own_ref, s16[144,1024]{1,0:T(8,128)(2,1)S(1)} %collective-permute-done.10.other_ref, ...), custom_call_target="tpu_custom_call" | custom-call | flops 1132462080 | bytes 3932160 | tf_op jit(solution)/shard_map/late_angles/pallas_call | solution.py:199
  37.8 0.4 collective-permute-start.12
  38.2 1.0 %collective-permute-done.12 = bf16[64,1024]{1,0:T(8,128)(2,1)S(1)} collective-permute-done((bf16[64,1024]{1,0:T(8,128)(2,1)S(1)}, bf16[64,1024]{1,0:T(8,128)(2,1)S(1)}, u32[]{:S(2)}, u32[]{:S(2)}) %collective-permute-start.12) | collective-permute-done | bytes 131104 | tf_op jit(solution)/shard_map/ppermute | solution.py:55
  39.2 0.4 collective-permute-start.19
  39.6 1.5 %collective-permute-start.13 = (bf16[16,1024]{1,0:T(8,128)(2,1)S(1)}, bf16[16,1024]{1,0:T(8,128)(2,1)S(1)}, u32[]{:S(2)}, u32[]{:S(2)}) collective-permute-start(bf16[16,1024]{1,0:T(8,128)(2,1)S(1)} %get-tuple-element.74), channel_id=1, source_target_pairs={{0,6},{1,7},{2,4},{3,5},{4,2},{5,3},{6,0},{7,1},{8,14},{9,15},{10,... | collective-permute-start | bytes 98312 | tf_op jit(solution)/shard_map/ppermute | solution.py:60
  41.1 1.6 %collective-permute-start.14 = (bf16[16,1024]{1,0:T(8,128)(2,1)S(1)}, bf16[16,1024]{1,0:T(8,128)(2,1)S(1)}, u32[]{:S(2)}, u32[]{:S(2)}) collective-permute-start(bf16[16,1024]{1,0:T(8,128)(2,1)S(1)} %get-tuple-element.76), channel_id=1, source_target_pairs={{0,4},{1,5},{2,6},{3,7},{4,0},{5,1},{6,2},{7,3},{8,12},{9,13},{10,... | collective-permute-start | bytes 98312 | tf_op jit(solution)/shard_map/ppermute | solution.py:60
  42.7 1.3 %collective-permute-start.15 = (bf16[16,1024]{1,0:T(8,128)(2,1)S(1)}, bf16[16,1024]{1,0:T(8,128)(2,1)S(1)}, u32[]{:S(2)}, u32[]{:S(2)}) collective-permute-start(bf16[16,1024]{1,0:T(8,128)(2,1)S(1)} %get-tuple-element.75), channel_id=1, source_target_pairs={{0,2},{1,3},{2,0},{3,1},{4,6},{5,7},{6,4},{7,5},{8,10},{9,11},{10,... | collective-permute-start | bytes 98312 | tf_op jit(solution)/shard_map/ppermute | solution.py:60
  44.4 1.0 collective-permute-done.13
  45.4 0.9 collective-permute-done.14
  46.3 0.4 collective-permute-done.15
  46.7 2.5 %collective-permute-start.16 = (bf16[16,1024]{1,0:T(8,128)(2,1)S(1)}, bf16[16,1024]{1,0:T(8,128)(2,1)S(1)}, u32[]{:S(2)}, u32[]{:S(2)}) collective-permute-start(bf16[16,1024]{1,0:T(8,128)(2,1)S(1)} %fusion.32), channel_id=1, source_target_pairs={{0,6},{1,7},{2,4},{3,5},{4,2},{5,3},{6,0},{7,1},{8,14},{9,15},{10,... | collective-permute-start | bytes 98312 | tf_op jit(solution)/shard_map/ppermute | solution.py:60
  49.5 1.6 %collective-permute-start.18 = (bf16[16,1024]{1,0:T(8,128)(2,1)S(1)}, bf16[16,1024]{1,0:T(8,128)(2,1)S(1)}, u32[]{:S(2)}, u32[]{:S(2)}) collective-permute-start(bf16[16,1024]{1,0:T(8,128)(2,1)S(1)} %fusion.32), channel_id=1, source_target_pairs={{0,2},{1,3},{2,0},{3,1},{4,6},{5,7},{6,4},{7,5},{8,10},{9,11},{10,... | collective-permute-start | bytes 98312 | tf_op jit(solution)/shard_map/ppermute | solution.py:60
  51.2 1.6 %pad_maximum_fusion = bf16[1280,1024]{1,0:T(8,128)(2,1)S(1)} fusion(bf16[640,1024]{1,0:T(8,128)(2,1)} %collective-permute-done.19, bf16[640,1024]{1,0:T(8,128)(2,1)S(1)} %get-tuple-element.45), kind=kLoop, calls=%fused_computation | loop fusion | flops 5242880 | bytes 5242880 | tf_op jit(solution)/shard_map/concatenate | solution.py:335
  52.7 1.3 %collective-permute-done.17 = bf16[16,1024]{1,0:T(8,128)(2,1)S(1)} collective-permute-done((bf16[16,1024]{1,0:T(8,128)(2,1)S(1)}, bf16[16,1024]{1,0:T(8,128)(2,1)S(1)}, u32[]{:S(2)}, u32[]{:S(2)}) %collective-permute-start.17) | collective-permute-done | bytes 32800 | tf_op jit(solution)/shard_map/ppermute | solution.py:60
  54.0 0.9 fusion.47
  55.0 2.5 %collective-permute-start.20 = (bf16[64,1280]{1,0:T(8,128)(2,1)S(1)}, bf16[64,1280]{1,0:T(8,128)(2,1)S(1)}, u32[]{:S(2)}, u32[]{:S(2)}) collective-permute-start(bf16[64,1280]{1,0:T(8,128)(2,1)S(1)} %get-tuple-element.79), channel_id=1, source_target_pairs={{0,24},{8,16},{16,8},{24,0},{1,25},{9,17},{17,9},{25,1},{2,26},{10... | collective-permute-start | bytes 491528 | tf_op jit(solution)/shard_map/ppermute | solution.py:69
  57.5 0.5 collective-permute-start.21
  58.0 0.5 collective-permute-start.22
  58.5 4.3 %collective-permute-done.20 = bf16[64,1280]{1,0:T(8,128)(2,1)S(1)} collective-permute-done((bf16[64,1280]{1,0:T(8,128)(2,1)S(1)}, bf16[64,1280]{1,0:T(8,128)(2,1)S(1)}, u32[]{:S(2)}, u32[]{:S(2)}) %collective-permute-start.20) | collective-permute-done | bytes 163872 | tf_op jit(solution)/shard_map/ppermute | solution.py:69
  62.8 1.0 %collective-permute-done.21 = bf16[64,1280]{1,0:T(8,128)(2,1)S(1)} collective-permute-done((bf16[64,1280]{1,0:T(8,128)(2,1)S(1)}, bf16[64,1280]{1,0:T(8,128)(2,1)S(1)}, u32[]{:S(2)}, u32[]{:S(2)}) %collective-permute-start.21) | collective-permute-done | bytes 163872 | tf_op jit(solution)/shard_map/ppermute | solution.py:69
  64.1 0.6 fusion.48
  64.7 1.6 %collective-permute-start.23 = (bf16[16,1024]{1,0:T(8,128)(2,1)S(1)}, bf16[16,1024]{1,0:T(8,128)(2,1)S(1)}, u32[]{:S(2)}, u32[]{:S(2)}) collective-permute-start(bf16[16,1024]{1,0:T(8,128)(2,1)S(1)} %get-tuple-element.71), channel_id=1, source_target_pairs={{0,6},{1,7},{2,4},{3,5},{4,2},{5,3},{6,0},{7,1},{8,14},{9,15},{10,... | collective-permute-start | bytes 98312 | tf_op jit(solution)/shard_map/ppermute | solution.py:60
  66.3 1.0 %collective-permute-start.24 = (bf16[16,1024]{1,0:T(8,128)(2,1)S(1)}, bf16[16,1024]{1,0:T(8,128)(2,1)S(1)}, u32[]{:S(2)}, u32[]{:S(2)}) collective-permute-start(bf16[16,1024]{1,0:T(8,128)(2,1)S(1)} %get-tuple-element.73), channel_id=1, source_target_pairs={{0,4},{1,5},{2,6},{3,7},{4,0},{5,1},{6,2},{7,3},{8,12},{9,13},{10,... | collective-permute-start | bytes 98312 | tf_op jit(solution)/shard_map/ppermute | solution.py:60
  67.3 1.8 %collective-permute-start.25 = (bf16[16,1024]{1,0:T(8,128)(2,1)S(1)}, bf16[16,1024]{1,0:T(8,128)(2,1)S(1)}, u32[]{:S(2)}, u32[]{:S(2)}) collective-permute-start(bf16[16,1024]{1,0:T(8,128)(2,1)S(1)} %get-tuple-element.72), channel_id=1, source_target_pairs={{0,2},{1,3},{2,0},{3,1},{4,6},{5,7},{6,4},{7,5},{8,10},{9,11},{10,... | collective-permute-start | bytes 98312 | tf_op jit(solution)/shard_map/ppermute | solution.py:60
  69.1 1.3 %collective-permute-done.23 = bf16[16,1024]{1,0:T(8,128)(2,1)S(1)} collective-permute-done((bf16[16,1024]{1,0:T(8,128)(2,1)S(1)}, bf16[16,1024]{1,0:T(8,128)(2,1)S(1)}, u32[]{:S(2)}, u32[]{:S(2)}) %collective-permute-start.23) | collective-permute-done | bytes 32800 | tf_op jit(solution)/shard_map/ppermute | solution.py:60
  70.5 1.1 %collective-permute-done.24 = bf16[16,1024]{1,0:T(8,128)(2,1)S(1)} collective-permute-done((bf16[16,1024]{1,0:T(8,128)(2,1)S(1)}, bf16[16,1024]{1,0:T(8,128)(2,1)S(1)}, u32[]{:S(2)}, u32[]{:S(2)}) %collective-permute-start.24) | collective-permute-done | bytes 32800 | tf_op jit(solution)/shard_map/ppermute | solution.py:60
  71.6 2.3 %collective-permute-start.26 = (bf16[16,1024]{1,0:T(8,128)(2,1)S(1)}, bf16[16,1024]{1,0:T(8,128)(2,1)S(1)}, u32[]{:S(2)}, u32[]{:S(2)}) collective-permute-start(bf16[16,1024]{1,0:T(8,128)(2,1)S(1)} %fusion.33), channel_id=1, source_target_pairs={{0,6},{1,7},{2,4},{3,5},{4,2},{5,3},{6,0},{7,1},{8,14},{9,15},{10,... | collective-permute-start | bytes 98312 | tf_op jit(solution)/shard_map/ppermute | solution.py:60
  73.8 1.1 %collective-permute-start.27 = (bf16[16,1024]{1,0:T(8,128)(2,1)S(1)}, bf16[16,1024]{1,0:T(8,128)(2,1)S(1)}, u32[]{:S(2)}, u32[]{:S(2)}) collective-permute-start(bf16[16,1024]{1,0:T(8,128)(2,1)S(1)} %fusion.33), channel_id=1, source_target_pairs={{0,4},{1,5},{2,6},{3,7},{4,0},{5,1},{6,2},{7,3},{8,12},{9,13},{10,... | collective-permute-start | bytes 98312 | tf_op jit(solution)/shard_map/ppermute | solution.py:60
  75.0 1.0 %collective-permute-start.28 = (bf16[16,1024]{1,0:T(8,128)(2,1)S(1)}, bf16[16,1024]{1,0:T(8,128)(2,1)S(1)}, u32[]{:S(2)}, u32[]{:S(2)}) collective-permute-start(bf16[16,1024]{1,0:T(8,128)(2,1)S(1)} %fusion.33), channel_id=1, source_target_pairs={{0,2},{1,3},{2,0},{3,1},{4,6},{5,7},{6,4},{7,5},{8,10},{9,11},{10,... | collective-permute-start | bytes 98312 | tf_op jit(solution)/shard_map/ppermute | solution.py:60
  76.0 1.3 %collective-permute-done.26 = bf16[16,1024]{1,0:T(8,128)(2,1)S(1)} collective-permute-done((bf16[16,1024]{1,0:T(8,128)(2,1)S(1)}, bf16[16,1024]{1,0:T(8,128)(2,1)S(1)}, u32[]{:S(2)}, u32[]{:S(2)}) %collective-permute-start.26) | collective-permute-done | bytes 32800 | tf_op jit(solution)/shard_map/ppermute | solution.py:60
  77.3 1.3 %collective-permute-done.27 = bf16[16,1024]{1,0:T(8,128)(2,1)S(1)} collective-permute-done((bf16[16,1024]{1,0:T(8,128)(2,1)S(1)}, bf16[16,1024]{1,0:T(8,128)(2,1)S(1)}, u32[]{:S(2)}, u32[]{:S(2)}) %collective-permute-start.27) | collective-permute-done | bytes 32800 | tf_op jit(solution)/shard_map/ppermute | solution.py:60
  78.7 0.3 collective-permute-done.28
  79.0 0.9 fusion.49
  79.9 1.7 %collective-permute-start.29 = (bf16[64,1280]{1,0:T(8,128)(2,1)S(1)}, bf16[64,1280]{1,0:T(8,128)(2,1)S(1)}, u32[]{:S(2)}, u32[]{:S(2)}) collective-permute-start(bf16[64,1280]{1,0:T(8,128)(2,1)S(1)} %get-tuple-element.83), channel_id=1, source_target_pairs={{0,24},{8,16},{16,8},{24,0},{1,25},{9,17},{17,9},{25,1},{2,26},{10... | collective-permute-start | bytes 491528 | tf_op jit(solution)/shard_map/ppermute | solution.py:69
  81.6 1.1 %collective-permute-start.30 = (bf16[64,1280]{1,0:T(8,128)(2,1)S(1)}, bf16[64,1280]{1,0:T(8,128)(2,1)S(1)}, u32[]{:S(2)}, u32[]{:S(2)}) collective-permute-start(bf16[64,1280]{1,0:T(8,128)(2,1)S(1)} %get-tuple-element.83), channel_id=1, source_target_pairs={{0,16},{8,24},{16,0},{24,8},{1,17},{9,25},{17,1},{25,9},{2,18},{10... | collective-permute-start | bytes 491528 | tf_op jit(solution)/shard_map/ppermute | solution.py:69
  82.7 0.8 collective-permute-start.31
  83.5 2.8 %collective-permute-done.29 = bf16[64,1280]{1,0:T(8,128)(2,1)S(1)} collective-permute-done((bf16[64,1280]{1,0:T(8,128)(2,1)S(1)}, bf16[64,1280]{1,0:T(8,128)(2,1)S(1)}, u32[]{:S(2)}, u32[]{:S(2)}) %collective-permute-start.29) | collective-permute-done | bytes 163872 | tf_op jit(solution)/shard_map/ppermute | solution.py:69
  86.3 1.7 %collective-permute-done.30 = bf16[64,1280]{1,0:T(8,128)(2,1)S(1)} collective-permute-done((bf16[64,1280]{1,0:T(8,128)(2,1)S(1)}, bf16[64,1280]{1,0:T(8,128)(2,1)S(1)}, u32[]{:S(2)}, u32[]{:S(2)}) %collective-permute-start.30) | collective-permute-done | bytes 163872 | tf_op jit(solution)/shard_map/ppermute | solution.py:69
  88.2 2.3 %fusion.50 = (bf16[64,1024]{1,0:T(8,128)(2,1)S(1)}, f32[64,1024]{1,0:T(8,128)S(1)}) fusion(bf16[64,1280]{1,0:T(8,128)(2,1)S(1)} %get-tuple-element.50, bf16[1280,1024]{1,0:T(8,128)(2,1)} %copy-done.1), kind=kOutput, calls=%fused_computation.94 | convolution fusion | flops 167837696 | bytes 3178496 | tf_op jit(solution)/shard_map/dot_general | solution.py:50
  90.7 1.9 %collective-permute-start.33 = (bf16[16,1024]{1,0:T(8,128)(2,1)S(1)}, bf16[16,1024]{1,0:T(8,128)(2,1)S(1)}, u32[]{:S(2)}, u32[]{:S(2)}) collective-permute-start(bf16[16,1024]{1,0:T(8,128)(2,1)S(1)} %get-tuple-element.68), channel_id=1, source_target_pairs={{0,6},{1,7},{2,4},{3,5},{4,2},{5,3},{6,0},{7,1},{8,14},{9,15},{10,... | collective-permute-start | bytes 98312 | tf_op jit(solution)/shard_map/ppermute | solution.py:60
  92.6 0.8 collective-permute-start.34
  93.4 1.8 %collective-permute-start.35 = (bf16[16,1024]{1,0:T(8,128)(2,1)S(1)}, bf16[16,1024]{1,0:T(8,128)(2,1)S(1)}, u32[]{:S(2)}, u32[]{:S(2)}) collective-permute-start(bf16[16,1024]{1,0:T(8,128)(2,1)S(1)} %get-tuple-element.69), channel_id=1, source_target_pairs={{0,2},{1,3},{2,0},{3,1},{4,6},{5,7},{6,4},{7,5},{8,10},{9,11},{10,... | collective-permute-start | bytes 98312 | tf_op jit(solution)/shard_map/ppermute | solution.py:60
  95.2 0.6 fusion.17
  95.9 1.0 %collective-permute-done.33 = bf16[16,1024]{1,0:T(8,128)(2,1)S(1)} collective-permute-done((bf16[16,1024]{1,0:T(8,128)(2,1)S(1)}, bf16[16,1024]{1,0:T(8,128)(2,1)S(1)}, u32[]{:S(2)}, u32[]{:S(2)}) %collective-permute-start.33) | collective-permute-done | bytes 32800 | tf_op jit(solution)/shard_map/ppermute | solution.py:60
  96.9 1.0 %collective-permute-done.34 = bf16[16,1024]{1,0:T(8,128)(2,1)S(1)} collective-permute-done((bf16[16,1024]{1,0:T(8,128)(2,1)S(1)}, bf16[16,1024]{1,0:T(8,128)(2,1)S(1)}, u32[]{:S(2)}, u32[]{:S(2)}) %collective-permute-start.34) | collective-permute-done | bytes 32800 | tf_op jit(solution)/shard_map/ppermute | solution.py:60
  97.9 0.7 add_bitcast_fusion
  (62 shorter events, 2.2 us)
Async XLA Ops:
  0.6 43.4 %copy-start = (s32[1024,128]{1,0:T(8,128)S(1)}, s32[1024,128]{1,0:T(8,128)}, u32[]{:S(2)}) copy-start(s32[1024,128]{1,0:T(8,128)} %param.9) | copy-start | bytes 1572868
  0.6 22.2 %copy-start.3 = (f32[640]{0:T(1024)S(1)}, f32[640]{0:T(1024)}, u32[]{:S(2)}) copy-start(f32[640]{0:T(1024)} %param.7) | copy-start | bytes 7684
  1.9 10.4 %collective-permute-start.1 = (s16[144,1024]{1,0:T(8,128)(2,1)S(1)}, s16[144,1024]{1,0:T(8,128)(2,1)S(1)}, u32[]{:S(2)}, u32[]{:S(2)}) collective-permute-start(s16[144,1024]{1,0:T(8,128)(2,1)S(1)} %fusion.refs_0_), channel_id=1, source_target_pairs={{0,4},{1,5},{4,6},{5,7},{6,2},{7,3},{2,0},{3,1},{8,12},{9,13},{12,... | collective-permute-start | bytes 884744 | tf_op jit(solution)/shard_map/ppermute | solution.py:64
  8.1 11.0 %collective-permute-start.2 = (s16[320,640]{1,0:T(8,128)(2,1)S(1)}, s16[320,640]{1,0:T(8,128)(2,1)S(1)}, u32[]{:S(2)}, u32[]{:S(2)}) collective-permute-start(s16[320,640]{1,0:T(8,128)(2,1)S(1)} %pad_add_fusion.refs_6_), channel_id=1, source_target_pairs={{0,8},{8,0},{16,24},{24,16},{1,9},{9,1},{17,25},{25,17},{2,10},{10... | collective-permute-start | bytes 1228808 | tf_op jit(solution)/shard_map/ppermute | solution.py:69
  9.6 11.0 %collective-permute-start.4 = (s16[320,640]{1,0:T(8,128)(2,1)S(1)}, s16[320,640]{1,0:T(8,128)(2,1)S(1)}, u32[]{:S(2)}, u32[]{:S(2)}) collective-permute-start(s16[320,640]{1,0:T(8,128)(2,1)S(1)} %pad_add_fusion.refs_6_), channel_id=1, source_target_pairs={{0,16},{8,24},{16,0},{24,8},{1,17},{9,25},{17,1},{25,9},{2,18},{10... | collective-permute-start | bytes 1228808 | tf_op jit(solution)/shard_map/ppermute | solution.py:69
  12.2 6.8 %collective-permute-start.3 = (s16[144,1024]{1,0:T(8,128)(2,1)S(1)}, s16[144,1024]{1,0:T(8,128)(2,1)S(1)}, u32[]{:S(2)}, u32[]{:S(2)}) collective-permute-start(s16[144,1024]{1,0:T(8,128)(2,1)S(1)} %collective-permute-done.1.refs_2_), channel_id=1, source_target_pairs={{0,1},{1,0},{2,3},{3,2},{4,5},{5,4},{6,7},{7,6},{8,9},{9,8},{10,11... | collective-permute-start | bytes 884744 | tf_op jit(solution)/shard_map/ppermute | solution.py:55
  12.2 15.4 %collective-permute-start = (s16[144,1024]{1,0:T(8,128)(2,1)S(1)}, s16[144,1024]{1,0:T(8,128)(2,1)}, u32[]{:S(2)}, u32[]{:S(2)}) collective-permute-start(s16[144,1024]{1,0:T(8,128)(2,1)S(1)} %fusion.refs_0_), channel_id=1, source_target_pairs={{0,1},{1,0},{2,3},{3,2},{4,5},{5,4},{6,7},{7,6},{8,9},{9,8},{10,11... | collective-permute-start | bytes 884744 | tf_op jit(solution)/shard_map/ppermute | solution.py:55
  12.7 10.4 %collective-permute-start.7 = (s16[144,1024]{1,0:T(8,128)(2,1)S(1)}, s16[144,1024]{1,0:T(8,128)(2,1)S(1)}, u32[]{:S(2)}, u32[]{:S(2)}) collective-permute-start(s16[144,1024]{1,0:T(8,128)(2,1)S(1)} %collective-permute-done.1.refs_2_), channel_id=1, source_target_pairs={{0,4},{1,5},{4,6},{5,7},{6,2},{7,3},{2,0},{3,1},{8,12},{9,13},{12,... | collective-permute-start | bytes 884744 | tf_op jit(solution)/shard_map/ppermute | solution.py:64
  19.1 8.3 %collective-permute-start.5 = (s16[160,640]{1,0:T(8,128)(2,1)S(1)}, s16[160,640]{1,0:T(8,128)(2,1)S(1)}, u32[]{:S(2)}, u32[]{:S(2)}) collective-permute-start(s16[160,640]{1,0:T(8,128)(2,1)S(1)} %slice.101), channel_id=1, source_target_pairs={{0,16},{8,24},{16,0},{24,8},{1,17},{9,25},{17,1},{25,9},{2,18},{10... | collective-permute-start | bytes 614408 | tf_op jit(solution)/shard_map/ppermute | solution.py:69
  21.4 6.0 %collective-permute-start.6 = (s16[160,640]{1,0:T(8,128)(2,1)}, s16[160,640]{1,0:T(8,128)(2,1)S(1)}, u32[]{:S(2)}, u32[]{:S(2)}) collective-permute-start(s16[160,640]{1,0:T(8,128)(2,1)} %slice.102), channel_id=1, source_target_pairs={{0,8},{8,0},{16,24},{24,16},{1,9},{9,1},{17,25},{25,17},{2,10},{10... | collective-permute-start | bytes 614408 | tf_op jit(solution)/shard_map/ppermute | solution.py:69
  23.1 4.5 %collective-permute-start.8 = (s16[144,1024]{1,0:T(8,128)(2,1)S(1)}, s16[144,1024]{1,0:T(8,128)(2,1)S(1)}, u32[]{:S(2)}, u32[]{:S(2)}) collective-permute-start(s16[144,1024]{1,0:T(8,128)(2,1)S(1)} %collective-permute-done.7.refs_4_), channel_id=1, source_target_pairs={{0,1},{1,0},{2,3},{3,2},{4,5},{5,4},{6,7},{7,6},{8,9},{9,8},{10,11... | collective-permute-start | bytes 884744 | tf_op jit(solution)/shard_map/ppermute | solution.py:55
  23.1 10.1 %collective-permute-start.9 = (s16[144,1024]{1,0:T(8,128)(2,1)S(1)}, s16[144,1024]{1,0:T(8,128)(2,1)S(1)}, u32[]{:S(2)}, u32[]{:S(2)}) collective-permute-start(s16[144,1024]{1,0:T(8,128)(2,1)S(1)} %collective-permute-done.7.refs_4_), channel_id=1, source_target_pairs={{0,4},{1,5},{4,6},{5,7},{6,2},{7,3},{2,0},{3,1},{8,12},{9,13},{12,... | collective-permute-start | bytes 884744 | tf_op jit(solution)/shard_map/ppermute | solution.py:64
  27.5 6.4 %collective-permute-start.11 = (s16[64,640]{1,0:T(8,128)(2,1)S(1)}, s16[64,640]{1,0:T(8,128)(2,1)S(1)}, u32[]{:S(2)}, u32[]{:S(2)}) collective-permute-start(s16[64,640]{1,0:T(8,128)(2,1)S(1)} %get-tuple-element.40), channel_id=1, source_target_pairs={{0,1},{1,0},{2,3},{3,2},{4,5},{5,4},{6,7},{7,6},{8,9},{9,8},{10,11... | collective-permute-start | bytes 245768 | tf_op jit(solution)/shard_map/ppermute | solution.py:55
  33.3 1.8 %collective-permute-start.10 = (s16[144,1024]{1,0:T(8,128)(2,1)S(1)}, s16[144,1024]{1,0:T(8,128)(2,1)S(1)}, u32[]{:S(2)}, u32[]{:S(2)}) collective-permute-start(s16[144,1024]{1,0:T(8,128)(2,1)S(1)} %collective-permute-done.9.own_ref), channel_id=1, source_target_pairs={{0,1},{1,0},{2,3},{3,2},{4,5},{5,4},{6,7},{7,6},{8,9},{9,8},{10,11... | collective-permute-start | bytes 884744 | tf_op jit(solution)/shard_map/ppermute | solution.py:55
  37.8 1.4 %collective-permute-start.12 = (bf16[64,1024]{1,0:T(8,128)(2,1)S(1)}, bf16[64,1024]{1,0:T(8,128)(2,1)S(1)}, u32[]{:S(2)}, u32[]{:S(2)}) collective-permute-start(bf16[64,1024]{1,0:T(8,128)(2,1)S(1)} %get-tuple-element.43), channel_id=1, source_target_pairs={{0,1},{1,0},{2,3},{3,2},{4,5},{5,4},{6,7},{7,6},{8,9},{9,8},{10,11... | collective-permute-start | bytes 393224 | tf_op jit(solution)/shard_map/ppermute | solution.py:55
  39.2 12.0 %collective-permute-start.19 = (bf16[640,1024]{1,0:T(8,128)(2,1)S(1)}, bf16[640,1024]{1,0:T(8,128)(2,1)}, u32[]{:S(2)}, u32[]{:S(2)}) collective-permute-start(bf16[640,1024]{1,0:T(8,128)(2,1)S(1)} %get-tuple-element.45), channel_id=1, source_target_pairs={{0,1},{1,0},{2,3},{3,2},{4,5},{5,4},{6,7},{7,6},{8,9},{9,8},{10,11... | collective-permute-start | bytes 3932168 | tf_op jit(solution)/shard_map/ppermute | solution.py:55
  39.6 5.8 %collective-permute-start.13 = (bf16[16,1024]{1,0:T(8,128)(2,1)S(1)}, bf16[16,1024]{1,0:T(8,128)(2,1)S(1)}, u32[]{:S(2)}, u32[]{:S(2)}) collective-permute-start(bf16[16,1024]{1,0:T(8,128)(2,1)S(1)} %get-tuple-element.74), channel_id=1, source_target_pairs={{0,6},{1,7},{2,4},{3,5},{4,2},{5,3},{6,0},{7,1},{8,14},{9,15},{10,... | collective-permute-start | bytes 98312 | tf_op jit(solution)/shard_map/ppermute | solution.py:60
  41.1 5.2 %collective-permute-start.14 = (bf16[16,1024]{1,0:T(8,128)(2,1)S(1)}, bf16[16,1024]{1,0:T(8,128)(2,1)S(1)}, u32[]{:S(2)}, u32[]{:S(2)}) collective-permute-start(bf16[16,1024]{1,0:T(8,128)(2,1)S(1)} %get-tuple-element.76), channel_id=1, source_target_pairs={{0,4},{1,5},{2,6},{3,7},{4,0},{5,1},{6,2},{7,3},{8,12},{9,13},{10,... | collective-permute-start | bytes 98312 | tf_op jit(solution)/shard_map/ppermute | solution.py:60
  42.7 3.9 %collective-permute-start.15 = (bf16[16,1024]{1,0:T(8,128)(2,1)S(1)}, bf16[16,1024]{1,0:T(8,128)(2,1)S(1)}, u32[]{:S(2)}, u32[]{:S(2)}) collective-permute-start(bf16[16,1024]{1,0:T(8,128)(2,1)S(1)} %get-tuple-element.75), channel_id=1, source_target_pairs={{0,2},{1,3},{2,0},{3,1},{4,6},{5,7},{6,4},{7,5},{8,10},{9,11},{10,... | collective-permute-start | bytes 98312 | tf_op jit(solution)/shard_map/ppermute | solution.py:60
  46.7 6.0 %collective-permute-start.16 = (bf16[16,1024]{1,0:T(8,128)(2,1)S(1)}, bf16[16,1024]{1,0:T(8,128)(2,1)S(1)}, u32[]{:S(2)}, u32[]{:S(2)}) collective-permute-start(bf16[16,1024]{1,0:T(8,128)(2,1)S(1)} %fusion.32), channel_id=1, source_target_pairs={{0,6},{1,7},{2,4},{3,5},{4,2},{5,3},{6,0},{7,1},{8,14},{9,15},{10,... | collective-permute-start | bytes 98312 | tf_op jit(solution)/shard_map/ppermute | solution.py:60
  49.2 4.8 %collective-permute-start.17 = (bf16[16,1024]{1,0:T(8,128)(2,1)S(1)}, bf16[16,1024]{1,0:T(8,128)(2,1)S(1)}, u32[]{:S(2)}, u32[]{:S(2)}) collective-permute-start(bf16[16,1024]{1,0:T(8,128)(2,1)S(1)} %fusion.32), channel_id=1, source_target_pairs={{0,4},{1,5},{2,6},{3,7},{4,0},{5,1},{6,2},{7,3},{8,12},{9,13},{10,... | collective-permute-start | bytes 98312 | tf_op jit(solution)/shard_map/ppermute | solution.py:60
  49.5 4.5 %collective-permute-start.18 = (bf16[16,1024]{1,0:T(8,128)(2,1)S(1)}, bf16[16,1024]{1,0:T(8,128)(2,1)S(1)}, u32[]{:S(2)}, u32[]{:S(2)}) collective-permute-start(bf16[16,1024]{1,0:T(8,128)(2,1)S(1)} %fusion.32), channel_id=1, source_target_pairs={{0,2},{1,3},{2,0},{3,1},{4,6},{5,7},{6,4},{7,5},{8,10},{9,11},{10,... | collective-permute-start | bytes 98312 | tf_op jit(solution)/shard_map/ppermute | solution.py:60
  52.7 26.3 %copy-start.1 = (bf16[1280,1024]{1,0:T(8,128)(2,1)}, bf16[1280,1024]{1,0:T(8,128)(2,1)S(1)}, u32[]{:S(2)}) copy-start(bf16[1280,1024]{1,0:T(8,128)(2,1)S(1)} %pad_maximum_fusion) | copy-start | bytes 7864324
  55.0 7.9 %collective-permute-start.20 = (bf16[64,1280]{1,0:T(8,128)(2,1)S(1)}, bf16[64,1280]{1,0:T(8,128)(2,1)S(1)}, u32[]{:S(2)}, u32[]{:S(2)}) collective-permute-start(bf16[64,1280]{1,0:T(8,128)(2,1)S(1)} %get-tuple-element.79), channel_id=1, source_target_pairs={{0,24},{8,16},{16,8},{24,0},{1,25},{9,17},{17,9},{25,1},{2,26},{10... | collective-permute-start | bytes 491528 | tf_op jit(solution)/shard_map/ppermute | solution.py:69
  57.5 6.4 %collective-permute-start.21 = (bf16[64,1280]{1,0:T(8,128)(2,1)S(1)}, bf16[64,1280]{1,0:T(8,128)(2,1)S(1)}, u32[]{:S(2)}, u32[]{:S(2)}) collective-permute-start(bf16[64,1280]{1,0:T(8,128)(2,1)S(1)} %get-tuple-element.79), channel_id=1, source_target_pairs={{0,16},{8,24},{16,0},{24,8},{1,17},{9,25},{17,1},{25,9},{2,18},{10... | collective-permute-start | bytes 491528 | tf_op jit(solution)/shard_map/ppermute | solution.py:69
  58.0 6.0 %collective-permute-start.22 = (bf16[64,1280]{1,0:T(8,128)(2,1)S(1)}, bf16[64,1280]{1,0:T(8,128)(2,1)S(1)}, u32[]{:S(2)}, u32[]{:S(2)}) collective-permute-start(bf16[64,1280]{1,0:T(8,128)(2,1)S(1)} %get-tuple-element.79), channel_id=1, source_target_pairs={{0,8},{8,0},{16,24},{24,16},{1,9},{9,1},{17,25},{25,17},{2,10},{10... | collective-permute-start | bytes 491528 | tf_op jit(solution)/shard_map/ppermute | solution.py:69
  64.7 5.8 %collective-permute-start.23 = (bf16[16,1024]{1,0:T(8,128)(2,1)S(1)}, bf16[16,1024]{1,0:T(8,128)(2,1)S(1)}, u32[]{:S(2)}, u32[]{:S(2)}) collective-permute-start(bf16[16,1024]{1,0:T(8,128)(2,1)S(1)} %get-tuple-element.71), channel_id=1, source_target_pairs={{0,6},{1,7},{2,4},{3,5},{4,2},{5,3},{6,0},{7,1},{8,14},{9,15},{10,... | collective-permute-start | bytes 98312 | tf_op jit(solution)/shard_map/ppermute | solution.py:60
  66.3 5.2 %collective-permute-start.24 = (bf16[16,1024]{1,0:T(8,128)(2,1)S(1)}, bf16[16,1024]{1,0:T(8,128)(2,1)S(1)}, u32[]{:S(2)}, u32[]{:S(2)}) collective-permute-start(bf16[16,1024]{1,0:T(8,128)(2,1)S(1)} %get-tuple-element.73), channel_id=1, source_target_pairs={{0,4},{1,5},{2,6},{3,7},{4,0},{5,1},{6,2},{7,3},{8,12},{9,13},{10,... | collective-permute-start | bytes 98312 | tf_op jit(solution)/shard_map/ppermute | solution.py:60
  67.3 4.2 %collective-permute-start.25 = (bf16[16,1024]{1,0:T(8,128)(2,1)S(1)}, bf16[16,1024]{1,0:T(8,128)(2,1)S(1)}, u32[]{:S(2)}, u32[]{:S(2)}) collective-permute-start(bf16[16,1024]{1,0:T(8,128)(2,1)S(1)} %get-tuple-element.72), channel_id=1, source_target_pairs={{0,2},{1,3},{2,0},{3,1},{4,6},{5,7},{6,4},{7,5},{8,10},{9,11},{10,... | collective-permute-start | bytes 98312 | tf_op jit(solution)/shard_map/ppermute | solution.py:60
  71.6 5.8 %collective-permute-start.26 = (bf16[16,1024]{1,0:T(8,128)(2,1)S(1)}, bf16[16,1024]{1,0:T(8,128)(2,1)S(1)}, u32[]{:S(2)}, u32[]{:S(2)}) collective-permute-start(bf16[16,1024]{1,0:T(8,128)(2,1)S(1)} %fusion.33), channel_id=1, source_target_pairs={{0,6},{1,7},{2,4},{3,5},{4,2},{5,3},{6,0},{7,1},{8,14},{9,15},{10,... | collective-permute-start | bytes 98312 | tf_op jit(solution)/shard_map/ppermute | solution.py:60
  73.8 4.8 %collective-permute-start.27 = (bf16[16,1024]{1,0:T(8,128)(2,1)S(1)}, bf16[16,1024]{1,0:T(8,128)(2,1)S(1)}, u32[]{:S(2)}, u32[]{:S(2)}) collective-permute-start(bf16[16,1024]{1,0:T(8,128)(2,1)S(1)} %fusion.33), channel_id=1, source_target_pairs={{0,4},{1,5},{2,6},{3,7},{4,0},{5,1},{6,2},{7,3},{8,12},{9,13},{10,... | collective-permute-start | bytes 98312 | tf_op jit(solution)/shard_map/ppermute | solution.py:60
  75.0 4.0 %collective-permute-start.28 = (bf16[16,1024]{1,0:T(8,128)(2,1)S(1)}, bf16[16,1024]{1,0:T(8,128)(2,1)S(1)}, u32[]{:S(2)}, u32[]{:S(2)}) collective-permute-start(bf16[16,1024]{1,0:T(8,128)(2,1)S(1)} %fusion.33), channel_id=1, source_target_pairs={{0,2},{1,3},{2,0},{3,1},{4,6},{5,7},{6,4},{7,5},{8,10},{9,11},{10,... | collective-permute-start | bytes 98312 | tf_op jit(solution)/shard_map/ppermute | solution.py:60
  79.9 6.4 %collective-permute-start.29 = (bf16[64,1280]{1,0:T(8,128)(2,1)S(1)}, bf16[64,1280]{1,0:T(8,128)(2,1)S(1)}, u32[]{:S(2)}, u32[]{:S(2)}) collective-permute-start(bf16[64,1280]{1,0:T(8,128)(2,1)S(1)} %get-tuple-element.83), channel_id=1, source_target_pairs={{0,24},{8,16},{16,8},{24,0},{1,25},{9,17},{17,9},{25,1},{2,26},{10... | collective-permute-start | bytes 491528 | tf_op jit(solution)/shard_map/ppermute | solution.py:69
  81.6 6.3 %collective-permute-start.30 = (bf16[64,1280]{1,0:T(8,128)(2,1)S(1)}, bf16[64,1280]{1,0:T(8,128)(2,1)S(1)}, u32[]{:S(2)}, u32[]{:S(2)}) collective-permute-start(bf16[64,1280]{1,0:T(8,128)(2,1)S(1)} %get-tuple-element.83), channel_id=1, source_target_pairs={{0,16},{8,24},{16,0},{24,8},{1,17},{9,25},{17,1},{25,9},{2,18},{10... | collective-permute-start | bytes 491528 | tf_op jit(solution)/shard_map/ppermute | solution.py:69
  82.7 5.3 %collective-permute-start.31 = (bf16[64,1280]{1,0:T(8,128)(2,1)S(1)}, bf16[64,1280]{1,0:T(8,128)(2,1)S(1)}, u32[]{:S(2)}, u32[]{:S(2)}) collective-permute-start(bf16[64,1280]{1,0:T(8,128)(2,1)S(1)} %get-tuple-element.83), channel_id=1, source_target_pairs={{0,8},{8,0},{16,24},{24,16},{1,9},{9,1},{17,25},{25,17},{2,10},{10... | collective-permute-start | bytes 491528 | tf_op jit(solution)/shard_map/ppermute | solution.py:69
  88.2 7.0 %copy-start.2 = (f32[640,32]{0,1:T(8,128)S(1)}, f32[640,32]{0,1:T(8,128)}, u32[]{:S(2)}) copy-start(f32[640,32]{0,1:T(8,128)} %param.8) | copy-start | bytes 245764
  90.6 4.6 %collective-permute-start.32 = (f32[64,640]{1,0:T(8,128)S(1)}, f32[64,640]{1,0:T(8,128)S(1)}, u32[]{:S(2)}, u32[]{:S(2)}) collective-permute-start(f32[64,640]{1,0:T(8,128)S(1)} %get-tuple-element.59), channel_id=1, source_target_pairs={{0,1},{1,0},{2,3},{3,2},{4,5},{5,4},{6,7},{7,6},{8,9},{9,8},{10,11... | collective-permute-start | bytes 491528 | tf_op jit(solution)/shard_map/ppermute | solution.py:55
  90.7 6.2 %collective-permute-start.33 = (bf16[16,1024]{1,0:T(8,128)(2,1)S(1)}, bf16[16,1024]{1,0:T(8,128)(2,1)S(1)}, u32[]{:S(2)}, u32[]{:S(2)}) collective-permute-start(bf16[16,1024]{1,0:T(8,128)(2,1)S(1)} %get-tuple-element.68), channel_id=1, source_target_pairs={{0,6},{1,7},{2,4},{3,5},{4,2},{5,3},{6,0},{7,1},{8,14},{9,15},{10,... | collective-permute-start | bytes 98312 | tf_op jit(solution)/shard_map/ppermute | solution.py:60
  92.6 5.3 %collective-permute-start.34 = (bf16[16,1024]{1,0:T(8,128)(2,1)S(1)}, bf16[16,1024]{1,0:T(8,128)(2,1)S(1)}, u32[]{:S(2)}, u32[]{:S(2)}) collective-permute-start(bf16[16,1024]{1,0:T(8,128)(2,1)S(1)} %get-tuple-element.70), channel_id=1, source_target_pairs={{0,4},{1,5},{2,6},{3,7},{4,0},{5,1},{6,2},{7,3},{8,12},{9,13},{10,... | collective-permute-start | bytes 98312 | tf_op jit(solution)/shard_map/ppermute | solution.py:60
  93.4 4.5 %collective-permute-start.35 = (bf16[16,1024]{1,0:T(8,128)(2,1)S(1)}, bf16[16,1024]{1,0:T(8,128)(2,1)S(1)}, u32[]{:S(2)}, u32[]{:S(2)}) collective-permute-start(bf16[16,1024]{1,0:T(8,128)(2,1)S(1)} %get-tuple-element.69), channel_id=1, source_target_pairs={{0,2},{1,3},{2,0},{3,1},{4,6},{5,7},{6,4},{7,5},{8,10},{9,11},{10,... | collective-permute-start | bytes 98312 | tf_op jit(solution)/shard_map/ppermute | solution.py:60
